TPU v7x, 128 devices: a whole 4x4x4 slice. The times are simulated.
128 devices in a mesh: grp: 2 (over core), dp: 16 (over z, x), mp: 4 (over y).
Axes of the slice: x: 4, y: 4, z: 4, core: 2. Of those that a mesh axis runs over, the one named last changes fastest.
Arguments:
- hidden: bfloat16 [4096, 5120], P(('dp', 'mp')), may hold values from -6 to 6
- enc_weight: bfloat16 [5120, 8192], P(None, 'mp'), may hold values from -0.078125 to 0.078125
- enc_bias: bfloat16 [8192], P('mp'), may hold values from -5 to 5
- enc_frozen: bfloat16 [5120, 64], replicated, may hold values from -0.078125 to 0.078125
- enc_adapter: bfloat16 [64, 8192], P(None, 'mp'), may hold values from -0.75 to 0.75
- text_rows: bfloat16 [10240, 8192], P(('dp', 'mp')), may hold values from -6 to 6
- norm_gain: bfloat16 [8192], replicated, may hold values from 0.5 to 1.5
- value_weight: bfloat16 [8192, 1024], P(('dp', 'mp')), may hold values from -0.0625 to 0.0625
- value_bias: bfloat16 [1024], replicated, may hold values from -5 to 5
- llm_frozen: bfloat16 [8192, 64], P(('dp', 'mp')), may hold values from -0.0625 to 0.0625
- llm_adapter: bfloat16 [64, 1024], replicated, may hold values from -0.75 to 0.75
- targets: bfloat16 [10240, 1024], P(('dp', 'mp')), may hold values from -6 to 6
- dest_owner: int32 [4096, 1], replicated, may hold values from 0 to 63; in each aligned block of 256 rows (0 to 255, 256 to 511, ...) at most 8 rows name the same one
- seq_length: int32 [64], P(('dp', 'mp')), may hold values from 128 to 160
Outputs:
- grad_enc: float32 [64, 8192], P('grp', 'mp')
- grad_llm: float32 [64, 1024], P('grp')
Inputs may be any that keep to these rules, and one draw needn't show every extreme that they name: `dest_owner`: within the tokens of one encoder block (aligned blocks of 256 rows) no LLM device is named more than 8 times, and some device is named exactly 8 times in some blocks.
All inputs are finite; a program needn't handle non-finite values.
Results may differ from a plain program's by a relative error of at most 0.003.
Values may be sent and summed in bfloat16 or wider, within the bound.
No kernel may reach another device: no remote copies, remote signals or barrier semaphores. Data moves between devices by JAX's collectives and lax.ppermute only.
A program may use at most 128 MiB of HBM per device.

v0:
```python
import jax
import jax.numpy as jnp
from jax import lax
from jax.sharding import PartitionSpec as P

ENC_DEV = 256


epsilon = 1e-06


def joined_along(parts, dim):
    parts = jnp.moveaxis(parts, 0, dim)
    lengths = parts.shape
    return parts.reshape(*lengths[:dim], lengths[dim] * lengths[dim + 1], *lengths[dim + 2 :])


def from_everyone(array, axis):
    devices = lax.axis_size(axis)
    return lax.all_to_all(
        jnp.broadcast_to(array[None], (devices, *array.shape)), axis, 0, 0, tiled=True
    )


def gathered_copies(array, axis, dim):
    return joined_along(from_everyone(array, axis), dim)


def passed_along(value, axis, steps):
    count = lax.axis_size(axis)
    first, last = (max(0, -steps), min(count, count - steps))
    return lax.ppermute(value, axis, [(source, source + steps) for source in range(first, last)])


def sent_together(arrays, axis, dim, along):
    ends, at = ([], 0)
    for a in arrays[:-1]:
        at += a.shape[along]
        ends.append(at)
    both = jnp.concatenate(arrays, axis=along)
    return tuple(jnp.split(lax.all_gather(both, axis, axis=dim, tiled=True), ends, axis=along))


def rows_for(lines, devices):
    spare = -lines.shape[0] % devices
    if not spare:
        return lines
    return jnp.concatenate([lines, jnp.zeros((spare, *lines.shape[1:]), lines.dtype)])


def split_up(array, dim, devices):
    lengths = array.shape
    parts = array.reshape(*lengths[:dim], devices, lengths[dim] // devices, *lengths[dim + 1 :])
    return jnp.moveaxis(parts, dim, 0)


def summed_on_arrival(array, axis, dim):
    devices = lax.axis_size(axis)
    parts = lax.all_to_all(split_up(array, dim, devices), axis, 0, 0, tiled=True)
    return jnp.sum(parts, axis=0)


def nested_sum(array, axes):
    lines = array.reshape(-1, array.shape[-1])
    padded = rows_for(lines, lax.axis_size(axes))
    whole = gathered_copies(summed_on_arrival(padded, axes, 0), axes, 0)
    return lax.slice_in_dim(whole, 0, len(lines)).reshape(array.shape)


def swapped(array, axis, bit):
    return lax.ppermute(array, axis, [(i, i ^ 1 << bit) for i in range(lax.axis_size(axis))])


def slot_ranks(destiny, owners):
    markers = (destiny[:, None] == jnp.arange(owners, dtype=jnp.int32)[None, :]).astype(jnp.int32)
    return jnp.sum((jnp.cumsum(markers, axis=0) - markers) * markers, axis=1)


def body(
    hidden,
    enc_weight,
    enc_bias,
    enc_frozen,
    enc_adapter,
    text_rows,
    norm_gain,
    value_weight,
    value_bias,
    llm_frozen,
    llm_adapter,
    targets,
    dest_owner,
    seq_length,
):
    data_ways = lax.axis_size("dp")
    model_ways = lax.axis_size("mp")
    owners = data_ways * model_ways
    capacity = 2 * ENC_DEV // owners
    area = capacity * data_ways
    encoder = lax.axis_index("grp") == 0
    data_index = lax.axis_index("dp")
    owner_index = data_index * model_ways + lax.axis_index("mp")
    part_width = enc_weight.shape[1]
    rank_width = enc_frozen.shape[1]
    kv_width = llm_adapter.shape[1]
    group_rows = gathered_copies(hidden, "mp", 0)

    def encode(source):
        low_rank = jnp.dot(source, enc_frozen, preferred_element_type=jnp.float32).astype(
            jnp.bfloat16
        )
        merged = jnp.dot(source, enc_weight, preferred_element_type=jnp.float32) + enc_bias.astype(
            jnp.float32
        )
        merged = merged + jnp.dot(low_rank, enc_adapter, preferred_element_type=jnp.float32)
        return (merged.astype(jnp.bfloat16), low_rank)

    def rest_encode(source):
        return (
            jnp.zeros((source.shape[0], part_width), jnp.bfloat16),
            jnp.zeros((source.shape[0], rank_width), jnp.bfloat16),
        )

    merged_rows, enc_low = lax.cond(encoder, encode, rest_encode, group_rows)
    destiny = dest_owner[:, 0]
    own_dest = lax.dynamic_slice_in_dim(destiny, data_index * ENC_DEV, ENC_DEV)
    bucket_index = slot_ranks(own_dest, owners) * owners + own_dest
    outgoing = (
        jnp.zeros((capacity * owners, part_width), jnp.bfloat16).at[bucket_index].set(merged_rows)
    )
    outgoing = outgoing.reshape(capacity, owners, part_width)
    grouped = lax.all_to_all(outgoing, ("dp", "mp"), split_axis=1, concat_axis=1, tiled=True)
    arrived = passed_along(grouped, "grp", 1)
    counts = jnp.sum((destiny.reshape(data_ways, ENC_DEV) == owner_index).astype(jnp.int32), axis=1)
    usable = (jnp.arange(capacity, dtype=jnp.int32)[:, None] < counts[None, :]).reshape(area, 1)
    gathered = sent_together((value_weight, llm_frozen), ("dp", "mp"), 0, 1)

    def learn_layer(operands):
        incoming, whole_value, whole_frozen = operands
        image_rows = incoming.reshape(area, -1)
        head_rows = jnp.where(usable, image_rows, text_rows[:area])
        all_rows = jnp.concatenate([head_rows, text_rows[area:]], axis=0)
        wide_rows = all_rows.astype(jnp.float32)
        inverse = lax.rsqrt(jnp.mean(wide_rows * wide_rows, axis=1, keepdims=True) + epsilon)
        gain_wide = norm_gain.astype(jnp.float32)
        normed = (wide_rows * inverse * gain_wide).astype(jnp.bfloat16)
        low_rank = jnp.dot(normed, whole_frozen, preferred_element_type=jnp.float32).astype(
            jnp.bfloat16
        )
        values_out = jnp.dot(
            normed, whole_value, preferred_element_type=jnp.float32
        ) + value_bias.astype(jnp.float32)
        values_out = values_out + jnp.dot(low_rank, llm_adapter, preferred_element_type=jnp.float32)
        length = seq_length[0]
        position = jnp.arange(all_rows.shape[0], dtype=jnp.int32)
        row_weight = jnp.where(position < length, 1.0 / length.astype(jnp.float32), 0.0)
        dvalues = ((values_out - targets.astype(jnp.float32)) * row_weight[:, None]).astype(
            jnp.bfloat16
        )
        grad_part = jnp.dot(low_rank.T, dvalues, preferred_element_type=jnp.float32)
        head_dv = dvalues[:area]
        low_grad = jnp.dot(head_dv, llm_adapter.T, preferred_element_type=jnp.float32).astype(
            jnp.bfloat16
        )
        dnormed = jnp.dot(head_dv, whole_value.T, preferred_element_type=jnp.float32)
        dnormed = dnormed + jnp.dot(low_grad, whole_frozen.T, preferred_element_type=jnp.float32)
        scaled = gain_wide * dnormed
        head_wide = wide_rows[:area]
        head_inverse = inverse[:area]
        cubed = head_inverse * head_inverse * head_inverse
        image_grad = head_inverse * scaled - head_wide * cubed * jnp.mean(
            scaled * head_wide, axis=1, keepdims=True
        )
        image_grad = image_grad.astype(jnp.bfloat16)
        reply_rows = jnp.where(usable, image_grad, jnp.zeros_like(image_grad))
        return (grad_part, reply_rows.reshape(capacity, owners, part_width))

    def rest_learn(operands):
        return (
            jnp.zeros((rank_width, kv_width), jnp.float32),
            jnp.zeros((capacity, owners, part_width), jnp.bfloat16),
        )

    llm_part, reply_rows = lax.cond(
        encoder, rest_learn, learn_layer, (arrived, gathered[0], gathered[1])
    )
    llm_total = nested_sum(llm_part, ("dp", "mp"))
    grouped_back = lax.all_to_all(reply_rows, ("dp", "mp"), split_axis=1, concat_axis=1, tiled=True)
    returned = passed_along(grouped_back, "grp", -1)

    def adapt_grad(operands):
        back_rows, low_rank = operands
        image_grad = back_rows.reshape(capacity * owners, part_width)[bucket_index]
        return jnp.dot(low_rank.T, image_grad, preferred_element_type=jnp.float32)

    def rest_adapt(operands):
        return jnp.zeros((rank_width, part_width), jnp.float32)

    enc_part = lax.cond(encoder, adapt_grad, rest_adapt, (returned, enc_low))
    enc_total = nested_sum(enc_part, "dp")
    half_rank = rank_width // 2
    enc_count = half_rank * part_width
    llm_count = half_rank * kv_width
    span = max(enc_count, llm_count)
    enc_upper = enc_total[half_rank:].reshape(-1)
    llm_lower = jnp.pad(llm_total[:half_rank].reshape(-1), (0, span - llm_count))
    sending = jnp.where(encoder, enc_upper, llm_lower)
    received = swapped(sending, "grp", 0)
    grad_enc = jnp.where(encoder, enc_total[:half_rank], received.reshape(half_rank, part_width))
    grad_llm = jnp.where(
        encoder, received[:llm_count].reshape(half_rank, kv_width), llm_total[half_rank:]
    )
    return (grad_enc, grad_llm)


def solution(mesh):
    return jax.shard_map(
        body,
        mesh=mesh,
        in_specs=(
            P(("dp", "mp"), None),
            P(None, "mp"),
            P("mp"),
            P(),
            P(None, "mp"),
            P(("dp", "mp"), None),
            P(),
            P(("dp", "mp"), None),
            P(),
            P(("dp", "mp"), None),
            P(),
            P(("dp", "mp"), None),
            P(),
            P(("dp", "mp")),
        ),
        out_specs=(P("grp", "mp"), P("grp", None)),
        check_vma=False,
    )
```

profile of v0, /device:TPU:0, one launch (start us, length us, event | category | flops | bytes accessed | tf_op | source)
XLA Modules:
  0.0 300.4 jit_solution(5743155375363100392)
XLA Ops:
  8.0 1.7 pad_maximum_fusion
  9.8 2.9 broadcast_in_dim.37
  12.7 4.7 %all-to-all-start = ((bf16[4,64,5120]{2,1,0:T(8,128)(2,1)}), bf16[4,64,5120]{2,1,0:T(8,128)(2,1)S(1)}, u32[]{:S(2)}, u32[]{:S(2)}) async-start(bf16[4,64,5120]{2,1,0:T(8,128)(2,1)} %broadcast_in_dim.37), calls=%async_computation | async-start | bytes 5242880 | tf_op jit(solution)/shard_map/all_to_all | solution.py:20
  18.9 37.7 %all-to-all-done = bf16[4,64,5120]{2,1,0:T(8,128)(2,1)S(1)} async-done(((bf16[4,64,5120]{2,1,0:T(8,128)(2,1)}), bf16[4,64,5120]{2,1,0:T(8,128)(2,1)S(1)}, u32[]{:S(2)}, u32[]{:S(2)}) %all-to-all-start) | async-done | bytes 2621472 | tf_op jit(solution)/shard_map/all_to_all | solution.py:20
  56.6 13.9 %conditional.3 = (bf16[256,2048]{1,0:T(8,128)(2,1)S(1)}, bf16[256,64]{0,1:T(8,128)(2,1)}) conditional(s32[]{:T(128)} %convert_element_type.60, () %tuple.31, (bf16[4,64,5120]{2,1,0:T(8,128)(2,1)S(1)}, bf16[5120,2048]{1,0:T(8,128)(2,1)}, bf16[2048]{0:T(1024)(128)(2,1)}, bf16[5120,64]{0,1:T(8,128)(2,1)S(1)}, bf16[64,2048]{1,0:T(8,128)(2,1)}) %tuple.61), branch_computations={%region_3.4_spmd, %region_4.5_spmd} | conditional | flops 5605181440 | bytes 33509420 | solution.py:124
  57.4 1.5 convolution_convert_fusion
  60.1 10.4 %fusion.1 = bf16[256,2048]{1,0:T(8,128)(2,1)S(1)} fusion(f32[256,2048]{1,0:T(8,128)S(1)} %fusion.34, bf16[256,5120]{1,0:T(8,128)(2,1)S(1)} %bitcast.55, bf16[5120,2048]{1,0:T(8,128)(2,1)} %get-tuple-element.88, f32[2048]{0:T(1024)S(1)} %convert_element_type.42), kind=kOutput, calls=%fused_computation.4 | convolution fusion | flops 5370281984 | bytes 26746880 | tf_op jit(solution)/shard_map/cond/branch_1_fun/dot_general | solution.py:112
  71.5 3.5 %scatter_custom_fusion = bf16[512,2048]{1,0:T(8,128)(2,1)S(1)} fusion(s32[256]{0:T(256)} %bitcast.63, bf16[256,2048]{1,0:T(8,128)(2,1)} %copy-done.1, bf16[]{:T(256)} %constant.56.clone.1), kind=kCustom, calls=%fused_computation.42 | custom fusion | bytes 2097664 | tf_op jit(solution)/shard_map/scatter | solution.py:129
  76.3 52.7 %all_to_all.35 = bf16[8,64,2048]{2,0,1:T(8,128)(2,1)} all-to-all(bf16[8,64,2048]{2,0,1:T(8,128)(2,1)S(1)} %copy.48), channel_id=1, replica_groups=mesh['grp'=2,'dp'=16,'mp'=4] {'dp','mp'}, dimensions={1} | all-to-all | bytes 4194304 | tf_op jit(solution)/shard_map/all_to_all | solution.py:132
  129.0 1.4 collective-permute-start
  130.4 3.8 %collective-permute-done = bf16[8,64,2048]{2,0,1:T(8,128)(2,1)S(1)} collective-permute-done((bf16[8,64,2048]{2,0,1:T(8,128)(2,1)}, bf16[8,64,2048]{2,0,1:T(8,128)(2,1)S(1)}, u32[]{:S(2)}, u32[]{:S(2)}) %collective-permute-start) | collective-permute-done | bytes 2097184 | tf_op jit(solution)/shard_map/ppermute | solution.py:32
  134.2 13.8 %all-gather.2.cloned.1.call-done = bf16[8192,1088]{1,0:T(8,128)(2,1)} async-done(((bf16[128,1088]{1,0:T(8,128)(2,1)}), bf16[8192,1088]{1,0:T(8,128)(2,1)}) %all-gather.2.cloned.1.call-update) | async-done | bytes 17825808 | tf_op jit(solution)/shard_map/all_gather | solution.py:41
  150.0 27.1 %all_to_all.36 = bf16[8,64,2048]{2,0,1:T(8,128)(2,1)} all-to-all(bf16[8,64,2048]{2,0,1:T(8,128)(2,1)S(1)} %copy.51), channel_id=1, replica_groups=mesh['grp'=2,'dp'=16,'mp'=4] {'dp','mp'}, dimensions={1} | all-to-all | bytes 4194304 | tf_op jit(solution)/shard_map/all_to_all | solution.py:188
  179.2 5.4 %all-to-all-start.5 = ((f32[64,1,1024]{2,1,0:T(1,128)}), f32[64,1,1024]{2,1,0:T(1,128)S(1)}, u32[]{:S(2)}, u32[]{:S(2)}) async-start(f32[64,1,1024]{2,1,0:T(1,128)} %reshape.147), calls=%async_computation.5 | async-start | bytes 524288 | tf_op jit(solution)/shard_map/all_to_all | solution.py:59
  184.7 50.4 %collective-permute-done.1 = bf16[8,64,2048]{2,0,1:T(8,128)(2,1)S(1)} collective-permute-done((bf16[8,64,2048]{2,0,1:T(8,128)(2,1)}, bf16[8,64,2048]{2,0,1:T(8,128)(2,1)S(1)}, u32[]{:S(2)}, u32[]{:S(2)}) %collective-permute-start.1) | collective-permute-done | bytes 2097184 | tf_op jit(solution)/shard_map/ppermute | solution.py:32
  235.1 6.5 %conditional.5 = (f32[64,2048]{1,0:T(8,128)S(1)}) conditional(s32[]{:T(128)} %convert_element_type.60, () %tuple.30, (bf16[8,64,2048]{2,0,1:T(8,128)(2,1)S(1)}, s32[256]{0:T(256)S(1)}, s32[256]{0:T(256)S(1)}, bf16[256,64]{0,1:T(8,128)(2,1)}) %tuple.67), branch_computations={%region_11.12_spmd, %region_12.13_spmd} | conditional | flops 67111168 | bytes 16294948 | solution.py:199
  236.4 2.7 copy.52
  239.2 1.4 gather_fusion
  242.6 3.8 %all-to-all-start.3 = ((f32[16,4,2048]{2,1,0:T(4,128)}), f32[16,4,2048]{2,1,0:T(4,128)S(1)}, u32[]{:S(2)}, u32[]{:S(2)}) async-start(f32[16,4,2048]{2,1,0:T(4,128)} %reshape.145), calls=%async_computation.3 | async-start | bytes 1048576 | tf_op jit(solution)/shard_map/all_to_all | solution.py:59
  246.5 10.2 %all-to-all-done.3 = f32[16,4,2048]{2,1,0:T(4,128)S(1)} async-done(((f32[16,4,2048]{2,1,0:T(4,128)}), f32[16,4,2048]{2,1,0:T(4,128)S(1)}, u32[]{:S(2)}, u32[]{:S(2)}) %all-to-all-start.3) | async-done | bytes 524320 | tf_op jit(solution)/shard_map/all_to_all | solution.py:59
  257.5 4.9 %all-to-all-start.6 = ((f32[64,1,1024]{2,1,0:T(1,128)}), f32[64,1,1024]{2,1,0:T(1,128)S(1)}, u32[]{:S(2)}, u32[]{:S(2)}) async-start(f32[64,1,1024]{2,1,0:T(1,128)} %broadcast_in_dim.40), calls=%async_computation.6 | async-start | bytes 524288 | tf_op jit(solution)/shard_map/all_to_all | solution.py:20
  262.6 10.5 %all-to-all-done.6 = f32[64,1,1024]{2,1,0:T(1,128)S(1)} async-done(((f32[64,1,1024]{2,1,0:T(1,128)}), f32[64,1,1024]{2,1,0:T(1,128)S(1)}, u32[]{:S(2)}, u32[]{:S(2)}) %all-to-all-start.6) | async-done | bytes 262176 | tf_op jit(solution)/shard_map/all_to_all | solution.py:20
  274.0 3.6 %all-to-all-start.4 = ((f32[16,4,2048]{2,1,0:T(4,128)}), f32[16,4,2048]{2,1,0:T(4,128)S(1)}, u32[]{:S(2)}, u32[]{:S(2)}) async-start(f32[16,4,2048]{2,1,0:T(4,128)} %broadcast_in_dim.38), calls=%async_computation.4 | async-start | bytes 1048576 | tf_op jit(solution)/shard_map/all_to_all | solution.py:20
  277.6 12.8 %all-to-all-done.4 = f32[16,4,2048]{2,1,0:T(4,128)S(1)} async-done(((f32[16,4,2048]{2,1,0:T(4,128)}), f32[16,4,2048]{2,1,0:T(4,128)S(1)}, u32[]{:S(2)}, u32[]{:S(2)}) %all-to-all-start.4) | async-done | bytes 524320 | tf_op jit(solution)/shard_map/all_to_all | solution.py:20
  (69 shorter events, 19.4 us)
Async XLA Ops:
  7.2 140.9 %all-gather.2.cloned.1.call-start = ((), (), s32[]{:S(2)}) async-start(), calls=%async_computation.7 | async-start | bytes 19169280 | tf_op jit(solution)/shard_map/all_gather | solution.py:41
  12.7 4.7 %copy-start.6 = (s32[4096,1]{0,1:T(1,128)S(1)}, s32[4096,1]{0,1:T(1,128)}, u32[]{:S(2)}) copy-start(s32[4096,1]{0,1:T(1,128)} %param.32) | copy-start | bytes 49156
  12.7 43.9 %copy-start.2 = (bf16[5120,64]{0,1:T(8,128)(2,1)S(1)}, bf16[5120,64]{0,1:T(8,128)(2,1)}, u32[]{:S(2)}) copy-start(bf16[5120,64]{0,1:T(8,128)(2,1)} %param.23) | copy-start | bytes 1966084
  12.7 43.9 %all-to-all-start = ((bf16[4,64,5120]{2,1,0:T(8,128)(2,1)}), bf16[4,64,5120]{2,1,0:T(8,128)(2,1)S(1)}, u32[]{:S(2)}, u32[]{:S(2)}) async-start(bf16[4,64,5120]{2,1,0:T(8,128)(2,1)} %broadcast_in_dim.37), calls=%async_computation | async-start | bytes 5242880 | tf_op jit(solution)/shard_map/all_to_all | solution.py:20
  17.4 39.2 %copy-start.7 = (s32[256,1]{0,1:T(1,128)}, s32[256,1]{0,1:T(1,128)S(1)}, u32[]{:S(2)}) copy-start(s32[256,1]{0,1:T(1,128)S(1)} %constant_dynamic-slice_fusion) | copy-start | bytes 3076
  18.3 38.3 %copy-start.10 = (s32[256]{0:T(256)}, s32[256]{0:T(256)S(1)}, u32[]{:S(2)}) copy-start(s32[256]{0:T(256)S(1)} %fusion.29) | copy-start | bytes 3076
  56.6 2.3 copy-start.5
  70.6 1.0 copy-start.1
  76.2 71.9 %copy-start.3 = (bf16[64,1024]{1,0:T(8,128)(2,1)S(1)}, bf16[64,1024]{1,0:T(8,128)(2,1)}, u32[]{:S(2)}) copy-start(bf16[64,1024]{1,0:T(8,128)(2,1)} %param.30) | copy-start | bytes 393220
  76.2 71.9 %copy-start.4 = (bf16[160,1024]{1,0:T(8,128)(2,1)S(1)}, bf16[160,1024]{1,0:T(8,128)(2,1)}, u32[]{:S(2)}) copy-start(bf16[160,1024]{1,0:T(8,128)(2,1)} %param.31) | copy-start | bytes 983044
  76.2 71.9 %copy-start.9 = (bf16[8192]{0:T(1024)(128)(2,1)S(1)}, bf16[8192]{0:T(1024)(128)(2,1)}, u32[]{:S(2)}) copy-start(bf16[8192]{0:T(1024)(128)(2,1)} %param.26) | copy-start | bytes 49156
  76.2 71.9 %copy-start.12 = (bf16[1024]{0:T(1024)(128)(2,1)S(1)}, bf16[1024]{0:T(1024)(128)(2,1)}, u32[]{:S(2)}) copy-start(bf16[1024]{0:T(1024)(128)(2,1)} %param.28) | copy-start | bytes 6148
  129.0 5.3 %collective-permute-start = (bf16[8,64,2048]{2,0,1:T(8,128)(2,1)}, bf16[8,64,2048]{2,0,1:T(8,128)(2,1)S(1)}, u32[]{:S(2)}, u32[]{:S(2)}) collective-permute-start(bf16[8,64,2048]{2,0,1:T(8,128)(2,1)} %all_to_all.35), channel_id=1, source_target_pairs={{0,64},{1,65},{2,66},{3,67},{4,68},{5,69},{6,70},{7,71},{8,72},{9,... | collective-permute-start | bytes 6291464 | tf_op jit(solution)/shard_map/ppermute | solution.py:32
  150.0 85.1 %copy-start.8 = (s32[256,1]{0,1:T(1,128)S(1)}, s32[256,1]{0,1:T(1,128)}, u32[]{:S(2)}) copy-start(s32[256,1]{0,1:T(1,128)} %copy-done.7) | copy-start | bytes 3076
  150.0 85.1 %copy-start.11 = (s32[256]{0:T(256)S(1)}, s32[256]{0:T(256)}, u32[]{:S(2)}) copy-start(s32[256]{0:T(256)} %copy-done.10) | copy-start | bytes 3076
  177.1 58.0 %collective-permute-start.1 = (bf16[8,64,2048]{2,0,1:T(8,128)(2,1)}, bf16[8,64,2048]{2,0,1:T(8,128)(2,1)S(1)}, u32[]{:S(2)}, u32[]{:S(2)}) collective-permute-start(bf16[8,64,2048]{2,0,1:T(8,128)(2,1)} %all_to_all.36), channel_id=1, source_target_pairs={{64,0},{65,1},{66,2},{67,3},{68,4},{69,5},{70,6},{71,7},{72,8},{73... | collective-permute-start | bytes 6291464 | tf_op jit(solution)/shard_map/ppermute | solution.py:32
  179.2 63.3 %all-to-all-start.5 = ((f32[64,1,1024]{2,1,0:T(1,128)}), f32[64,1,1024]{2,1,0:T(1,128)S(1)}, u32[]{:S(2)}, u32[]{:S(2)}) async-start(f32[64,1,1024]{2,1,0:T(1,128)} %reshape.147), calls=%async_computation.5 | async-start | bytes 524288 | tf_op jit(solution)/shard_map/all_to_all | solution.py:59
  235.1 1.3 copy-start
  242.6 14.1 %all-to-all-start.3 = ((f32[16,4,2048]{2,1,0:T(4,128)}), f32[16,4,2048]{2,1,0:T(4,128)S(1)}, u32[]{:S(2)}, u32[]{:S(2)}) async-start(f32[16,4,2048]{2,1,0:T(4,128)} %reshape.145), calls=%async_computation.3 | async-start | bytes 1048576 | tf_op jit(solution)/shard_map/all_to_all | solution.py:59
  257.5 15.5 %all-to-all-start.6 = ((f32[64,1,1024]{2,1,0:T(1,128)}), f32[64,1,1024]{2,1,0:T(1,128)S(1)}, u32[]{:S(2)}, u32[]{:S(2)}) async-start(f32[64,1,1024]{2,1,0:T(1,128)} %broadcast_in_dim.40), calls=%async_computation.6 | async-start | bytes 524288 | tf_op jit(solution)/shard_map/all_to_all | solution.py:20
  274.0 16.4 %all-to-all-start.4 = ((f32[16,4,2048]{2,1,0:T(4,128)}), f32[16,4,2048]{2,1,0:T(4,128)S(1)}, u32[]{:S(2)}, u32[]{:S(2)}) async-start(f32[16,4,2048]{2,1,0:T(4,128)} %broadcast_in_dim.38), calls=%async_computation.4 | async-start | bytes 1048576 | tf_op jit(solution)/shard_map/all_to_all | solution.py:20
  290.5 1.6 collective-permute-start.2
Sparse Core Ops, SparseCore 0:
  10.7 137.2 all-gather.1
where the time goes:
time: 303 us; the launch traced here: 300 us
  waiting for transfers between devices  141 us (47%)
  blocking collectives  79.8 us (26%)
  starting transfers between devices  25.3 us (8%)
  local copies, waits for them, and re-layouts  20.3 us (7%)
  between operations  14.3 us (5%)
  matrix products  14.2 us (5%)
  other arithmetic  5.53 us (2%)
    all_to_all x3, waiting for transfers between devices, from_everyone(): lax.all_to_all(jnp.broadcast_to(array[None], (devices, *array.shape)), ax...  60.9 us
    ppermute x2, waiting for transfers between devices, passed_along(): lax.ppermute(value, axis, [(source, source + steps) for source in range(f...  54.3 us
    all_to_all x1, blocking collectives, body(): lax.all_to_all(outgoing, ('dp', 'mp'), split_axis=1, concat_axis=1, tiled...  52.7 us
    all_to_all x1, blocking collectives, body(): lax.all_to_all(reply_rows, ('dp', 'mp'), split_axis=1, concat_axis=1, til...  27.1 us
    all_gather x1, waiting for transfers between devices, sent_together(): lax.all_gather(both, axis, axis=dim, tiled=True)  13.8 us
    all_to_all x3, starting transfers between devices, from_everyone(): lax.all_to_all(jnp.broadcast_to(array[None], (devices, *array.shape)), ax...  13.2 us
    dot_general x1, matrix products, encode(): jnp.dot(source, enc_weight, preferred_element_type=jnp.float32)  10.4 us
    all_to_all x2, waiting for transfers between devices, summed_on_arrival(): lax.all_to_all(split_up(array, dim, devices), axis, 0, 0, tiled=True)  10.2 us
  transfers between devices with their start and end apart: 9, of which 8 were waited for; matrix products, arithmetic and copies ran while one was open for 10% of the time, Pallas kernels for 0%

commit v1 on v0

--- a/solution.py
+++ b/solution.py
@@ -72,8 +72,10 @@
 
 
 def slot_ranks(destiny, owners):
-    markers = (destiny[:, None] == jnp.arange(owners, dtype=jnp.int32)[None, :]).astype(jnp.int32)
-    return jnp.sum((jnp.cumsum(markers, axis=0) - markers) * markers, axis=1)
+    count = destiny.shape[0]
+    place = jnp.arange(count, dtype=jnp.int32)
+    earlier = (destiny[:, None] == destiny[None, :]) & (place[None, :] < place[:, None])
+    return jnp.sum(earlier.astype(jnp.int32), axis=1)
 
 
 def body(

time: 303 us -> 303 us (level)
  no operation moved by 1% of the time
where the time goes in v1:
time: 303 us; the launch traced here: 301 us
  waiting for transfers between devices  141 us (47%)
  blocking collectives  79.8 us (26%)
  starting transfers between devices  25.3 us (8%)
  local copies, waits for them, and re-layouts  20.6 us (7%)
  matrix products  14.3 us (5%)
  between operations  14.3 us (5%)
  other arithmetic  4.9 us (2%)
    all_to_all x3, waiting for transfers between devices, from_everyone(): lax.all_to_all(jnp.broadcast_to(array[None], (devices, *array.shape)), ax...  61.1 us
    ppermute x2, waiting for transfers between devices, passed_along(): lax.ppermute(value, axis, [(source, source + steps) for source in range(f...  54.4 us
    all_to_all x1, blocking collectives, body(): lax.all_to_all(outgoing, ('dp', 'mp'), split_axis=1, concat_axis=1, tiled...  52.7 us
    all_to_all x1, blocking collectives, body(): lax.all_to_all(reply_rows, ('dp', 'mp'), split_axis=1, concat_axis=1, til...  27.2 us
    all_gather x1, waiting for transfers between devices, sent_together(): lax.all_gather(both, axis, axis=dim, tiled=True)  13.9 us
    all_to_all x3, starting transfers between devices, from_everyone(): lax.all_to_all(jnp.broadcast_to(array[None], (devices, *array.shape)), ax...  13.2 us
    dot_general x1, matrix products, encode(): jnp.dot(source, enc_weight, preferred_element_type=jnp.float32)  10.5 us
    all_to_all x2, waiting for transfers between devices, summed_on_arrival(): lax.all_to_all(split_up(array, dim, devices), axis, 0, 0, tiled=True)  10.2 us
  transfers between devices with their start and end apart: 9, of which 8 were waited for; matrix products, arithmetic and copies ran while one was open for 10% of the time, Pallas kernels for 0%

profile of v1, /device:TPU:0, one launch (start us, length us, event | category | flops | bytes accessed | tf_op | source)
XLA Modules:
  0.0 300.7 jit_solution(597676197417044225)
XLA Ops:
  8.0 1.7 pad_maximum_fusion
  9.8 2.9 broadcast_in_dim.37
  12.7 4.7 %all-to-all-start = ((bf16[4,64,5120]{2,1,0:T(8,128)(2,1)}), bf16[4,64,5120]{2,1,0:T(8,128)(2,1)S(1)}, u32[]{:S(2)}, u32[]{:S(2)}) async-start(bf16[4,64,5120]{2,1,0:T(8,128)(2,1)} %broadcast_in_dim.37), calls=%async_computation | async-start | bytes 5242880 | tf_op jit(solution)/shard_map/all_to_all | solution.py:20
  18.7 37.9 %all-to-all-done = bf16[4,64,5120]{2,1,0:T(8,128)(2,1)S(1)} async-done(((bf16[4,64,5120]{2,1,0:T(8,128)(2,1)}), bf16[4,64,5120]{2,1,0:T(8,128)(2,1)S(1)}, u32[]{:S(2)}, u32[]{:S(2)}) %all-to-all-start) | async-done | bytes 2621472 | tf_op jit(solution)/shard_map/all_to_all | solution.py:20
  56.6 13.9 %conditional.3 = (bf16[256,2048]{1,0:T(8,128)(2,1)S(1)}, bf16[256,64]{0,1:T(8,128)(2,1)}) conditional(s32[]{:T(128)} %convert_element_type.56, () %tuple.31, (bf16[4,64,5120]{2,1,0:T(8,128)(2,1)S(1)}, bf16[5120,2048]{1,0:T(8,128)(2,1)}, bf16[2048]{0:T(1024)(128)(2,1)}, bf16[5120,64]{0,1:T(8,128)(2,1)S(1)}, bf16[64,2048]{1,0:T(8,128)(2,1)S(1)}) %tuple.65), branch_computations={%region_1.0_spmd, %region_2.0_spmd} | conditional | flops 5605181440 | bytes 32460816 | solution.py:126
  57.3 1.5 convolution_convert_fusion
  60.0 10.5 %fusion.1 = bf16[256,2048]{1,0:T(8,128)(2,1)S(1)} fusion(f32[256,2048]{1,0:T(8,128)S(1)} %fusion.31, bf16[256,5120]{1,0:T(8,128)(2,1)S(1)} %bitcast.35, bf16[5120,2048]{1,0:T(8,128)(2,1)} %get-tuple-element.88, f32[2048]{0:T(1024)S(1)} %convert_element_type.39), kind=kOutput, calls=%fused_computation.4 | convolution fusion | flops 5370281984 | bytes 26746880 | tf_op jit(solution)/shard_map/cond/branch_1_fun/dot_general | solution.py:114
  71.5 3.5 %scatter_custom_fusion = bf16[512,2048]{1,0:T(8,128)(2,1)S(1)} fusion(s32[256]{0:T(256)} %bitcast.42, bf16[256,2048]{1,0:T(8,128)(2,1)} %copy-done.1, bf16[]{:T(256)} %constant.30.clone.1), kind=kCustom, calls=%fused_computation.42 | custom fusion | bytes 2097664 | tf_op jit(solution)/shard_map/scatter | solution.py:131
  76.2 52.7 %all_to_all.35 = bf16[8,64,2048]{2,0,1:T(8,128)(2,1)} all-to-all(bf16[8,64,2048]{2,0,1:T(8,128)(2,1)S(1)} %copy.49), channel_id=1, replica_groups=mesh['grp'=2,'dp'=16,'mp'=4] {'dp','mp'}, dimensions={1} | all-to-all | bytes 4194304 | tf_op jit(solution)/shard_map/all_to_all | solution.py:134
  128.9 1.4 collective-permute-start
  130.3 3.8 %collective-permute-done = bf16[8,64,2048]{2,0,1:T(8,128)(2,1)S(1)} collective-permute-done((bf16[8,64,2048]{2,0,1:T(8,128)(2,1)}, bf16[8,64,2048]{2,0,1:T(8,128)(2,1)S(1)}, u32[]{:S(2)}, u32[]{:S(2)}) %collective-permute-start) | collective-permute-done | bytes 2097184 | tf_op jit(solution)/shard_map/ppermute | solution.py:32
  134.1 13.9 %all-gather.2.cloned.1.call-done = bf16[8192,1088]{1,0:T(8,128)(2,1)} async-done(((bf16[128,1088]{1,0:T(8,128)(2,1)}), bf16[8192,1088]{1,0:T(8,128)(2,1)}) %all-gather.2.cloned.1.call-update) | async-done | bytes 17825808 | tf_op jit(solution)/shard_map/all_gather | solution.py:41
  150.0 27.2 %all_to_all.36 = bf16[8,64,2048]{2,0,1:T(8,128)(2,1)} all-to-all(bf16[8,64,2048]{2,0,1:T(8,128)(2,1)S(1)} %copy.52), channel_id=1, replica_groups=mesh['grp'=2,'dp'=16,'mp'=4] {'dp','mp'}, dimensions={1} | all-to-all | bytes 4194304 | tf_op jit(solution)/shard_map/all_to_all | solution.py:190
  179.3 5.4 %all-to-all-start.5 = ((f32[64,1,1024]{2,1,0:T(1,128)}), f32[64,1,1024]{2,1,0:T(1,128)S(1)}, u32[]{:S(2)}, u32[]{:S(2)}) async-start(f32[64,1,1024]{2,1,0:T(1,128)} %reshape.132), calls=%async_computation.5 | async-start | bytes 524288 | tf_op jit(solution)/shard_map/all_to_all | solution.py:59
  184.7 50.6 %collective-permute-done.1 = bf16[8,64,2048]{2,0,1:T(8,128)(2,1)S(1)} collective-permute-done((bf16[8,64,2048]{2,0,1:T(8,128)(2,1)}, bf16[8,64,2048]{2,0,1:T(8,128)(2,1)S(1)}, u32[]{:S(2)}, u32[]{:S(2)}) %collective-permute-start.1) | collective-permute-done | bytes 2097184 | tf_op jit(solution)/shard_map/ppermute | solution.py:32
  235.3 6.5 %conditional.5 = (f32[64,2048]{1,0:T(8,128)S(1)}) conditional(s32[]{:T(128)} %convert_element_type.56, () %tuple.30, (bf16[8,64,2048]{2,0,1:T(8,128)(2,1)S(1)}, s32[256]{0:T(256)S(1)}, s32[256]{0:T(256)S(1)}, bf16[256,64]{0,1:T(8,128)(2,1)}) %tuple.69), branch_computations={%region_9.10_spmd, %region_10.11_spmd} | conditional | flops 67111168 | bytes 16294948 | solution.py:201
  236.7 2.7 copy.53
  239.4 1.4 gather_fusion
  242.8 3.8 %all-to-all-start.3 = ((f32[16,4,2048]{2,1,0:T(4,128)}), f32[16,4,2048]{2,1,0:T(4,128)S(1)}, u32[]{:S(2)}, u32[]{:S(2)}) async-start(f32[16,4,2048]{2,1,0:T(4,128)} %reshape.130), calls=%async_computation.3 | async-start | bytes 1048576 | tf_op jit(solution)/shard_map/all_to_all | solution.py:59
  246.7 10.2 %all-to-all-done.3 = f32[16,4,2048]{2,1,0:T(4,128)S(1)} async-done(((f32[16,4,2048]{2,1,0:T(4,128)}), f32[16,4,2048]{2,1,0:T(4,128)S(1)}, u32[]{:S(2)}, u32[]{:S(2)}) %all-to-all-start.3) | async-done | bytes 524320 | tf_op jit(solution)/shard_map/all_to_all | solution.py:59
  257.8 5.0 %all-to-all-start.6 = ((f32[64,1,1024]{2,1,0:T(1,128)}), f32[64,1,1024]{2,1,0:T(1,128)S(1)}, u32[]{:S(2)}, u32[]{:S(2)}) async-start(f32[64,1,1024]{2,1,0:T(1,128)} %broadcast_in_dim.39), calls=%async_computation.6 | async-start | bytes 524288 | tf_op jit(solution)/shard_map/all_to_all | solution.py:20
  262.8 10.5 %all-to-all-done.6 = f32[64,1,1024]{2,1,0:T(1,128)S(1)} async-done(((f32[64,1,1024]{2,1,0:T(1,128)}), f32[64,1,1024]{2,1,0:T(1,128)S(1)}, u32[]{:S(2)}, u32[]{:S(2)}) %all-to-all-start.6) | async-done | bytes 262176 | tf_op jit(solution)/shard_map/all_to_all | solution.py:20
  274.2 3.6 %all-to-all-start.4 = ((f32[16,4,2048]{2,1,0:T(4,128)}), f32[16,4,2048]{2,1,0:T(4,128)S(1)}, u32[]{:S(2)}, u32[]{:S(2)}) async-start(f32[16,4,2048]{2,1,0:T(4,128)} %broadcast_in_dim.38), calls=%async_computation.4 | async-start | bytes 1048576 | tf_op jit(solution)/shard_map/all_to_all | solution.py:20
  277.8 12.8 %all-to-all-done.4 = f32[16,4,2048]{2,1,0:T(4,128)S(1)} async-done(((f32[16,4,2048]{2,1,0:T(4,128)}), f32[16,4,2048]{2,1,0:T(4,128)S(1)}, u32[]{:S(2)}, u32[]{:S(2)}) %all-to-all-start.4) | async-done | bytes 524320 | tf_op jit(solution)/shard_map/all_to_all | solution.py:20
  (64 shorter events, 19.1 us)
Async XLA Ops:
  7.2 140.9 %all-gather.2.cloned.1.call-start = ((), (), s32[]{:S(2)}) async-start(), calls=%async_computation.7 | async-start | bytes 19169280 | tf_op jit(solution)/shard_map/all_gather | solution.py:41
  12.7 4.7 %copy-start.6 = (s32[4096,1]{0,1:T(1,128)S(1)}, s32[4096,1]{0,1:T(1,128)}, u32[]{:S(2)}) copy-start(s32[4096,1]{0,1:T(1,128)} %param.32) | copy-start | bytes 49156
  12.7 43.9 %copy-start.2 = (bf16[5120,64]{0,1:T(8,128)(2,1)S(1)}, bf16[5120,64]{0,1:T(8,128)(2,1)}, u32[]{:S(2)}) copy-start(bf16[5120,64]{0,1:T(8,128)(2,1)} %param.23) | copy-start | bytes 1966084
  12.7 43.9 %copy-start.5 = (bf16[64,2048]{1,0:T(8,128)(2,1)S(1)}, bf16[64,2048]{1,0:T(8,128)(2,1)}, u32[]{:S(2)}) copy-start(bf16[64,2048]{1,0:T(8,128)(2,1)} %param.24) | copy-start | bytes 786436
  12.7 43.9 %all-to-all-start = ((bf16[4,64,5120]{2,1,0:T(8,128)(2,1)}), bf16[4,64,5120]{2,1,0:T(8,128)(2,1)S(1)}, u32[]{:S(2)}, u32[]{:S(2)}) async-start(bf16[4,64,5120]{2,1,0:T(8,128)(2,1)} %broadcast_in_dim.37), calls=%async_computation | async-start | bytes 5242880 | tf_op jit(solution)/shard_map/all_to_all | solution.py:20
  17.4 0.6 copy-start.8
  17.6 0.6 copy-start.10
  70.5 1.0 copy-start.1
  76.1 71.9 %copy-start.3 = (bf16[64,1024]{1,0:T(8,128)(2,1)S(1)}, bf16[64,1024]{1,0:T(8,128)(2,1)}, u32[]{:S(2)}) copy-start(bf16[64,1024]{1,0:T(8,128)(2,1)} %param.30) | copy-start | bytes 393220
  76.1 71.9 %copy-start.4 = (bf16[160,1024]{1,0:T(8,128)(2,1)S(1)}, bf16[160,1024]{1,0:T(8,128)(2,1)}, u32[]{:S(2)}) copy-start(bf16[160,1024]{1,0:T(8,128)(2,1)} %param.31) | copy-start | bytes 983044
  76.2 71.9 %copy-start.7 = (bf16[8192]{0:T(1024)(128)(2,1)S(1)}, bf16[8192]{0:T(1024)(128)(2,1)}, u32[]{:S(2)}) copy-start(bf16[8192]{0:T(1024)(128)(2,1)} %param.26) | copy-start | bytes 49156
  76.2 71.9 %copy-start.12 = (bf16[1024]{0:T(1024)(128)(2,1)S(1)}, bf16[1024]{0:T(1024)(128)(2,1)}, u32[]{:S(2)}) copy-start(bf16[1024]{0:T(1024)(128)(2,1)} %param.28) | copy-start | bytes 6148
  128.9 5.3 %collective-permute-start = (bf16[8,64,2048]{2,0,1:T(8,128)(2,1)}, bf16[8,64,2048]{2,0,1:T(8,128)(2,1)S(1)}, u32[]{:S(2)}, u32[]{:S(2)}) collective-permute-start(bf16[8,64,2048]{2,0,1:T(8,128)(2,1)} %all_to_all.35), channel_id=1, source_target_pairs={{0,64},{1,65},{2,66},{3,67},{4,68},{5,69},{6,70},{7,71},{8,72},{9,... | collective-permute-start | bytes 6291464 | tf_op jit(solution)/shard_map/ppermute | solution.py:32
  149.9 85.4 %copy-start.9 = (s32[256,1]{0,1:T(1,128)S(1)}, s32[256,1]{0,1:T(1,128)}, u32[]{:S(2)}) copy-start(s32[256,1]{0,1:T(1,128)} %copy-done.8) | copy-start | bytes 3076
  150.0 85.3 %copy-start.11 = (s32[256]{0:T(256)S(1)}, s32[256]{0:T(256)}, u32[]{:S(2)}) copy-start(s32[256]{0:T(256)} %copy-done.10) | copy-start | bytes 3076
  177.1 58.2 %collective-permute-start.1 = (bf16[8,64,2048]{2,0,1:T(8,128)(2,1)}, bf16[8,64,2048]{2,0,1:T(8,128)(2,1)S(1)}, u32[]{:S(2)}, u32[]{:S(2)}) collective-permute-start(bf16[8,64,2048]{2,0,1:T(8,128)(2,1)} %all_to_all.36), channel_id=1, source_target_pairs={{64,0},{65,1},{66,2},{67,3},{68,4},{69,5},{70,6},{71,7},{72,8},{73... | collective-permute-start | bytes 6291464 | tf_op jit(solution)/shard_map/ppermute | solution.py:32
  179.3 63.5 %all-to-all-start.5 = ((f32[64,1,1024]{2,1,0:T(1,128)}), f32[64,1,1024]{2,1,0:T(1,128)S(1)}, u32[]{:S(2)}, u32[]{:S(2)}) async-start(f32[64,1,1024]{2,1,0:T(1,128)} %reshape.132), calls=%async_computation.5 | async-start | bytes 524288 | tf_op jit(solution)/shard_map/all_to_all | solution.py:59
  235.3 1.3 copy-start
  242.8 14.2 %all-to-all-start.3 = ((f32[16,4,2048]{2,1,0:T(4,128)}), f32[16,4,2048]{2,1,0:T(4,128)S(1)}, u32[]{:S(2)}, u32[]{:S(2)}) async-start(f32[16,4,2048]{2,1,0:T(4,128)} %reshape.130), calls=%async_computation.3 | async-start | bytes 1048576 | tf_op jit(solution)/shard_map/all_to_all | solution.py:59
  257.8 15.5 %all-to-all-start.6 = ((f32[64,1,1024]{2,1,0:T(1,128)}), f32[64,1,1024]{2,1,0:T(1,128)S(1)}, u32[]{:S(2)}, u32[]{:S(2)}) async-start(f32[64,1,1024]{2,1,0:T(1,128)} %broadcast_in_dim.39), calls=%async_computation.6 | async-start | bytes 524288 | tf_op jit(solution)/shard_map/all_to_all | solution.py:20
  274.2 16.4 %all-to-all-start.4 = ((f32[16,4,2048]{2,1,0:T(4,128)}), f32[16,4,2048]{2,1,0:T(4,128)S(1)}, u32[]{:S(2)}, u32[]{:S(2)}) async-start(f32[16,4,2048]{2,1,0:T(4,128)} %broadcast_in_dim.38), calls=%async_computation.4 | async-start | bytes 1048576 | tf_op jit(solution)/shard_map/all_to_all | solution.py:20
  290.7 1.6 collective-permute-start.2
Sparse Core Ops, SparseCore 0:
  10.7 137.2 all-gather.1

commit v2 on v0

v2 whole, which is shorter than its diff:
```python
import jax
import jax.numpy as jnp
from jax import lax
from jax.sharding import PartitionSpec as P

ENC_DEV = 256
epsilon = 1e-06
f32 = jnp.float32
bf16 = jnp.bfloat16


def dot(a, b):
    return jnp.dot(a, b, preferred_element_type=f32)


def dot_tn(a, b):
    return lax.dot_general(a, b, (((0,), (0,)), ((), ())), preferred_element_type=f32)


def dot_nt(a, b):
    return lax.dot_general(a, b, (((1,), (1,)), ((), ())), preferred_element_type=f32)


def split_two(a):
    high = a.astype(bf16)
    return high, (a - high.astype(f32)).astype(bf16)


def split_three(a):
    high, rest = a.astype(bf16), a - a.astype(bf16).astype(f32)
    middle, last = split_two(rest)
    return high, middle, last


def turned(array, axis, step):
    count = lax.axis_size(axis)
    return lax.ppermute(array, axis, [(i, (i + step) % count) for i in range(count)])


def crossed(array):
    return lax.ppermute(array, "grp", [(0, 1), (1, 0)])


def to_everyone(array, axes):
    count = lax.axis_size(axes)
    return lax.all_to_all(
        jnp.broadcast_to(array[None], (count, *array.shape)), axes, 0, 0, tiled=True
    )


def body(
    hidden,
    enc_weight,
    enc_bias,
    enc_frozen,
    enc_adapter,
    text_rows,
    norm_gain,
    value_weight,
    value_bias,
    llm_frozen,
    llm_adapter,
    targets,
    dest_owner,
    seq_length,
):
    n_dp = lax.axis_size("dp")
    n_mp = lax.axis_size("mp")
    side = n_mp
    owners = n_dp * n_mp
    grp = lax.axis_index("grp")
    dp = lax.axis_index("dp")
    mp = lax.axis_index("mp")
    first = grp == 0
    width = text_rows.shape[1]
    part_width = enc_weight.shape[1]
    rank = enc_frozen.shape[1]
    half_rank = rank // 2
    kv = value_weight.shape[1]
    half_kv = kv // 2
    shard = value_weight.shape[0]
    block_rows = hidden.shape[0]
    mine_rows = block_rows // 2
    capacity = 2 * ENC_DEV // owners

    own_hidden = lax.dynamic_slice_in_dim(hidden, grp * mine_rows, mine_rows)
    hid = jnp.concatenate([own_hidden] + [turned(own_hidden, "mp", k) for k in range(1, n_mp)])

    swap = [
        ((z * side + x) * side + y, (y * side + x) * side + z)
        for z in range(side)
        for x in range(side)
        for y in range(side)
    ]
    w_half = lax.dynamic_slice_in_dim(value_weight, grp * half_kv, half_kv, axis=1)
    w_moved = lax.ppermute(w_half, ("dp", "mp"), swap)
    w_mine = to_everyone(w_moved, "dp")
    w_mine = w_mine.reshape(side, side, shard, half_kv).transpose(1, 0, 2, 3).reshape(-1, half_kv)
    w_other = crossed(w_mine)

    a_half = lax.dynamic_slice_in_dim(llm_frozen.T, grp * half_rank, half_rank)
    a_mine = to_everyone(a_half, ("dp", "mp")).transpose(1, 0, 2).reshape(half_rank, width)
    a_all = jnp.concatenate([a_mine, crossed(a_mine)])
    a_part = lax.dynamic_slice_in_dim(a_all, mp * part_width, part_width, axis=1)
    b_ranked = jnp.where(first, llm_adapter, jnp.roll(llm_adapter, half_rank, axis=0))
    b_local = jnp.where(first, b_ranked, jnp.roll(b_ranked, half_kv, axis=1))
    bias_wide = value_bias.astype(f32)
    bias_local = jnp.where(first, bias_wide, jnp.roll(bias_wide, half_kv))

    own_length = seq_length[0]
    area = capacity * n_dp
    t_half = lax.dynamic_slice(targets, (0, grp * half_kv), (area, half_kv))
    t_half = t_half.reshape(capacity, n_dp, half_kv).transpose(1, 0, 2)
    t_half = jnp.concatenate(
        [t_half, jnp.full((n_dp, capacity, 128), own_length.astype(bf16))], axis=2
    )
    t_here = lax.all_to_all(t_half, "dp", 0, 0, tiled=True).reshape(n_dp * capacity, -1)
    t_mine = jnp.concatenate([t_here] + [turned(t_here, "mp", k) for k in range(1, n_mp)])
    t_other = crossed(t_mine[:, :half_kv])
    t_table = jnp.concatenate([t_mine[:, :half_kv], t_other, t_mine[:, half_kv:]], axis=1)
    destiny = dest_owner[:, 0]
    block_dest = lax.dynamic_slice_in_dim(destiny, dp * ENC_DEV, ENC_DEV)
    start = mp * block_rows + grp * mine_rows
    own_dest = lax.dynamic_slice_in_dim(block_dest, start, mine_rows)
    place = start + jnp.arange(mine_rows, dtype=jnp.int32)
    earlier = (own_dest[:, None] == block_dest[None, :]) & (
        jnp.arange(ENC_DEV, dtype=jnp.int32)[None, :] < place[:, None]
    )
    slot = jnp.sum(earlier.astype(jnp.int32), axis=1)
    source = (mp - own_dest % n_mp) % n_mp
    line = source * (n_dp * capacity) + (own_dest // n_mp) * capacity + slot
    pick = (line[:, None] == jnp.arange(n_mp * n_dp * capacity, dtype=jnp.int32)[None, :]).astype(
        bf16
    )
    picked = dot(pick, t_table)
    own_targets = picked[:, :kv]
    length = picked[:, kv : kv + 1]
    position = (slot * n_dp + dp)[:, None].astype(f32)
    weight = jnp.where(position < length, 1.0 / length, 0.0)

    gain_wide = norm_gain.astype(f32)
    text_count = text_rows.shape[0] // 2
    text_wide = lax.dynamic_slice_in_dim(text_rows, grp * text_count, text_count).astype(f32)
    text_inverse = lax.rsqrt(jnp.mean(text_wide * text_wide, axis=1, keepdims=True) + epsilon)
    text_normed = (text_wide * text_inverse * gain_wide).astype(bf16)
    text_low = dot_nt(text_normed, a_all).astype(bf16)
    owner_index = dp * n_mp + mp
    counts = jnp.sum((destiny.reshape(n_dp, ENC_DEV) == owner_index).astype(jnp.int32), axis=1)
    row = grp * text_count + jnp.arange(text_count, dtype=jnp.int32)
    taken = (row < area) & (
        row // n_dp
        < jnp.sum(
            jnp.where(
                (row % n_dp)[:, None] == jnp.arange(n_dp, dtype=jnp.int32)[None, :], counts, 0
            ),
            axis=1,
        )
    )
    keep = (row < own_length) & ~taken
    text_kept = jnp.where(keep[:, None], text_low, jnp.zeros_like(text_low))
    text_weight = 1.0 / own_length.astype(f32)
    text_sum = dot_tn(text_kept, text_normed) * text_weight
    own_text_targets = lax.dynamic_slice_in_dim(targets, grp * text_count, text_count).astype(f32)
    rest = bias_wide + dot(text_low, b_ranked) - own_text_targets
    rest_high, rest_low = split_two(rest)
    rest_sum = dot_tn(
        jnp.concatenate([text_kept, text_kept]), jnp.concatenate([rest_high, rest_low])
    )
    rest_sum = rest_sum * text_weight
    both_sums = jnp.concatenate([text_sum, rest_sum], axis=1)
    both_sums = both_sums[:half_rank] + crossed(both_sums[half_rank:])
    text_parts = both_sums[:, :width].reshape(half_rank, owners, shard).transpose(1, 0, 2)
    text_parts = lax.all_to_all(text_parts.astype(bf16), ("dp", "mp"), 0, 0, tiled=True)
    text_here = jnp.sum(text_parts.astype(f32), axis=0)
    here_high, here_low = split_two(text_here)
    text_grad = dot(jnp.concatenate([here_high, here_low]), value_weight)
    text_grad = text_grad[:half_rank] + text_grad[half_rank:] + both_sums[:, width:]
    text_grad = text_grad + (
        turned(text_grad, "mp", 1) + turned(text_grad, "mp", 2) + turned(text_grad, "mp", 3)
    )

    enc_low = dot(hid, enc_frozen).astype(bf16)
    merged = dot(hid, enc_weight) + enc_bias.astype(f32) + dot(enc_low, enc_adapter)
    image = merged.astype(bf16)
    image_wide = image.astype(f32)
    gain_part = lax.dynamic_slice_in_dim(gain_wide, mp * part_width, part_width)
    scaled_rows = (image_wide * gain_part).astype(bf16)
    squares = jnp.sum(image_wide * image_wide, axis=1, keepdims=True)
    part = jnp.concatenate(
        [
            dot(scaled_rows, w_mine),
            dot(scaled_rows, w_other),
            dot_nt(scaled_rows, a_part),
            jnp.broadcast_to(squares, (squares.shape[0], 128 - rank)),
        ],
        axis=1,
    )
    total = part[:mine_rows]
    for k in range(1, n_mp):
        total = total + turned(part[k * mine_rows : (k + 1) * mine_rows], "mp", -k)
    raw_values = total[:, :kv]
    raw_low = total[:, kv : kv + rank]
    inverse = lax.rsqrt(total[:, kv + rank : kv + rank + 1] / width + epsilon)
    low = (raw_low * inverse).astype(bf16)
    values_out = raw_values * inverse + bias_local + dot(low, b_local)
    dvalues = ((values_out - own_targets) * weight).astype(bf16)
    dlow = dot_nt(dvalues, b_local).astype(bf16)
    centre = (
        jnp.sum(dvalues.astype(f32) * raw_values, axis=1, keepdims=True)
        + jnp.sum(dlow.astype(f32) * raw_low, axis=1, keepdims=True)
    ) / width
    factor = inverse * inverse * inverse * centre
    packed = jnp.concatenate(
        [dvalues, low, *split_three(inverse), *split_three(factor), jnp.zeros((mine_rows, 58), bf16)],
        axis=1,
    )
    packed = jnp.concatenate([packed] + [turned(packed, "mp", k) for k in range(1, n_mp)])
    dvalues = packed[:, :kv]
    low = packed[:, kv : kv + rank]
    numbers = packed[:, kv + rank :].astype(f32)
    inverse = numbers[:, 0:1] + numbers[:, 1:2] + numbers[:, 2:3]
    factor = numbers[:, 3:4] + numbers[:, 4:5] + numbers[:, 5:6]
    dlow = dot_nt(dvalues, b_local).astype(bf16)
    dnormed = (
        dot_nt(dvalues[:, :half_kv], w_mine)
        + dot_nt(dvalues[:, half_kv:], w_other)
        + dot(dlow, a_part)
    )
    dimage = (inverse * (gain_part * dnormed) - image_wide * factor).astype(bf16)
    enc_grad = dot_tn(enc_low, dimage)
    llm_grad = dot_tn(low, dvalues)
    llm_grad = jnp.where(first, llm_grad, jnp.roll(llm_grad, half_kv, axis=1))

    enc_mine = lax.dynamic_slice_in_dim(enc_grad, grp * half_rank, half_rank)
    enc_give = lax.dynamic_slice_in_dim(enc_grad, (1 - grp) * half_rank, half_rank)
    mine = jnp.concatenate([enc_mine, llm_grad[:half_rank] + text_grad], axis=1)
    give = jnp.concatenate([enc_give, llm_grad[half_rank:]], axis=1)
    mine = mine + crossed(give)
    mine = mine.reshape(n_dp, half_rank // n_dp, -1)
    mine = jnp.sum(lax.all_to_all(mine, "dp", 0, 0, tiled=True), axis=0)
    whole = to_everyone(mine, "dp").reshape(half_rank, -1)
    return whole[:, :part_width], whole[:, part_width:]


def solution(mesh):
    return jax.shard_map(
        body,
        mesh=mesh,
        in_specs=(
            P(("dp", "mp"), None),
            P(None, "mp"),
            P("mp"),
            P(),
            P(None, "mp"),
            P(("dp", "mp"), None),
            P(),
            P(("dp", "mp"), None),
            P(),
            P(("dp", "mp"), None),
            P(),
            P(("dp", "mp"), None),
            P(),
            P(("dp", "mp")),
        ),
        out_specs=(P("grp", "mp"), P("grp", None)),
        check_vma=False,
    )
```

time: 303 us -> 196 us (0.65)
  waiting for transfers between devices: 141 us -> 35 us
  blocking collectives: 79.8 us -> 26.1 us
  starting transfers between devices: 25.3 us -> 55.1 us
  matrix products: 14.2 us -> 34.7 us
  between operations: 14.3 us -> 2.28 us
  local copies, waits for them, and re-layouts: 20.3 us -> 30.1 us
  other arithmetic: 5.53 us -> 12 us
    all_to_all x2, blocking collectives: 79.8 us -> 26.1 us  [the longest x1 13.7 us: body(): mine = jnp.sum(lax.all_to_all(mine, 'dp', 0, 0, tiled=True), axis=0)]
    all_to_all x5 -> x4, waiting for transfers between devices: 71.1 us -> 21 us  [the longest x1 11 us: body(): lax.all_to_all(text_parts.astype(bf16), ('dp', 'mp'), 0, 0, tiled=True)]
    ppermute x3 -> x21, waiting for transfers between devices: 55.6 us -> 14 us  [the longest x15 10.5 us: turned(): lax.ppermute(array, axis, [(i, (i + step) % count) for i in range(count)])]
    ppermute x3 -> x21, starting transfers between devices: 2.89 us -> 25.7 us  [the longest x15 24.5 us: turned(): lax.ppermute(array, axis, [(i, (i + step) % count) for i in range(count)])]
    dot_general x4 -> x18, matrix products: 14.2 us -> 34.7 us  [the longest x10 25.2 us: dot(): return jnp.dot(a, b, preferred_element_type=f32)]
    all_gather x1 -> x0, waiting for transfers between devices: 13.8 us -> none  [sent_together(): lax.all_gather(both, axis, axis=dim, tiled=True)]
    slice x5 -> x12, local copies, waits for them, and re-layouts: 0.33 us -> 9.43 us  [the longest x4 6.28 us: body(): total = total + turned(part[k * mine_rows:(k + 1) * mine_rows], 'mp', -k)]
    all_to_all x5 -> x4, starting transfers between devices: 22.4 us -> 29.4 us  [the longest x2 14.4 us: to_everyone(): lax.all_to_all(jnp.broadcast_to(array[None], (count, *array.shape)), axes...]
  transfers between devices with their start and end apart: 9 -> 25, of which waited for: 8 -> 8; matrix products, arithmetic and copies ran while one was open for 10% -> 29% of each run, Pallas kernels for 0% -> 0%
where the time goes in v2:
time: 196 us; the launch traced here: 195 us
  starting transfers between devices  55.1 us (28%)
  waiting for transfers between devices  35 us (18%)
  matrix products  34.7 us (18%)
  local copies, waits for them, and re-layouts  30.1 us (15%)
  blocking collectives  26.1 us (13%)
  other arithmetic  12 us (6%)
  between operations  2.28 us (1%)
    dot_general x10, matrix products, dot(): return jnp.dot(a, b, preferred_element_type=f32)  25.2 us
    ppermute x15, starting transfers between devices, turned(): lax.ppermute(array, axis, [(i, (i + step) % count) for i in range(count)])  24.5 us
    all_to_all x2, starting transfers between devices, to_everyone(): lax.all_to_all(jnp.broadcast_to(array[None], (count, *array.shape)), axes...  14.4 us
    all_to_all x1, blocking collectives, body(): mine = jnp.sum(lax.all_to_all(mine, 'dp', 0, 0, tiled=True), axis=0)  13.7 us
    all_to_all x1, blocking collectives, to_everyone(): lax.all_to_all(jnp.broadcast_to(array[None], (count, *array.shape)), axes...  12.4 us
    all_to_all x1, waiting for transfers between devices, body(): lax.all_to_all(text_parts.astype(bf16), ('dp', 'mp'), 0, 0, tiled=True)  11 us
    ppermute x15, waiting for transfers between devices, turned(): lax.ppermute(array, axis, [(i, (i + step) % count) for i in range(count)])  10.5 us
    all_to_all x1, starting transfers between devices, body(): lax.all_to_all(t_half, 'dp', 0, 0, tiled=True).reshape(n_dp * capacity, -1)  7.88 us
  transfers between devices with their start and end apart: 25, of which 8 were waited for; matrix products, arithmetic and copies ran while one was open for 29% of the time, Pallas kernels for 0%

profile of v2, /device:TPU:0, one launch (start us, length us, event | category | flops | bytes accessed | tf_op | source)
XLA Modules:
  0.0 195.3 jit_solution(6302511440584078207)
XLA Ops:
  3.5 2.9 %collective-permute-start.1 = (bf16[32,5120]{1,0:T(8,128)(2,1)S(1)}, bf16[32,5120]{1,0:T(8,128)(2,1)}, u32[]{:S(2)}, u32[]{:S(2)}) collective-permute-start(bf16[32,5120]{1,0:T(8,128)(2,1)S(1)} %constant_dynamic-slice_fusion.6), channel_id=1, source_target_pairs={{0,2},{1,3},{2,0},{3,1},{4,6},{5,7},{6,4},{7,5},{8,10},{9,11},{10,... | collective-permute-start | bytes 983048 | tf_op jit(solution)/shard_map/ppermute | solution.py:37
  10.1 7.9 %all-to-all-start.2 = ((bf16[16,8,640]{2,1,0:T(8,128)(2,1)}), bf16[16,8,640]{2,1,0:T(8,128)(2,1)S(1)}, u32[]{:S(2)}, u32[]{:S(2)}) async-start(bf16[16,8,640]{2,1,0:T(8,128)(2,1)} %concatenate.64.clone), calls=%async_computation.2 | async-start | bytes 327680 | tf_op jit(solution)/shard_map/all_to_all | solution.py:117
  21.8 4.4 %all-to-all-done.2 = bf16[16,8,640]{2,1,0:T(8,128)(2,1)S(1)} async-done(((bf16[16,8,640]{2,1,0:T(8,128)(2,1)}), bf16[16,8,640]{2,1,0:T(8,128)(2,1)S(1)}, u32[]{:S(2)}, u32[]{:S(2)}) %all-to-all-start.2) | async-done | bytes 163872 | tf_op jit(solution)/shard_map/all_to_all | solution.py:117
  27.0 4.6 %all-to-all-start.1 = ((bf16[64,32,128]{2,1,0:T(8,128)(2,1)}), bf16[64,32,128]{2,1,0:T(8,128)(2,1)S(1)}, u32[]{:S(2)}, u32[]{:S(2)}) async-start(bf16[64,32,128]{2,1,0:T(8,128)(2,1)} %broadcast_in_dim.30), calls=%async_computation.1 | async-start | bytes 1048576 | tf_op jit(solution)/shard_map/all_to_all | solution.py:46
  31.6 3.0 %collective-permute-start.10 = (bf16[128,640]{1,0:T(8,128)(2,1)S(1)}, bf16[128,640]{1,0:T(8,128)(2,1)S(1)}, u32[]{:S(2)}, u32[]{:S(2)}) collective-permute-start(bf16[128,640]{1,0:T(8,128)(2,1)S(1)} %bitcast.68), channel_id=1, source_target_pairs={{0,2},{1,3},{2,0},{3,1},{4,6},{5,7},{6,4},{7,5},{8,10},{9,11},{10,... | collective-permute-start | bytes 491528 | tf_op jit(solution)/shard_map/ppermute | solution.py:37
  36.1 5.8 %collective-permute-done.10 = bf16[128,640]{1,0:T(8,128)(2,1)S(1)} collective-permute-done((bf16[128,640]{1,0:T(8,128)(2,1)S(1)}, bf16[128,640]{1,0:T(8,128)(2,1)S(1)}, u32[]{:S(2)}, u32[]{:S(2)}) %collective-permute-start.10) | collective-permute-done | bytes 163872 | tf_op jit(solution)/shard_map/ppermute | solution.py:37
  41.9 2.6 %collective-permute-start.9 = (bf16[128,640]{1,0:T(8,128)(2,1)S(1)}, bf16[128,640]{1,0:T(8,128)(2,1)S(1)}, u32[]{:S(2)}, u32[]{:S(2)}) collective-permute-start(bf16[128,640]{1,0:T(8,128)(2,1)S(1)} %bitcast.70), channel_id=1, source_target_pairs={{0,1},{1,2},{2,3},{3,0},{4,5},{5,6},{6,7},{7,4},{8,9},{9,10},{10,1... | collective-permute-start | bytes 491528 | tf_op jit(solution)/shard_map/ppermute | solution.py:37
  46.1 2.3 %collective-permute-done.9 = bf16[128,640]{1,0:T(8,128)(2,1)S(1)} collective-permute-done((bf16[128,640]{1,0:T(8,128)(2,1)S(1)}, bf16[128,640]{1,0:T(8,128)(2,1)S(1)}, u32[]{:S(2)}, u32[]{:S(2)}) %collective-permute-start.9) | collective-permute-done | bytes 163872 | tf_op jit(solution)/shard_map/ppermute | solution.py:37
  54.7 9.8 %all-to-all-start = ((bf16[16,128,512]{2,1,0:T(8,128)(2,1)}), bf16[16,128,512]{2,1,0:T(8,128)(2,1)S(1)}, u32[]{:S(2)}, u32[]{:S(2)}) async-start(bf16[16,128,512]{2,1,0:T(8,128)(2,1)} %broadcast_in_dim.29), calls=%async_computation | async-start | bytes 4194304 | tf_op jit(solution)/shard_map/all_to_all | solution.py:46
  70.8 11.4 %multiply_convert_fusion = (bf16[128,2048]{1,0:T(8,128)(2,1)S(1)}, f32[128]{0:T(128)S(1)}, f32[128,2048]{1,0:T(8,128)}) fusion(f32[2048]{0:T(1024)S(1)} %dynamic_slice.39, f32[128,2048]{1,0:T(8,128)S(1)} %copy-done.7, f32[2048]{0:T(1024)S(1)} %copy-done.28, bf16[5120,2048]{1,0:T(8,128)(2,1)} %param.15, bf16[32,5120]{1,0:T(8,128)(2,1)} %collective-permute-done.2, ...), kind=kOutput, calls=%fused_computation.48 | convolution fusion | flops 2691694592 | bytes 24920576 | tf_op jit(solution)/shard_map/dot_general | solution.py:13
  86.3 5.5 %all-to-all-done = bf16[16,128,512]{2,1,0:T(8,128)(2,1)S(1)} async-done(((bf16[16,128,512]{2,1,0:T(8,128)(2,1)}), bf16[16,128,512]{2,1,0:T(8,128)(2,1)S(1)}, u32[]{:S(2)}, u32[]{:S(2)}) %all-to-all-start) | async-done | bytes 2097184 | tf_op jit(solution)/shard_map/all_to_all | solution.py:46
  98.8 7.1 %all-to-all-start.3 = ((bf16[64,32,128]{2,1,0:T(8,128)(2,1)}), bf16[64,32,128]{2,1,0:T(8,128)(2,1)S(1)}, u32[]{:S(2)}, u32[]{:S(2)}) async-start(bf16[64,32,128]{2,1,0:T(8,128)(2,1)} %bitcast_bitcast_fusion), calls=%async_computation.3 | async-start | bytes 1048576 | tf_op jit(solution)/shard_map/all_to_all | solution.py:173
  108.8 11.0 %all-to-all-done.3 = bf16[64,32,128]{2,1,0:T(8,128)(2,1)S(1)} async-done(((bf16[64,32,128]{2,1,0:T(8,128)(2,1)}), bf16[64,32,128]{2,1,0:T(8,128)(2,1)S(1)}, u32[]{:S(2)}, u32[]{:S(2)}) %all-to-all-start.3) | async-done | bytes 524320 | tf_op jit(solution)/shard_map/all_to_all | solution.py:173
  120.0 2.5 %fusion.104 = f32[128,512]{0,1:T(8,128)S(1)} fusion(bf16[128,2048]{1,0:T(8,128)(2,1)S(1)} %get-tuple-element.14, bf16[2048,512]{1,0:T(8,128)(2,1)} %collective-permute-done.4), kind=kOutput, calls=%fused_computation.184 | convolution fusion | flops 268435456 | bytes 2883584 | tf_op jit(solution)/shard_map/dot_general | solution.py:13
  128.6 2.1 %collective-permute-start.7 = (f32[32,1152]{1,0:T(8,128)}, f32[32,1152]{1,0:T(8,128)}, u32[]{:S(2)}, u32[]{:S(2)}) collective-permute-start(f32[32,1152]{1,0:T(8,128)} %copy.57), channel_id=1, source_target_pairs={{0,2},{1,3},{2,0},{3,1},{4,6},{5,7},{6,4},{7,5},{8,10},{9,11},{10,... | collective-permute-start | bytes 442376 | tf_op jit(solution)/shard_map/ppermute | solution.py:37
  134.5 2.3 %collective-permute-done.7 = f32[32,1152]{1,0:T(8,128)} collective-permute-done((f32[32,1152]{1,0:T(8,128)}, f32[32,1152]{1,0:T(8,128)}, u32[]{:S(2)}, u32[]{:S(2)}) %collective-permute-start.7) | collective-permute-done | bytes 147488 | tf_op jit(solution)/shard_map/ppermute | solution.py:37
  144.1 2.3 %collective-permute-start.14 = (bf16[32,1152]{1,0:T(8,128)(2,1)S(1)}, bf16[32,1152]{1,0:T(8,128)(2,1)S(1)}, u32[]{:S(2)}, u32[]{:S(2)}) collective-permute-start(bf16[32,1152]{1,0:T(8,128)(2,1)S(1)} %concatenate.67), channel_id=1, source_target_pairs={{0,2},{1,3},{2,0},{3,1},{4,6},{5,7},{6,4},{7,5},{8,10},{9,11},{10,... | collective-permute-start | bytes 221192 | tf_op jit(solution)/shard_map/ppermute | solution.py:37
  146.4 2.0 %collective-permute-start.15 = (bf16[32,1152]{1,0:T(8,128)(2,1)S(1)}, bf16[32,1152]{1,0:T(8,128)(2,1)S(1)}, u32[]{:S(2)}, u32[]{:S(2)}) collective-permute-start(bf16[32,1152]{1,0:T(8,128)(2,1)S(1)} %concatenate.67), channel_id=1, source_target_pairs={{0,3},{1,0},{2,1},{3,2},{4,7},{5,4},{6,5},{7,6},{8,11},{9,8},{10,9... | collective-permute-start | bytes 221192 | tf_op jit(solution)/shard_map/ppermute | solution.py:37
  151.8 2.6 %collective-permute-start.19 = (f32[32,1024]{1,0:T(8,128)}, f32[32,1024]{1,0:T(8,128)}, u32[]{:S(2)}, u32[]{:S(2)}) collective-permute-start(f32[32,1024]{1,0:T(8,128)} %slice_add_fusion.1), channel_id=1, source_target_pairs={{0,3},{1,0},{2,1},{3,2},{4,7},{5,4},{6,5},{7,6},{8,11},{9,8},{10,9... | collective-permute-start | bytes 393224 | tf_op jit(solution)/shard_map/ppermute | solution.py:37
  154.7 2.6 %fusion.28 = f32[128,2048]{1,0:T(8,128)} fusion(bf16[64,1024]{1,0:T(8,128)(2,1)S(1)} %maximum_select_fusion.2, bf16[128,1152]{1,0:T(8,128)(2,1)S(1)} %pad_maximum_fusion.5, bf16[64,8192]{1,0:T(8,128)(2,1)} %copy-done.8, s32[]{:T(128)S(6)} %select_n.107), kind=kOutput, calls=%fused_computation.43 | convolution fusion | flops 50339840 | bytes 1703940 | tf_op jit(solution)/shard_map/dot_general | solution.py:13
  157.6 3.4 %fusion.49 = f32[128,2048]{1,0:T(8,128)} fusion(bf16[2048,512]{1,0:T(8,128)(2,1)} %collective-permute-done.4, bf16[128,1152]{1,0:T(8,128)(2,1)S(1)} %pad_maximum_fusion.5), kind=kOutput, calls=%fused_computation.80 | convolution fusion | flops 268435456 | bytes 3276800 | tf_op jit(solution)/shard_map/dot_general | solution.py:21
  161.0 2.9 %fusion.15 = f32[64,2048]{1,0:T(8,128)S(1)} fusion(bf16[128,64]{0,1:T(8,128)(2,1)S(1)} %convolution_convert_fusion, f32[128,2048]{1,0:T(8,128)} %fusion.28, f32[128,2048]{1,0:T(8,128)} %fusion.49, bf16[2048,512]{1,0:T(8,128)(2,1)S(1)} %bitcast.66, f32[128,2048]{1,0:T(8,128)} %get-tuple-element.35, f32[128]{0:T(128)S(1)} %get-tuple-element.3, ...), kind=kOutput, calls=%fused_computation.24 | convolution fusion | flops 303824896 | bytes 5923840 | tf_op jit(solution)/shard_map/dot_general | solution.py:17
  167.3 13.7 %all_to_all.30 = f32[16,2,3072]{2,1,0:T(2,128)S(1)} all-to-all(f32[16,2,3072]{2,1,0:T(2,128)S(1)} %reshape.136), channel_id=1, replica_groups=mesh['grp'=2,'dp'=16,'mp'=4] {'dp'}, dimensions={0} | all-to-all | bytes 786432 | tf_op jit(solution)/shard_map/all_to_all | solution.py:240
  181.2 12.4 %all_to_all.31 = f32[16,2,3072]{2,1,0:T(2,128)S(1)} all-to-all(f32[16,2,3072]{2,1,0:T(2,128)S(1)} %broadcast_in_dim.41), channel_id=1, replica_groups=mesh['grp'=2,'dp'=16,'mp'=4] {'dp'}, dimensions={0} | all-to-all | bytes 786432 | tf_op jit(solution)/shard_map/all_to_all | solution.py:46
  (203 shorter events, 65.7 us)
Async XLA Ops:
  1.8 48.1 %collective-permute-start = (bf16[32,5120]{1,0:T(8,128)(2,1)S(1)}, bf16[32,5120]{1,0:T(8,128)(2,1)S(1)}, u32[]{:S(2)}, u32[]{:S(2)}) collective-permute-start(bf16[32,5120]{1,0:T(8,128)(2,1)S(1)} %constant_dynamic-slice_fusion.6), channel_id=1, source_target_pairs={{0,1},{1,2},{2,3},{3,0},{4,5},{5,6},{6,7},{7,4},{8,9},{9,10},{10,1... | collective-permute-start | bytes 983048 | tf_op jit(solution)/shard_map/ppermute | solution.py:37
  3.5 46.4 %collective-permute-start.1 = (bf16[32,5120]{1,0:T(8,128)(2,1)S(1)}, bf16[32,5120]{1,0:T(8,128)(2,1)}, u32[]{:S(2)}, u32[]{:S(2)}) collective-permute-start(bf16[32,5120]{1,0:T(8,128)(2,1)S(1)} %constant_dynamic-slice_fusion.6), channel_id=1, source_target_pairs={{0,2},{1,3},{2,0},{3,1},{4,6},{5,7},{6,4},{7,5},{8,10},{9,11},{10,... | collective-permute-start | bytes 983048 | tf_op jit(solution)/shard_map/ppermute | solution.py:37
  6.4 43.5 %collective-permute-start.2 = (bf16[32,5120]{1,0:T(8,128)(2,1)S(1)}, bf16[32,5120]{1,0:T(8,128)(2,1)}, u32[]{:S(2)}, u32[]{:S(2)}) collective-permute-start(bf16[32,5120]{1,0:T(8,128)(2,1)S(1)} %constant_dynamic-slice_fusion.6), channel_id=1, source_target_pairs={{0,3},{1,0},{2,1},{3,2},{4,7},{5,4},{6,5},{7,6},{8,11},{9,8},{10,9... | collective-permute-start | bytes 983048 | tf_op jit(solution)/shard_map/ppermute | solution.py:37
  10.1 16.1 %all-to-all-start.2 = ((bf16[16,8,640]{2,1,0:T(8,128)(2,1)}), bf16[16,8,640]{2,1,0:T(8,128)(2,1)S(1)}, u32[]{:S(2)}, u32[]{:S(2)}) async-start(bf16[16,8,640]{2,1,0:T(8,128)(2,1)} %concatenate.64.clone), calls=%async_computation.2 | async-start | bytes 327680 | tf_op jit(solution)/shard_map/all_to_all | solution.py:117
  27.0 26.2 %all-to-all-start.1 = ((bf16[64,32,128]{2,1,0:T(8,128)(2,1)}), bf16[64,32,128]{2,1,0:T(8,128)(2,1)S(1)}, u32[]{:S(2)}, u32[]{:S(2)}) async-start(bf16[64,32,128]{2,1,0:T(8,128)(2,1)} %broadcast_in_dim.30), calls=%async_computation.1 | async-start | bytes 1048576 | tf_op jit(solution)/shard_map/all_to_all | solution.py:46
  31.6 10.3 %collective-permute-start.10 = (bf16[128,640]{1,0:T(8,128)(2,1)S(1)}, bf16[128,640]{1,0:T(8,128)(2,1)S(1)}, u32[]{:S(2)}, u32[]{:S(2)}) collective-permute-start(bf16[128,640]{1,0:T(8,128)(2,1)S(1)} %bitcast.68), channel_id=1, source_target_pairs={{0,2},{1,3},{2,0},{3,1},{4,6},{5,7},{6,4},{7,5},{8,10},{9,11},{10,... | collective-permute-start | bytes 491528 | tf_op jit(solution)/shard_map/ppermute | solution.py:37
  34.9 10.5 %collective-permute-start.11 = (bf16[128,640]{1,0:T(8,128)(2,1)S(1)}, bf16[128,640]{1,0:T(8,128)(2,1)S(1)}, u32[]{:S(2)}, u32[]{:S(2)}) collective-permute-start(bf16[128,640]{1,0:T(8,128)(2,1)S(1)} %bitcast.69), channel_id=1, source_target_pairs={{0,3},{1,0},{2,1},{3,2},{4,7},{5,4},{6,5},{7,6},{8,11},{9,8},{10,9... | collective-permute-start | bytes 491528 | tf_op jit(solution)/shard_map/ppermute | solution.py:37
  41.9 6.5 %collective-permute-start.9 = (bf16[128,640]{1,0:T(8,128)(2,1)S(1)}, bf16[128,640]{1,0:T(8,128)(2,1)S(1)}, u32[]{:S(2)}, u32[]{:S(2)}) collective-permute-start(bf16[128,640]{1,0:T(8,128)(2,1)S(1)} %bitcast.70), channel_id=1, source_target_pairs={{0,1},{1,2},{2,3},{3,0},{4,5},{5,6},{6,7},{7,4},{8,9},{9,10},{10,1... | collective-permute-start | bytes 491528 | tf_op jit(solution)/shard_map/ppermute | solution.py:37
  45.4 7.7 %collective-permute-start.3 = (bf16[128,512]{1,0:T(8,128)(2,1)S(1)}, bf16[128,512]{1,0:T(8,128)(2,1)S(1)}, u32[]{:S(2)}, u32[]{:S(2)}) collective-permute-start(bf16[128,512]{1,0:T(8,128)(2,1)S(1)} %constant_dynamic-slice_fusion.5), channel_id=1, source_target_pairs={{0,0},{1,16},{2,32},{3,48},{4,4},{5,20},{6,36},{7,52},{8,8},{9,24}... | collective-permute-start | bytes 393224 | tf_op jit(solution)/shard_map/ppermute | solution.py:96
  49.9 32.3 %collective-permute-start.12 = (bf16[512,512]{1,0:T(8,128)(2,1)}, bf16[512,512]{1,0:T(8,128)(2,1)}, u32[]{:S(2)}, u32[]{:S(2)}) collective-permute-start(bf16[512,512]{1,0:T(8,128)(2,1)} %slice.181), channel_id=1, source_target_pairs={{0,64},{64,0},{1,65},{65,1},{2,66},{66,2},{3,67},{67,3},{4,68},{68... | collective-permute-start | bytes 1572872 | tf_op jit(solution)/shard_map/ppermute | solution.py:41
  54.7 37.2 %all-to-all-start = ((bf16[16,128,512]{2,1,0:T(8,128)(2,1)}), bf16[16,128,512]{2,1,0:T(8,128)(2,1)S(1)}, u32[]{:S(2)}, u32[]{:S(2)}) async-start(bf16[16,128,512]{2,1,0:T(8,128)(2,1)} %broadcast_in_dim.29), calls=%async_computation | async-start | bytes 4194304 | tf_op jit(solution)/shard_map/all_to_all | solution.py:46
  64.5 2.0 %collective-permute-start.5 = (bf16[32,8192]{1,0:T(8,128)(2,1)S(1)}, bf16[32,8192]{1,0:T(8,128)(2,1)S(1)}, u32[]{:S(2)}, u32[]{:S(2)}) collective-permute-start(bf16[32,8192]{1,0:T(8,128)(2,1)S(1)} %copy_bitcast_fusion), channel_id=1, source_target_pairs={{0,64},{64,0},{1,65},{65,1},{2,66},{66,2},{3,67},{67,3},{4,68},{68... | collective-permute-start | bytes 1572872 | tf_op jit(solution)/shard_map/ppermute | solution.py:41
  70.7 24.8 %collective-permute-start.16 = (f32[32,9216]{1,0:T(8,128)}, f32[32,9216]{1,0:T(8,128)}, u32[]{:S(2)}, u32[]{:S(2)}) collective-permute-start(f32[32,9216]{1,0:T(8,128)} %pad_maximum_fusion.1), channel_id=1, source_target_pairs={{0,64},{64,0},{1,65},{65,1},{2,66},{66,2},{3,67},{67,3},{4,68},{68... | collective-permute-start | bytes 3538952 | tf_op jit(solution)/shard_map/ppermute | solution.py:41
  95.2 24.8 %collective-permute-start.4 = (bf16[2048,512]{1,0:T(8,128)(2,1)S(1)}, bf16[2048,512]{1,0:T(8,128)(2,1)}, u32[]{:S(2)}, u32[]{:S(2)}) collective-permute-start(bf16[2048,512]{1,0:T(8,128)(2,1)S(1)} %bitcast.64), channel_id=1, source_target_pairs={{0,64},{64,0},{1,65},{65,1},{2,66},{66,2},{3,67},{67,3},{4,68},{68... | collective-permute-start | bytes 6291464 | tf_op jit(solution)/shard_map/ppermute | solution.py:41
  98.8 21.0 %all-to-all-start.3 = ((bf16[64,32,128]{2,1,0:T(8,128)(2,1)}), bf16[64,32,128]{2,1,0:T(8,128)(2,1)S(1)}, u32[]{:S(2)}, u32[]{:S(2)}) async-start(bf16[64,32,128]{2,1,0:T(8,128)(2,1)} %bitcast_bitcast_fusion), calls=%async_computation.3 | async-start | bytes 1048576 | tf_op jit(solution)/shard_map/all_to_all | solution.py:173
  126.0 7.4 %collective-permute-start.6 = (f32[32,1152]{1,0:T(8,128)}, f32[32,1152]{1,0:T(8,128)}, u32[]{:S(2)}, u32[]{:S(2)}) collective-permute-start(f32[32,1152]{1,0:T(8,128)} %copy.55), channel_id=1, source_target_pairs={{0,3},{1,0},{2,1},{3,2},{4,7},{5,4},{6,5},{7,6},{8,11},{9,8},{10,9... | collective-permute-start | bytes 442376 | tf_op jit(solution)/shard_map/ppermute | solution.py:37
  128.6 8.3 %collective-permute-start.7 = (f32[32,1152]{1,0:T(8,128)}, f32[32,1152]{1,0:T(8,128)}, u32[]{:S(2)}, u32[]{:S(2)}) collective-permute-start(f32[32,1152]{1,0:T(8,128)} %copy.57), channel_id=1, source_target_pairs={{0,2},{1,3},{2,0},{3,1},{4,6},{5,7},{6,4},{7,5},{8,10},{9,11},{10,... | collective-permute-start | bytes 442376 | tf_op jit(solution)/shard_map/ppermute | solution.py:37
  131.6 7.3 %collective-permute-start.8 = (f32[32,1152]{1,0:T(8,128)}, f32[32,1152]{1,0:T(8,128)}, u32[]{:S(2)}, u32[]{:S(2)}) collective-permute-start(f32[32,1152]{1,0:T(8,128)} %copy.59), channel_id=1, source_target_pairs={{0,1},{1,2},{2,3},{3,0},{4,5},{5,6},{6,7},{7,4},{8,9},{9,10},{10,1... | collective-permute-start | bytes 442376 | tf_op jit(solution)/shard_map/ppermute | solution.py:37
  143.9 7.8 %collective-permute-start.13 = (bf16[32,1152]{1,0:T(8,128)(2,1)S(1)}, bf16[32,1152]{1,0:T(8,128)(2,1)S(1)}, u32[]{:S(2)}, u32[]{:S(2)}) collective-permute-start(bf16[32,1152]{1,0:T(8,128)(2,1)S(1)} %concatenate.67), channel_id=1, source_target_pairs={{0,1},{1,2},{2,3},{3,0},{4,5},{5,6},{6,7},{7,4},{8,9},{9,10},{10,1... | collective-permute-start | bytes 221192 | tf_op jit(solution)/shard_map/ppermute | solution.py:37
  144.1 10.3 %collective-permute-start.14 = (bf16[32,1152]{1,0:T(8,128)(2,1)S(1)}, bf16[32,1152]{1,0:T(8,128)(2,1)S(1)}, u32[]{:S(2)}, u32[]{:S(2)}) collective-permute-start(bf16[32,1152]{1,0:T(8,128)(2,1)S(1)} %concatenate.67), channel_id=1, source_target_pairs={{0,2},{1,3},{2,0},{3,1},{4,6},{5,7},{6,4},{7,5},{8,10},{9,11},{10,... | collective-permute-start | bytes 221192 | tf_op jit(solution)/shard_map/ppermute | solution.py:37
  146.4 8.0 %collective-permute-start.15 = (bf16[32,1152]{1,0:T(8,128)(2,1)S(1)}, bf16[32,1152]{1,0:T(8,128)(2,1)S(1)}, u32[]{:S(2)}, u32[]{:S(2)}) collective-permute-start(bf16[32,1152]{1,0:T(8,128)(2,1)S(1)} %concatenate.67), channel_id=1, source_target_pairs={{0,3},{1,0},{2,1},{3,2},{4,7},{5,4},{6,5},{7,6},{8,11},{9,8},{10,9... | collective-permute-start | bytes 221192 | tf_op jit(solution)/shard_map/ppermute | solution.py:37
  150.0 13.9 %collective-permute-start.17 = (f32[32,1024]{1,0:T(8,128)}, f32[32,1024]{1,0:T(8,128)}, u32[]{:S(2)}, u32[]{:S(2)}) collective-permute-start(f32[32,1024]{1,0:T(8,128)} %slice_add_fusion.1), channel_id=1, source_target_pairs={{0,1},{1,2},{2,3},{3,0},{4,5},{5,6},{6,7},{7,4},{8,9},{9,10},{10,1... | collective-permute-start | bytes 393224 | tf_op jit(solution)/shard_map/ppermute | solution.py:37
  150.0 13.9 %collective-permute-start.18 = (f32[32,1024]{1,0:T(8,128)}, f32[32,1024]{1,0:T(8,128)}, u32[]{:S(2)}, u32[]{:S(2)}) collective-permute-start(f32[32,1024]{1,0:T(8,128)} %slice_add_fusion.1), channel_id=1, source_target_pairs={{0,2},{1,3},{2,0},{3,1},{4,6},{5,7},{6,4},{7,5},{8,10},{9,11},{10,... | collective-permute-start | bytes 393224 | tf_op jit(solution)/shard_map/ppermute | solution.py:37
  151.8 12.2 %collective-permute-start.19 = (f32[32,1024]{1,0:T(8,128)}, f32[32,1024]{1,0:T(8,128)}, u32[]{:S(2)}, u32[]{:S(2)}) collective-permute-start(f32[32,1024]{1,0:T(8,128)} %slice_add_fusion.1), channel_id=1, source_target_pairs={{0,3},{1,0},{2,1},{3,2},{4,7},{5,4},{6,5},{7,6},{8,11},{9,8},{10,9... | collective-permute-start | bytes 393224 | tf_op jit(solution)/shard_map/ppermute | solution.py:37
  (36 other events, 366.2 us)

commit v3 on v2

v3 whole, which is shorter than its diff:
```python
import jax
import jax.numpy as jnp
from jax import lax
from jax.sharding import PartitionSpec as P

ENC_DEV = 256
epsilon = 1e-06
f32 = jnp.float32
bf16 = jnp.bfloat16


def dot(a, b):
    return jnp.dot(a, b, preferred_element_type=f32)


def dot_tn(a, b):
    return lax.dot_general(a, b, (((0,), (0,)), ((), ())), preferred_element_type=f32)


def dot_nt(a, b):
    return lax.dot_general(a, b, (((1,), (1,)), ((), ())), preferred_element_type=f32)


def split_two(a):
    high = lax.reduce_precision(a, 8, 7)
    return high.astype(bf16), (a - high).astype(bf16)


def split_three(a):
    high = lax.reduce_precision(a, 8, 7)
    return (high.astype(bf16), *split_two(a - high))


def turned(array, axis, step):
    count = lax.axis_size(axis)
    return lax.ppermute(array, axis, [(i, (i + step) % count) for i in range(count)])


def crossed(array):
    return lax.ppermute(array, "grp", [(0, 1), (1, 0)])


def along(array, z_step, x_step, side):
    pairs = [
        (z * side + x, (z + z_step) % side * side + (x + x_step) % side)
        for z in range(side)
        for x in range(side)
    ]
    return lax.ppermute(array, "dp", pairs)


def to_everyone(array, axes):
    count = lax.axis_size(axes)
    return lax.all_to_all(
        jnp.broadcast_to(array[None], (count, *array.shape)), axes, 0, 0, tiled=True
    )


def body(
    hidden,
    enc_weight,
    enc_bias,
    enc_frozen,
    enc_adapter,
    text_rows,
    norm_gain,
    value_weight,
    value_bias,
    llm_frozen,
    llm_adapter,
    targets,
    dest_owner,
    seq_length,
):
    n_dp = lax.axis_size("dp")
    n_mp = lax.axis_size("mp")
    side = n_mp
    owners = n_dp * n_mp
    grp = lax.axis_index("grp")
    dp = lax.axis_index("dp")
    mp = lax.axis_index("mp")
    first = grp == 0
    width = text_rows.shape[1]
    part_width = enc_weight.shape[1]
    rank = enc_frozen.shape[1]
    half_rank = rank // 2
    kv = value_weight.shape[1]
    half_kv = kv // 2
    shard = value_weight.shape[0]
    block_rows = hidden.shape[0]
    mine_rows = block_rows // 2
    capacity = 2 * ENC_DEV // owners

    swap = [
        ((z * side + x) * side + y, (y * side + x) * side + z)
        for z in range(side)
        for x in range(side)
        for y in range(side)
    ]
    col = dp % side
    w_half = lax.dynamic_slice_in_dim(value_weight, grp * half_kv, half_kv, axis=1)
    w_moved = lax.ppermute(w_half, ("dp", "mp"), swap)

    own_hidden = lax.dynamic_slice_in_dim(hidden, grp * mine_rows, mine_rows)
    hid = jnp.concatenate([own_hidden] + [turned(own_hidden, "mp", k) for k in range(1, n_mp)])

    w_line = [along(w_moved, k, 0, side) for k in (3, 2, 1)] + [w_moved]
    w_line = lax.dynamic_slice_in_dim(
        jnp.concatenate(w_line + w_line), ((side - 1 - dp // side) % side) * shard, side * shard
    )
    w_mine = jnp.zeros((side * side * shard, half_kv), bf16)
    for k in range(side):
        piece = along(w_line, 0, k, side) if k else w_line
        w_mine = lax.dynamic_update_slice_in_dim(
            w_mine, piece, ((col - k) % side) * (side * shard), axis=0
        )

    a_all = to_everyone(llm_frozen.T, ("dp", "mp")).transpose(1, 0, 2).reshape(rank, width)
    a_part = lax.dynamic_slice_in_dim(a_all, mp * part_width, part_width, axis=1)
    b_half = lax.dynamic_slice_in_dim(llm_adapter, grp * half_kv, half_kv, axis=1)
    bias_wide = value_bias.astype(f32)
    bias_half = lax.dynamic_slice_in_dim(bias_wide, grp * half_kv, half_kv)

    own_length = seq_length[0]
    area = capacity * n_dp
    t_half = lax.dynamic_slice(targets, (0, grp * half_kv), (area, half_kv))
    t_half = t_half.reshape(capacity, n_dp, half_kv).transpose(1, 0, 2)
    t_half = jnp.concatenate(
        [t_half, jnp.full((n_dp, capacity, 128), own_length.astype(bf16))], axis=2
    )
    t_here = lax.all_to_all(t_half, "dp", 0, 0, tiled=True).reshape(n_dp * capacity, -1)
    t_table = jnp.concatenate([t_here] + [turned(t_here, "mp", k) for k in range(1, n_mp)])
    destiny = dest_owner[:, 0]
    block_dest = lax.dynamic_slice_in_dim(destiny, dp * ENC_DEV, ENC_DEV)
    local = jnp.arange(ENC_DEV, dtype=jnp.int32)
    from_mp = (mp - local % (ENC_DEV // 2) // mine_rows) % n_mp
    from_grp = (grp + local // (ENC_DEV // 2)) % 2
    place = from_mp * block_rows + from_grp * mine_rows + local % mine_rows
    own_dest = jnp.sum(jnp.where(place[:, None] == local[None, :], block_dest[None, :], 0), axis=1)
    earlier = (own_dest[:, None] == block_dest[None, :]) & (local[None, :] < place[:, None])
    slot = jnp.sum(earlier.astype(jnp.int32), axis=1)
    source = (mp - own_dest % n_mp) % n_mp
    line = source * (n_dp * capacity) + (own_dest // n_mp) * capacity + slot
    pick = (line[:, None] == jnp.arange(n_mp * n_dp * capacity, dtype=jnp.int32)[None, :]).astype(
        bf16
    )
    picked = dot(pick, t_table)
    own_targets = picked[:, :half_kv]
    length = picked[:, half_kv : half_kv + 1]
    position = (slot * n_dp + dp)[:, None].astype(f32)
    weight = jnp.where(position < length, 1.0 / length, 0.0)

    gain_wide = norm_gain.astype(f32)
    text_count = text_rows.shape[0] // 2
    text_wide = lax.dynamic_slice_in_dim(text_rows, grp * text_count, text_count).astype(f32)
    text_inverse = lax.rsqrt(jnp.mean(text_wide * text_wide, axis=1, keepdims=True) + epsilon)
    text_normed = (text_wide * text_inverse * gain_wide).astype(bf16)
    text_low = dot_nt(text_normed, a_all).astype(bf16)
    owner_index = dp * n_mp + mp
    counts = jnp.sum((destiny.reshape(n_dp, ENC_DEV) == owner_index).astype(jnp.int32), axis=1)
    row = grp * text_count + jnp.arange(text_count, dtype=jnp.int32)
    taken = (row < area) & (
        row // n_dp
        < jnp.sum(
            jnp.where(
                (row % n_dp)[:, None] == jnp.arange(n_dp, dtype=jnp.int32)[None, :], counts, 0
            ),
            axis=1,
        )
    )
    keep = (row < own_length) & ~taken
    text_kept = jnp.where(keep[:, None], text_low, jnp.zeros_like(text_low))
    text_weight = 1.0 / own_length.astype(f32)
    text_sum = dot_tn(text_kept, text_normed) * text_weight
    own_text_targets = lax.dynamic_slice_in_dim(targets, grp * text_count, text_count).astype(f32)
    rest = bias_wide + dot(text_low, llm_adapter) - own_text_targets
    rest_high, rest_low = split_two(rest)
    rest_sum = dot_tn(
        jnp.concatenate([text_kept, text_kept]), jnp.concatenate([rest_high, rest_low])
    )
    rest_sum = rest_sum * text_weight
    text_here = lax.dynamic_slice_in_dim(text_sum, mp * part_width, part_width, axis=1)
    text_sent = text_sum.astype(bf16)
    for k in range(1, n_mp):
        block = lax.dynamic_slice_in_dim(
            text_sent, ((mp - k) % n_mp) * part_width, part_width, axis=1
        )
        text_here = text_here + turned(block, "mp", -k).astype(f32)
    rest_mine = lax.dynamic_slice_in_dim(rest_sum, grp * half_kv, half_kv, axis=1)
    rest_give = lax.dynamic_slice_in_dim(rest_sum, (1 - grp) * half_kv, half_kv, axis=1)
    came = crossed(jnp.concatenate([text_here, rest_give], axis=1))
    here_high, here_low = split_two(text_here + came[:, :part_width])
    text_grad = dot(jnp.concatenate([here_high, here_low]), w_mine)
    text_grad = text_grad[:rank] + text_grad[rank:] + rest_mine + came[:, part_width:]
    text_grad = text_grad + (
        turned(text_grad, "mp", 1) + turned(text_grad, "mp", 2) + turned(text_grad, "mp", 3)
    )

    enc_low = dot(hid, enc_frozen).astype(bf16)
    merged = dot(hid, enc_weight) + enc_bias.astype(f32) + dot(enc_low, enc_adapter)
    image = merged.astype(bf16)
    image = jnp.concatenate([image, crossed(image)])
    enc_low = jnp.concatenate([enc_low, crossed(enc_low)])
    image_wide = image.astype(f32)
    gain_part = lax.dynamic_slice_in_dim(gain_wide, mp * part_width, part_width)
    scaled_rows = (image_wide * gain_part).astype(bf16)
    squares = jnp.sum(image_wide * image_wide, axis=1, keepdims=True)
    part_values = dot(scaled_rows, w_mine)
    part_low = dot_nt(scaled_rows, a_part)
    pad = jnp.zeros((ENC_DEV, 128 - rank - 3), bf16)
    sent = jnp.concatenate(
        [part_values.astype(bf16), part_low.astype(bf16), *split_three(squares), pad], axis=1
    )
    total = jnp.concatenate(
        [part_values, part_low, squares, jnp.zeros((ENC_DEV, 128 - rank - 1), f32)], axis=1
    ).reshape(2, n_mp, mine_rows, -1)
    for k in range(1, n_mp):
        other = turned(sent, "mp", k).astype(f32)
        edge = half_kv + rank
        other_squares = (
            other[:, edge : edge + 1] + other[:, edge + 1 : edge + 2] + other[:, edge + 2 : edge + 3]
        )
        other = jnp.concatenate(
            [other[:, :edge], other_squares, jnp.zeros((ENC_DEV, 128 - rank - 1), f32)], axis=1
        )
        total = total + jnp.roll(other.reshape(2, n_mp, mine_rows, -1), k, axis=1)
    total = total.reshape(ENC_DEV, -1)
    raw_values = total[:, :half_kv]
    raw_low = total[:, half_kv : half_kv + rank]
    inverse = lax.rsqrt(total[:, half_kv + rank : half_kv + rank + 1] / width + epsilon)
    low = (raw_low * inverse).astype(bf16)
    values_out = raw_values * inverse + bias_half + dot(low, b_half)
    dvalues = ((values_out - own_targets) * weight).astype(bf16)
    dlow = dot_nt(dvalues, b_half).astype(bf16)
    centre = (
        jnp.sum(dvalues.astype(f32) * raw_values, axis=1, keepdims=True)
        + jnp.sum(dlow.astype(f32) * raw_low, axis=1, keepdims=True)
    ) / width
    factor = inverse * inverse * inverse * centre
    dnormed = dot_nt(dvalues, w_mine) + dot(dlow, a_part)
    dimage = (inverse * (gain_part * dnormed) - image_wide * factor).astype(bf16)
    enc_grad = dot_tn(enc_low, dimage)
    llm_grad = dot_tn(low, dvalues) + text_grad

    both = jnp.concatenate([enc_grad, llm_grad], axis=1)
    mine = lax.dynamic_slice_in_dim(both, grp * half_rank, half_rank)
    came = crossed(lax.dynamic_slice_in_dim(both, (1 - grp) * half_rank, half_rank))
    llm_mine, llm_came = mine[:, part_width:], came[:, part_width:]
    mine = jnp.concatenate(
        [
            mine[:, :part_width] + came[:, :part_width],
            jnp.where(first, llm_mine, llm_came),
            jnp.where(first, llm_came, llm_mine),
        ],
        axis=1,
    )
    mine = mine.reshape(n_dp, half_rank // n_dp, -1)
    mine = jnp.sum(lax.all_to_all(mine, "dp", 0, 0, tiled=True), axis=0)
    whole = to_everyone(mine, "dp").reshape(half_rank, -1)
    return whole[:, :part_width], whole[:, part_width:]


def solution(mesh):
    return jax.shard_map(
        body,
        mesh=mesh,
        in_specs=(
            P(("dp", "mp"), None),
            P(None, "mp"),
            P("mp"),
            P(),
            P(None, "mp"),
            P(("dp", "mp"), None),
            P(),
            P(("dp", "mp"), None),
            P(),
            P(("dp", "mp"), None),
            P(),
            P(("dp", "mp"), None),
            P(),
            P(("dp", "mp")),
        ),
        out_specs=(P("grp", "mp"), P("grp", None)),
        check_vma=False,
    )
```

time: 196 us -> 194 us (0.990)
  waiting for transfers between devices: 35 us -> 20.3 us
  starting transfers between devices: 55.1 us -> 59.9 us
  local copies, waits for them, and re-layouts: 30.1 us -> 34.2 us
  other arithmetic: 12 us -> 15.6 us
    ppermute x0 -> x6, starting transfers between devices: none -> 12.5 us  [along(): return lax.ppermute(array, 'dp', pairs)]
    all_to_all x1 -> x0, waiting for transfers between devices: 11 us -> none  [body(): lax.all_to_all(text_parts.astype(bf16), ('dp', 'mp'), 0, 0, tiled=True)]
    all_to_all x1 -> x0, starting transfers between devices: 7.09 us -> none  [body(): lax.all_to_all(text_parts.astype(bf16), ('dp', 'mp'), 0, 0, tiled=True)]
    slice x10 -> x9, local copies, waits for them, and re-layouts: 8.05 us -> 1.94 us  [the longest x5 0.94 us: body(): total = total + jnp.roll(other.reshape(2, n_mp, mine_rows, -1), k, axis=1)]
    concatenate x2 -> x7, local copies, waits for them, and re-layouts: 0.15 us -> 6.21 us  [the longest x3 4.34 us: body(): total = total + jnp.roll(other.reshape(2, n_mp, mine_rows, -1), k, axis=1)]
    all_to_all x2 -> x1, waiting for transfers between devices: 5.55 us -> 0.01 us  [to_everyone(): lax.all_to_all(jnp.broadcast_to(array[None], (count, *array.shape)), axes...]
    dynamic_update_slice x0 -> x4, local copies, waits for them, and re-layouts: none -> 5.17 us  [body(): lax.dynamic_update_slice_in_dim(w_mine, piece, (col - k) % side * (side *...]
    ppermute x3 -> x0, local copies, waits for them, and re-layouts: 5.06 us -> none  [turned(): lax.ppermute(array, axis, [(i, (i + step) % count) for i in range(count)])]
  transfers between devices with their start and end apart: 25 -> 28, of which waited for: 8 -> 9; matrix products, arithmetic and copies ran while one was open for 29% -> 39% of each run, Pallas kernels for 0% -> 0%
where the time goes in v3:
time: 194 us; the launch traced here: 192 us
  starting transfers between devices  59.9 us (31%)
  local copies, waits for them, and re-layouts  34.2 us (18%)
  matrix products  32.9 us (17%)
  blocking collectives  27.3 us (14%)
  waiting for transfers between devices  20.3 us (10%)
  other arithmetic  15.6 us (8%)
  between operations  2.24 us (1%)
    ppermute x15, starting transfers between devices, turned(): lax.ppermute(array, axis, [(i, (i + step) % count) for i in range(count)])  26 us
    dot_general x9, matrix products, dot(): return jnp.dot(a, b, preferred_element_type=f32)  21.6 us
    all_to_all x1, blocking collectives, body(): mine = jnp.sum(lax.all_to_all(mine, 'dp', 0, 0, tiled=True), axis=0)  14.9 us
    ppermute x15, waiting for transfers between devices, turned(): lax.ppermute(array, axis, [(i, (i + step) % count) for i in range(count)])  14.1 us
    ppermute x6, starting transfers between devices, along(): return lax.ppermute(array, 'dp', pairs)  12.5 us
    all_to_all x1, blocking collectives, to_everyone(): lax.all_to_all(jnp.broadcast_to(array[None], (count, *array.shape)), axes...  12.4 us
    all_to_all x1, starting transfers between devices, to_everyone(): lax.all_to_all(jnp.broadcast_to(array[None], (count, *array.shape)), axes...  11 us
    unnamed x49, local copies, waits for them, and re-layouts  9.73 us
  transfers between devices with their start and end apart: 28, of which 9 were waited for; matrix products, arithmetic and copies ran while one was open for 39% of the time, Pallas kernels for 0%

profile of v3, /device:TPU:0, one launch (start us, length us, event | category | flops | bytes accessed | tf_op | source)
XLA Modules:
  0.0 192.4 jit_solution(10301908823760062145)
XLA Ops:
  4.1 2.9 %collective-permute-start.1 = (bf16[32,5120]{1,0:T(8,128)(2,1)}, bf16[32,5120]{1,0:T(8,128)(2,1)}, u32[]{:S(2)}, u32[]{:S(2)}) collective-permute-start(bf16[32,5120]{1,0:T(8,128)(2,1)} %constant_dynamic-slice_fusion.8), channel_id=1, source_target_pairs={{0,2},{1,3},{2,0},{3,1},{4,6},{5,7},{6,4},{7,5},{8,10},{9,11},{10,... | collective-permute-start | bytes 983048 | tf_op jit(solution)/shard_map/ppermute | solution.py:36
  12.3 9.1 %all-to-all-start.1 = ((bf16[16,8,640]{2,1,0:T(8,128)(2,1)}), bf16[16,8,640]{2,1,0:T(8,128)(2,1)S(1)}, u32[]{:S(2)}, u32[]{:S(2)}) async-start(bf16[16,8,640]{2,1,0:T(8,128)(2,1)} %concatenate.92.clone), calls=%async_computation.1 | async-start | bytes 327680 | tf_op jit(solution)/shard_map/all_to_all | solution.py:131
  23.9 6.9 %collective-permute-start.6 = (bf16[128,512]{1,0:T(8,128)(2,1)S(1)}, bf16[128,512]{1,0:T(8,128)(2,1)S(1)}, u32[]{:S(2)}, u32[]{:S(2)}) collective-permute-start(bf16[128,512]{1,0:T(8,128)(2,1)S(1)} %collective-permute-done.5), channel_id=1, source_target_pairs={{0,48},{4,52},{8,56},{12,60},{16,0},{20,4},{24,8},{28,12},{32,16},... | collective-permute-start | bytes 393224 | tf_op jit(solution)/shard_map/ppermute | solution.py:49
  32.1 4.2 %collective-permute-done.6 = bf16[128,512]{1,0:T(8,128)(2,1)S(1)} collective-permute-done((bf16[128,512]{1,0:T(8,128)(2,1)S(1)}, bf16[128,512]{1,0:T(8,128)(2,1)S(1)}, u32[]{:S(2)}, u32[]{:S(2)}) %collective-permute-start.6) | collective-permute-done | bytes 131104 | tf_op jit(solution)/shard_map/ppermute | solution.py:49
  38.2 11.0 %all-to-all-start = ((bf16[64,64,128]{2,1,0:T(8,128)(2,1)}), bf16[64,64,128]{2,1,0:T(8,128)(2,1)S(1)}, u32[]{:S(2)}, u32[]{:S(2)}) async-start(bf16[64,64,128]{2,1,0:T(8,128)(2,1)} %broadcast_in_dim.45), calls=%async_computation | async-start | bytes 2097152 | tf_op jit(solution)/shard_map/all_to_all | solution.py:54
  51.6 2.7 %collective-permute-start.16 = (bf16[128,640]{1,0:T(8,128)(2,1)S(1)}, bf16[128,640]{1,0:T(8,128)(2,1)S(1)}, u32[]{:S(2)}, u32[]{:S(2)}) collective-permute-start(bf16[128,640]{1,0:T(8,128)(2,1)S(1)} %bitcast.57), channel_id=1, source_target_pairs={{0,2},{1,3},{2,0},{3,1},{4,6},{5,7},{6,4},{7,5},{8,10},{9,11},{10,... | collective-permute-start | bytes 491528 | tf_op jit(solution)/shard_map/ppermute | solution.py:36
  63.2 2.7 %collective-permute-start.10 = (bf16[512,512]{1,0:T(8,128)(2,1)}, bf16[512,512]{1,0:T(8,128)(2,1)}, u32[]{:S(2)}, u32[]{:S(2)}) collective-permute-start(bf16[512,512]{1,0:T(8,128)(2,1)} %get-tuple-element.3), channel_id=1, source_target_pairs={{0,8},{4,12},{8,0},{12,4},{16,24},{20,28},{24,16},{28,20},{32,40},... | collective-permute-start | bytes 1572872 | tf_op jit(solution)/shard_map/ppermute | solution.py:49
  65.9 2.4 %convolution_convert_fusion.1 = bf16[128,64]{0,1:T(8,128)(2,1)} fusion(bf16[5120,64]{0,1:T(8,128)(2,1)S(1)} %copy-done.19, bf16[32,5120]{1,0:T(8,128)(2,1)} %collective-permute-done.2, bf16[32,5120]{1,0:T(8,128)(2,1)} %collective-permute-done.1, bf16[32,5120]{1,0:T(8,128)(2,1)} %collective-permute-done, bf16[32,5120]{1,0:T(8,128)(2,1)} %constant_dynamic-slice_fusion.8), kind=kOutput, calls=%fused_computation.26 | convolution fusion | flops 89137152 | bytes 1982464 | tf_op jit(solution)/shard_map/dot_general | solution.py:13
  69.4 11.1 %fusion.8 = bf16[128,2048]{1,0:T(8,128)(2,1)} fusion(f32[128,2048]{1,0:T(8,128)S(1)} %fusion.91, bf16[5120,2048]{1,0:T(8,128)(2,1)} %param.15, f32[2048]{0:T(1024)S(1)} %convert_element_type.158, bf16[32,5120]{1,0:T(8,128)(2,1)} %collective-permute-done.2, bf16[32,5120]{1,0:T(8,128)(2,1)} %collective-permute-done.1, ...), kind=kOutput, calls=%fused_computation.16 | convolution fusion | flops 2690383872 | bytes 23863296 | tf_op jit(solution)/shard_map/dot_general | solution.py:13
  84.1 2.1 %copy.92 = f32[256,512]{0,1:T(8,128)} copy(f32[256,512]{1,0:T(8,128)} %slice.159) | data formatting | bytes 1048576
  93.8 2.8 %fusion.88 = (bf16[256,512]{1,0:T(8,128)(2,1)}, f32[256,512]{1,0:T(8,128)}) fusion(bf16[2048,512]{1,0:T(8,128)(2,1)S(1)} %constant_dynamic-update-slice_fusion.8, f32[2048]{0:T(1024)S(1)} %dynamic_slice.58, bf16[128,2048]{1,0:T(8,128)(2,1)} %collective-permute-done.4, bf16[128,2048]{1,0:T(8,128)(2,1)} %fusion.8), kind=kOutput, calls=%fused_computation.206 | convolution fusion | flops 540147712 | bytes 3940352 | tf_op jit(solution)/shard_map/dot_general | solution.py:13
  98.6 2.1 %broadcast_select_fusion = (bf16[80,64]{0,1:T(8,128)(2,1)S(1)}, bf16[80,64]{0,1:T(8,128)(2,1)S(1)}) fusion(pred[80]{0:T(512)(128)(4,1)S(1)} %not_and_fusion, f32[8192]{0:T(1024)S(1)} %convert_element_type.161, f32[80]{0:T(128)S(1)} %add_rsqrt_fusion, bf16[160,8192]{1,0:T(8,128)(2,1)} %param.19, s32[]{:T(128)S(6)} %select_n.246, ...), kind=kOutput, calls=%fused_computation.121 | convolution fusion | flops 86517760 | bytes 2412948 | tf_op jit(solution)/shard_map/dot_general | solution.py:21
  104.1 2.3 %collective-permute-start.19 = (bf16[64,2048]{1,0:T(8,128)(2,1)}, bf16[64,2048]{1,0:T(8,128)(2,1)}, u32[]{:S(2)}, u32[]{:S(2)}) collective-permute-start(bf16[64,2048]{1,0:T(8,128)(2,1)} %get-tuple-element.8), channel_id=1, source_target_pairs={{0,2},{1,3},{2,0},{3,1},{4,6},{5,7},{6,4},{7,5},{8,10},{9,11},{10,... | collective-permute-start | bytes 786440 | tf_op jit(solution)/shard_map/ppermute | solution.py:36
  107.5 2.3 %fusion.89 = (bf16[256,64]{0,1:T(8,128)(2,1)S(1)}, f32[256,64]{0,1:T(8,128)}) fusion(bf16[64,8192]{1,0:T(8,128)(2,1)S(1)} %copy_bitcast_fusion, s32[]{:T(128)S(6)} %select_n.217, f32[2048]{0:T(1024)S(1)} %dynamic_slice.58, bf16[128,2048]{1,0:T(8,128)(2,1)} %collective-permute-done.4, bf16[128,2048]{1,0:T(8,128)(2,1)} %fusion.8), kind=kOutput, calls=%fused_computation.207 | convolution fusion | flops 70270976 | bytes 1417220 | tf_op jit(solution)/shard_map/dot_general | solution.py:21
  111.1 3.3 %collective-permute-start.14 = (bf16[256,640]{1,0:T(8,128)(2,1)S(1)}, bf16[256,640]{1,0:T(8,128)(2,1)S(1)}, u32[]{:S(2)}, u32[]{:S(2)}) collective-permute-start(bf16[256,640]{1,0:T(8,128)(2,1)S(1)} %concatenate.82), channel_id=1, source_target_pairs={{0,3},{1,0},{2,1},{3,2},{4,7},{5,4},{6,5},{7,6},{8,11},{9,8},{10,9... | collective-permute-start | bytes 983048 | tf_op jit(solution)/shard_map/ppermute | solution.py:36
  114.9 2.4 %collective-permute-start.13 = (bf16[256,640]{1,0:T(8,128)(2,1)S(1)}, bf16[256,640]{1,0:T(8,128)(2,1)S(1)}, u32[]{:S(2)}, u32[]{:S(2)}) collective-permute-start(bf16[256,640]{1,0:T(8,128)(2,1)S(1)} %concatenate.82), channel_id=1, source_target_pairs={{0,2},{1,3},{2,0},{3,1},{4,6},{5,7},{6,4},{7,5},{8,10},{9,11},{10,... | collective-permute-start | bytes 983048 | tf_op jit(solution)/shard_map/ppermute | solution.py:36
  122.7 3.1 %collective-permute-done.14 = bf16[256,640]{1,0:T(8,128)(2,1)S(1)} collective-permute-done((bf16[256,640]{1,0:T(8,128)(2,1)S(1)}, bf16[256,640]{1,0:T(8,128)(2,1)S(1)}, u32[]{:S(2)}, u32[]{:S(2)}) %collective-permute-start.14) | collective-permute-done | bytes 327712 | tf_op jit(solution)/shard_map/ppermute | solution.py:36
  127.6 5.4 %collective-permute-done.12 = bf16[256,640]{1,0:T(8,128)(2,1)S(1)} collective-permute-done((bf16[256,640]{1,0:T(8,128)(2,1)S(1)}, bf16[256,640]{1,0:T(8,128)(2,1)S(1)}, u32[]{:S(2)}, u32[]{:S(2)}) %collective-permute-start.12) | collective-permute-done | bytes 327712 | tf_op jit(solution)/shard_map/ppermute | solution.py:36
  135.5 2.2 %copy.82 = f32[256,640]{0,1:T(8,128)} copy(f32[256,640]{1,0:T(8,128)} %bitcast.52) | data formatting | bytes 1310720 | tf_op jit(solution)/shard_map/jit(_roll_static)/concatenate | solution.py:226
  143.5 2.8 %fusion.43 = f32[256,2048]{1,0:T(8,128)} fusion(bf16[256,64]{0,1:T(8,128)(2,1)S(1)} %get-tuple-element.32, bf16[64,8192]{1,0:T(8,128)(2,1)} %copy-done.3, s32[]{:T(128)S(6)} %select_n.217), kind=kOutput, calls=%fused_computation.85 | convolution fusion | flops 67108864 | bytes 2392068 | tf_op jit(solution)/shard_map/dot_general | solution.py:13
  153.9 3.1 %fusion.11 = f32[64,2048]{1,0:T(8,128)S(1)} fusion(f32[256,2048]{1,0:T(8,128)} %fusion.43, bf16[256,512]{0,1:T(8,128)(2,1)S(1)} %get-tuple-element.30, bf16[2048,512]{1,0:T(8,128)(2,1)S(1)} %constant_dynamic-update-slice_fusion.8, f32[256]{0:T(256)S(1)} %bitcast.70, f32[256]{0:T(256)S(1)} %bitcast.67, f32[2048]{0:T(1024)S(1)} %dynamic_slice.58, ...), kind=kOutput, calls=%fused_computation.19 | convolution fusion | flops 609288192 | bytes 6072320 | tf_op jit(solution)/shard_map/dot_general | solution.py:17
  157.0 2.2 %collective-permute-done.22 = f32[64,512]{1,0:T(8,128)} collective-permute-done((f32[64,512]{1,0:T(8,128)}, f32[64,512]{1,0:T(8,128)}, u32[]{:S(2)}, u32[]{:S(2)}) %collective-permute-start.22) | collective-permute-done | bytes 131104 | tf_op jit(solution)/shard_map/ppermute | solution.py:36
  163.2 14.9 %all_to_all.20 = f32[16,2,3072]{2,1,0:T(2,128)S(1)} all-to-all(f32[16,2,3072]{2,1,0:T(2,128)S(1)} %reshape.308), channel_id=1, replica_groups=mesh['grp'=2,'dp'=16,'mp'=4] {'dp'}, dimensions={0} | all-to-all | bytes 786432 | tf_op jit(solution)/shard_map/all_to_all | solution.py:258
  178.3 12.4 %all_to_all.21 = f32[16,2,3072]{2,1,0:T(2,128)S(1)} all-to-all(f32[16,2,3072]{2,1,0:T(2,128)S(1)} %broadcast_in_dim.90), channel_id=1, replica_groups=mesh['grp'=2,'dp'=16,'mp'=4] {'dp'}, dimensions={0} | all-to-all | bytes 786432 | tf_op jit(solution)/shard_map/all_to_all | solution.py:54
  (184 shorter events, 73.8 us)
Async XLA Ops:
  2.5 57.8 %collective-permute-start = (bf16[32,5120]{1,0:T(8,128)(2,1)}, bf16[32,5120]{1,0:T(8,128)(2,1)}, u32[]{:S(2)}, u32[]{:S(2)}) collective-permute-start(bf16[32,5120]{1,0:T(8,128)(2,1)} %constant_dynamic-slice_fusion.8), channel_id=1, source_target_pairs={{0,1},{1,2},{2,3},{3,0},{4,5},{5,6},{6,7},{7,4},{8,9},{9,10},{10,1... | collective-permute-start | bytes 983048 | tf_op jit(solution)/shard_map/ppermute | solution.py:36
  4.1 57.6 %collective-permute-start.1 = (bf16[32,5120]{1,0:T(8,128)(2,1)}, bf16[32,5120]{1,0:T(8,128)(2,1)}, u32[]{:S(2)}, u32[]{:S(2)}) collective-permute-start(bf16[32,5120]{1,0:T(8,128)(2,1)} %constant_dynamic-slice_fusion.8), channel_id=1, source_target_pairs={{0,2},{1,3},{2,0},{3,1},{4,6},{5,7},{6,4},{7,5},{8,10},{9,11},{10,... | collective-permute-start | bytes 983048 | tf_op jit(solution)/shard_map/ppermute | solution.py:36
  7.0 56.2 %collective-permute-start.2 = (bf16[32,5120]{1,0:T(8,128)(2,1)}, bf16[32,5120]{1,0:T(8,128)(2,1)}, u32[]{:S(2)}, u32[]{:S(2)}) collective-permute-start(bf16[32,5120]{1,0:T(8,128)(2,1)} %constant_dynamic-slice_fusion.8), channel_id=1, source_target_pairs={{0,3},{1,0},{2,1},{3,2},{4,7},{5,4},{6,5},{7,6},{8,11},{9,8},{10,9... | collective-permute-start | bytes 983048 | tf_op jit(solution)/shard_map/ppermute | solution.py:36
  9.3 14.6 %collective-permute-start.5 = (bf16[128,512]{1,0:T(8,128)(2,1)S(1)}, bf16[128,512]{1,0:T(8,128)(2,1)S(1)}, u32[]{:S(2)}, u32[]{:S(2)}) collective-permute-start(bf16[128,512]{1,0:T(8,128)(2,1)S(1)} %constant_dynamic-slice_fusion.7), channel_id=1, source_target_pairs={{0,0},{1,16},{2,32},{3,48},{4,4},{5,20},{6,36},{7,52},{8,8},{9,24}... | collective-permute-start | bytes 393224 | tf_op jit(solution)/shard_map/ppermute | solution.py:102
  12.3 24.6 %all-to-all-start.1 = ((bf16[16,8,640]{2,1,0:T(8,128)(2,1)}), bf16[16,8,640]{2,1,0:T(8,128)(2,1)S(1)}, u32[]{:S(2)}, u32[]{:S(2)}) async-start(bf16[16,8,640]{2,1,0:T(8,128)(2,1)} %concatenate.92.clone), calls=%async_computation.1 | async-start | bytes 327680 | tf_op jit(solution)/shard_map/all_to_all | solution.py:131
  23.9 12.4 %collective-permute-start.6 = (bf16[128,512]{1,0:T(8,128)(2,1)S(1)}, bf16[128,512]{1,0:T(8,128)(2,1)S(1)}, u32[]{:S(2)}, u32[]{:S(2)}) collective-permute-start(bf16[128,512]{1,0:T(8,128)(2,1)S(1)} %collective-permute-done.5), channel_id=1, source_target_pairs={{0,48},{4,52},{8,56},{12,60},{16,0},{20,4},{24,8},{28,12},{32,16},... | collective-permute-start | bytes 393224 | tf_op jit(solution)/shard_map/ppermute | solution.py:49
  30.9 18.4 %collective-permute-start.7 = (bf16[128,512]{1,0:T(8,128)(2,1)S(1)}, bf16[128,512]{1,0:T(8,128)(2,1)S(1)}, u32[]{:S(2)}, u32[]{:S(2)}) collective-permute-start(bf16[128,512]{1,0:T(8,128)(2,1)S(1)} %collective-permute-done.5), channel_id=1, source_target_pairs={{0,32},{4,36},{8,40},{12,44},{16,48},{20,52},{24,56},{28,60},{32,0... | collective-permute-start | bytes 393224 | tf_op jit(solution)/shard_map/ppermute | solution.py:49
  36.3 15.3 %collective-permute-start.8 = (bf16[128,512]{1,0:T(8,128)(2,1)S(1)}, bf16[128,512]{1,0:T(8,128)(2,1)S(1)}, u32[]{:S(2)}, u32[]{:S(2)}) collective-permute-start(bf16[128,512]{1,0:T(8,128)(2,1)S(1)} %collective-permute-done.5), channel_id=1, source_target_pairs={{0,16},{4,20},{8,24},{12,28},{16,32},{20,36},{24,40},{28,44},{32,4... | collective-permute-start | bytes 393224 | tf_op jit(solution)/shard_map/ppermute | solution.py:49
  38.2 60.4 %all-to-all-start = ((bf16[64,64,128]{2,1,0:T(8,128)(2,1)}), bf16[64,64,128]{2,1,0:T(8,128)(2,1)S(1)}, u32[]{:S(2)}, u32[]{:S(2)}) async-start(bf16[64,64,128]{2,1,0:T(8,128)(2,1)} %broadcast_in_dim.45), calls=%async_computation | async-start | bytes 2097152 | tf_op jit(solution)/shard_map/all_to_all | solution.py:54
  49.2 31.3 %collective-permute-start.15 = (bf16[128,640]{1,0:T(8,128)(2,1)S(1)}, bf16[128,640]{1,0:T(8,128)(2,1)S(1)}, u32[]{:S(2)}, u32[]{:S(2)}) collective-permute-start(bf16[128,640]{1,0:T(8,128)(2,1)S(1)} %bitcast.56), channel_id=1, source_target_pairs={{0,1},{1,2},{2,3},{3,0},{4,5},{5,6},{6,7},{7,4},{8,9},{9,10},{10,1... | collective-permute-start | bytes 491528 | tf_op jit(solution)/shard_map/ppermute | solution.py:36
  51.6 30.4 %collective-permute-start.16 = (bf16[128,640]{1,0:T(8,128)(2,1)S(1)}, bf16[128,640]{1,0:T(8,128)(2,1)S(1)}, u32[]{:S(2)}, u32[]{:S(2)}) collective-permute-start(bf16[128,640]{1,0:T(8,128)(2,1)S(1)} %bitcast.57), channel_id=1, source_target_pairs={{0,2},{1,3},{2,0},{3,1},{4,6},{5,7},{6,4},{7,5},{8,10},{9,11},{10,... | collective-permute-start | bytes 491528 | tf_op jit(solution)/shard_map/ppermute | solution.py:36
  60.3 21.7 %collective-permute-start.17 = (bf16[128,640]{1,0:T(8,128)(2,1)S(1)}, bf16[128,640]{1,0:T(8,128)(2,1)S(1)}, u32[]{:S(2)}, u32[]{:S(2)}) collective-permute-start(bf16[128,640]{1,0:T(8,128)(2,1)S(1)} %bitcast.58), channel_id=1, source_target_pairs={{0,3},{1,0},{2,1},{3,2},{4,7},{5,4},{6,5},{7,6},{8,11},{9,8},{10,9... | collective-permute-start | bytes 491528 | tf_op jit(solution)/shard_map/ppermute | solution.py:36
  61.8 26.5 %collective-permute-start.9 = (bf16[512,512]{1,0:T(8,128)(2,1)}, bf16[512,512]{1,0:T(8,128)(2,1)}, u32[]{:S(2)}, u32[]{:S(2)}) collective-permute-start(bf16[512,512]{1,0:T(8,128)(2,1)} %get-tuple-element.3), channel_id=1, source_target_pairs={{0,4},{4,8},{8,12},{12,0},{16,20},{20,24},{24,28},{28,16},{32,36},... | collective-permute-start | bytes 1572872 | tf_op jit(solution)/shard_map/ppermute | solution.py:49
  63.2 26.1 %collective-permute-start.10 = (bf16[512,512]{1,0:T(8,128)(2,1)}, bf16[512,512]{1,0:T(8,128)(2,1)}, u32[]{:S(2)}, u32[]{:S(2)}) collective-permute-start(bf16[512,512]{1,0:T(8,128)(2,1)} %get-tuple-element.3), channel_id=1, source_target_pairs={{0,8},{4,12},{8,0},{12,4},{16,24},{20,28},{24,16},{28,20},{32,40},... | collective-permute-start | bytes 1572872 | tf_op jit(solution)/shard_map/ppermute | solution.py:49
  80.5 10.2 %collective-permute-start.11 = (bf16[512,512]{1,0:T(8,128)(2,1)}, bf16[512,512]{1,0:T(8,128)(2,1)}, u32[]{:S(2)}, u32[]{:S(2)}) collective-permute-start(bf16[512,512]{1,0:T(8,128)(2,1)} %get-tuple-element.3), channel_id=1, source_target_pairs={{0,12},{4,0},{8,4},{12,8},{16,28},{20,16},{24,20},{28,24},{32,44},... | collective-permute-start | bytes 1572872 | tf_op jit(solution)/shard_map/ppermute | solution.py:49
  82.0 9.9 %collective-permute-start.4 = (bf16[128,2048]{1,0:T(8,128)(2,1)}, bf16[128,2048]{1,0:T(8,128)(2,1)}, u32[]{:S(2)}, u32[]{:S(2)}) collective-permute-start(bf16[128,2048]{1,0:T(8,128)(2,1)} %fusion.8), channel_id=1, source_target_pairs={{0,64},{64,0},{1,65},{65,1},{2,66},{66,2},{3,67},{67,3},{4,68},{68... | collective-permute-start | bytes 1572872 | tf_op jit(solution)/shard_map/ppermute | solution.py:40
  87.7 66.2 %collective-permute-start.3 = (bf16[128,64]{0,1:T(8,128)(2,1)}, bf16[128,64]{0,1:T(8,128)(2,1)}, u32[]{:S(2)}, u32[]{:S(2)}) collective-permute-start(bf16[128,64]{0,1:T(8,128)(2,1)} %convolution_convert_fusion.1), channel_id=1, source_target_pairs={{0,64},{64,0},{1,65},{65,1},{2,66},{66,2},{3,67},{67,3},{4,68},{68... | collective-permute-start | bytes 49160 | tf_op jit(solution)/shard_map/ppermute | solution.py:40
  103.7 11.2 %collective-permute-start.18 = (bf16[64,2048]{1,0:T(8,128)(2,1)}, bf16[64,2048]{1,0:T(8,128)(2,1)}, u32[]{:S(2)}, u32[]{:S(2)}) collective-permute-start(bf16[64,2048]{1,0:T(8,128)(2,1)} %get-tuple-element.6), channel_id=1, source_target_pairs={{0,3},{1,0},{2,1},{3,2},{4,7},{5,4},{6,5},{7,6},{8,11},{9,8},{10,9... | collective-permute-start | bytes 786440 | tf_op jit(solution)/shard_map/ppermute | solution.py:36
  104.1 13.2 %collective-permute-start.19 = (bf16[64,2048]{1,0:T(8,128)(2,1)}, bf16[64,2048]{1,0:T(8,128)(2,1)}, u32[]{:S(2)}, u32[]{:S(2)}) collective-permute-start(bf16[64,2048]{1,0:T(8,128)(2,1)} %get-tuple-element.8), channel_id=1, source_target_pairs={{0,2},{1,3},{2,0},{3,1},{4,6},{5,7},{6,4},{7,5},{8,10},{9,11},{10,... | collective-permute-start | bytes 786440 | tf_op jit(solution)/shard_map/ppermute | solution.py:36
  106.4 14.1 %collective-permute-start.20 = (bf16[64,2048]{1,0:T(8,128)(2,1)}, bf16[64,2048]{1,0:T(8,128)(2,1)}, u32[]{:S(2)}, u32[]{:S(2)}) collective-permute-start(bf16[64,2048]{1,0:T(8,128)(2,1)} %get-tuple-element.7), channel_id=1, source_target_pairs={{0,1},{1,2},{2,3},{3,0},{4,5},{5,6},{6,7},{7,4},{8,9},{9,10},{10,1... | collective-permute-start | bytes 786440 | tf_op jit(solution)/shard_map/ppermute | solution.py:36
  111.1 14.7 %collective-permute-start.14 = (bf16[256,640]{1,0:T(8,128)(2,1)S(1)}, bf16[256,640]{1,0:T(8,128)(2,1)S(1)}, u32[]{:S(2)}, u32[]{:S(2)}) collective-permute-start(bf16[256,640]{1,0:T(8,128)(2,1)S(1)} %concatenate.82), channel_id=1, source_target_pairs={{0,3},{1,0},{2,1},{3,2},{4,7},{5,4},{6,5},{7,6},{8,11},{9,8},{10,9... | collective-permute-start | bytes 983048 | tf_op jit(solution)/shard_map/ppermute | solution.py:36
  114.9 12.4 %collective-permute-start.13 = (bf16[256,640]{1,0:T(8,128)(2,1)S(1)}, bf16[256,640]{1,0:T(8,128)(2,1)S(1)}, u32[]{:S(2)}, u32[]{:S(2)}) collective-permute-start(bf16[256,640]{1,0:T(8,128)(2,1)S(1)} %concatenate.82), channel_id=1, source_target_pairs={{0,2},{1,3},{2,0},{3,1},{4,6},{5,7},{6,4},{7,5},{8,10},{9,11},{10,... | collective-permute-start | bytes 983048 | tf_op jit(solution)/shard_map/ppermute | solution.py:36
  117.3 15.7 %collective-permute-start.12 = (bf16[256,640]{1,0:T(8,128)(2,1)S(1)}, bf16[256,640]{1,0:T(8,128)(2,1)S(1)}, u32[]{:S(2)}, u32[]{:S(2)}) collective-permute-start(bf16[256,640]{1,0:T(8,128)(2,1)S(1)} %concatenate.82), channel_id=1, source_target_pairs={{0,1},{1,2},{2,3},{3,0},{4,5},{5,6},{6,7},{7,4},{8,9},{9,10},{10,1... | collective-permute-start | bytes 983048 | tf_op jit(solution)/shard_map/ppermute | solution.py:36
  122.7 23.6 %collective-permute-start.21 = (f32[64,2560]{1,0:T(8,128)}, f32[64,2560]{1,0:T(8,128)}, u32[]{:S(2)}, u32[]{:S(2)}) collective-permute-start(f32[64,2560]{1,0:T(8,128)} %pad_maximum_fusion.5), channel_id=1, source_target_pairs={{0,64},{64,0},{1,65},{65,1},{2,66},{66,2},{3,67},{67,3},{4,68},{68... | collective-permute-start | bytes 1966088 | tf_op jit(solution)/shard_map/ppermute | solution.py:40
  (24 other events, 256.6 us)

commit v4 on v3

v4 whole, which is shorter than its diff:
```python
import functools

import jax
import jax.numpy as jnp
from jax import lax
from jax.experimental import pallas as pl
from jax.experimental.pallas import tpu as pltpu
from jax.sharding import PartitionSpec as P

ENC_DEV = 256
epsilon = 1e-06
f32 = jnp.float32
bf16 = jnp.bfloat16


def dot(a, b):
    return jnp.dot(a, b, preferred_element_type=f32)


def dot_tn(a, b):
    return lax.dot_general(a, b, (((0,), (0,)), ((), ())), preferred_element_type=f32)


def dot_nt(a, b):
    return lax.dot_general(a, b, (((1,), (1,)), ((), ())), preferred_element_type=f32)


def split_two(a):
    high = lax.reduce_precision(a, 8, 7)
    return high.astype(bf16), (a - high).astype(bf16)


def split_three(a):
    high = lax.reduce_precision(a, 8, 7)
    return (high.astype(bf16), *split_two(a - high))


def turned(array, axis, step):
    count = lax.axis_size(axis)
    return lax.ppermute(array, axis, [(i, (i + step) % count) for i in range(count)])


def crossed(array):
    return lax.ppermute(array, "grp", [(0, 1), (1, 0)])


def along(array, z_step, x_step, side):
    pairs = [
        (z * side + x, (z + z_step) % side * side + (x + x_step) % side)
        for z in range(side)
        for x in range(side)
    ]
    return lax.ppermute(array, "dp", pairs)


def to_everyone(array, axes):
    count = lax.axis_size(axes)
    return lax.all_to_all(
        jnp.broadcast_to(array[None], (count, *array.shape)), axes, 0, 0, tiled=True
    )


def cut(array, start, size, axis=0):
    starts = [jnp.int32(0)] * array.ndim
    starts[axis] = start
    sizes = list(array.shape)
    sizes[axis] = size
    return lax.dynamic_slice(array, starts, sizes, allow_negative_indices=False)


VMEM = pl.BlockSpec(memory_space=pltpu.VMEM)
SMEM = pl.BlockSpec(memory_space=pltpu.SMEM)
PARAMS = pltpu.CompilerParams(vmem_limit_bytes=48 * 1024 * 1024)


def block_start(col, k, side, size):
    return pl.multiple_of(((col + side - k) & (side - 1)) * size, 128)


def partial_kernel(
    place, near, far, gain, a_part, w0, w1, w2, w3, sent, kept, *, block, half_kv, rank, chunk
):
    rows = near.shape[0]
    pieces = (w0, w1, w2, w3)
    side = len(pieces)
    for h, source in enumerate((near, far)):
        values = jnp.zeros((rows, half_kv), f32)
        low = jnp.zeros((rows, rank), f32)
        squares = jnp.zeros((rows, 1), f32)
        for k, piece in enumerate(pieces):
            here = pl.ds(block_start(place[0], k, side, block), block)
            wide = source[:, here].astype(f32)
            scaled = (wide * gain[:, here]).astype(bf16)
            squares = squares + jnp.sum(wide * wide, axis=1, keepdims=True)
            values = values + dot(scaled, piece[:block, :])
            low = low + dot_nt(scaled, a_part[:, here])
        out = slice(h * rows, (h + 1) * rows)
        kept[out, :half_kv] = values
        high = squares.astype(bf16)
        left = squares - high.astype(f32)
        middle = left.astype(bf16)
        last = left - middle.astype(f32)
        lane = lax.broadcasted_iota(jnp.int32, (rows, rank), 1)
        three = jnp.where(
            lane == 0,
            high.astype(f32),
            jnp.where(lane == 1, middle.astype(f32), jnp.where(lane == 2, last, 0.0)),
        )
        extra = jnp.concatenate([low, three], axis=1)
        kept[out, half_kv:] = extra
        sent[out, :half_kv] = values.astype(bf16)
        sent[out, half_kv:] = extra.astype(bf16)
    per = chunk // 2
    for k, piece in enumerate(pieces):
        for pair in range(side // 2):
            wide, lengths = [], []
            for z in (2 * pair, 2 * pair + 1):
                both = piece[block + z * chunk : block + (z + 1) * chunk, :].astype(f32)
                wide.append(both[:per])
                lengths.append(both[per:, :128])
            at = 2 * rows + (k * side + 2 * pair) * per
            sent[at : at + chunk, :half_kv] = jnp.concatenate(wide).astype(bf16)
            sent[at : at + chunk, half_kv:] = jnp.concatenate(lengths).astype(bf16)


def image_kernel(
    place,
    kept,
    sent,
    got1,
    got2,
    got3,
    near,
    far,
    low_near,
    low_far,
    gain,
    a_part,
    w0,
    w1,
    w2,
    w3,
    b_half,
    bias,
    line,
    position,
    out,
    *,
    block,
    half_kv,
    rank,
    width,
    step,
):
    pieces = (w0, w1, w2, w3)
    side = len(pieces)
    got = (got1, got2, got3)
    count = kept.shape[0]
    parts = []
    for h in range(2):
        for p in range(side):
            at = h * side * step + p * step
            total = kept[at : at + step, :]
            for k in range(1, side):
                there = h * side * step + ((p - k) % side) * step
                total = total + got[k - 1][there : there + step, :].astype(f32)
            parts.append(total)
    total = jnp.concatenate(parts)
    raw_values = total[:, :half_kv]
    raw_low = total[:, half_kv : half_kv + rank]
    squares = jnp.sum(total[:, half_kv + rank :], axis=1, keepdims=True)
    lines = side * (sent.shape[0] - count)
    pick = (line[...] == lax.broadcasted_iota(jnp.int32, (count, lines), 1)).astype(bf16)
    table = jnp.concatenate([sent[count:, :]] + [g[count:, :] for g in got])
    picked = dot(pick, table)
    length = picked[:, half_kv : half_kv + 1]
    weight = jnp.where(position[...] < length, 1.0 / length, 0.0)
    inverse = lax.rsqrt(squares / width + epsilon)
    low = (raw_low * inverse).astype(bf16)
    values_out = raw_values * inverse + bias[...] + dot(low, b_half[...])
    dvalues = ((values_out - picked[:, :half_kv]) * weight).astype(bf16)
    dlow = dot_nt(dvalues, b_half[...]).astype(bf16)
    centre = (
        jnp.sum(dvalues.astype(f32) * raw_values, axis=1, keepdims=True)
        + jnp.sum(dlow.astype(f32) * raw_low, axis=1, keepdims=True)
    ) / width
    factor = inverse * inverse * inverse * centre
    out[:, side * block :] = dot_tn(low, dvalues)
    enc_low = jnp.concatenate([low_near[...], low_far[...]])
    for k, piece in enumerate(pieces):
        here = pl.ds(block_start(place[0], k, side, block), block)
        dnormed = dot_nt(dvalues, piece[:block, :]) + dot(dlow, a_part[:, here])
        wide = jnp.concatenate([near[:, here], far[:, here]]).astype(f32)
        dimage = (inverse * (gain[:, here] * dnormed) - wide * factor).astype(bf16)
        out[:, here] = dot_tn(enc_low, dimage)


def body(
    hidden,
    enc_weight,
    enc_bias,
    enc_frozen,
    enc_adapter,
    text_rows,
    norm_gain,
    value_weight,
    value_bias,
    llm_frozen,
    llm_adapter,
    targets,
    dest_owner,
    seq_length,
):
    n_dp = lax.axis_size("dp")
    n_mp = lax.axis_size("mp")
    side = n_mp
    owners = n_dp * n_mp
    grp = lax.axis_index("grp")
    dp = lax.axis_index("dp")
    mp = lax.axis_index("mp")
    first = grp == 0
    width = text_rows.shape[1]
    part_width = enc_weight.shape[1]
    rank = enc_frozen.shape[1]
    half_rank = rank // 2
    kv = value_weight.shape[1]
    half_kv = kv // 2
    shard = value_weight.shape[0]
    block = side * shard
    block_rows = hidden.shape[0]
    mine_rows = block_rows // 2
    capacity = 2 * ENC_DEV // owners
    chunk = 2 * capacity
    area = capacity * n_dp
    slab, col = dp // side, dp & (side - 1)
    wrap = side - 1

    swap = [
        ((z * side + x) * side + y, (y * side + x) * side + z)
        for z in range(side)
        for x in range(side)
        for y in range(side)
    ]
    w_half = cut(value_weight, grp * half_kv, half_kv, 1)
    w_moved = lax.ppermute(w_half, ("dp", "mp"), swap)

    own_hidden = cut(hidden, grp * mine_rows, mine_rows)
    hid = jnp.concatenate([own_hidden] + [turned(own_hidden, "mp", k) for k in range(1, n_mp)])

    own_length = seq_length[0]
    t_half = cut(targets[:area], grp * half_kv, half_kv, 1)
    t_half = t_half.reshape(capacity, n_dp, half_kv).transpose(1, 0, 2)
    t_half = jnp.concatenate([t_half, jnp.full_like(t_half, own_length.astype(bf16))], axis=1)
    t_half = t_half.reshape(side, side * chunk, half_kv)
    w_line, t_line = [w_moved], [cut(t_half, slab, 1)[0]]
    for k in range(1, side):
        t_given = cut(t_half, (slab + k) & wrap, 1)[0]
        came = along(jnp.concatenate([w_moved, t_given]), k, 0, side)
        w_line.append(came[:shard])
        t_line.append(came[shard:])
    w_line = w_line[::-1]
    w_line = cut(jnp.concatenate(w_line + w_line), ((2 * side - 1 - slab) & wrap) * shard, block)
    t_line = jnp.stack(t_line).reshape(side, side, chunk, half_kv)
    pieces = []
    for k in range(side):
        t_given = cut(t_line, (col + k) & wrap, 1, 1).reshape(side * chunk, half_kv)
        piece = jnp.concatenate([w_line, t_given])
        pieces.append(along(piece, 0, k, side) if k else piece)

    a_turned = jnp.where(first, llm_frozen.T, jnp.roll(llm_frozen.T, half_rank, axis=0))
    a_all = to_everyone(a_turned, ("dp", "mp")).transpose(1, 0, 2).reshape(rank, width)
    a_part = cut(a_all, mp * part_width, part_width, 1)
    b_all = jnp.where(first, llm_adapter, jnp.roll(llm_adapter, half_rank, axis=0))
    b_half = cut(b_all, grp * half_kv, half_kv, 1)
    bias_wide = value_bias.astype(f32)[None]
    bias_half = cut(bias_wide, grp * half_kv, half_kv, 1)

    destiny = dest_owner[:, 0]
    block_dest = cut(destiny, dp * ENC_DEV, ENC_DEV)
    local = jnp.arange(ENC_DEV, dtype=jnp.int32)
    from_mp = (mp - (local % (ENC_DEV // 2)) // mine_rows) & wrap
    from_grp = (grp + local // (ENC_DEV // 2)) & 1
    place = from_mp * block_rows + from_grp * mine_rows + (local & (mine_rows - 1))
    own_dest = jnp.sum(jnp.where(place[:, None] == local[None, :], block_dest[None, :], 0), axis=1)
    earlier = (own_dest[:, None] == block_dest[None, :]) & (local[None, :] < place[:, None])
    slot = jnp.sum(earlier.astype(jnp.int32), axis=1)
    own_mp, own_col, own_slab = own_dest & wrap, (own_dest // side) & wrap, own_dest // (side * side)
    line = (((mp - own_mp) & wrap) * side + ((col - own_col) & wrap)) * side
    line = (line + ((slab - own_slab) & wrap)) * capacity + slot
    position = (slot * n_dp + dp).astype(f32)

    gain_wide = norm_gain.astype(f32)[None]
    text_count = text_rows.shape[0] // 2
    text_wide = cut(text_rows, grp * text_count, text_count).astype(f32)
    text_inverse = lax.rsqrt(jnp.mean(text_wide * text_wide, axis=1, keepdims=True) + epsilon)
    text_normed = (text_wide * text_inverse * gain_wide).astype(bf16)
    text_low = dot_nt(text_normed, a_all).astype(bf16)
    owner_index = dp * n_mp + mp
    counts = jnp.sum((destiny.reshape(n_dp, ENC_DEV) == owner_index).astype(jnp.int32), axis=1)
    row = grp * text_count + jnp.arange(text_count, dtype=jnp.int32)
    taken = (row < area) & (
        row // n_dp
        < jnp.sum(
            jnp.where(
                (row & (n_dp - 1))[:, None] == jnp.arange(n_dp, dtype=jnp.int32)[None, :],
                counts,
                0,
            ),
            axis=1,
        )
    )
    keep = (row < own_length) & ~taken
    text_kept = jnp.where(keep[:, None], text_low, jnp.zeros_like(text_low))
    text_weight = 1.0 / own_length.astype(f32)
    text_sum = dot_tn(text_kept, text_normed) * text_weight
    own_text_targets = cut(targets, grp * text_count, text_count).astype(f32)
    rest = bias_wide + dot(text_low, b_all) - own_text_targets
    rest_high, rest_low = split_two(rest)
    rest_sum = dot_tn(
        jnp.concatenate([text_kept, text_kept]), jnp.concatenate([rest_high, rest_low])
    )
    rest_sum = rest_sum * text_weight
    text_here = cut(text_sum, mp * part_width, part_width, 1)
    text_sent = text_sum.astype(bf16)
    for k in range(1, n_mp):
        given = cut(text_sent, ((mp - k) & wrap) * part_width, part_width, 1)
        text_here = text_here + turned(given, "mp", -k).astype(f32)
    rest_mine = cut(rest_sum, grp * half_kv, half_kv, 1)
    rest_give = cut(rest_sum, (1 - grp) * half_kv, half_kv, 1)
    came = jnp.roll(crossed(jnp.concatenate([text_here, rest_give], axis=1)), half_rank, axis=0)
    here_high, here_low = split_two(text_here + came[:, :part_width])
    here_both = jnp.concatenate([here_high, here_low])
    text_grad = jnp.zeros((2 * rank, half_kv), f32)
    for k in range(side):
        given = cut(here_both, ((col - k) & wrap) * block, block, 1)
        text_grad = text_grad + dot(given, pieces[k][:block])
    text_grad = text_grad[:rank] + text_grad[rank:] + rest_mine + came[:, part_width:]
    text_grad = text_grad + (
        turned(text_grad, "mp", 1) + turned(text_grad, "mp", 2) + turned(text_grad, "mp", 3)
    )

    enc_low = dot(hid, enc_frozen).astype(bf16)
    merged = dot(hid, enc_weight) + enc_bias.astype(f32) + dot(enc_low, enc_adapter)
    image = merged.astype(bf16)
    image_far = crossed(image)
    enc_low = jnp.where(first, enc_low, jnp.roll(enc_low, half_rank, axis=1))
    enc_low_far = jnp.roll(crossed(enc_low), half_rank, axis=1)
    gain_part = cut(gain_wide, mp * part_width, part_width, 1)
    where = col[None].astype(jnp.int32)
    sizes = dict(block=block, half_kv=half_kv, rank=rank)
    sent, kept = pl.pallas_call(
        functools.partial(partial_kernel, chunk=chunk, **sizes),
        out_shape=(
            jax.ShapeDtypeStruct((ENC_DEV + area, half_kv + 128), bf16),
            jax.ShapeDtypeStruct((ENC_DEV, half_kv + 128), f32),
        ),
        in_specs=[SMEM] + [VMEM] * 8,
        out_specs=(VMEM, VMEM),
        compiler_params=PARAMS,
        name="partial_products",
    )(where, image, image_far, gain_part, a_part, *pieces)
    got = [turned(sent, "mp", k) for k in range(1, n_mp)]
    both = pl.pallas_call(
        functools.partial(image_kernel, width=float(width), step=mine_rows, **sizes),
        out_shape=jax.ShapeDtypeStruct((rank, part_width + half_kv), f32),
        in_specs=[SMEM] + [VMEM] * 19,
        out_specs=VMEM,
        compiler_params=PARAMS,
        name="image_gradients",
    )(
        where,
        kept,
        sent,
        *got,
        image,
        image_far,
        enc_low,
        enc_low_far,
        gain_part,
        a_part,
        *pieces,
        b_half,
        bias_half,
        line[:, None],
        position[:, None],
    )

    both = jnp.concatenate([both[:, :part_width], both[:, part_width:] + text_grad], axis=1)
    mine = both[:half_rank]
    came = crossed(both[half_rank:])
    llm_mine, llm_came = mine[:, part_width:], came[:, part_width:]
    mine = jnp.concatenate(
        [
            mine[:, :part_width] + came[:, :part_width],
            jnp.where(first, llm_mine, llm_came),
            jnp.where(first, llm_came, llm_mine),
        ],
        axis=1,
    )
    mine = mine.reshape(n_dp, half_rank // n_dp, -1)
    mine = jnp.sum(lax.all_to_all(mine, "dp", 0, 0, tiled=True), axis=0)
    whole = to_everyone(mine, "dp").reshape(half_rank, -1)
    return whole[:, :part_width], whole[:, part_width:]


def solution(mesh):
    return jax.shard_map(
        body,
        mesh=mesh,
        in_specs=(
            P(("dp", "mp"), None),
            P(None, "mp"),
            P("mp"),
            P(),
            P(None, "mp"),
            P(("dp", "mp"), None),
            P(),
            P(("dp", "mp"), None),
            P(),
            P(("dp", "mp"), None),
            P(),
            P(("dp", "mp"), None),
            P(),
            P(("dp", "mp")),
        ),
        out_specs=(P("grp", "mp"), P("grp", None)),
        check_vma=False,
    )
```

time: 194 us -> 166 us (0.86)
  local copies, waits for them, and re-layouts: 34.2 us -> 8.86 us
  waiting for transfers between devices: 20.3 us -> 45.6 us
  matrix products: 32.9 us -> 16.5 us
  starting transfers between devices: 59.9 us -> 51.5 us
  other arithmetic: 15.6 us -> 7.46 us
  Pallas kernels: 0 us -> 6.1 us
    ppermute x15 -> x12, waiting for transfers between devices: 14.1 us -> 28.8 us  [turned(): lax.ppermute(array, axis, [(i, (i + step) % count) for i in range(count)])]
    ppermute x6, waiting for transfers between devices: 4.54 us -> 15.2 us  [along(): return lax.ppermute(array, 'dp', pairs)]
    ppermute x6, starting transfers between devices: 12.5 us -> 22.5 us  [along(): return lax.ppermute(array, 'dp', pairs)]
    all_to_all x1 -> x0, starting transfers between devices: 9.13 us -> none  [body(): lax.all_to_all(t_half, 'dp', 0, 0, tiled=True).reshape(n_dp * capacity, -1)]
    dot_general x9 -> x8, matrix products: 21.6 us -> 13.2 us  [dot(): return jnp.dot(a, b, preferred_element_type=f32)]
    ppermute x15 -> x12, starting transfers between devices: 26 us -> 17.7 us  [turned(): lax.ppermute(array, axis, [(i, (i + step) % count) for i in range(count)])]
    unnamed x49 -> x40, local copies, waits for them, and re-layouts: 9.73 us -> 1.55 us
    concatenate x7 -> x1, local copies, waits for them, and re-layouts: 6.22 us -> 0.02 us  [body(): jnp.concatenate([t_half, jnp.full_like(t_half, own_length.astype(bf16))],...]
  transfers between devices with their start and end apart: 28 -> 24, of which waited for: 9 -> 9; matrix products, arithmetic and copies ran while one was open for 39% -> 16% of each run, Pallas kernels for 0% -> 4%
where the time goes in v4:
time: 166 us; the launch traced here: 165 us
  starting transfers between devices  51.5 us (31%)
  waiting for transfers between devices  45.6 us (27%)
  blocking collectives  27.2 us (16%)
  matrix products  16.5 us (10%)
  local copies, waits for them, and re-layouts  8.86 us (5%)
  other arithmetic  7.46 us (4%)
  Pallas kernels  6.1 us (4%)
  between operations  2.18 us (1%)
    ppermute x12, waiting for transfers between devices, turned(): lax.ppermute(array, axis, [(i, (i + step) % count) for i in range(count)])  28.8 us
    ppermute x6, starting transfers between devices, along(): return lax.ppermute(array, 'dp', pairs)  22.5 us
    ppermute x12, starting transfers between devices, turned(): lax.ppermute(array, axis, [(i, (i + step) % count) for i in range(count)])  17.7 us
    ppermute x6, waiting for transfers between devices, along(): return lax.ppermute(array, 'dp', pairs)  15.2 us
    all_to_all x1, blocking collectives, body(): mine = jnp.sum(lax.all_to_all(mine, 'dp', 0, 0, tiled=True), axis=0)  14.8 us
    dot_general x8, matrix products, dot(): return jnp.dot(a, b, preferred_element_type=f32)  13.2 us
    all_to_all x1, blocking collectives, to_everyone(): lax.all_to_all(jnp.broadcast_to(array[None], (count, *array.shape)), axes...  12.4 us
    all_to_all x1, starting transfers between devices, to_everyone(): lax.all_to_all(jnp.broadcast_to(array[None], (count, *array.shape)), axes...  9.96 us
  transfers between devices with their start and end apart: 24, of which 9 were waited for; matrix products, arithmetic and copies ran while one was open for 16% of the time, Pallas kernels for 4%

profile of v4, /device:TPU:0, one launch (start us, length us, event | category | flops | bytes accessed | tf_op | source)
XLA Modules:
  0.0 165.4 jit_solution(3207594272775465812)
XLA Ops:
  1.8 1.7 %collective-permute-start = (bf16[32,5120]{1,0:T(8,128)(2,1)S(1)}, bf16[32,5120]{1,0:T(8,128)(2,1)}, u32[]{:S(2)}, u32[]{:S(2)}) collective-permute-start(bf16[32,5120]{1,0:T(8,128)(2,1)S(1)} %constant_dynamic-slice_fusion.15), channel_id=1, source_target_pairs={{0,1},{1,2},{2,3},{3,0},{4,5},{5,6},{6,7},{7,4},{8,9},{9,10},{10,1... | collective-permute-start | bytes 983048 | tf_op jit(solution)/shard_map/ppermute | solution.py:40
  3.5 2.9 %collective-permute-start.1 = (bf16[32,5120]{1,0:T(8,128)(2,1)S(1)}, bf16[32,5120]{1,0:T(8,128)(2,1)}, u32[]{:S(2)}, u32[]{:S(2)}) collective-permute-start(bf16[32,5120]{1,0:T(8,128)(2,1)S(1)} %constant_dynamic-slice_fusion.15), channel_id=1, source_target_pairs={{0,2},{1,3},{2,0},{3,1},{4,6},{5,7},{6,4},{7,5},{8,10},{9,11},{10,... | collective-permute-start | bytes 983048 | tf_op jit(solution)/shard_map/ppermute | solution.py:40
  9.1 10.0 %all-to-all-start = ((bf16[64,64,128]{2,1,0:T(8,128)(2,1)}), bf16[64,64,128]{2,1,0:T(8,128)(2,1)}, u32[]{:S(2)}, u32[]{:S(2)}) async-start(bf16[64,64,128]{2,1,0:T(8,128)(2,1)} %broadcast_in_dim.39), calls=%async_computation | async-start | bytes 2097152 | tf_op jit(solution)/shard_map/all_to_all | solution.py:58
  20.0 1.7 %fusion = f32[80]{0:T(128)S(1)} fusion(bf16[160,8192]{1,0:T(8,128)(2,1)} %param.19, s32[]{:T(128)S(6)} %mul.159), kind=kLoop, calls=%fused_computation.3 | loop fusion | flops 1966000 | bytes 1311044 | tf_op jit(solution)/shard_map/reduce_sum | solution.py:295
  24.0 17.0 %collective-permute-start.5 = (bf16[192,512]{1,0:T(8,128)(2,1)S(1)}, bf16[192,512]{1,0:T(8,128)(2,1)S(1)}, u32[]{:S(2)}, u32[]{:S(2)}) collective-permute-start(bf16[192,512]{1,0:T(8,128)(2,1)S(1)} %get-tuple-element.35), channel_id=1, source_target_pairs={{0,48},{4,52},{8,56},{12,60},{16,0},{20,4},{24,8},{28,12},{32,16},... | collective-permute-start | bytes 589832 | tf_op jit(solution)/shard_map/ppermute | solution.py:53
  42.1 11.0 %collective-permute-done.7 = bf16[192,512]{1,0:T(8,128)(2,1)S(1)} collective-permute-done((bf16[192,512]{1,0:T(8,128)(2,1)S(1)}, bf16[192,512]{1,0:T(8,128)(2,1)S(1)}, u32[]{:S(2)}, u32[]{:S(2)}) %collective-permute-start.7) | collective-permute-done | bytes 196640 | tf_op jit(solution)/shard_map/ppermute | solution.py:53
  54.5 1.4 pad_maximum_fusion.5
  56.6 2.4 %collective-permute-start.9 = (bf16[576,512]{1,0:T(8,128)(2,1)}, bf16[576,512]{1,0:T(8,128)(2,1)S(1)}, u32[]{:S(2)}, u32[]{:S(2)}) collective-permute-start(bf16[576,512]{1,0:T(8,128)(2,1)} %get-tuple-element.15), channel_id=1, source_target_pairs={{0,8},{4,12},{8,0},{12,4},{16,24},{20,28},{24,16},{28,20},{32,40},... | collective-permute-start | bytes 1769480 | tf_op jit(solution)/shard_map/ppermute | solution.py:53
  59.0 3.4 %collective-permute-done.2 = bf16[32,5120]{1,0:T(8,128)(2,1)S(1)} collective-permute-done((bf16[32,5120]{1,0:T(8,128)(2,1)S(1)}, bf16[32,5120]{1,0:T(8,128)(2,1)S(1)}, u32[]{:S(2)}, u32[]{:S(2)}) %collective-permute-start.2) | collective-permute-done | bytes 327712 | tf_op jit(solution)/shard_map/ppermute | solution.py:40
  62.4 1.6 convolution_convert_fusion
  64.4 10.2 %fusion.4.near = bf16[128,2048]{1,0:T(8,128)(2,1)S(1)} fusion(f32[128,2048]{1,0:T(8,128)S(1)} %fusion.76, bf16[5120,2048]{1,0:T(8,128)(2,1)} %param.15, f32[2048]{0:T(1024)S(1)} %convert_element_type.80, bf16[32,5120]{1,0:T(8,128)(2,1)S(1)} %collective-permute-done.2, bf16[32,5120]{1,0:T(8,128)(2,1)} %collective-permute-done.1, ...), kind=kOutput, calls=%fused_computation.8 | convolution fusion | flops 2690383872 | bytes 23863296 | tf_op jit(solution)/shard_map/dot_general | solution.py:17
  74.7 2.4 %broadcast_select_fusion = (bf16[80,64]{0,1:T(8,128)(2,1)S(1)}, bf16[80,64]{0,1:T(8,128)(2,1)S(1)}) fusion(pred[80]{0:T(512)(128)(4,1)S(1)} %not_and_fusion, f32[8192]{0:T(1024)S(1)} %convert_element_type.83, f32[80]{0:T(128)S(1)} %add_rsqrt_fusion, bf16[160,8192]{1,0:T(8,128)(2,1)} %param.19, s32[]{:T(128)S(6)} %mul.159, ...), kind=kOutput, calls=%fused_computation.117 | convolution fusion | flops 86517760 | bytes 2412948 | tf_op jit(solution)/shard_map/dot_general | solution.py:25
  77.9 2.7 %collective-permute-start.15 = (bf16[64,2048]{1,0:T(8,128)(2,1)S(1)}, bf16[64,2048]{1,0:T(8,128)(2,1)S(1)}, u32[]{:S(2)}, u32[]{:S(2)}) collective-permute-start(bf16[64,2048]{1,0:T(8,128)(2,1)S(1)} %get-tuple-element.8), channel_id=1, source_target_pairs={{0,3},{1,0},{2,1},{3,2},{4,7},{5,4},{6,5},{7,6},{8,11},{9,8},{10,9... | collective-permute-start | bytes 786440 | tf_op jit(solution)/shard_map/ppermute | solution.py:40
  82.0 9.1 %collective-permute-done.15 = bf16[64,2048]{1,0:T(8,128)(2,1)S(1)} collective-permute-done((bf16[64,2048]{1,0:T(8,128)(2,1)S(1)}, bf16[64,2048]{1,0:T(8,128)(2,1)S(1)}, u32[]{:S(2)}, u32[]{:S(2)}) %collective-permute-start.15) | collective-permute-done | bytes 262176 | tf_op jit(solution)/shard_map/ppermute | solution.py:40
  92.5 2.0 %collective-permute-done.17 = bf16[64,2048]{1,0:T(8,128)(2,1)S(1)} collective-permute-done((bf16[64,2048]{1,0:T(8,128)(2,1)S(1)}, bf16[64,2048]{1,0:T(8,128)(2,1)S(1)}, u32[]{:S(2)}, u32[]{:S(2)}) %collective-permute-start.17) | collective-permute-done | bytes 262176 | tf_op jit(solution)/shard_map/ppermute | solution.py:40
  96.7 4.2 %collective-permute-done.10.w3 = bf16[576,512]{1,0:T(8,128)(2,1)S(1)} collective-permute-done((bf16[576,512]{1,0:T(8,128)(2,1)S(1)}, bf16[576,512]{1,0:T(8,128)(2,1)S(1)}, u32[]{:S(2)}, u32[]{:S(2)}) %collective-permute-start.10) | collective-permute-done | bytes 589856 | tf_op jit(solution)/shard_map/ppermute | solution.py:53
  102.1 5.1 %collective-permute-start.12 = (bf16[384,640]{1,0:T(8,128)(2,1)S(1)}, bf16[384,640]{1,0:T(8,128)(2,1)S(1)}, u32[]{:S(2)}, u32[]{:S(2)}) collective-permute-start(bf16[384,640]{1,0:T(8,128)(2,1)S(1)} %get-tuple-element.5.sent), channel_id=1, source_target_pairs={{0,2},{1,3},{2,0},{3,1},{4,6},{5,7},{6,4},{7,5},{8,10},{9,11},{10,... | collective-permute-start | bytes 1474568 | tf_op jit(solution)/shard_map/ppermute | solution.py:40
  108.7 2.1 %collective-permute-start.19 = (f32[64,512]{1,0:T(8,128)S(1)}, f32[64,512]{1,0:T(8,128)S(1)}, u32[]{:S(2)}, u32[]{:S(2)}) collective-permute-start(f32[64,512]{1,0:T(8,128)S(1)} %fusion.44), channel_id=1, source_target_pairs={{0,1},{1,2},{2,3},{3,0},{4,5},{5,6},{6,7},{7,4},{8,9},{9,10},{10,1... | collective-permute-start | bytes 393224 | tf_op jit(solution)/shard_map/ppermute | solution.py:40
  110.8 8.2 %collective-permute-done.11.got1 = bf16[384,640]{1,0:T(8,128)(2,1)S(1)} collective-permute-done((bf16[384,640]{1,0:T(8,128)(2,1)S(1)}, bf16[384,640]{1,0:T(8,128)(2,1)S(1)}, u32[]{:S(2)}, u32[]{:S(2)}) %collective-permute-start.11) | collective-permute-done | bytes 491552 | tf_op jit(solution)/shard_map/ppermute | solution.py:40
  120.1 6.0 %collective-permute-done.12.got2 = bf16[384,640]{1,0:T(8,128)(2,1)S(1)} collective-permute-done((bf16[384,640]{1,0:T(8,128)(2,1)S(1)}, bf16[384,640]{1,0:T(8,128)(2,1)S(1)}, u32[]{:S(2)}, u32[]{:S(2)}) %collective-permute-start.12) | collective-permute-done | bytes 491552 | tf_op jit(solution)/shard_map/ppermute | solution.py:40
  126.2 5.0 %image_gradients.1 = f32[64,2560]{1,0:T(8,128)} custom-call(s32[1]{0:T(128)} %bitcast.place, f32[256,640]{1,0:T(8,128)} %copy-done.1, bf16[384,640]{1,0:T(8,128)(2,1)S(1)} %get-tuple-element.5.sent, bf16[384,640]{1,0:T(8,128)(2,1)S(1)} %collective-permute-done.11.got1, bf16[384,640]{1,0:T(8,128)(2,1)S(1)} %collective-permute-done.12.got2, ...), custom_call_target="tpu_custom_call" | custom-call | tf_op jit(solution)/shard_map/image_gradients/pallas_call | solution.py:363
  133.5 1.6 collective-permute-done.22
  136.4 14.8 %all_to_all.15 = f32[16,2,3072]{2,1,0:T(2,128)S(1)} all-to-all(f32[16,2,3072]{2,1,0:T(2,128)S(1)} %reshape.282), channel_id=1, replica_groups=mesh['grp'=2,'dp'=16,'mp'=4] {'dp'}, dimensions={0} | all-to-all | bytes 786432 | tf_op jit(solution)/shard_map/all_to_all | solution.py:401
  151.4 12.4 %all_to_all.16 = f32[16,2,3072]{2,1,0:T(2,128)S(1)} all-to-all(f32[16,2,3072]{2,1,0:T(2,128)S(1)} %broadcast_in_dim.74), channel_id=1, replica_groups=mesh['grp'=2,'dp'=16,'mp'=4] {'dp'}, dimensions={0} | all-to-all | bytes 786432 | tf_op jit(solution)/shard_map/all_to_all | solution.py:58
  (146 shorter events, 24.4 us)
Async XLA Ops:
  1.8 57.2 %collective-permute-start = (bf16[32,5120]{1,0:T(8,128)(2,1)S(1)}, bf16[32,5120]{1,0:T(8,128)(2,1)}, u32[]{:S(2)}, u32[]{:S(2)}) collective-permute-start(bf16[32,5120]{1,0:T(8,128)(2,1)S(1)} %constant_dynamic-slice_fusion.15), channel_id=1, source_target_pairs={{0,1},{1,2},{2,3},{3,0},{4,5},{5,6},{6,7},{7,4},{8,9},{9,10},{10,1... | collective-permute-start | bytes 983048 | tf_op jit(solution)/shard_map/ppermute | solution.py:40
  3.5 55.5 %collective-permute-start.1 = (bf16[32,5120]{1,0:T(8,128)(2,1)S(1)}, bf16[32,5120]{1,0:T(8,128)(2,1)}, u32[]{:S(2)}, u32[]{:S(2)}) collective-permute-start(bf16[32,5120]{1,0:T(8,128)(2,1)S(1)} %constant_dynamic-slice_fusion.15), channel_id=1, source_target_pairs={{0,2},{1,3},{2,0},{3,1},{4,6},{5,7},{6,4},{7,5},{8,10},{9,11},{10,... | collective-permute-start | bytes 983048 | tf_op jit(solution)/shard_map/ppermute | solution.py:40
  9.1 65.6 %all-to-all-start = ((bf16[64,64,128]{2,1,0:T(8,128)(2,1)}), bf16[64,64,128]{2,1,0:T(8,128)(2,1)}, u32[]{:S(2)}, u32[]{:S(2)}) async-start(bf16[64,64,128]{2,1,0:T(8,128)(2,1)} %broadcast_in_dim.39), calls=%async_computation | async-start | bytes 2097152 | tf_op jit(solution)/shard_map/all_to_all | solution.py:58
  19.1 4.8 %collective-permute-start.4 = (bf16[128,512]{1,0:T(8,128)(2,1)S(1)}, bf16[128,512]{1,0:T(8,128)(2,1)S(1)}, u32[]{:S(2)}, u32[]{:S(2)}) collective-permute-start(bf16[128,512]{1,0:T(8,128)(2,1)S(1)} %constant_dynamic-slice_fusion.13), channel_id=1, source_target_pairs={{0,0},{1,16},{2,32},{3,48},{4,4},{5,20},{6,36},{7,52},{8,8},{9,24}... | collective-permute-start | bytes 393224 | tf_op jit(solution)/shard_map/ppermute | solution.py:245
  24.0 30.2 %collective-permute-start.5 = (bf16[192,512]{1,0:T(8,128)(2,1)S(1)}, bf16[192,512]{1,0:T(8,128)(2,1)S(1)}, u32[]{:S(2)}, u32[]{:S(2)}) collective-permute-start(bf16[192,512]{1,0:T(8,128)(2,1)S(1)} %get-tuple-element.35), channel_id=1, source_target_pairs={{0,48},{4,52},{8,56},{12,60},{16,0},{20,4},{24,8},{28,12},{32,16},... | collective-permute-start | bytes 589832 | tf_op jit(solution)/shard_map/ppermute | solution.py:53
  41.0 13.1 %collective-permute-start.6 = (bf16[192,512]{1,0:T(8,128)(2,1)S(1)}, bf16[192,512]{1,0:T(8,128)(2,1)S(1)}, u32[]{:S(2)}, u32[]{:S(2)}) collective-permute-start(bf16[192,512]{1,0:T(8,128)(2,1)S(1)} %get-tuple-element.34), channel_id=1, source_target_pairs={{0,32},{4,36},{8,40},{12,44},{16,48},{20,52},{24,56},{28,60},{32,0... | collective-permute-start | bytes 589832 | tf_op jit(solution)/shard_map/ppermute | solution.py:53
  41.0 12.0 %collective-permute-start.7 = (bf16[192,512]{1,0:T(8,128)(2,1)S(1)}, bf16[192,512]{1,0:T(8,128)(2,1)S(1)}, u32[]{:S(2)}, u32[]{:S(2)}) collective-permute-start(bf16[192,512]{1,0:T(8,128)(2,1)S(1)} %get-tuple-element.33), channel_id=1, source_target_pairs={{0,16},{4,20},{8,24},{12,28},{16,32},{20,36},{24,40},{28,44},{32,4... | collective-permute-start | bytes 589832 | tf_op jit(solution)/shard_map/ppermute | solution.py:53
  53.1 9.3 %collective-permute-start.2 = (bf16[32,5120]{1,0:T(8,128)(2,1)S(1)}, bf16[32,5120]{1,0:T(8,128)(2,1)S(1)}, u32[]{:S(2)}, u32[]{:S(2)}) collective-permute-start(bf16[32,5120]{1,0:T(8,128)(2,1)S(1)} %constant_dynamic-slice_fusion.15), channel_id=1, source_target_pairs={{0,3},{1,0},{2,1},{3,2},{4,7},{5,4},{6,5},{7,6},{8,11},{9,8},{10,9... | collective-permute-start | bytes 983048 | tf_op jit(solution)/shard_map/ppermute | solution.py:40
  55.9 40.8 %collective-permute-start.8 = (bf16[576,512]{1,0:T(8,128)(2,1)}, bf16[576,512]{1,0:T(8,128)(2,1)S(1)}, u32[]{:S(2)}, u32[]{:S(2)}) collective-permute-start(bf16[576,512]{1,0:T(8,128)(2,1)} %get-tuple-element.14), channel_id=1, source_target_pairs={{0,4},{4,8},{8,12},{12,0},{16,20},{20,24},{24,28},{28,16},{32,36},... | collective-permute-start | bytes 1769480 | tf_op jit(solution)/shard_map/ppermute | solution.py:53
  56.6 40.2 %collective-permute-start.9 = (bf16[576,512]{1,0:T(8,128)(2,1)}, bf16[576,512]{1,0:T(8,128)(2,1)S(1)}, u32[]{:S(2)}, u32[]{:S(2)}) collective-permute-start(bf16[576,512]{1,0:T(8,128)(2,1)} %get-tuple-element.15), channel_id=1, source_target_pairs={{0,8},{4,12},{8,0},{12,4},{16,24},{20,28},{24,16},{28,20},{32,40},... | collective-permute-start | bytes 1769480 | tf_op jit(solution)/shard_map/ppermute | solution.py:53
  77.9 13.2 %collective-permute-start.15 = (bf16[64,2048]{1,0:T(8,128)(2,1)S(1)}, bf16[64,2048]{1,0:T(8,128)(2,1)S(1)}, u32[]{:S(2)}, u32[]{:S(2)}) collective-permute-start(bf16[64,2048]{1,0:T(8,128)(2,1)S(1)} %get-tuple-element.8), channel_id=1, source_target_pairs={{0,3},{1,0},{2,1},{3,2},{4,7},{5,4},{6,5},{7,6},{8,11},{9,8},{10,9... | collective-permute-start | bytes 786440 | tf_op jit(solution)/shard_map/ppermute | solution.py:40
  80.5 11.9 %collective-permute-start.16 = (bf16[64,2048]{1,0:T(8,128)(2,1)S(1)}, bf16[64,2048]{1,0:T(8,128)(2,1)S(1)}, u32[]{:S(2)}, u32[]{:S(2)}) collective-permute-start(bf16[64,2048]{1,0:T(8,128)(2,1)S(1)} %get-tuple-element.10), channel_id=1, source_target_pairs={{0,2},{1,3},{2,0},{3,1},{4,6},{5,7},{6,4},{7,5},{8,10},{9,11},{10,... | collective-permute-start | bytes 786440 | tf_op jit(solution)/shard_map/ppermute | solution.py:40
  80.6 13.8 %collective-permute-start.17 = (bf16[64,2048]{1,0:T(8,128)(2,1)S(1)}, bf16[64,2048]{1,0:T(8,128)(2,1)S(1)}, u32[]{:S(2)}, u32[]{:S(2)}) collective-permute-start(bf16[64,2048]{1,0:T(8,128)(2,1)S(1)} %get-tuple-element.9), channel_id=1, source_target_pairs={{0,1},{1,2},{2,3},{3,0},{4,5},{5,6},{6,7},{7,4},{8,9},{9,10},{10,1... | collective-permute-start | bytes 786440 | tf_op jit(solution)/shard_map/ppermute | solution.py:40
  91.1 9.9 %collective-permute-start.10 = (bf16[576,512]{1,0:T(8,128)(2,1)S(1)}, bf16[576,512]{1,0:T(8,128)(2,1)S(1)}, u32[]{:S(2)}, u32[]{:S(2)}) collective-permute-start(bf16[576,512]{1,0:T(8,128)(2,1)S(1)} %copy-done.6), channel_id=1, source_target_pairs={{0,12},{4,0},{8,4},{12,8},{16,28},{20,16},{24,20},{28,24},{32,44},... | collective-permute-start | bytes 1769480 | tf_op jit(solution)/shard_map/ppermute | solution.py:53
  92.5 3.7 %collective-permute-start.3 = (bf16[128,2048]{1,0:T(8,128)(2,1)S(1)}, bf16[128,2048]{1,0:T(8,128)(2,1)S(1)}, u32[]{:S(2)}, u32[]{:S(2)}) collective-permute-start(bf16[128,2048]{1,0:T(8,128)(2,1)S(1)} %fusion.4.near), channel_id=1, source_target_pairs={{0,64},{64,0},{1,65},{65,1},{2,66},{66,2},{3,67},{67,3},{4,68},{68... | collective-permute-start | bytes 1572872 | tf_op jit(solution)/shard_map/ppermute | solution.py:44
  94.6 12.6 %collective-permute-start.18 = (f32[64,2560]{1,0:T(8,128)S(1)}, f32[64,2560]{1,0:T(8,128)S(1)}, u32[]{:S(2)}, u32[]{:S(2)}) collective-permute-start(f32[64,2560]{1,0:T(8,128)S(1)} %pad_maximum_fusion.1), channel_id=1, source_target_pairs={{0,64},{64,0},{1,65},{65,1},{2,66},{66,2},{3,67},{67,3},{4,68},{68... | collective-permute-start | bytes 1966088 | tf_op jit(solution)/shard_map/ppermute | solution.py:44
  96.1 14.6 %collective-permute-start.14 = (bf16[128,64]{1,0:T(8,128)(2,1)S(1)}, bf16[128,64]{1,0:T(8,128)(2,1)S(1)}, u32[]{:S(2)}, u32[]{:S(2)}) collective-permute-start(bf16[128,64]{1,0:T(8,128)(2,1)S(1)} %maximum_select_fusion.1.low_near), channel_id=1, source_target_pairs={{0,64},{64,0},{1,65},{65,1},{2,66},{66,2},{3,67},{67,3},{4,68},{68... | collective-permute-start | bytes 49160 | tf_op jit(solution)/shard_map/ppermute | solution.py:44
  102.0 16.9 %collective-permute-start.11 = (bf16[384,640]{1,0:T(8,128)(2,1)S(1)}, bf16[384,640]{1,0:T(8,128)(2,1)S(1)}, u32[]{:S(2)}, u32[]{:S(2)}) collective-permute-start(bf16[384,640]{1,0:T(8,128)(2,1)S(1)} %get-tuple-element.5.sent), channel_id=1, source_target_pairs={{0,1},{1,2},{2,3},{3,0},{4,5},{5,6},{6,7},{7,4},{8,9},{9,10},{10,1... | collective-permute-start | bytes 1474568 | tf_op jit(solution)/shard_map/ppermute | solution.py:40
  102.1 24.0 %collective-permute-start.12 = (bf16[384,640]{1,0:T(8,128)(2,1)S(1)}, bf16[384,640]{1,0:T(8,128)(2,1)S(1)}, u32[]{:S(2)}, u32[]{:S(2)}) collective-permute-start(bf16[384,640]{1,0:T(8,128)(2,1)S(1)} %get-tuple-element.5.sent), channel_id=1, source_target_pairs={{0,2},{1,3},{2,0},{3,1},{4,6},{5,7},{6,4},{7,5},{8,10},{9,11},{10,... | collective-permute-start | bytes 1474568 | tf_op jit(solution)/shard_map/ppermute | solution.py:40
  107.3 19.0 %collective-permute-start.13 = (bf16[384,640]{1,0:T(8,128)(2,1)S(1)}, bf16[384,640]{1,0:T(8,128)(2,1)S(1)}, u32[]{:S(2)}, u32[]{:S(2)}) collective-permute-start(bf16[384,640]{1,0:T(8,128)(2,1)S(1)} %get-tuple-element.5.sent), channel_id=1, source_target_pairs={{0,3},{1,0},{2,1},{3,2},{4,7},{5,4},{6,5},{7,6},{8,11},{9,8},{10,9... | collective-permute-start | bytes 1474568 | tf_op jit(solution)/shard_map/ppermute | solution.py:40
  108.7 23.7 %collective-permute-start.19 = (f32[64,512]{1,0:T(8,128)S(1)}, f32[64,512]{1,0:T(8,128)S(1)}, u32[]{:S(2)}, u32[]{:S(2)}) collective-permute-start(f32[64,512]{1,0:T(8,128)S(1)} %fusion.44), channel_id=1, source_target_pairs={{0,1},{1,2},{2,3},{3,0},{4,5},{5,6},{6,7},{7,4},{8,9},{9,10},{10,1... | collective-permute-start | bytes 393224 | tf_op jit(solution)/shard_map/ppermute | solution.py:40
  110.8 21.6 %collective-permute-start.20 = (f32[64,512]{1,0:T(8,128)S(1)}, f32[64,512]{1,0:T(8,128)S(1)}, u32[]{:S(2)}, u32[]{:S(2)}) collective-permute-start(f32[64,512]{1,0:T(8,128)S(1)} %fusion.44), channel_id=1, source_target_pairs={{0,2},{1,3},{2,0},{3,1},{4,6},{5,7},{6,4},{7,5},{8,10},{9,11},{10,... | collective-permute-start | bytes 393224 | tf_op jit(solution)/shard_map/ppermute | solution.py:40
  119.0 13.4 %collective-permute-start.21 = (f32[64,512]{1,0:T(8,128)S(1)}, f32[64,512]{1,0:T(8,128)S(1)}, u32[]{:S(2)}, u32[]{:S(2)}) collective-permute-start(f32[64,512]{1,0:T(8,128)S(1)} %fusion.44), channel_id=1, source_target_pairs={{0,3},{1,0},{2,1},{3,2},{4,7},{5,4},{6,5},{7,6},{8,11},{9,8},{10,9... | collective-permute-start | bytes 393224 | tf_op jit(solution)/shard_map/ppermute | solution.py:40
  133.4 1.7 %collective-permute-start.22 = (f32[32,2560]{1,0:T(8,128)S(1)}, f32[32,2560]{1,0:T(8,128)S(1)}, u32[]{:S(2)}, u32[]{:S(2)}) collective-permute-start(f32[32,2560]{1,0:T(8,128)S(1)} %pad_maximum_fusion.7), channel_id=1, source_target_pairs={{0,64},{64,0},{1,65},{65,1},{2,66},{66,2},{3,67},{67,3},{4,68},{68... | collective-permute-start | bytes 983048 | tf_op jit(solution)/shard_map/ppermute | solution.py:44
  (17 other events, 210.3 us)

commit v5 on v4

--- a/solution.py
+++ b/solution.py
@@ -144,7 +144,8 @@
     bias,
     line,
     position,
-    out,
+    mine,
+    give,
     *,
     block,
     half_kv,
@@ -185,14 +186,19 @@
         + jnp.sum(dlow.astype(f32) * raw_low, axis=1, keepdims=True)
     ) / width
     factor = inverse * inverse * inverse * centre
-    out[:, side * block :] = dot_tn(low, dvalues)
+    grad = dot_tn(low, dvalues)
+    half = rank // 2
+    mine[:, side * block :] = grad[:half]
+    give[:, side * block :] = grad[half:]
     enc_low = jnp.concatenate([low_near[...], low_far[...]])
     for k, piece in enumerate(pieces):
         here = pl.ds(block_start(place[0], k, side, block), block)
         dnormed = dot_nt(dvalues, piece[:block, :]) + dot(dlow, a_part[:, here])
         wide = jnp.concatenate([near[:, here], far[:, here]]).astype(f32)
         dimage = (inverse * (gain[:, here] * dnormed) - wide * factor).astype(bf16)
-        out[:, here] = dot_tn(enc_low, dimage)
+        grad = dot_tn(enc_low, dimage)
+        mine[:, here] = grad[:half]
+        give[:, here] = grad[half:]
 
 
 def body(
@@ -245,7 +251,8 @@
     w_moved = lax.ppermute(w_half, ("dp", "mp"), swap)
 
     own_hidden = cut(hidden, grp * mine_rows, mine_rows)
-    hid = jnp.concatenate([own_hidden] + [turned(own_hidden, "mp", k) for k in range(1, n_mp)])
+    hid_next, hid_last = turned(own_hidden, "mp", 1), turned(own_hidden, "mp", -1)
+    hid = jnp.concatenate([own_hidden, hid_next, turned(hid_next, "mp", 1), hid_last])
 
     own_length = seq_length[0]
     t_half = cut(targets[:area], grp * half_kv, half_kv, 1)
@@ -267,8 +274,9 @@
         piece = jnp.concatenate([w_line, t_given])
         pieces.append(along(piece, 0, k, side) if k else piece)
 
-    a_turned = jnp.where(first, llm_frozen.T, jnp.roll(llm_frozen.T, half_rank, axis=0))
-    a_all = to_everyone(a_turned, ("dp", "mp")).transpose(1, 0, 2).reshape(rank, width)
+    a_half, _ = lax.optimization_barrier((cut(llm_frozen.T, grp * half_rank, half_rank), w_moved))
+    a_mine = to_everyone(a_half, ("dp", "mp")).transpose(1, 0, 2).reshape(half_rank, width)
+    a_all = jnp.concatenate([a_mine, crossed(a_mine)])
     a_part = cut(a_all, mp * part_width, part_width, 1)
     b_all = jnp.where(first, llm_adapter, jnp.roll(llm_adapter, half_rank, axis=0))
     b_half = cut(b_all, grp * half_kv, half_kv, 1)
@@ -320,21 +328,14 @@
         jnp.concatenate([text_kept, text_kept]), jnp.concatenate([rest_high, rest_low])
     )
     rest_sum = rest_sum * text_weight
-    text_here = cut(text_sum, mp * part_width, part_width, 1)
-    text_sent = text_sum.astype(bf16)
-    for k in range(1, n_mp):
-        given = cut(text_sent, ((mp - k) & wrap) * part_width, part_width, 1)
-        text_here = text_here + turned(given, "mp", -k).astype(f32)
-    rest_mine = cut(rest_sum, grp * half_kv, half_kv, 1)
-    rest_give = cut(rest_sum, (1 - grp) * half_kv, half_kv, 1)
-    came = jnp.roll(crossed(jnp.concatenate([text_here, rest_give], axis=1)), half_rank, axis=0)
-    here_high, here_low = split_two(text_here + came[:, :part_width])
-    here_both = jnp.concatenate([here_high, here_low])
-    text_grad = jnp.zeros((2 * rank, half_kv), f32)
-    for k in range(side):
-        given = cut(here_both, ((col - k) & wrap) * block, block, 1)
-        text_grad = text_grad + dot(given, pieces[k][:block])
-    text_grad = text_grad[:rank] + text_grad[rank:] + rest_mine + came[:, part_width:]
+    both_sums = jnp.concatenate([text_sum, rest_sum], axis=1)
+    both_sums = both_sums[:half_rank] + crossed(both_sums[half_rank:])
+    text_parts = both_sums[:, :width].reshape(half_rank, owners, shard).transpose(1, 0, 2)
+    text_parts = lax.all_to_all(text_parts.astype(bf16), ("dp", "mp"), 0, 0, tiled=True)
+    text_here = jnp.sum(text_parts.astype(f32), axis=0)
+    here_high, here_low = split_two(text_here)
+    text_grad = dot(jnp.concatenate([here_high, here_low]), value_weight)
+    text_grad = text_grad[:half_rank] + text_grad[half_rank:] + both_sums[:, width:]
     text_grad = text_grad + (
         turned(text_grad, "mp", 1) + turned(text_grad, "mp", 2) + turned(text_grad, "mp", 3)
     )
@@ -360,11 +361,11 @@
         name="partial_products",
     )(where, image, image_far, gain_part, a_part, *pieces)
     got = [turned(sent, "mp", k) for k in range(1, n_mp)]
-    both = pl.pallas_call(
+    mine, give = pl.pallas_call(
         functools.partial(image_kernel, width=float(width), step=mine_rows, **sizes),
-        out_shape=jax.ShapeDtypeStruct((rank, part_width + half_kv), f32),
+        out_shape=(jax.ShapeDtypeStruct((half_rank, part_width + half_kv), f32),) * 2,
         in_specs=[SMEM] + [VMEM] * 19,
-        out_specs=VMEM,
+        out_specs=(VMEM, VMEM),
         compiler_params=PARAMS,
         name="image_gradients",
     )(
@@ -385,15 +386,13 @@
         position[:, None],
     )
 
-    both = jnp.concatenate([both[:, :part_width], both[:, part_width:] + text_grad], axis=1)
-    mine = both[:half_rank]
-    came = crossed(both[half_rank:])
+    came = crossed(give)
     llm_mine, llm_came = mine[:, part_width:], came[:, part_width:]
     mine = jnp.concatenate(
         [
             mine[:, :part_width] + came[:, :part_width],
-            jnp.where(first, llm_mine, llm_came),
-            jnp.where(first, llm_came, llm_mine),
+            jnp.where(first, llm_mine, llm_came) + text_grad[:, :half_kv],
+            jnp.where(first, llm_came, llm_mine) + text_grad[:, half_kv:],
         ],
         axis=1,
     )

time: 166 us -> 164 us (0.988)
  waiting for transfers between devices: 45.6 us -> 25.2 us
  other arithmetic: 7.46 us -> 14.2 us
  local copies, waits for them, and re-layouts: 8.86 us -> 15.1 us
  blocking collectives: 27.2 us -> 30.7 us
  Pallas kernels: 6.1 us -> 9.12 us
    ppermute x6, waiting for transfers between devices: 15.2 us -> 0.02 us  [along(): return lax.ppermute(array, 'dp', pairs)]
    all_to_all x0 -> x1, starting transfers between devices: none -> 11.9 us  [body(): lax.all_to_all(text_parts.astype(bf16), ('dp', 'mp'), 0, 0, tiled=True)]
    ppermute x12 -> x9, waiting for transfers between devices: 28.8 us -> 19.3 us  [turned(): lax.ppermute(array, axis, [(i, (i + step) % count) for i in range(count)])]
    ppermute x6, starting transfers between devices: 22.5 us -> 14.6 us  [along(): return lax.ppermute(array, 'dp', pairs)]
    all_to_all x1, waiting for transfers between devices: 0.01 us -> 5.59 us  [to_everyone(): lax.all_to_all(jnp.broadcast_to(array[None], (count, *array.shape)), axes...]
    ppermute x12 -> x9, starting transfers between devices: 17.7 us -> 12.4 us  [turned(): lax.ppermute(array, axis, [(i, (i + step) % count) for i in range(count)])]
    dynamic_slice x11 -> x10, local copies, waits for them, and re-layouts: 0.31 us -> 4.45 us  [cut(): return lax.dynamic_slice(array, starts, sizes, allow_negative_indices=False)]
    all_to_all x1, blocking collectives: 14.8 us -> 18.4 us  [body(): mine = jnp.sum(lax.all_to_all(mine, 'dp', 0, 0, tiled=True), axis=0)]
  transfers between devices with their start and end apart: 24 -> 23, of which waited for: 9 -> 7; matrix products, arithmetic and copies ran while one was open for 16% -> 24% of each run, Pallas kernels for 4% -> 6%
where the time goes in v5:
time: 164 us; the launch traced here: 163 us
  starting transfers between devices  50.6 us (31%)
  blocking collectives  30.7 us (19%)
  waiting for transfers between devices  25.2 us (15%)
  matrix products  16.2 us (10%)
  local copies, waits for them, and re-layouts  15.1 us (9%)
  other arithmetic  14.2 us (9%)
  Pallas kernels  9.12 us (6%)
  between operations  2.08 us (1%)
    ppermute x9, waiting for transfers between devices, turned(): lax.ppermute(array, axis, [(i, (i + step) % count) for i in range(count)])  19.3 us
    all_to_all x1, blocking collectives, body(): mine = jnp.sum(lax.all_to_all(mine, 'dp', 0, 0, tiled=True), axis=0)  18.4 us
    dot_general x5, matrix products, dot(): return jnp.dot(a, b, preferred_element_type=f32)  14.7 us
    ppermute x6, starting transfers between devices, along(): return lax.ppermute(array, 'dp', pairs)  14.6 us
    ppermute x9, starting transfers between devices, turned(): lax.ppermute(array, axis, [(i, (i + step) % count) for i in range(count)])  12.4 us
    all_to_all x1, blocking collectives, to_everyone(): lax.all_to_all(jnp.broadcast_to(array[None], (count, *array.shape)), axes...  12.3 us
    all_to_all x1, starting transfers between devices, body(): lax.all_to_all(text_parts.astype(bf16), ('dp', 'mp'), 0, 0, tiled=True)  11.9 us
    all_to_all x1, starting transfers between devices, to_everyone(): lax.all_to_all(jnp.broadcast_to(array[None], (count, *array.shape)), axes...  10.5 us
  transfers between devices with their start and end apart: 23, of which 7 were waited for; matrix products, arithmetic and copies ran while one was open for 24% of the time, Pallas kernels for 6%

profile of v5, /device:TPU:0, one launch (start us, length us, event | category | flops | bytes accessed | tf_op | source)
XLA Modules:
  0.0 163.2 jit_solution(15162749977596049742)
XLA Ops:
  2.5 3.1 %collective-permute-start.2 = (bf16[32,5120]{1,0:T(8,128)(2,1)}, bf16[32,5120]{1,0:T(8,128)(2,1)}, u32[]{:S(2)}, u32[]{:S(2)}) collective-permute-start(bf16[32,5120]{1,0:T(8,128)(2,1)} %constant_dynamic-slice_fusion.11), channel_id=1, source_target_pairs={{0,3},{1,0},{2,1},{3,2},{4,7},{5,4},{6,5},{7,6},{8,11},{9,8},{10,9... | collective-permute-start | bytes 983048 | tf_op jit(solution)/shard_map/ppermute | solution.py:40
  8.1 1.7 %fusion = f32[80]{0:T(128)S(1)} fusion(bf16[160,8192]{1,0:T(8,128)(2,1)} %param.19, s32[]{:T(128)S(6)} %mul.134), kind=kLoop, calls=%fused_computation.3 | loop fusion | flops 1966000 | bytes 1311044 | tf_op jit(solution)/shard_map/reduce_sum | solution.py:303
  16.7 7.9 %collective-permute-start.6 = (bf16[192,512]{1,0:T(8,128)(2,1)S(1)}, bf16[192,512]{1,0:T(8,128)(2,1)S(1)}, u32[]{:S(2)}, u32[]{:S(2)}) collective-permute-start(bf16[192,512]{1,0:T(8,128)(2,1)S(1)} %get-tuple-element.32), channel_id=1, source_target_pairs={{0,48},{4,52},{8,56},{12,60},{16,0},{20,4},{24,8},{28,12},{32,16},... | collective-permute-start | bytes 589832 | tf_op jit(solution)/shard_map/ppermute | solution.py:53
  27.0 10.5 %all-to-all-start = ((bf16[64,32,128]{2,1,0:T(8,128)(2,1)}), bf16[64,32,128]{2,1,0:T(8,128)(2,1)S(1)}, u32[]{:S(2)}, u32[]{:S(2)}) async-start(bf16[64,32,128]{2,1,0:T(8,128)(2,1)} %broadcast_in_dim.39), calls=%async_computation | async-start | bytes 1048576 | tf_op jit(solution)/shard_map/all_to_all | solution.py:58
  39.2 1.6 collective-permute-start.9
  40.8 2.7 %collective-permute-start.10 = (bf16[576,512]{1,0:T(8,128)(2,1)}, bf16[576,512]{1,0:T(8,128)(2,1)S(1)}, u32[]{:S(2)}, u32[]{:S(2)}) collective-permute-start(bf16[576,512]{1,0:T(8,128)(2,1)} %get-tuple-element.16), channel_id=1, source_target_pairs={{0,8},{4,12},{8,0},{12,4},{16,24},{20,28},{24,16},{28,20},{32,40},... | collective-permute-start | bytes 1769480 | tf_op jit(solution)/shard_map/ppermute | solution.py:53
  43.4 1.5 collective-permute-start.11
  44.9 1.5 collective-permute-start.1
  46.4 5.6 %all-to-all-done = bf16[64,32,128]{2,1,0:T(8,128)(2,1)S(1)} async-done(((bf16[64,32,128]{2,1,0:T(8,128)(2,1)}), bf16[64,32,128]{2,1,0:T(8,128)(2,1)S(1)}, u32[]{:S(2)}, u32[]{:S(2)}) %all-to-all-start) | async-done | bytes 524320 | tf_op jit(solution)/shard_map/all_to_all | solution.py:58
  52.2 1.9 %collective-permute-done.1 = bf16[32,5120]{1,0:T(8,128)(2,1)} collective-permute-done((bf16[32,5120]{1,0:T(8,128)(2,1)}, bf16[32,5120]{1,0:T(8,128)(2,1)}, u32[]{:S(2)}, u32[]{:S(2)}) %collective-permute-start.1) | collective-permute-done | bytes 327712 | tf_op jit(solution)/shard_map/ppermute | solution.py:40
  54.0 1.9 %convolution_convert_fusion = bf16[128,64]{1,0:T(8,128)(2,1)S(1)} fusion(bf16[5120,64]{0,1:T(8,128)(2,1)S(1)} %copy-done.26, bf16[32,5120]{1,0:T(8,128)(2,1)} %collective-permute-done.2, bf16[32,5120]{1,0:T(8,128)(2,1)} %collective-permute-done.1, bf16[32,5120]{1,0:T(8,128)(2,1)} %collective-permute-done, bf16[32,5120]{1,0:T(8,128)(2,1)} %constant_dynamic-slice_fusion.11), kind=kOutput, calls=%fused_computation.18 | convolution fusion | flops 89137152 | bytes 1982464 | tf_op jit(solution)/shard_map/dot_general | solution.py:17
  61.3 11.2 %fusion.4.near = bf16[128,2048]{1,0:T(8,128)(2,1)} fusion(f32[128,2048]{1,0:T(8,128)S(1)} %fusion.53, bf16[5120,2048]{1,0:T(8,128)(2,1)} %param.15, f32[2048]{0:T(1024)S(1)} %copy-done.22, bf16[32,5120]{1,0:T(8,128)(2,1)} %collective-permute-done.2, bf16[32,5120]{1,0:T(8,128)(2,1)} %collective-permute-done.1, bf16[32,5120]{1,0:T(8,128)(2,1)} %collective-permute-done, ...), kind=kOutput, calls=%fused_computation.8 | convolution fusion | flops 2690383872 | bytes 23863296 | tf_op jit(solution)/shard_map/dot_general | solution.py:17
  75.0 3.2 %partial_products.1 = (bf16[384,640]{1,0:T(8,128)(2,1)}, f32[256,640]{1,0:T(8,128)S(1)}) custom-call(s32[1]{0:T(128)} %bitcast.place, bf16[128,2048]{1,0:T(8,128)(2,1)} %fusion.4.near, bf16[128,2048]{1,0:T(8,128)(2,1)} %collective-permute-done.3.far, f32[1,2048]{1,0:T(1,128)S(1)} %bitcast.62, bf16[64,2048]{1,0:T(8,128)(2,1)S(1)} %constant_dynamic-slice_fusion.9.a_part, ...), custom_call_target="tpu_custom_call" | custom-call | tf_op jit(solution)/shard_map/partial_products/pallas_call | solution.py:352
  78.3 2.4 %collective-permute-start.13 = (bf16[384,640]{1,0:T(8,128)(2,1)}, bf16[384,640]{1,0:T(8,128)(2,1)}, u32[]{:S(2)}, u32[]{:S(2)}) collective-permute-start(bf16[384,640]{1,0:T(8,128)(2,1)} %get-tuple-element.9.sent), channel_id=1, source_target_pairs={{0,2},{1,3},{2,0},{3,1},{4,6},{5,7},{6,4},{7,5},{8,10},{9,11},{10,... | collective-permute-start | bytes 1474568 | tf_op jit(solution)/shard_map/ppermute | solution.py:40
  80.7 1.5 collective-permute-start.14
  85.5 11.9 %all-to-all-start.1 = ((bf16[64,32,128]{2,1,0:T(8,128)(2,1)}), bf16[64,32,128]{2,1,0:T(8,128)(2,1)}, u32[]{:S(2)}, u32[]{:S(2)}) async-start(bf16[64,32,128]{2,1,0:T(8,128)(2,1)} %bitcast_bitcast_fusion), calls=%async_computation.1 | async-start | bytes 1048576 | tf_op jit(solution)/shard_map/all_to_all | solution.py:334
  99.7 9.1 %collective-permute-done.12.got1 = bf16[384,640]{1,0:T(8,128)(2,1)} collective-permute-done((bf16[384,640]{1,0:T(8,128)(2,1)}, bf16[384,640]{1,0:T(8,128)(2,1)}, u32[]{:S(2)}, u32[]{:S(2)}) %collective-permute-start.12) | collective-permute-done | bytes 491552 | tf_op jit(solution)/shard_map/ppermute | solution.py:40
  109.0 5.9 %image_gradients.1 = (f32[32,2560]{1,0:T(8,128)S(1)}, f32[32,2560]{1,0:T(8,128)}) custom-call(s32[1]{0:T(128)} %bitcast.place, f32[256,640]{1,0:T(8,128)} %copy-done.2, bf16[384,640]{1,0:T(8,128)(2,1)} %get-tuple-element.9.sent, bf16[384,640]{1,0:T(8,128)(2,1)} %collective-permute-done.12.got1, bf16[384,640]{1,0:T(8,128)(2,1)} %collective-permute-done.13.got2, ...), custom_call_target="tpu_custom_call" | custom-call | tf_op jit(solution)/shard_map/image_gradients/pallas_call | solution.py:364
  118.2 2.4 %collective-permute-start.20 = (f32[32,1024]{1,0:T(8,128)S(1)}, f32[32,1024]{1,0:T(8,128)S(1)}, u32[]{:S(2)}, u32[]{:S(2)}) collective-permute-start(f32[32,1024]{1,0:T(8,128)S(1)} %slice_add_fusion.1), channel_id=1, source_target_pairs={{0,3},{1,0},{2,1},{3,2},{4,7},{5,4},{6,5},{7,6},{8,11},{9,8},{10,9... | collective-permute-start | bytes 393224 | tf_op jit(solution)/shard_map/ppermute | solution.py:40
  120.6 1.5 collective-permute-start.19
  122.2 2.0 %collective-permute-done.20 = f32[32,1024]{1,0:T(8,128)S(1)} collective-permute-done((f32[32,1024]{1,0:T(8,128)S(1)}, f32[32,1024]{1,0:T(8,128)S(1)}, u32[]{:S(2)}, u32[]{:S(2)}) %collective-permute-start.20) | collective-permute-done | bytes 131104 | tf_op jit(solution)/shard_map/ppermute | solution.py:40
  124.1 6.1 %collective-permute-done.18 = f32[32,1024]{1,0:T(8,128)S(1)} collective-permute-done((f32[32,1024]{1,0:T(8,128)S(1)}, f32[32,1024]{1,0:T(8,128)S(1)}, u32[]{:S(2)}, u32[]{:S(2)}) %collective-permute-start.18) | collective-permute-done | bytes 131104 | tf_op jit(solution)/shard_map/ppermute | solution.py:40
  130.6 18.4 %all_to_all.20 = f32[16,2,3072]{2,1,0:T(2,128)S(1)} all-to-all(f32[16,2,3072]{2,1,0:T(2,128)S(1)} %reshape.284), channel_id=1, replica_groups=mesh['grp'=2,'dp'=16,'mp'=4] {'dp'}, dimensions={0} | all-to-all | bytes 786432 | tf_op jit(solution)/shard_map/all_to_all | solution.py:400
  149.2 12.3 %all_to_all.21 = f32[16,2,3072]{2,1,0:T(2,128)S(1)} all-to-all(f32[16,2,3072]{2,1,0:T(2,128)S(1)} %broadcast_in_dim.74), channel_id=1, replica_groups=mesh['grp'=2,'dp'=16,'mp'=4] {'dp'}, dimensions={0} | all-to-all | bytes 786432 | tf_op jit(solution)/shard_map/all_to_all | solution.py:58
  (163 shorter events, 33.6 us)
Async XLA Ops:
  2.5 49.6 %collective-permute-start.2 = (bf16[32,5120]{1,0:T(8,128)(2,1)}, bf16[32,5120]{1,0:T(8,128)(2,1)}, u32[]{:S(2)}, u32[]{:S(2)}) collective-permute-start(bf16[32,5120]{1,0:T(8,128)(2,1)} %constant_dynamic-slice_fusion.11), channel_id=1, source_target_pairs={{0,3},{1,0},{2,1},{3,2},{4,7},{5,4},{6,5},{7,6},{8,11},{9,8},{10,9... | collective-permute-start | bytes 983048 | tf_op jit(solution)/shard_map/ppermute | solution.py:40
  5.6 39.3 %collective-permute-start = (bf16[32,5120]{1,0:T(8,128)(2,1)}, bf16[32,5120]{1,0:T(8,128)(2,1)}, u32[]{:S(2)}, u32[]{:S(2)}) collective-permute-start(bf16[32,5120]{1,0:T(8,128)(2,1)} %constant_dynamic-slice_fusion.11), channel_id=1, source_target_pairs={{0,1},{1,2},{2,3},{3,0},{4,5},{5,6},{6,7},{7,4},{8,9},{9,10},{10,1... | collective-permute-start | bytes 983048 | tf_op jit(solution)/shard_map/ppermute | solution.py:40
  6.5 10.1 %collective-permute-start.4 = (bf16[128,512]{1,0:T(8,128)(2,1)S(1)}, bf16[128,512]{1,0:T(8,128)(2,1)S(1)}, u32[]{:S(2)}, u32[]{:S(2)}) collective-permute-start(bf16[128,512]{1,0:T(8,128)(2,1)S(1)} %constant_dynamic-slice_fusion.10), channel_id=1, source_target_pairs={{0,0},{1,16},{2,32},{3,48},{4,4},{5,20},{6,36},{7,52},{8,8},{9,24}... | collective-permute-start | bytes 393224 | tf_op jit(solution)/shard_map/ppermute | solution.py:251
  16.7 20.8 %collective-permute-start.6 = (bf16[192,512]{1,0:T(8,128)(2,1)S(1)}, bf16[192,512]{1,0:T(8,128)(2,1)S(1)}, u32[]{:S(2)}, u32[]{:S(2)}) collective-permute-start(bf16[192,512]{1,0:T(8,128)(2,1)S(1)} %get-tuple-element.32), channel_id=1, source_target_pairs={{0,48},{4,52},{8,56},{12,60},{16,0},{20,4},{24,8},{28,12},{32,16},... | collective-permute-start | bytes 589832 | tf_op jit(solution)/shard_map/ppermute | solution.py:53
  24.6 12.9 %collective-permute-start.7 = (bf16[192,512]{1,0:T(8,128)(2,1)S(1)}, bf16[192,512]{1,0:T(8,128)(2,1)S(1)}, u32[]{:S(2)}, u32[]{:S(2)}) collective-permute-start(bf16[192,512]{1,0:T(8,128)(2,1)S(1)} %get-tuple-element.31), channel_id=1, source_target_pairs={{0,32},{4,36},{8,40},{12,44},{16,48},{20,52},{24,56},{28,60},{32,0... | collective-permute-start | bytes 589832 | tf_op jit(solution)/shard_map/ppermute | solution.py:53
  24.6 12.9 %collective-permute-start.8 = (bf16[192,512]{1,0:T(8,128)(2,1)S(1)}, bf16[192,512]{1,0:T(8,128)(2,1)S(1)}, u32[]{:S(2)}, u32[]{:S(2)}) collective-permute-start(bf16[192,512]{1,0:T(8,128)(2,1)S(1)} %get-tuple-element.30), channel_id=1, source_target_pairs={{0,16},{4,20},{8,24},{12,28},{16,32},{20,36},{24,40},{28,44},{32,4... | collective-permute-start | bytes 589832 | tf_op jit(solution)/shard_map/ppermute | solution.py:53
  27.0 25.0 %all-to-all-start = ((bf16[64,32,128]{2,1,0:T(8,128)(2,1)}), bf16[64,32,128]{2,1,0:T(8,128)(2,1)S(1)}, u32[]{:S(2)}, u32[]{:S(2)}) async-start(bf16[64,32,128]{2,1,0:T(8,128)(2,1)} %broadcast_in_dim.39), calls=%async_computation | async-start | bytes 1048576 | tf_op jit(solution)/shard_map/all_to_all | solution.py:58
  39.2 35.8 %collective-permute-start.9 = (bf16[576,512]{1,0:T(8,128)(2,1)}, bf16[576,512]{1,0:T(8,128)(2,1)S(1)}, u32[]{:S(2)}, u32[]{:S(2)}) collective-permute-start(bf16[576,512]{1,0:T(8,128)(2,1)} %get-tuple-element.15), channel_id=1, source_target_pairs={{0,4},{4,8},{8,12},{12,0},{16,20},{20,24},{24,28},{28,16},{32,36},... | collective-permute-start | bytes 1769480 | tf_op jit(solution)/shard_map/ppermute | solution.py:53
  40.8 34.2 %collective-permute-start.10 = (bf16[576,512]{1,0:T(8,128)(2,1)}, bf16[576,512]{1,0:T(8,128)(2,1)S(1)}, u32[]{:S(2)}, u32[]{:S(2)}) collective-permute-start(bf16[576,512]{1,0:T(8,128)(2,1)} %get-tuple-element.16), channel_id=1, source_target_pairs={{0,8},{4,12},{8,0},{12,4},{16,24},{20,28},{24,16},{28,20},{32,40},... | collective-permute-start | bytes 1769480 | tf_op jit(solution)/shard_map/ppermute | solution.py:53
  43.4 31.6 %collective-permute-start.11 = (bf16[576,512]{1,0:T(8,128)(2,1)}, bf16[576,512]{1,0:T(8,128)(2,1)S(1)}, u32[]{:S(2)}, u32[]{:S(2)}) collective-permute-start(bf16[576,512]{1,0:T(8,128)(2,1)} %get-tuple-element.14), channel_id=1, source_target_pairs={{0,12},{4,0},{8,4},{12,8},{16,28},{20,16},{24,20},{28,24},{32,44},... | collective-permute-start | bytes 1769480 | tf_op jit(solution)/shard_map/ppermute | solution.py:53
  44.9 9.1 %collective-permute-start.1 = (bf16[32,5120]{1,0:T(8,128)(2,1)}, bf16[32,5120]{1,0:T(8,128)(2,1)}, u32[]{:S(2)}, u32[]{:S(2)}) collective-permute-start(bf16[32,5120]{1,0:T(8,128)(2,1)} %collective-permute-done), channel_id=1, source_target_pairs={{0,1},{1,2},{2,3},{3,0},{4,5},{5,6},{6,7},{7,4},{8,9},{9,10},{10,1... | collective-permute-start | bytes 983048 | tf_op jit(solution)/shard_map/ppermute | solution.py:40
  52.1 4.2 %collective-permute-start.5 = (bf16[32,8192]{1,0:T(8,128)(2,1)S(1)}, bf16[32,8192]{1,0:T(8,128)(2,1)S(1)}, u32[]{:S(2)}, u32[]{:S(2)}) collective-permute-start(bf16[32,8192]{1,0:T(8,128)(2,1)S(1)} %copy_bitcast_fusion), channel_id=1, source_target_pairs={{0,64},{64,0},{1,65},{65,1},{2,66},{66,2},{3,67},{67,3},{4,68},{68... | collective-permute-start | bytes 1572872 | tf_op jit(solution)/shard_map/ppermute | solution.py:44
  56.0 17.2 %copy-start.15 = (bf16[128,64]{1,0:T(8,128)(2,1)}, bf16[128,64]{1,0:T(8,128)(2,1)S(1)}, u32[]{:S(2)}) copy-start(bf16[128,64]{1,0:T(8,128)(2,1)S(1)} %convolution_convert_fusion) | copy-start | bytes 49156
  61.3 20.8 %collective-permute-start.17 = (f32[32,9216]{1,0:T(8,128)}, f32[32,9216]{1,0:T(8,128)}, u32[]{:S(2)}, u32[]{:S(2)}) collective-permute-start(f32[32,9216]{1,0:T(8,128)} %pad_maximum_fusion.1), channel_id=1, source_target_pairs={{0,64},{64,0},{1,65},{65,1},{2,66},{66,2},{3,67},{67,3},{4,68},{68... | collective-permute-start | bytes 3538952 | tf_op jit(solution)/shard_map/ppermute | solution.py:44
  72.5 2.6 %collective-permute-start.3 = (bf16[128,2048]{1,0:T(8,128)(2,1)}, bf16[128,2048]{1,0:T(8,128)(2,1)}, u32[]{:S(2)}, u32[]{:S(2)}) collective-permute-start(bf16[128,2048]{1,0:T(8,128)(2,1)} %fusion.4.near), channel_id=1, source_target_pairs={{0,64},{64,0},{1,65},{65,1},{2,66},{66,2},{3,67},{67,3},{4,68},{68... | collective-permute-start | bytes 1572872 | tf_op jit(solution)/shard_map/ppermute | solution.py:44
  78.3 30.5 %collective-permute-start.12 = (bf16[384,640]{1,0:T(8,128)(2,1)}, bf16[384,640]{1,0:T(8,128)(2,1)}, u32[]{:S(2)}, u32[]{:S(2)}) collective-permute-start(bf16[384,640]{1,0:T(8,128)(2,1)} %get-tuple-element.9.sent), channel_id=1, source_target_pairs={{0,1},{1,2},{2,3},{3,0},{4,5},{5,6},{6,7},{7,4},{8,9},{9,10},{10,1... | collective-permute-start | bytes 1474568 | tf_op jit(solution)/shard_map/ppermute | solution.py:40
  78.3 30.5 %collective-permute-start.13 = (bf16[384,640]{1,0:T(8,128)(2,1)}, bf16[384,640]{1,0:T(8,128)(2,1)}, u32[]{:S(2)}, u32[]{:S(2)}) collective-permute-start(bf16[384,640]{1,0:T(8,128)(2,1)} %get-tuple-element.9.sent), channel_id=1, source_target_pairs={{0,2},{1,3},{2,0},{3,1},{4,6},{5,7},{6,4},{7,5},{8,10},{9,11},{10,... | collective-permute-start | bytes 1474568 | tf_op jit(solution)/shard_map/ppermute | solution.py:40
  80.7 28.4 %collective-permute-start.14 = (bf16[384,640]{1,0:T(8,128)(2,1)}, bf16[384,640]{1,0:T(8,128)(2,1)}, u32[]{:S(2)}, u32[]{:S(2)}) collective-permute-start(bf16[384,640]{1,0:T(8,128)(2,1)} %get-tuple-element.9.sent), channel_id=1, source_target_pairs={{0,3},{1,0},{2,1},{3,2},{4,7},{5,4},{6,5},{7,6},{8,11},{9,8},{10,9... | collective-permute-start | bytes 1474568 | tf_op jit(solution)/shard_map/ppermute | solution.py:40
  85.5 29.5 %all-to-all-start.1 = ((bf16[64,32,128]{2,1,0:T(8,128)(2,1)}), bf16[64,32,128]{2,1,0:T(8,128)(2,1)}, u32[]{:S(2)}, u32[]{:S(2)}) async-start(bf16[64,32,128]{2,1,0:T(8,128)(2,1)} %bitcast_bitcast_fusion), calls=%async_computation.1 | async-start | bytes 1048576 | tf_op jit(solution)/shard_map/all_to_all | solution.py:334
  98.2 1.3 collective-permute-start.15
  114.9 7.2 %collective-permute-start.16 = (f32[32,2560]{1,0:T(8,128)}, f32[32,2560]{1,0:T(8,128)S(1)}, u32[]{:S(2)}, u32[]{:S(2)}) collective-permute-start(f32[32,2560]{1,0:T(8,128)} %get-tuple-element.11), channel_id=1, source_target_pairs={{0,64},{64,0},{1,65},{65,1},{2,66},{66,2},{3,67},{67,3},{4,68},{68... | collective-permute-start | bytes 983048 | tf_op jit(solution)/shard_map/ppermute | solution.py:44
  118.2 6.0 %collective-permute-start.20 = (f32[32,1024]{1,0:T(8,128)S(1)}, f32[32,1024]{1,0:T(8,128)S(1)}, u32[]{:S(2)}, u32[]{:S(2)}) collective-permute-start(f32[32,1024]{1,0:T(8,128)S(1)} %slice_add_fusion.1), channel_id=1, source_target_pairs={{0,3},{1,0},{2,1},{3,2},{4,7},{5,4},{6,5},{7,6},{8,11},{9,8},{10,9... | collective-permute-start | bytes 393224 | tf_op jit(solution)/shard_map/ppermute | solution.py:40
  120.6 9.6 %collective-permute-start.18 = (f32[32,1024]{1,0:T(8,128)S(1)}, f32[32,1024]{1,0:T(8,128)S(1)}, u32[]{:S(2)}, u32[]{:S(2)}) collective-permute-start(f32[32,1024]{1,0:T(8,128)S(1)} %slice_add_fusion.1), channel_id=1, source_target_pairs={{0,1},{1,2},{2,3},{3,0},{4,5},{5,6},{6,7},{7,4},{8,9},{9,10},{10,1... | collective-permute-start | bytes 393224 | tf_op jit(solution)/shard_map/ppermute | solution.py:40
  120.6 9.6 %collective-permute-start.19 = (f32[32,1024]{1,0:T(8,128)S(1)}, f32[32,1024]{1,0:T(8,128)S(1)}, u32[]{:S(2)}, u32[]{:S(2)}) collective-permute-start(f32[32,1024]{1,0:T(8,128)S(1)} %slice_add_fusion.1), channel_id=1, source_target_pairs={{0,2},{1,3},{2,0},{3,1},{4,6},{5,7},{6,4},{7,5},{8,10},{9,11},{10,... | collective-permute-start | bytes 393224 | tf_op jit(solution)/shard_map/ppermute | solution.py:40
  (28 other events, 160.7 us)

commit v6 on v5

--- a/solution.py
+++ b/solution.py
@@ -78,12 +78,44 @@
 
 
 def partial_kernel(
-    place, near, far, gain, a_part, w0, w1, w2, w3, sent, kept, *, block, half_kv, rank, chunk
+    place,
+    near,
+    far,
+    gain,
+    a_part,
+    w0,
+    w1,
+    w2,
+    w3,
+    line,
+    position,
+    own,
+    to1,
+    to2,
+    to3,
+    sums,
+    *,
+    block,
+    half_kv,
+    rank,
+    chunk,
+    step,
 ):
     rows = near.shape[0]
     pieces = (w0, w1, w2, w3)
     side = len(pieces)
+    per = chunk // 2
+    wide_rows, lengths = [], []
+    for piece in pieces:
+        for z in range(side):
+            both = piece[block + z * chunk : block + (z + 1) * chunk, :].astype(f32)
+            wide_rows.append(both[:per])
+            lengths.append(both[per:, :128])
+    table = jnp.concatenate(wide_rows).astype(bf16)
+    lengths = jnp.concatenate(lengths).astype(bf16)
+    lane = lax.broadcasted_iota(jnp.int32, (rows, rank), 1)
     for h, source in enumerate((near, far)):
+        out = slice(h * rows, (h + 1) * rows)
         values = jnp.zeros((rows, half_kv), f32)
         low = jnp.zeros((rows, rank), f32)
         squares = jnp.zeros((rows, 1), f32)
@@ -94,39 +126,65 @@
             squares = squares + jnp.sum(wide * wide, axis=1, keepdims=True)
             values = values + dot(scaled, piece[:block, :])
             low = low + dot_nt(scaled, a_part[:, here])
-        out = slice(h * rows, (h + 1) * rows)
-        kept[out, :half_kv] = values
-        high = squares.astype(bf16)
-        left = squares - high.astype(f32)
-        middle = left.astype(bf16)
-        last = left - middle.astype(f32)
-        lane = lax.broadcasted_iota(jnp.int32, (rows, rank), 1)
-        three = jnp.where(
-            lane == 0,
-            high.astype(f32),
-            jnp.where(lane == 1, middle.astype(f32), jnp.where(lane == 2, last, 0.0)),
-        )
-        extra = jnp.concatenate([low, three], axis=1)
-        kept[out, half_kv:] = extra
-        sent[out, :half_kv] = values.astype(bf16)
-        sent[out, half_kv:] = extra.astype(bf16)
-    per = chunk // 2
-    for k, piece in enumerate(pieces):
-        for pair in range(side // 2):
-            wide, lengths = [], []
-            for z in (2 * pair, 2 * pair + 1):
-                both = piece[block + z * chunk : block + (z + 1) * chunk, :].astype(f32)
-                wide.append(both[:per])
-                lengths.append(both[per:, :128])
-            at = 2 * rows + (k * side + 2 * pair) * per
-            sent[at : at + chunk, :half_kv] = jnp.concatenate(wide).astype(bf16)
-            sent[at : at + chunk, half_kv:] = jnp.concatenate(lengths).astype(bf16)
+        entries = lax.broadcasted_iota(jnp.int32, (rows, table.shape[0]), 1)
+        pick = (line[out, :] == entries).astype(bf16)
+        length = dot(pick, lengths)[:, :1]
+        high = squares.astype(bf16).astype(f32)
+        middle = (squares - high).astype(bf16).astype(f32)
+        last = squares - high - middle
+        extra = jnp.zeros((rows, rank), f32)
+        for i, number in enumerate((high, middle, last, length)):
+            extra = jnp.where(lane == i, number, extra)
+        sums[out, :half_kv] = values
+        sums[out, half_kv : half_kv + 2 * rank] = jnp.concatenate([low, extra], axis=1)
+        sums[out, half_kv + 2 * rank :] = dot(pick, table)
+    lane = lax.broadcasted_iota(jnp.int32, (step, 2 * rank), 1)
+    for k, target in enumerate((own, to1, to2, to3)):
+        there = (place[1] + side - k) & (side - 1)
+        for h in range(2):
+            start = pl.multiple_of(h * rows + there * step, step)
+            target[h * step : (h + 1) * step, :] = sums[pl.ds(start, step), :].astype(target.dtype)
+            if k == 0:
+                extra = sums[pl.ds(start, step), half_kv : half_kv + 2 * rank]
+                extra = jnp.where(lane == rank + 4, position[pl.ds(start, step), :], extra)
+                own[h * step : (h + 1) * step, half_kv : half_kv + 2 * rank] = extra
+
+
+def row_kernel(own, got1, got2, got3, b_half, bias, packed, *, half_kv, rank, width):
+    total = own[...]
+    for got in (got1, got2, got3):
+        total = total + got[...].astype(f32)
+    raw_values = total[:, :half_kv]
+    raw_low = total[:, half_kv : half_kv + rank]
+    at = half_kv + rank
+    squares = total[:, at : at + 1] + total[:, at + 1 : at + 2] + total[:, at + 2 : at + 3]
+    length = total[:, at + 3 : at + 4]
+    position = total[:, at + 4 : at + 5]
+    weight = jnp.where(position < length, 1.0 / length, 0.0)
+    inverse = lax.rsqrt(squares / width + epsilon)
+    low = (raw_low * inverse).astype(bf16)
+    values_out = raw_values * inverse + bias[...] + dot(low, b_half[...])
+    dvalues = ((values_out - total[:, half_kv + 2 * rank :]) * weight).astype(bf16)
+    dlow = dot_nt(dvalues, b_half[...]).astype(bf16)
+    centre = (
+        jnp.sum(dvalues.astype(f32) * raw_values, axis=1, keepdims=True)
+        + jnp.sum(dlow.astype(f32) * raw_low, axis=1, keepdims=True)
+    ) / width
+    factor = inverse * inverse * inverse * centre
+    lane = lax.broadcasted_iota(jnp.int32, (total.shape[0], rank), 1)
+    extra = jnp.zeros((total.shape[0], rank), f32)
+    for i, number in enumerate((inverse, factor)):
+        for j in range(3):
+            part = number.astype(bf16).astype(f32)
+            extra = jnp.where(lane == 3 * i + j, part, extra)
+            number = number - part
+    packed[:, :half_kv] = dvalues
+    packed[:, half_kv:] = jnp.concatenate([low.astype(f32), extra], axis=1).astype(bf16)
 
 
 def image_kernel(
     place,
-    kept,
-    sent,
+    packed,
     got1,
     got2,
     got3,
@@ -141,53 +199,32 @@
     w2,
     w3,
     b_half,
-    bias,
-    line,
-    position,
     mine,
     give,
+    rows,
     *,
     block,
     half_kv,
     rank,
-    width,
     step,
 ):
     pieces = (w0, w1, w2, w3)
     side = len(pieces)
-    got = (got1, got2, got3)
-    count = kept.shape[0]
-    parts = []
-    for h in range(2):
-        for p in range(side):
-            at = h * side * step + p * step
-            total = kept[at : at + step, :]
-            for k in range(1, side):
-                there = h * side * step + ((p - k) % side) * step
-                total = total + got[k - 1][there : there + step, :].astype(f32)
-            parts.append(total)
-    total = jnp.concatenate(parts)
-    raw_values = total[:, :half_kv]
-    raw_low = total[:, half_kv : half_kv + rank]
-    squares = jnp.sum(total[:, half_kv + rank :], axis=1, keepdims=True)
-    lines = side * (sent.shape[0] - count)
-    pick = (line[...] == lax.broadcasted_iota(jnp.int32, (count, lines), 1)).astype(bf16)
-    table = jnp.concatenate([sent[count:, :]] + [g[count:, :] for g in got])
-    picked = dot(pick, table)
-    length = picked[:, half_kv : half_kv + 1]
-    weight = jnp.where(position[...] < length, 1.0 / length, 0.0)
-    inverse = lax.rsqrt(squares / width + epsilon)
-    low = (raw_low * inverse).astype(bf16)
-    values_out = raw_values * inverse + bias[...] + dot(low, b_half[...])
-    dvalues = ((values_out - picked[:, :half_kv]) * weight).astype(bf16)
+    count = near.shape[0]
+    for k, source in enumerate((packed, got1, got2, got3)):
+        there = (place[1] + side - k) & (side - 1)
+        for h in range(2):
+            start = pl.multiple_of(h * count + there * step, step)
+            rows[pl.ds(start, step), :] = source[h * step : (h + 1) * step, :]
+    dvalues = rows[:, :half_kv]
+    extra = rows[:, half_kv:]
+    low = extra[:, :rank]
+    numbers = extra[:, rank:].astype(f32)
+    inverse = numbers[:, 0:1] + numbers[:, 1:2] + numbers[:, 2:3]
+    factor = numbers[:, 3:4] + numbers[:, 4:5] + numbers[:, 5:6]
     dlow = dot_nt(dvalues, b_half[...]).astype(bf16)
-    centre = (
-        jnp.sum(dvalues.astype(f32) * raw_values, axis=1, keepdims=True)
-        + jnp.sum(dlow.astype(f32) * raw_low, axis=1, keepdims=True)
-    ) / width
-    factor = inverse * inverse * inverse * centre
+    half = rank // 2
     grad = dot_tn(low, dvalues)
-    half = rank // 2
     mine[:, side * block :] = grad[:half]
     give[:, side * block :] = grad[half:]
     enc_low = jnp.concatenate([low_near[...], low_far[...]])
@@ -250,9 +287,7 @@
     w_half = cut(value_weight, grp * half_kv, half_kv, 1)
     w_moved = lax.ppermute(w_half, ("dp", "mp"), swap)
 
-    own_hidden = cut(hidden, grp * mine_rows, mine_rows)
-    hid_next, hid_last = turned(own_hidden, "mp", 1), turned(own_hidden, "mp", -1)
-    hid = jnp.concatenate([own_hidden, hid_next, turned(hid_next, "mp", 1), hid_last])
+    hid = lax.all_gather(cut(hidden, grp * mine_rows, mine_rows), "mp", axis=0, tiled=True)
 
     own_length = seq_length[0]
     t_half = cut(targets[:area], grp * half_kv, half_kv, 1)
@@ -286,15 +321,15 @@
     destiny = dest_owner[:, 0]
     block_dest = cut(destiny, dp * ENC_DEV, ENC_DEV)
     local = jnp.arange(ENC_DEV, dtype=jnp.int32)
-    from_mp = (mp - (local % (ENC_DEV // 2)) // mine_rows) & wrap
+    from_mp = (local % (ENC_DEV // 2)) // mine_rows
     from_grp = (grp + local // (ENC_DEV // 2)) & 1
     place = from_mp * block_rows + from_grp * mine_rows + (local & (mine_rows - 1))
     own_dest = jnp.sum(jnp.where(place[:, None] == local[None, :], block_dest[None, :], 0), axis=1)
     earlier = (own_dest[:, None] == block_dest[None, :]) & (local[None, :] < place[:, None])
     slot = jnp.sum(earlier.astype(jnp.int32), axis=1)
     own_mp, own_col, own_slab = own_dest & wrap, (own_dest // side) & wrap, own_dest // (side * side)
-    line = (((mp - own_mp) & wrap) * side + ((col - own_col) & wrap)) * side
-    line = (line + ((slab - own_slab) & wrap)) * capacity + slot
+    line = (((col - own_col) & wrap) * side + ((slab - own_slab) & wrap)) * capacity + slot
+    line = jnp.where(own_mp == mp, line, -1)
     position = (slot * n_dp + dp).astype(f32)
 
     gain_wide = norm_gain.astype(f32)[None]
@@ -347,31 +382,41 @@
     enc_low = jnp.where(first, enc_low, jnp.roll(enc_low, half_rank, axis=1))
     enc_low_far = jnp.roll(crossed(enc_low), half_rank, axis=1)
     gain_part = cut(gain_wide, mp * part_width, part_width, 1)
-    where = col[None].astype(jnp.int32)
-    sizes = dict(block=block, half_kv=half_kv, rank=rank)
-    sent, kept = pl.pallas_call(
-        functools.partial(partial_kernel, chunk=chunk, **sizes),
-        out_shape=(
-            jax.ShapeDtypeStruct((ENC_DEV + area, half_kv + 128), bf16),
-            jax.ShapeDtypeStruct((ENC_DEV, half_kv + 128), f32),
-        ),
-        in_specs=[SMEM] + [VMEM] * 8,
-        out_specs=(VMEM, VMEM),
+    where = jnp.stack([col, mp]).astype(jnp.int32)
+    sizes = dict(half_kv=half_kv, rank=rank)
+    lanes = kv + 2 * rank
+    tokens = 2 * mine_rows
+    to_one = jax.ShapeDtypeStruct((tokens, lanes), bf16)
+    own, *to = pl.pallas_call(
+        functools.partial(partial_kernel, chunk=chunk, block=block, step=mine_rows, **sizes),
+        out_shape=(jax.ShapeDtypeStruct((tokens, lanes), f32), to_one, to_one, to_one),
+        in_specs=[SMEM] + [VMEM] * 10,
+        out_specs=(VMEM,) * 4,
+        scratch_shapes=[pltpu.VMEM((ENC_DEV, lanes), f32)],
         compiler_params=PARAMS,
         name="partial_products",
-    )(where, image, image_far, gain_part, a_part, *pieces)
-    got = [turned(sent, "mp", k) for k in range(1, n_mp)]
+    )(where, image, image_far, gain_part, a_part, *pieces, line[:, None], position[:, None])
+    got = [turned(to[k - 1], "mp", -k) for k in range(1, n_mp)]
+    packed = pl.pallas_call(
+        functools.partial(row_kernel, width=float(width), **sizes),
+        out_shape=jax.ShapeDtypeStruct((tokens, half_kv + 2 * rank), bf16),
+        in_specs=[VMEM] * 6,
+        out_specs=VMEM,
+        compiler_params=PARAMS,
+        name="row_work",
+    )(own, *got, b_half, bias_half)
+    got = [turned(packed, "mp", k) for k in range(1, n_mp)]
     mine, give = pl.pallas_call(
-        functools.partial(image_kernel, width=float(width), step=mine_rows, **sizes),
+        functools.partial(image_kernel, block=block, step=mine_rows, **sizes),
         out_shape=(jax.ShapeDtypeStruct((half_rank, part_width + half_kv), f32),) * 2,
-        in_specs=[SMEM] + [VMEM] * 19,
+        in_specs=[SMEM] + [VMEM] * 15,
         out_specs=(VMEM, VMEM),
+        scratch_shapes=[pltpu.VMEM((ENC_DEV, half_kv + 2 * rank), bf16)],
         compiler_params=PARAMS,
         name="image_gradients",
     )(
         where,
-        kept,
-        sent,
+        packed,
         *got,
         image,
         image_far,
@@ -381,9 +426,6 @@
         a_part,
         *pieces,
         b_half,
-        bias_half,
-        line[:, None],
-        position[:, None],
     )
 
     came = crossed(give)

time: 164 us -> 157 us (0.957)
  between operations: 2.08 us -> 15.7 us
  starting transfers between devices: 50.6 us -> 43.1 us
  waiting for transfers between devices: 25.2 us -> 20 us
  Pallas kernels: 9.12 us -> 6.7 us
  blocking collectives: 30.7 us -> 28.4 us
  matrix products: 16.2 us -> 14 us
    ppermute x9, waiting for transfers between devices: 19.3 us -> 11 us  [turned(): lax.ppermute(array, axis, [(i, (i + step) % count) for i in range(count)])]
    all_to_all x1, starting transfers between devices: 11.9 us -> 5.52 us  [body(): lax.all_to_all(text_parts.astype(bf16), ('dp', 'mp'), 0, 0, tiled=True)]
    pallas_call x2 -> x3, Pallas kernels: 9.12 us -> 6.7 us  [the longest x1 2.99 us: body(): pl.pallas_call(functools.partial(image_kernel, block=block, step=mine_row...]
    all_to_all x1, blocking collectives: 18.4 us -> 16.1 us  [body(): mine = jnp.sum(lax.all_to_all(mine, 'dp', 0, 0, tiled=True), axis=0)]
    dot_general x5, matrix products: 14.7 us -> 12.4 us  [dot(): return jnp.dot(a, b, preferred_element_type=f32)]
    all_to_all x1, starting transfers between devices: 10.5 us -> 8.4 us  [to_everyone(): lax.all_to_all(jnp.broadcast_to(array[None], (count, *array.shape)), axes...]
    unnamed x65 -> x81, local copies, waits for them, and re-layouts: 4.28 us -> 5.08 us
  transfers between devices with their start and end apart: 23 -> 24, of which waited for: 7 -> 7; matrix products, arithmetic and copies ran while one was open for 24% -> 22% of each run, Pallas kernels for 6% -> 4%
where the time goes in v6:
time: 157 us; the launch traced here: 156 us
  starting transfers between devices  43.1 us (27%)
  blocking collectives  28.4 us (18%)
  waiting for transfers between devices  20 us (13%)
  between operations  15.7 us (10%)
  local copies, waits for them, and re-layouts  14.2 us (9%)
  matrix products  14 us (9%)
  other arithmetic  13.7 us (9%)
  Pallas kernels  6.7 us (4%)
    all_to_all x1, blocking collectives, body(): mine = jnp.sum(lax.all_to_all(mine, 'dp', 0, 0, tiled=True), axis=0)  16.1 us
    ppermute x6, starting transfers between devices, along(): return lax.ppermute(array, 'dp', pairs)  15.3 us
    dot_general x5, matrix products, dot(): return jnp.dot(a, b, preferred_element_type=f32)  12.4 us
    all_to_all x1, blocking collectives, to_everyone(): lax.all_to_all(jnp.broadcast_to(array[None], (count, *array.shape)), axes...  12.3 us
    ppermute x9, starting transfers between devices, turned(): lax.ppermute(array, axis, [(i, (i + step) % count) for i in range(count)])  12.1 us
    ppermute x9, waiting for transfers between devices, turned(): lax.ppermute(array, axis, [(i, (i + step) % count) for i in range(count)])  11 us
    all_to_all x1, starting transfers between devices, to_everyone(): lax.all_to_all(jnp.broadcast_to(array[None], (count, *array.shape)), axes...  8.4 us
    all_to_all x1, waiting for transfers between devices, to_everyone(): lax.all_to_all(jnp.broadcast_to(array[None], (count, *array.shape)), axes...  7.15 us
  transfers between devices with their start and end apart: 24, of which 7 were waited for; matrix products, arithmetic and copies ran while one was open for 22% of the time, Pallas kernels for 4%

profile of v6, /device:TPU:0, one launch (start us, length us, event | category | flops | bytes accessed | tf_op | source)
XLA Modules:
  0.0 155.8 jit_solution(13816379125751619213)
XLA Ops:
  9.8 1.7 %fusion = f32[80]{0:T(128)S(1)} fusion(bf16[160,8192]{1,0:T(8,128)(2,1)} %param.19, s32[]{:T(128)S(6)} %mul.124), kind=kLoop, calls=%fused_computation.3 | loop fusion | flops 1966000 | bytes 1311044 | tf_op jit(solution)/shard_map/reduce_sum | solution.py:338
  18.2 4.4 %collective-permute-start.5 = (bf16[192,512]{1,0:T(8,128)(2,1)S(1)}, bf16[192,512]{1,0:T(8,128)(2,1)S(1)}, u32[]{:S(2)}, u32[]{:S(2)}) collective-permute-start(bf16[192,512]{1,0:T(8,128)(2,1)S(1)} %get-tuple-element.34), channel_id=1, source_target_pairs={{0,16},{4,20},{8,24},{12,28},{16,32},{20,36},{24,40},{28,44},{32,4... | collective-permute-start | bytes 589832 | tf_op jit(solution)/shard_map/ppermute | solution.py:53
  22.7 4.5 %collective-permute-start.4 = (bf16[192,512]{1,0:T(8,128)(2,1)S(1)}, bf16[192,512]{1,0:T(8,128)(2,1)S(1)}, u32[]{:S(2)}, u32[]{:S(2)}) collective-permute-start(bf16[192,512]{1,0:T(8,128)(2,1)S(1)} %get-tuple-element.35), channel_id=1, source_target_pairs={{0,32},{4,36},{8,40},{12,44},{16,48},{20,52},{24,56},{28,60},{32,0... | collective-permute-start | bytes 589832 | tf_op jit(solution)/shard_map/ppermute | solution.py:53
  29.9 8.4 %all-to-all-start = ((bf16[64,32,128]{2,1,0:T(8,128)(2,1)}), bf16[64,32,128]{2,1,0:T(8,128)(2,1)S(1)}, u32[]{:S(2)}, u32[]{:S(2)}) async-start(bf16[64,32,128]{2,1,0:T(8,128)(2,1)} %broadcast_in_dim.35), calls=%async_computation | async-start | bytes 1048576 | tf_op jit(solution)/shard_map/all_to_all | solution.py:58
  38.6 1.4 pad_maximum_fusion.4
  40.0 2.8 %collective-permute-start.8 = (bf16[576,512]{1,0:T(8,128)(2,1)}, bf16[576,512]{1,0:T(8,128)(2,1)S(1)}, u32[]{:S(2)}, u32[]{:S(2)}) collective-permute-start(bf16[576,512]{1,0:T(8,128)(2,1)} %get-tuple-element.18), channel_id=1, source_target_pairs={{0,12},{4,0},{8,4},{12,8},{16,28},{20,16},{24,20},{28,24},{32,44},... | collective-permute-start | bytes 1769480 | tf_op jit(solution)/shard_map/ppermute | solution.py:53
  42.8 2.3 %collective-permute-start.7 = (bf16[576,512]{1,0:T(8,128)(2,1)}, bf16[576,512]{1,0:T(8,128)(2,1)S(1)}, u32[]{:S(2)}, u32[]{:S(2)}) collective-permute-start(bf16[576,512]{1,0:T(8,128)(2,1)} %get-tuple-element.20), channel_id=1, source_target_pairs={{0,8},{4,12},{8,0},{12,4},{16,24},{20,28},{24,16},{28,20},{32,40},... | collective-permute-start | bytes 1769480 | tf_op jit(solution)/shard_map/ppermute | solution.py:53
  45.1 7.1 %all-to-all-done = bf16[64,32,128]{2,1,0:T(8,128)(2,1)S(1)} async-done(((bf16[64,32,128]{2,1,0:T(8,128)(2,1)}), bf16[64,32,128]{2,1,0:T(8,128)(2,1)S(1)}, u32[]{:S(2)}, u32[]{:S(2)}) %all-to-all-start) | async-done | bytes 524320 | tf_op jit(solution)/shard_map/all_to_all | solution.py:58
  52.5 1.9 %collective-permute-done.2 = bf16[32,8192]{1,0:T(8,128)(2,1)S(1)} collective-permute-done((bf16[32,8192]{1,0:T(8,128)(2,1)S(1)}, bf16[32,8192]{1,0:T(8,128)(2,1)S(1)}, u32[]{:S(2)}, u32[]{:S(2)}) %collective-permute-start.2) | collective-permute-done | bytes 524320 | tf_op jit(solution)/shard_map/ppermute | solution.py:44
  58.9 10.3 %convolution_add_fusion.1 = f32[128,2048]{1,0:T(8,128)S(1)} fusion(bf16[128,5120]{1,0:T(8,128)(2,1)} %all-gather.2.cloned.1.call-done, bf16[5120,2048]{1,0:T(8,128)(2,1)} %param.15, f32[2048]{0:T(1024)S(1)} %copy-done.28), kind=kOutput, calls=%fused_computation.7 | convolution fusion | flops 2684616704 | bytes 23339008 | tf_op jit(solution)/shard_map/dot_general | solution.py:17
  71.2 1.4 fusion.6
  74.5 5.5 %all-to-all-start.1 = ((bf16[64,32,128]{2,1,0:T(8,128)(2,1)}), bf16[64,32,128]{2,1,0:T(8,128)(2,1)}, u32[]{:S(2)}, u32[]{:S(2)}) async-start(bf16[64,32,128]{2,1,0:T(8,128)(2,1)} %bitcast_bitcast_fusion), calls=%async_computation.1 | async-start | bytes 1048576 | tf_op jit(solution)/shard_map/all_to_all | solution.py:369
  84.2 2.4 %partial_products.1 = (f32[64,1152]{1,0:T(8,128)S(1)}, bf16[64,1152]{1,0:T(8,128)(2,1)S(1)}, bf16[64,1152]{1,0:T(8,128)(2,1)S(1)}, bf16[64,1152]{1,0:T(8,128)(2,1)S(1)}) custom-call(s32[2]{0:T(128)S(1)} %pad_add_fusion.place, bf16[128,2048]{1,0:T(8,128)(2,1)S(1)} %fusion.3.near, bf16[128,2048]{1,0:T(8,128)(2,1)} %collective-permute-done.far, ...), custom_call_target="tpu_custom_call" | custom-call | tf_op jit(solution)/shard_map/partial_products/pallas_call | solution.py:390
  86.7 2.7 %collective-permute-start.9 = (bf16[64,1152]{1,0:T(8,128)(2,1)S(1)}, bf16[64,1152]{1,0:T(8,128)(2,1)S(1)}, u32[]{:S(2)}, u32[]{:S(2)}) collective-permute-start(bf16[64,1152]{1,0:T(8,128)(2,1)S(1)} %get-tuple-element.11), channel_id=1, source_target_pairs={{0,3},{1,0},{2,1},{3,2},{4,7},{5,4},{6,5},{7,6},{8,11},{9,8},{10,9... | collective-permute-start | bytes 442376 | tf_op jit(solution)/shard_map/ppermute | solution.py:40
  91.8 4.5 %collective-permute-done.9.got1 = bf16[64,1152]{1,0:T(8,128)(2,1)S(1)} collective-permute-done((bf16[64,1152]{1,0:T(8,128)(2,1)S(1)}, bf16[64,1152]{1,0:T(8,128)(2,1)S(1)}, u32[]{:S(2)}, u32[]{:S(2)}) %collective-permute-start.9) | collective-permute-done | bytes 147488 | tf_op jit(solution)/shard_map/ppermute | solution.py:40
  97.6 2.4 %collective-permute-done.11.got3 = bf16[64,1152]{1,0:T(8,128)(2,1)S(1)} collective-permute-done((bf16[64,1152]{1,0:T(8,128)(2,1)S(1)}, bf16[64,1152]{1,0:T(8,128)(2,1)S(1)}, u32[]{:S(2)}, u32[]{:S(2)}) %collective-permute-start.11) | collective-permute-done | bytes 147488 | tf_op jit(solution)/shard_map/ppermute | solution.py:40
  106.9 2.5 %collective-permute-start.20 = (f32[32,1024]{1,0:T(8,128)S(1)}, f32[32,1024]{1,0:T(8,128)S(1)}, u32[]{:S(2)}, u32[]{:S(2)}) collective-permute-start(f32[32,1024]{1,0:T(8,128)S(1)} %slice_add_fusion.1), channel_id=1, source_target_pairs={{0,3},{1,0},{2,1},{3,2},{4,7},{5,4},{6,5},{7,6},{8,11},{9,8},{10,9... | collective-permute-start | bytes 393224 | tf_op jit(solution)/shard_map/ppermute | solution.py:40
  109.4 1.5 collective-permute-start.19
  110.9 1.3 collective-permute-start.18
  112.4 3.0 %image_gradients.1 = (f32[32,2560]{1,0:T(8,128)S(1)}, f32[32,2560]{1,0:T(8,128)S(1)}) custom-call(s32[2]{0:T(128)S(1)} %pad_add_fusion.place, bf16[64,640]{1,0:T(8,128)(2,1)} %row_work.1.packed, bf16[64,640]{1,0:T(8,128)(2,1)} %collective-permute-done.12.got1, bf16[64,640]{1,0:T(8,128)(2,1)} %collective-permute-done.13.got2, ...), custom_call_target="tpu_custom_call" | custom-call | tf_op jit(solution)/shard_map/image_gradients/pallas_call | solution.py:409
  115.5 1.4 collective-permute-done.19
  116.9 1.4 collective-permute-done.18
  118.6 16.1 %all_to_all.20 = f32[16,2,3072]{2,1,0:T(2,128)S(1)} all-to-all(f32[16,2,3072]{2,1,0:T(2,128)S(1)} %reshape.276), channel_id=1, replica_groups=mesh['grp'=2,'dp'=16,'mp'=4] {'dp'}, dimensions={0} | all-to-all | bytes 786432 | tf_op jit(solution)/shard_map/all_to_all | solution.py:442
  135.0 12.3 %all_to_all.21 = f32[16,2,3072]{2,1,0:T(2,128)S(1)} all-to-all(f32[16,2,3072]{2,1,0:T(2,128)S(1)} %broadcast_in_dim.72), channel_id=1, replica_groups=mesh['grp'=2,'dp'=16,'mp'=4] {'dp'}, dimensions={0} | all-to-all | bytes 786432 | tf_op jit(solution)/shard_map/all_to_all | solution.py:58
  (184 shorter events, 36.8 us)
Async XLA Ops:
  7.2 51.7 %all-gather.2.cloned.1.call-start = ((), (), s32[]{:S(2)}) async-start(), calls=%async_computation.4 | async-start | bytes 1638400 | tf_op jit(solution)/shard_map/all_gather | solution.py:290
  8.2 9.9 %collective-permute-start.1 = (bf16[128,512]{1,0:T(8,128)(2,1)S(1)}, bf16[128,512]{1,0:T(8,128)(2,1)S(1)}, u32[]{:S(2)}, u32[]{:S(2)}) collective-permute-start(bf16[128,512]{1,0:T(8,128)(2,1)S(1)} %constant_dynamic-slice_fusion.10), channel_id=1, source_target_pairs={{0,0},{1,16},{2,32},{3,48},{4,4},{5,20},{6,36},{7,52},{8,8},{9,24}... | collective-permute-start | bytes 393224 | tf_op jit(solution)/shard_map/ppermute | solution.py:288
  18.2 20.1 %collective-permute-start.5 = (bf16[192,512]{1,0:T(8,128)(2,1)S(1)}, bf16[192,512]{1,0:T(8,128)(2,1)S(1)}, u32[]{:S(2)}, u32[]{:S(2)}) collective-permute-start(bf16[192,512]{1,0:T(8,128)(2,1)S(1)} %get-tuple-element.34), channel_id=1, source_target_pairs={{0,16},{4,20},{8,24},{12,28},{16,32},{20,36},{24,40},{28,44},{32,4... | collective-permute-start | bytes 589832 | tf_op jit(solution)/shard_map/ppermute | solution.py:53
  22.7 15.7 %collective-permute-start.4 = (bf16[192,512]{1,0:T(8,128)(2,1)S(1)}, bf16[192,512]{1,0:T(8,128)(2,1)S(1)}, u32[]{:S(2)}, u32[]{:S(2)}) collective-permute-start(bf16[192,512]{1,0:T(8,128)(2,1)S(1)} %get-tuple-element.35), channel_id=1, source_target_pairs={{0,32},{4,36},{8,40},{12,44},{16,48},{20,52},{24,56},{28,60},{32,0... | collective-permute-start | bytes 589832 | tf_op jit(solution)/shard_map/ppermute | solution.py:53
  27.2 11.2 %collective-permute-start.3 = (bf16[192,512]{1,0:T(8,128)(2,1)S(1)}, bf16[192,512]{1,0:T(8,128)(2,1)S(1)}, u32[]{:S(2)}, u32[]{:S(2)}) collective-permute-start(bf16[192,512]{1,0:T(8,128)(2,1)S(1)} %get-tuple-element.36), channel_id=1, source_target_pairs={{0,48},{4,52},{8,56},{12,60},{16,0},{20,4},{24,8},{28,12},{32,16},... | collective-permute-start | bytes 589832 | tf_op jit(solution)/shard_map/ppermute | solution.py:53
  29.9 22.4 %all-to-all-start = ((bf16[64,32,128]{2,1,0:T(8,128)(2,1)}), bf16[64,32,128]{2,1,0:T(8,128)(2,1)S(1)}, u32[]{:S(2)}, u32[]{:S(2)}) async-start(bf16[64,32,128]{2,1,0:T(8,128)(2,1)} %broadcast_in_dim.35), calls=%async_computation | async-start | bytes 1048576 | tf_op jit(solution)/shard_map/all_to_all | solution.py:58
  40.0 42.3 %collective-permute-start.8 = (bf16[576,512]{1,0:T(8,128)(2,1)}, bf16[576,512]{1,0:T(8,128)(2,1)S(1)}, u32[]{:S(2)}, u32[]{:S(2)}) collective-permute-start(bf16[576,512]{1,0:T(8,128)(2,1)} %get-tuple-element.18), channel_id=1, source_target_pairs={{0,12},{4,0},{8,4},{12,8},{16,28},{20,16},{24,20},{28,24},{32,44},... | collective-permute-start | bytes 1769480 | tf_op jit(solution)/shard_map/ppermute | solution.py:53
  42.8 39.5 %collective-permute-start.6 = (bf16[576,512]{1,0:T(8,128)(2,1)}, bf16[576,512]{1,0:T(8,128)(2,1)S(1)}, u32[]{:S(2)}, u32[]{:S(2)}) collective-permute-start(bf16[576,512]{1,0:T(8,128)(2,1)} %get-tuple-element.19), channel_id=1, source_target_pairs={{0,4},{4,8},{8,12},{12,0},{16,20},{20,24},{24,28},{28,16},{32,36},... | collective-permute-start | bytes 1769480 | tf_op jit(solution)/shard_map/ppermute | solution.py:53
  42.8 39.5 %collective-permute-start.7 = (bf16[576,512]{1,0:T(8,128)(2,1)}, bf16[576,512]{1,0:T(8,128)(2,1)S(1)}, u32[]{:S(2)}, u32[]{:S(2)}) collective-permute-start(bf16[576,512]{1,0:T(8,128)(2,1)} %get-tuple-element.20), channel_id=1, source_target_pairs={{0,8},{4,12},{8,0},{12,4},{16,24},{20,28},{24,16},{28,20},{32,40},... | collective-permute-start | bytes 1769480 | tf_op jit(solution)/shard_map/ppermute | solution.py:53
  52.4 2.0 %collective-permute-start.2 = (bf16[32,8192]{1,0:T(8,128)(2,1)S(1)}, bf16[32,8192]{1,0:T(8,128)(2,1)S(1)}, u32[]{:S(2)}, u32[]{:S(2)}) collective-permute-start(bf16[32,8192]{1,0:T(8,128)(2,1)S(1)} %copy_bitcast_fusion), channel_id=1, source_target_pairs={{0,64},{64,0},{1,65},{65,1},{2,66},{66,2},{3,67},{67,3},{4,68},{68... | collective-permute-start | bytes 1572872 | tf_op jit(solution)/shard_map/ppermute | solution.py:44
  58.7 12.4 %collective-permute-start.17 = (f32[32,9216]{1,0:T(8,128)}, f32[32,9216]{1,0:T(8,128)}, u32[]{:S(2)}, u32[]{:S(2)}) collective-permute-start(f32[32,9216]{1,0:T(8,128)} %pad_maximum_fusion), channel_id=1, source_target_pairs={{0,64},{64,0},{1,65},{65,1},{2,66},{66,2},{3,67},{67,3},{4,68},{68... | collective-permute-start | bytes 3538952 | tf_op jit(solution)/shard_map/ppermute | solution.py:44
  70.0 12.3 %collective-permute-start = (bf16[128,2048]{1,0:T(8,128)(2,1)S(1)}, bf16[128,2048]{1,0:T(8,128)(2,1)}, u32[]{:S(2)}, u32[]{:S(2)}) collective-permute-start(bf16[128,2048]{1,0:T(8,128)(2,1)S(1)} %fusion.3.near), channel_id=1, source_target_pairs={{0,64},{64,0},{1,65},{65,1},{2,66},{66,2},{3,67},{67,3},{4,68},{68... | collective-permute-start | bytes 1572872 | tf_op jit(solution)/shard_map/ppermute | solution.py:44
  74.5 29.0 %all-to-all-start.1 = ((bf16[64,32,128]{2,1,0:T(8,128)(2,1)}), bf16[64,32,128]{2,1,0:T(8,128)(2,1)}, u32[]{:S(2)}, u32[]{:S(2)}) async-start(bf16[64,32,128]{2,1,0:T(8,128)(2,1)} %bitcast_bitcast_fusion), calls=%async_computation.1 | async-start | bytes 1048576 | tf_op jit(solution)/shard_map/all_to_all | solution.py:369
  81.0 10.1 %collective-permute-start.15 = (bf16[128,64]{1,0:T(8,128)(2,1)S(1)}, bf16[128,64]{1,0:T(8,128)(2,1)S(1)}, u32[]{:S(2)}, u32[]{:S(2)}) collective-permute-start(bf16[128,64]{1,0:T(8,128)(2,1)S(1)} %maximum_select_fusion.1.low_near), channel_id=1, source_target_pairs={{0,64},{64,0},{1,65},{65,1},{2,66},{66,2},{3,67},{67,3},{4,68},{68... | collective-permute-start | bytes 49160 | tf_op jit(solution)/shard_map/ppermute | solution.py:44
  86.7 9.6 %collective-permute-start.9 = (bf16[64,1152]{1,0:T(8,128)(2,1)S(1)}, bf16[64,1152]{1,0:T(8,128)(2,1)S(1)}, u32[]{:S(2)}, u32[]{:S(2)}) collective-permute-start(bf16[64,1152]{1,0:T(8,128)(2,1)S(1)} %get-tuple-element.11), channel_id=1, source_target_pairs={{0,3},{1,0},{2,1},{3,2},{4,7},{5,4},{6,5},{7,6},{8,11},{9,8},{10,9... | collective-permute-start | bytes 442376 | tf_op jit(solution)/shard_map/ppermute | solution.py:40
  89.4 8.2 %collective-permute-start.10 = (bf16[64,1152]{1,0:T(8,128)(2,1)S(1)}, bf16[64,1152]{1,0:T(8,128)(2,1)S(1)}, u32[]{:S(2)}, u32[]{:S(2)}) collective-permute-start(bf16[64,1152]{1,0:T(8,128)(2,1)S(1)} %get-tuple-element.12), channel_id=1, source_target_pairs={{0,2},{1,3},{2,0},{3,1},{4,6},{5,7},{6,4},{7,5},{8,10},{9,11},{10,... | collective-permute-start | bytes 442376 | tf_op jit(solution)/shard_map/ppermute | solution.py:40
  90.2 9.8 %collective-permute-start.11 = (bf16[64,1152]{1,0:T(8,128)(2,1)S(1)}, bf16[64,1152]{1,0:T(8,128)(2,1)S(1)}, u32[]{:S(2)}, u32[]{:S(2)}) collective-permute-start(bf16[64,1152]{1,0:T(8,128)(2,1)S(1)} %get-tuple-element.13), channel_id=1, source_target_pairs={{0,1},{1,2},{2,3},{3,0},{4,5},{5,6},{6,7},{7,4},{8,9},{9,10},{10,1... | collective-permute-start | bytes 442376 | tf_op jit(solution)/shard_map/ppermute | solution.py:40
  101.3 9.6 %collective-permute-start.14 = (bf16[64,640]{1,0:T(8,128)(2,1)}, bf16[64,640]{1,0:T(8,128)(2,1)}, u32[]{:S(2)}, u32[]{:S(2)}) collective-permute-start(bf16[64,640]{1,0:T(8,128)(2,1)} %row_work.1.packed), channel_id=1, source_target_pairs={{0,3},{1,0},{2,1},{3,2},{4,7},{5,4},{6,5},{7,6},{8,11},{9,8},{10,9... | collective-permute-start | bytes 245768 | tf_op jit(solution)/shard_map/ppermute | solution.py:40
  101.9 10.5 %collective-permute-start.13 = (bf16[64,640]{1,0:T(8,128)(2,1)}, bf16[64,640]{1,0:T(8,128)(2,1)}, u32[]{:S(2)}, u32[]{:S(2)}) collective-permute-start(bf16[64,640]{1,0:T(8,128)(2,1)} %row_work.1.packed), channel_id=1, source_target_pairs={{0,2},{1,3},{2,0},{3,1},{4,6},{5,7},{6,4},{7,5},{8,10},{9,11},{10,... | collective-permute-start | bytes 245768 | tf_op jit(solution)/shard_map/ppermute | solution.py:40
  102.7 9.6 %collective-permute-start.12 = (bf16[64,640]{1,0:T(8,128)(2,1)}, bf16[64,640]{1,0:T(8,128)(2,1)}, u32[]{:S(2)}, u32[]{:S(2)}) collective-permute-start(bf16[64,640]{1,0:T(8,128)(2,1)} %row_work.1.packed), channel_id=1, source_target_pairs={{0,1},{1,2},{2,3},{3,0},{4,5},{5,6},{6,7},{7,4},{8,9},{9,10},{10,1... | collective-permute-start | bytes 245768 | tf_op jit(solution)/shard_map/ppermute | solution.py:40
  106.9 8.6 %collective-permute-start.20 = (f32[32,1024]{1,0:T(8,128)S(1)}, f32[32,1024]{1,0:T(8,128)S(1)}, u32[]{:S(2)}, u32[]{:S(2)}) collective-permute-start(f32[32,1024]{1,0:T(8,128)S(1)} %slice_add_fusion.1), channel_id=1, source_target_pairs={{0,3},{1,0},{2,1},{3,2},{4,7},{5,4},{6,5},{7,6},{8,11},{9,8},{10,9... | collective-permute-start | bytes 393224 | tf_op jit(solution)/shard_map/ppermute | solution.py:40
  109.4 7.5 %collective-permute-start.19 = (f32[32,1024]{1,0:T(8,128)S(1)}, f32[32,1024]{1,0:T(8,128)S(1)}, u32[]{:S(2)}, u32[]{:S(2)}) collective-permute-start(f32[32,1024]{1,0:T(8,128)S(1)} %slice_add_fusion.1), channel_id=1, source_target_pairs={{0,2},{1,3},{2,0},{3,1},{4,6},{5,7},{6,4},{7,5},{8,10},{9,11},{10,... | collective-permute-start | bytes 393224 | tf_op jit(solution)/shard_map/ppermute | solution.py:40
  110.9 7.3 %collective-permute-start.18 = (f32[32,1024]{1,0:T(8,128)S(1)}, f32[32,1024]{1,0:T(8,128)S(1)}, u32[]{:S(2)}, u32[]{:S(2)}) collective-permute-start(f32[32,1024]{1,0:T(8,128)S(1)} %slice_add_fusion.1), channel_id=1, source_target_pairs={{0,1},{1,2},{2,3},{3,0},{4,5},{5,6},{6,7},{7,4},{8,9},{9,10},{10,1... | collective-permute-start | bytes 393224 | tf_op jit(solution)/shard_map/ppermute | solution.py:40
  115.4 2.9 %collective-permute-start.16 = (f32[32,2560]{1,0:T(8,128)S(1)}, f32[32,2560]{1,0:T(8,128)S(1)}, u32[]{:S(2)}, u32[]{:S(2)}) collective-permute-start(f32[32,2560]{1,0:T(8,128)S(1)} %get-tuple-element.15), channel_id=1, source_target_pairs={{0,64},{64,0},{1,65},{65,1},{2,66},{66,2},{3,67},{67,3},{4,68},{68... | collective-permute-start | bytes 983048 | tf_op jit(solution)/shard_map/ppermute | solution.py:44
  (37 other events, 162.4 us)
Sparse Core Ops, SparseCore 0:
  9.8 30.1 all-gather.1

commit v7 on v6

--- a/solution.py
+++ b/solution.py
@@ -140,9 +140,8 @@
         sums[out, half_kv + 2 * rank :] = dot(pick, table)
     lane = lax.broadcasted_iota(jnp.int32, (step, 2 * rank), 1)
     for k, target in enumerate((own, to1, to2, to3)):
-        there = (place[1] + side - k) & (side - 1)
         for h in range(2):
-            start = pl.multiple_of(h * rows + there * step, step)
+            start = h * rows + k * step
             target[h * step : (h + 1) * step, :] = sums[pl.ds(start, step), :].astype(target.dtype)
             if k == 0:
                 extra = sums[pl.ds(start, step), half_kv : half_kv + 2 * rank]
@@ -212,9 +211,8 @@
     side = len(pieces)
     count = near.shape[0]
     for k, source in enumerate((packed, got1, got2, got3)):
-        there = (place[1] + side - k) & (side - 1)
         for h in range(2):
-            start = pl.multiple_of(h * count + there * step, step)
+            start = h * count + k * step
             rows[pl.ds(start, step), :] = source[h * step : (h + 1) * step, :]
     dvalues = rows[:, :half_kv]
     extra = rows[:, half_kv:]
@@ -287,8 +285,6 @@
     w_half = cut(value_weight, grp * half_kv, half_kv, 1)
     w_moved = lax.ppermute(w_half, ("dp", "mp"), swap)
 
-    hid = lax.all_gather(cut(hidden, grp * mine_rows, mine_rows), "mp", axis=0, tiled=True)
-
     own_length = seq_length[0]
     t_half = cut(targets[:area], grp * half_kv, half_kv, 1)
     t_half = t_half.reshape(capacity, n_dp, half_kv).transpose(1, 0, 2)
@@ -300,6 +296,7 @@
         came = along(jnp.concatenate([w_moved, t_given]), k, 0, side)
         w_line.append(came[:shard])
         t_line.append(came[shard:])
+    dest_owner, text_rows, hidden, _ = lax.optimization_barrier((dest_owner, text_rows, hidden, came))
     w_line = w_line[::-1]
     w_line = cut(jnp.concatenate(w_line + w_line), ((2 * side - 1 - slab) & wrap) * shard, block)
     t_line = jnp.stack(t_line).reshape(side, side, chunk, half_kv)
@@ -309,7 +306,15 @@
         piece = jnp.concatenate([w_line, t_given])
         pieces.append(along(piece, 0, k, side) if k else piece)
 
-    a_half, _ = lax.optimization_barrier((cut(llm_frozen.T, grp * half_rank, half_rank), w_moved))
+    own_hidden = cut(hidden, grp * mine_rows, mine_rows)
+    hid_next, hid_last = turned(own_hidden, "mp", 1), turned(own_hidden, "mp", -1)
+    hid = jnp.concatenate([own_hidden, hid_next, turned(hid_next, "mp", 1), hid_last])
+
+    text_count = text_rows.shape[0] // 2
+    text_wide = cut(text_rows, grp * text_count, text_count).astype(f32)
+    text_inverse = lax.rsqrt(jnp.mean(text_wide * text_wide, axis=1, keepdims=True) + epsilon)
+
+    a_half = cut(llm_frozen.T, grp * half_rank, half_rank)
     a_mine = to_everyone(a_half, ("dp", "mp")).transpose(1, 0, 2).reshape(half_rank, width)
     a_all = jnp.concatenate([a_mine, crossed(a_mine)])
     a_part = cut(a_all, mp * part_width, part_width, 1)
@@ -321,7 +326,7 @@
     destiny = dest_owner[:, 0]
     block_dest = cut(destiny, dp * ENC_DEV, ENC_DEV)
     local = jnp.arange(ENC_DEV, dtype=jnp.int32)
-    from_mp = (local % (ENC_DEV // 2)) // mine_rows
+    from_mp = (mp - (local % (ENC_DEV // 2)) // mine_rows) & wrap
     from_grp = (grp + local // (ENC_DEV // 2)) & 1
     place = from_mp * block_rows + from_grp * mine_rows + (local & (mine_rows - 1))
     own_dest = jnp.sum(jnp.where(place[:, None] == local[None, :], block_dest[None, :], 0), axis=1)
@@ -332,12 +337,13 @@
     line = jnp.where(own_mp == mp, line, -1)
     position = (slot * n_dp + dp).astype(f32)
 
+    enc_low = dot(hid, enc_frozen).astype(bf16)
+    merged = dot(hid, enc_weight) + enc_bias.astype(f32) + dot(enc_low, enc_adapter)
+    image = merged.astype(bf16)
     gain_wide = norm_gain.astype(f32)[None]
-    text_count = text_rows.shape[0] // 2
-    text_wide = cut(text_rows, grp * text_count, text_count).astype(f32)
-    text_inverse = lax.rsqrt(jnp.mean(text_wide * text_wide, axis=1, keepdims=True) + epsilon)
     text_normed = (text_wide * text_inverse * gain_wide).astype(bf16)
-    text_low = dot_nt(text_normed, a_all).astype(bf16)
+    a_text = a_all
+    text_low = dot_nt(text_normed, a_text).astype(bf16)
     owner_index = dp * n_mp + mp
     counts = jnp.sum((destiny.reshape(n_dp, ENC_DEV) == owner_index).astype(jnp.int32), axis=1)
     row = grp * text_count + jnp.arange(text_count, dtype=jnp.int32)
@@ -365,24 +371,11 @@
     rest_sum = rest_sum * text_weight
     both_sums = jnp.concatenate([text_sum, rest_sum], axis=1)
     both_sums = both_sums[:half_rank] + crossed(both_sums[half_rank:])
-    text_parts = both_sums[:, :width].reshape(half_rank, owners, shard).transpose(1, 0, 2)
-    text_parts = lax.all_to_all(text_parts.astype(bf16), ("dp", "mp"), 0, 0, tiled=True)
-    text_here = jnp.sum(text_parts.astype(f32), axis=0)
-    here_high, here_low = split_two(text_here)
-    text_grad = dot(jnp.concatenate([here_high, here_low]), value_weight)
-    text_grad = text_grad[:half_rank] + text_grad[half_rank:] + both_sums[:, width:]
-    text_grad = text_grad + (
-        turned(text_grad, "mp", 1) + turned(text_grad, "mp", 2) + turned(text_grad, "mp", 3)
-    )
-
-    enc_low = dot(hid, enc_frozen).astype(bf16)
-    merged = dot(hid, enc_weight) + enc_bias.astype(f32) + dot(enc_low, enc_adapter)
-    image = merged.astype(bf16)
     image_far = crossed(image)
     enc_low = jnp.where(first, enc_low, jnp.roll(enc_low, half_rank, axis=1))
     enc_low_far = jnp.roll(crossed(enc_low), half_rank, axis=1)
     gain_part = cut(gain_wide, mp * part_width, part_width, 1)
-    where = jnp.stack([col, mp]).astype(jnp.int32)
+    where = col[None].astype(jnp.int32)
     sizes = dict(half_kv=half_kv, rank=rank)
     lanes = kv + 2 * rank
     tokens = 2 * mine_rows
@@ -405,7 +398,10 @@
         compiler_params=PARAMS,
         name="row_work",
     )(own, *got, b_half, bias_half)
+    text_parts = both_sums[:, :width].reshape(half_rank, owners, shard).transpose(1, 0, 2)
+    text_parts = lax.all_to_all(text_parts.astype(bf16), ("dp", "mp"), 0, 0, tiled=True)
     got = [turned(packed, "mp", k) for k in range(1, n_mp)]
+    enc_low_far, text_parts = lax.optimization_barrier((enc_low_far, text_parts))
     mine, give = pl.pallas_call(
         functools.partial(image_kernel, block=block, step=mine_rows, **sizes),
         out_shape=(jax.ShapeDtypeStruct((half_rank, part_width + half_kv), f32),) * 2,
@@ -428,20 +424,28 @@
         b_half,
     )
 
+    text_here = jnp.sum(text_parts.astype(f32), axis=0)
+    here_high, here_low = split_two(text_here)
+    text_grad = dot(jnp.concatenate([here_high, here_low]), value_weight)
+    text_grad = text_grad[:half_rank] + text_grad[half_rank:] + both_sums[:, width:]
+    text_grad = text_grad + (
+        turned(text_grad, "mp", 1) + turned(text_grad, "mp", 2) + turned(text_grad, "mp", 3)
+    )
+
     came = crossed(give)
     llm_mine, llm_came = mine[:, part_width:], came[:, part_width:]
-    mine = jnp.concatenate(
-        [
-            mine[:, :part_width] + came[:, :part_width],
-            jnp.where(first, llm_mine, llm_came) + text_grad[:, :half_kv],
-            jnp.where(first, llm_came, llm_mine) + text_grad[:, half_kv:],
-        ],
-        axis=1,
-    )
-    mine = mine.reshape(n_dp, half_rank // n_dp, -1)
+    enc = (mine[:, :part_width] + came[:, :part_width]).reshape(side, 8, side, -1)
+    llm = (
+        jnp.concatenate(
+            [jnp.where(first, llm_mine, llm_came), jnp.where(first, llm_came, llm_mine)], axis=1
+        )
+        + text_grad
+    ).reshape(side, 8, side, -1)
+    mine = jnp.concatenate([enc, llm], axis=3).transpose(0, 2, 1, 3).reshape(n_dp, 8, -1)
     mine = jnp.sum(lax.all_to_all(mine, "dp", 0, 0, tiled=True), axis=0)
-    whole = to_everyone(mine, "dp").reshape(half_rank, -1)
-    return whole[:, :part_width], whole[:, part_width:]
+    whole = to_everyone(mine, "dp").reshape(side, side, 8, -1).transpose(0, 2, 1, 3)
+    at = part_width // side
+    return whole[..., :at].reshape(half_rank, -1), whole[..., at:].reshape(half_rank, -1)
 
 
 def solution(mesh):

time: 157 us -> 158 us (level)
  between operations: 15.7 us -> 2.1 us
  waiting for transfers between devices: 20 us -> 33.4 us
  starting transfers between devices: 43.1 us -> 47.3 us
  other arithmetic: 13.7 us -> 10.5 us
    ppermute x9 -> x12, waiting for transfers between devices: 11 us -> 27.1 us  [turned(): lax.ppermute(array, axis, [(i, (i + step) % count) for i in range(count)])]
    all_to_all x1, waiting for transfers between devices: 7.15 us -> 0.01 us  [to_everyone(): lax.all_to_all(jnp.broadcast_to(array[None], (count, *array.shape)), axes...]
    ppermute x6, starting transfers between devices: 15.3 us -> 8.66 us  [along(): return lax.ppermute(array, 'dp', pairs)]
    ppermute x6, waiting for transfers between devices: 0.02 us -> 6.32 us  [along(): return lax.ppermute(array, 'dp', pairs)]
    all_to_all x1, starting transfers between devices: 8.4 us -> 14.5 us  [to_everyone(): lax.all_to_all(jnp.broadcast_to(array[None], (count, *array.shape)), axes...]
    ppermute x9 -> x12, starting transfers between devices: 12.1 us -> 15.3 us  [turned(): lax.ppermute(array, axis, [(i, (i + step) % count) for i in range(count)])]
    ppermute x5, waiting for transfers between devices: 1.86 us -> 0.01 us  [crossed(): return lax.ppermute(array, 'grp', [(0, 1), (1, 0)])]
    all_to_all x1, starting transfers between devices: 5.52 us -> 7.33 us  [body(): lax.all_to_all(text_parts.astype(bf16), ('dp', 'mp'), 0, 0, tiled=True)]
  transfers between devices with their start and end apart: 24 -> 26, of which waited for: 7 -> 9; matrix products, arithmetic and copies ran while one was open for 22% -> 21% of each run, Pallas kernels for 4% -> 2%
where the time goes in v7:
time: 158 us; the launch traced here: 157 us
  starting transfers between devices  47.3 us (30%)
  waiting for transfers between devices  33.4 us (21%)
  blocking collectives  28.9 us (18%)
  matrix products  14.9 us (9%)
  local copies, waits for them, and re-layouts  13.6 us (9%)
  other arithmetic  10.5 us (7%)
  Pallas kernels  6.22 us (4%)
  between operations  2.1 us (1%)
    ppermute x12, waiting for transfers between devices, turned(): lax.ppermute(array, axis, [(i, (i + step) % count) for i in range(count)])  27.1 us
    all_to_all x1, blocking collectives, body(): mine = jnp.sum(lax.all_to_all(mine, 'dp', 0, 0, tiled=True), axis=0)  16.6 us
    ppermute x12, starting transfers between devices, turned(): lax.ppermute(array, axis, [(i, (i + step) % count) for i in range(count)])  15.3 us
    all_to_all x1, starting transfers between devices, to_everyone(): lax.all_to_all(jnp.broadcast_to(array[None], (count, *array.shape)), axes...  14.5 us
    dot_general x5, matrix products, dot(): return jnp.dot(a, b, preferred_element_type=f32)  13.4 us
    all_to_all x1, blocking collectives, to_everyone(): lax.all_to_all(jnp.broadcast_to(array[None], (count, *array.shape)), axes...  12.3 us
    ppermute x6, starting transfers between devices, along(): return lax.ppermute(array, 'dp', pairs)  8.66 us
    all_to_all x1, starting transfers between devices, body(): lax.all_to_all(text_parts.astype(bf16), ('dp', 'mp'), 0, 0, tiled=True)  7.33 us
  transfers between devices with their start and end apart: 26, of which 9 were waited for; matrix products, arithmetic and copies ran while one was open for 21% of the time, Pallas kernels for 2%

profile of v7, /device:TPU:0, one launch (start us, length us, event | category | flops | bytes accessed | tf_op | source)
XLA Modules:
  0.0 156.9 jit_solution(13188263511865020326)
XLA Ops:
  4.0 14.5 %all-to-all-start = ((bf16[64,32,128]{2,1,0:T(8,128)(2,1)}), bf16[64,32,128]{2,1,0:T(8,128)(2,1)}, u32[]{:S(2)}, u32[]{:S(2)}) async-start(bf16[64,32,128]{2,1,0:T(8,128)(2,1)} %broadcast_in_dim.41), calls=%async_computation | async-start | bytes 1048576 | tf_op jit(solution)/shard_map/all_to_all | solution.py:58
  20.8 3.0 %collective-permute-start.1 = (bf16[192,512]{1,0:T(8,128)(2,1)S(1)}, bf16[192,512]{1,0:T(8,128)(2,1)S(1)}, u32[]{:S(2)}, u32[]{:S(2)}) collective-permute-start(bf16[192,512]{1,0:T(8,128)(2,1)S(1)} %get-tuple-element.46), channel_id=1, source_target_pairs={{0,48},{4,52},{8,56},{12,60},{16,0},{20,4},{24,8},{28,12},{32,16},... | collective-permute-start | bytes 589832 | tf_op jit(solution)/shard_map/ppermute | solution.py:53
  25.5 6.3 %collective-permute-done.1 = bf16[192,512]{1,0:T(8,128)(2,1)S(1)} collective-permute-done((bf16[192,512]{1,0:T(8,128)(2,1)S(1)}, bf16[192,512]{1,0:T(8,128)(2,1)S(1)}, u32[]{:S(2)}, u32[]{:S(2)}) %collective-permute-start.1) | collective-permute-done | bytes 196640 | tf_op jit(solution)/shard_map/ppermute | solution.py:53
  33.1 2.7 %collective-permute-start.4 = (bf16[32,5120]{1,0:T(8,128)(2,1)}, bf16[32,5120]{1,0:T(8,128)(2,1)}, u32[]{:S(2)}, u32[]{:S(2)}) collective-permute-start(bf16[32,5120]{1,0:T(8,128)(2,1)} %constant_dynamic-slice_fusion.9), channel_id=1, source_target_pairs={{0,3},{1,0},{2,1},{3,2},{4,7},{5,4},{6,5},{7,6},{8,11},{9,8},{10,9... | collective-permute-start | bytes 983048 | tf_op jit(solution)/shard_map/ppermute | solution.py:40
  36.0 1.7 %fusion = f32[80]{0:T(128)S(1)} fusion(bf16[160,8192]{1,0:T(8,128)(2,1)} %param.19, s32[]{:T(128)S(6)} %mul.124), kind=kLoop, calls=%fused_computation.3 | loop fusion | flops 1966000 | bytes 1311044 | tf_op jit(solution)/shard_map/reduce_sum | solution.py:315
  40.0 2.0 %collective-permute-start.10 = (bf16[576,512]{1,0:T(8,128)(2,1)}, bf16[576,512]{1,0:T(8,128)(2,1)S(1)}, u32[]{:S(2)}, u32[]{:S(2)}) collective-permute-start(bf16[576,512]{1,0:T(8,128)(2,1)} %get-tuple-element.28), channel_id=1, source_target_pairs={{0,8},{4,12},{8,0},{12,4},{16,24},{20,28},{24,16},{28,20},{32,40},... | collective-permute-start | bytes 1769480 | tf_op jit(solution)/shard_map/ppermute | solution.py:53
  46.0 1.8 %add_convert_fusion = (f32[256,1]{1,0:T(8,128)S(1)}, s32[256,1]{1,0:T(8,128)}) fusion(s32[256,1]{1,0:T(8,128)S(1)} %copy.87, s32[]{:T(128)S(6)} %axis_index.33, s32[]{:T(128)S(6)} %select_n.111, s32[256,1]{1,0:T(8,128)} %copy.77, s32[]{:T(128)} %and.209, s32[]{:T(128)S(6)} %axis_index.38), kind=kLoop, calls=%fused_computation.69 | loop fusion | flops 10240 | bytes 4112 | tf_op jit(solution)/shard_map/convert_element_type | solution.py:338
  50.2 8.3 %collective-permute-done.3 = bf16[32,5120]{1,0:T(8,128)(2,1)S(1)} collective-permute-done((bf16[32,5120]{1,0:T(8,128)(2,1)}, bf16[32,5120]{1,0:T(8,128)(2,1)S(1)}, u32[]{:S(2)}, u32[]{:S(2)}) %collective-permute-start.3) | collective-permute-done | bytes 327712 | tf_op jit(solution)/shard_map/ppermute | solution.py:40
  58.5 1.7 %convolution_convert_fusion = bf16[128,64]{1,0:T(8,128)(2,1)S(1)} fusion(bf16[5120,64]{0,1:T(8,128)(2,1)S(1)} %copy-done.16, bf16[32,5120]{1,0:T(8,128)(2,1)} %collective-permute-done.4, bf16[32,5120]{1,0:T(8,128)(2,1)S(1)} %collective-permute-done.3, bf16[32,5120]{1,0:T(8,128)(2,1)} %collective-permute-done.2, ...), kind=kOutput, calls=%fused_computation.18 | convolution fusion | flops 89137152 | bytes 1982464 | tf_op jit(solution)/shard_map/dot_general | solution.py:17
  64.2 11.0 %fusion.4.near = bf16[128,2048]{1,0:T(8,128)(2,1)} fusion(f32[128,2048]{1,0:T(8,128)S(1)} %fusion.53, bf16[5120,2048]{1,0:T(8,128)(2,1)} %param.15, f32[2048]{0:T(1024)S(1)} %copy-done.13, bf16[32,5120]{1,0:T(8,128)(2,1)} %collective-permute-done.4, bf16[32,5120]{1,0:T(8,128)(2,1)S(1)} %collective-permute-done.3, ...), kind=kOutput, calls=%fused_computation.8 | convolution fusion | flops 2690383872 | bytes 23863296 | tf_op jit(solution)/shard_map/dot_general | solution.py:17
  77.7 7.3 %all-to-all-start.1 = ((bf16[64,32,128]{2,1,0:T(8,128)(2,1)}), bf16[64,32,128]{2,1,0:T(8,128)(2,1)}, u32[]{:S(2)}, u32[]{:S(2)}) async-start(bf16[64,32,128]{2,1,0:T(8,128)(2,1)} %bitcast_bitcast_fusion), calls=%async_computation.1 | async-start | bytes 1048576 | tf_op jit(solution)/shard_map/all_to_all | solution.py:402
  87.0 2.5 %partial_products.1 = (f32[64,1152]{1,0:T(8,128)S(1)}, bf16[64,1152]{1,0:T(8,128)(2,1)S(1)}, bf16[64,1152]{1,0:T(8,128)(2,1)S(1)}, bf16[64,1152]{1,0:T(8,128)(2,1)S(1)}) custom-call(s32[1]{0:T(128)} %bitcast.place, bf16[128,2048]{1,0:T(8,128)(2,1)} %fusion.4.near, bf16[128,2048]{1,0:T(8,128)(2,1)} %collective-permute-done.5.far, f32[1,2048]{1,0:T(1,128)S(1)} %bitcast.72, ...), custom_call_target="tpu_custom_call" | custom-call | tf_op jit(solution)/shard_map/partial_products/pallas_call | solution.py:383
  89.4 2.8 %collective-permute-start.12 = (bf16[64,1152]{1,0:T(8,128)(2,1)S(1)}, bf16[64,1152]{1,0:T(8,128)(2,1)S(1)}, u32[]{:S(2)}, u32[]{:S(2)}) collective-permute-start(bf16[64,1152]{1,0:T(8,128)(2,1)S(1)} %get-tuple-element.16), channel_id=1, source_target_pairs={{0,3},{1,0},{2,1},{3,2},{4,7},{5,4},{6,5},{7,6},{8,11},{9,8},{10,9... | collective-permute-start | bytes 442376 | tf_op jit(solution)/shard_map/ppermute | solution.py:40
  94.0 2.8 %collective-permute-done.12.got1 = bf16[64,1152]{1,0:T(8,128)(2,1)S(1)} collective-permute-done((bf16[64,1152]{1,0:T(8,128)(2,1)S(1)}, bf16[64,1152]{1,0:T(8,128)(2,1)S(1)}, u32[]{:S(2)}, u32[]{:S(2)}) %collective-permute-start.12) | collective-permute-done | bytes 147488 | tf_op jit(solution)/shard_map/ppermute | solution.py:40
  96.8 3.7 %collective-permute-done.13.got2 = bf16[64,1152]{1,0:T(8,128)(2,1)S(1)} collective-permute-done((bf16[64,1152]{1,0:T(8,128)(2,1)S(1)}, bf16[64,1152]{1,0:T(8,128)(2,1)S(1)}, u32[]{:S(2)}, u32[]{:S(2)}) %collective-permute-start.13) | collective-permute-done | bytes 147488 | tf_op jit(solution)/shard_map/ppermute | solution.py:40
  100.5 1.5 collective-permute-done.14.got3
  102.7 2.1 %collective-permute-start.16 = (bf16[64,640]{1,0:T(8,128)(2,1)S(1)}, bf16[64,640]{1,0:T(8,128)(2,1)}, u32[]{:S(2)}, u32[]{:S(2)}) collective-permute-start(bf16[64,640]{1,0:T(8,128)(2,1)S(1)} %row_work.1.packed), channel_id=1, source_target_pairs={{0,2},{1,3},{2,0},{3,1},{4,6},{5,7},{6,4},{7,5},{8,10},{9,11},{10,... | collective-permute-start | bytes 245768 | tf_op jit(solution)/shard_map/ppermute | solution.py:40
  106.3 3.6 %collective-permute-done.15.got1 = bf16[64,640]{1,0:T(8,128)(2,1)} collective-permute-done((bf16[64,640]{1,0:T(8,128)(2,1)S(1)}, bf16[64,640]{1,0:T(8,128)(2,1)}, u32[]{:S(2)}, u32[]{:S(2)}) %collective-permute-start.15) | collective-permute-done | bytes 81952 | tf_op jit(solution)/shard_map/ppermute | solution.py:40
  110.5 3.1 %image_gradients.1 = (f32[32,2560]{1,0:T(8,128)S(1)}, f32[32,2560]{1,0:T(8,128)S(1)}) custom-call(s32[1]{0:T(128)} %bitcast.place, bf16[64,640]{1,0:T(8,128)(2,1)S(1)} %row_work.1.packed, bf16[64,640]{1,0:T(8,128)(2,1)} %collective-permute-done.15.got1, bf16[64,640]{1,0:T(8,128)(2,1)} %collective-permute-done.16.got2, ...), custom_call_target="tpu_custom_call" | custom-call | tf_op jit(solution)/shard_map/image_gradients/pallas_call | solution.py:405
  116.9 3.0 %collective-permute-start.22 = (f32[32,1024]{1,0:T(8,128)S(1)}, f32[32,1024]{1,0:T(8,128)S(1)}, u32[]{:S(2)}, u32[]{:S(2)}) collective-permute-start(f32[32,1024]{1,0:T(8,128)S(1)} %slice_add_fusion.1), channel_id=1, source_target_pairs={{0,2},{1,3},{2,0},{3,1},{4,6},{5,7},{6,4},{7,5},{8,10},{9,11},{10,... | collective-permute-start | bytes 393224 | tf_op jit(solution)/shard_map/ppermute | solution.py:40
  119.9 3.2 %collective-permute-done.21 = f32[32,1024]{1,0:T(8,128)S(1)} collective-permute-done((f32[32,1024]{1,0:T(8,128)S(1)}, f32[32,1024]{1,0:T(8,128)S(1)}, u32[]{:S(2)}, u32[]{:S(2)}) %collective-permute-start.21) | collective-permute-done | bytes 131104 | tf_op jit(solution)/shard_map/ppermute | solution.py:40
  123.1 3.4 %collective-permute-done.22 = f32[32,1024]{1,0:T(8,128)S(1)} collective-permute-done((f32[32,1024]{1,0:T(8,128)S(1)}, f32[32,1024]{1,0:T(8,128)S(1)}, u32[]{:S(2)}, u32[]{:S(2)}) %collective-permute-start.22) | collective-permute-done | bytes 131104 | tf_op jit(solution)/shard_map/ppermute | solution.py:40
  126.6 16.6 %all_to_all.20 = f32[16,8,768]{2,1,0:T(8,128)S(1)} all-to-all(f32[16,8,768]{2,1,0:T(8,128)S(1)} %bitcast.75), channel_id=1, replica_groups=mesh['grp'=2,'dp'=16,'mp'=4] {'dp'}, dimensions={0} | all-to-all | bytes 786432 | tf_op jit(solution)/shard_map/all_to_all | solution.py:445
  143.2 12.3 %all_to_all.21 = f32[16,8,768]{2,1,0:T(8,128)S(1)} all-to-all(f32[16,8,768]{2,1,0:T(8,128)S(1)} %broadcast_in_dim.76), channel_id=1, replica_groups=mesh['grp'=2,'dp'=16,'mp'=4] {'dp'}, dimensions={0} | all-to-all | bytes 786432 | tf_op jit(solution)/shard_map/all_to_all | solution.py:58
  (148 shorter events, 34.1 us)
Async XLA Ops:
  1.7 19.1 %collective-permute-start = (bf16[128,512]{1,0:T(8,128)(2,1)S(1)}, bf16[128,512]{1,0:T(8,128)(2,1)S(1)}, u32[]{:S(2)}, u32[]{:S(2)}) collective-permute-start(bf16[128,512]{1,0:T(8,128)(2,1)S(1)} %constant_dynamic-slice_fusion.11), channel_id=1, source_target_pairs={{0,0},{1,16},{2,32},{3,48},{4,4},{5,20},{6,36},{7,52},{8,8},{9,24}... | collective-permute-start | bytes 393224 | tf_op jit(solution)/shard_map/ppermute | solution.py:286
  4.0 43.8 %all-to-all-start = ((bf16[64,32,128]{2,1,0:T(8,128)(2,1)}), bf16[64,32,128]{2,1,0:T(8,128)(2,1)}, u32[]{:S(2)}, u32[]{:S(2)}) async-start(bf16[64,32,128]{2,1,0:T(8,128)(2,1)} %broadcast_in_dim.41), calls=%async_computation | async-start | bytes 1048576 | tf_op jit(solution)/shard_map/all_to_all | solution.py:58
  20.8 11.0 %collective-permute-start.1 = (bf16[192,512]{1,0:T(8,128)(2,1)S(1)}, bf16[192,512]{1,0:T(8,128)(2,1)S(1)}, u32[]{:S(2)}, u32[]{:S(2)}) collective-permute-start(bf16[192,512]{1,0:T(8,128)(2,1)S(1)} %get-tuple-element.46), channel_id=1, source_target_pairs={{0,48},{4,52},{8,56},{12,60},{16,0},{20,4},{24,8},{28,12},{32,16},... | collective-permute-start | bytes 589832 | tf_op jit(solution)/shard_map/ppermute | solution.py:53
  23.8 13.9 %collective-permute-start.7 = (bf16[192,512]{1,0:T(8,128)(2,1)S(1)}, bf16[192,512]{1,0:T(8,128)(2,1)S(1)}, u32[]{:S(2)}, u32[]{:S(2)}) collective-permute-start(bf16[192,512]{1,0:T(8,128)(2,1)S(1)} %get-tuple-element.45), channel_id=1, source_target_pairs={{0,32},{4,36},{8,40},{12,44},{16,48},{20,52},{24,56},{28,60},{32,0... | collective-permute-start | bytes 589832 | tf_op jit(solution)/shard_map/ppermute | solution.py:53
  24.6 13.8 %collective-permute-start.8 = (bf16[192,512]{1,0:T(8,128)(2,1)S(1)}, bf16[192,512]{1,0:T(8,128)(2,1)S(1)}, u32[]{:S(2)}, u32[]{:S(2)}) collective-permute-start(bf16[192,512]{1,0:T(8,128)(2,1)S(1)} %get-tuple-element.44), channel_id=1, source_target_pairs={{0,16},{4,20},{8,24},{12,28},{16,32},{20,36},{24,40},{28,44},{32,4... | collective-permute-start | bytes 589832 | tf_op jit(solution)/shard_map/ppermute | solution.py:53
  32.6 16.3 %collective-permute-start.2 = (bf16[32,5120]{1,0:T(8,128)(2,1)}, bf16[32,5120]{1,0:T(8,128)(2,1)}, u32[]{:S(2)}, u32[]{:S(2)}) collective-permute-start(bf16[32,5120]{1,0:T(8,128)(2,1)} %constant_dynamic-slice_fusion.9), channel_id=1, source_target_pairs={{0,1},{1,2},{2,3},{3,0},{4,5},{5,6},{6,7},{7,4},{8,9},{9,10},{10,1... | collective-permute-start | bytes 983048 | tf_op jit(solution)/shard_map/ppermute | solution.py:40
  33.1 17.0 %collective-permute-start.4 = (bf16[32,5120]{1,0:T(8,128)(2,1)}, bf16[32,5120]{1,0:T(8,128)(2,1)}, u32[]{:S(2)}, u32[]{:S(2)}) collective-permute-start(bf16[32,5120]{1,0:T(8,128)(2,1)} %constant_dynamic-slice_fusion.9), channel_id=1, source_target_pairs={{0,3},{1,0},{2,1},{3,2},{4,7},{5,4},{6,5},{7,6},{8,11},{9,8},{10,9... | collective-permute-start | bytes 983048 | tf_op jit(solution)/shard_map/ppermute | solution.py:40
  40.0 46.0 %collective-permute-start.10 = (bf16[576,512]{1,0:T(8,128)(2,1)}, bf16[576,512]{1,0:T(8,128)(2,1)S(1)}, u32[]{:S(2)}, u32[]{:S(2)}) collective-permute-start(bf16[576,512]{1,0:T(8,128)(2,1)} %get-tuple-element.28), channel_id=1, source_target_pairs={{0,8},{4,12},{8,0},{12,4},{16,24},{20,28},{24,16},{28,20},{32,40},... | collective-permute-start | bytes 1769480 | tf_op jit(solution)/shard_map/ppermute | solution.py:53
  42.0 44.1 %collective-permute-start.11 = (bf16[576,512]{1,0:T(8,128)(2,1)}, bf16[576,512]{1,0:T(8,128)(2,1)S(1)}, u32[]{:S(2)}, u32[]{:S(2)}) collective-permute-start(bf16[576,512]{1,0:T(8,128)(2,1)} %get-tuple-element.26), channel_id=1, source_target_pairs={{0,12},{4,0},{8,4},{12,8},{16,28},{20,16},{24,20},{28,24},{32,44},... | collective-permute-start | bytes 1769480 | tf_op jit(solution)/shard_map/ppermute | solution.py:53
  43.1 42.9 %collective-permute-start.9 = (bf16[576,512]{1,0:T(8,128)(2,1)}, bf16[576,512]{1,0:T(8,128)(2,1)S(1)}, u32[]{:S(2)}, u32[]{:S(2)}) collective-permute-start(bf16[576,512]{1,0:T(8,128)(2,1)} %get-tuple-element.27), channel_id=1, source_target_pairs={{0,4},{4,8},{8,12},{12,0},{16,20},{20,24},{24,28},{28,16},{32,36},... | collective-permute-start | bytes 1769480 | tf_op jit(solution)/shard_map/ppermute | solution.py:53
  48.9 9.6 %collective-permute-start.3 = (bf16[32,5120]{1,0:T(8,128)(2,1)}, bf16[32,5120]{1,0:T(8,128)(2,1)S(1)}, u32[]{:S(2)}, u32[]{:S(2)}) collective-permute-start(bf16[32,5120]{1,0:T(8,128)(2,1)} %collective-permute-done.2), channel_id=1, source_target_pairs={{0,1},{1,2},{2,3},{3,0},{4,5},{5,6},{6,7},{7,4},{8,9},{9,10},{10,1... | collective-permute-start | bytes 983048 | tf_op jit(solution)/shard_map/ppermute | solution.py:40
  50.1 10.7 %collective-permute-start.6 = (bf16[32,8192]{1,0:T(8,128)(2,1)S(1)}, bf16[32,8192]{1,0:T(8,128)(2,1)S(1)}, u32[]{:S(2)}, u32[]{:S(2)}) collective-permute-start(bf16[32,8192]{1,0:T(8,128)(2,1)S(1)} %copy_bitcast_fusion), channel_id=1, source_target_pairs={{0,64},{64,0},{1,65},{65,1},{2,66},{66,2},{3,67},{67,3},{4,68},{68... | collective-permute-start | bytes 1572872 | tf_op jit(solution)/shard_map/ppermute | solution.py:44
  60.4 33.5 %collective-permute-start.18 = (bf16[128,64]{1,0:T(8,128)(2,1)S(1)}, bf16[128,64]{1,0:T(8,128)(2,1)S(1)}, u32[]{:S(2)}, u32[]{:S(2)}) collective-permute-start(bf16[128,64]{1,0:T(8,128)(2,1)S(1)} %maximum_select_fusion.1.low_near), channel_id=1, source_target_pairs={{0,64},{64,0},{1,65},{65,1},{2,66},{66,2},{3,67},{67,3},{4,68},{68... | collective-permute-start | bytes 49160 | tf_op jit(solution)/shard_map/ppermute | solution.py:44
  63.8 11.4 %collective-permute-start.19 = (f32[32,9216]{1,0:T(8,128)S(1)}, f32[32,9216]{1,0:T(8,128)S(1)}, u32[]{:S(2)}, u32[]{:S(2)}) collective-permute-start(f32[32,9216]{1,0:T(8,128)S(1)} %pad_maximum_fusion.1), channel_id=1, source_target_pairs={{0,64},{64,0},{1,65},{65,1},{2,66},{66,2},{3,67},{67,3},{4,68},{68... | collective-permute-start | bytes 3538952 | tf_op jit(solution)/shard_map/ppermute | solution.py:44
  75.2 10.8 %collective-permute-start.5 = (bf16[128,2048]{1,0:T(8,128)(2,1)}, bf16[128,2048]{1,0:T(8,128)(2,1)}, u32[]{:S(2)}, u32[]{:S(2)}) collective-permute-start(bf16[128,2048]{1,0:T(8,128)(2,1)} %fusion.4.near), channel_id=1, source_target_pairs={{0,64},{64,0},{1,65},{65,1},{2,66},{66,2},{3,67},{67,3},{4,68},{68... | collective-permute-start | bytes 1572872 | tf_op jit(solution)/shard_map/ppermute | solution.py:44
  77.7 28.6 %all-to-all-start.1 = ((bf16[64,32,128]{2,1,0:T(8,128)(2,1)}), bf16[64,32,128]{2,1,0:T(8,128)(2,1)}, u32[]{:S(2)}, u32[]{:S(2)}) async-start(bf16[64,32,128]{2,1,0:T(8,128)(2,1)} %bitcast_bitcast_fusion), calls=%async_computation.1 | async-start | bytes 1048576 | tf_op jit(solution)/shard_map/all_to_all | solution.py:402
  89.4 7.4 %collective-permute-start.12 = (bf16[64,1152]{1,0:T(8,128)(2,1)S(1)}, bf16[64,1152]{1,0:T(8,128)(2,1)S(1)}, u32[]{:S(2)}, u32[]{:S(2)}) collective-permute-start(bf16[64,1152]{1,0:T(8,128)(2,1)S(1)} %get-tuple-element.16), channel_id=1, source_target_pairs={{0,3},{1,0},{2,1},{3,2},{4,7},{5,4},{6,5},{7,6},{8,11},{9,8},{10,9... | collective-permute-start | bytes 442376 | tf_op jit(solution)/shard_map/ppermute | solution.py:40
  92.2 8.3 %collective-permute-start.13 = (bf16[64,1152]{1,0:T(8,128)(2,1)S(1)}, bf16[64,1152]{1,0:T(8,128)(2,1)S(1)}, u32[]{:S(2)}, u32[]{:S(2)}) collective-permute-start(bf16[64,1152]{1,0:T(8,128)(2,1)S(1)} %get-tuple-element.17), channel_id=1, source_target_pairs={{0,2},{1,3},{2,0},{3,1},{4,6},{5,7},{6,4},{7,5},{8,10},{9,11},{10,... | collective-permute-start | bytes 442376 | tf_op jit(solution)/shard_map/ppermute | solution.py:40
  93.1 8.9 %collective-permute-start.14 = (bf16[64,1152]{1,0:T(8,128)(2,1)S(1)}, bf16[64,1152]{1,0:T(8,128)(2,1)S(1)}, u32[]{:S(2)}, u32[]{:S(2)}) collective-permute-start(bf16[64,1152]{1,0:T(8,128)(2,1)S(1)} %get-tuple-element.18), channel_id=1, source_target_pairs={{0,1},{1,2},{2,3},{3,0},{4,5},{5,6},{6,7},{7,4},{8,9},{9,10},{10,1... | collective-permute-start | bytes 442376 | tf_op jit(solution)/shard_map/ppermute | solution.py:40
  102.6 7.3 %collective-permute-start.15 = (bf16[64,640]{1,0:T(8,128)(2,1)S(1)}, bf16[64,640]{1,0:T(8,128)(2,1)}, u32[]{:S(2)}, u32[]{:S(2)}) collective-permute-start(bf16[64,640]{1,0:T(8,128)(2,1)S(1)} %row_work.1.packed), channel_id=1, source_target_pairs={{0,1},{1,2},{2,3},{3,0},{4,5},{5,6},{6,7},{7,4},{8,9},{9,10},{10,1... | collective-permute-start | bytes 245768 | tf_op jit(solution)/shard_map/ppermute | solution.py:40
  102.7 7.2 %collective-permute-start.16 = (bf16[64,640]{1,0:T(8,128)(2,1)S(1)}, bf16[64,640]{1,0:T(8,128)(2,1)}, u32[]{:S(2)}, u32[]{:S(2)}) collective-permute-start(bf16[64,640]{1,0:T(8,128)(2,1)S(1)} %row_work.1.packed), channel_id=1, source_target_pairs={{0,2},{1,3},{2,0},{3,1},{4,6},{5,7},{6,4},{7,5},{8,10},{9,11},{10,... | collective-permute-start | bytes 245768 | tf_op jit(solution)/shard_map/ppermute | solution.py:40
  115.9 7.2 %collective-permute-start.21 = (f32[32,1024]{1,0:T(8,128)S(1)}, f32[32,1024]{1,0:T(8,128)S(1)}, u32[]{:S(2)}, u32[]{:S(2)}) collective-permute-start(f32[32,1024]{1,0:T(8,128)S(1)} %slice_add_fusion.1), channel_id=1, source_target_pairs={{0,1},{1,2},{2,3},{3,0},{4,5},{5,6},{6,7},{7,4},{8,9},{9,10},{10,1... | collective-permute-start | bytes 393224 | tf_op jit(solution)/shard_map/ppermute | solution.py:40
  116.9 9.7 %collective-permute-start.22 = (f32[32,1024]{1,0:T(8,128)S(1)}, f32[32,1024]{1,0:T(8,128)S(1)}, u32[]{:S(2)}, u32[]{:S(2)}) collective-permute-start(f32[32,1024]{1,0:T(8,128)S(1)} %slice_add_fusion.1), channel_id=1, source_target_pairs={{0,2},{1,3},{2,0},{3,1},{4,6},{5,7},{6,4},{7,5},{8,10},{9,11},{10,... | collective-permute-start | bytes 393224 | tf_op jit(solution)/shard_map/ppermute | solution.py:40
  119.9 6.7 %collective-permute-start.23 = (f32[32,1024]{1,0:T(8,128)S(1)}, f32[32,1024]{1,0:T(8,128)S(1)}, u32[]{:S(2)}, u32[]{:S(2)}) collective-permute-start(f32[32,1024]{1,0:T(8,128)S(1)} %slice_add_fusion.1), channel_id=1, source_target_pairs={{0,3},{1,0},{2,1},{3,2},{4,7},{5,4},{6,5},{7,6},{8,11},{9,8},{10,9... | collective-permute-start | bytes 393224 | tf_op jit(solution)/shard_map/ppermute | solution.py:40
  (21 other events, 206.6 us)

commit v8 on v7

--- a/solution.py
+++ b/solution.py
@@ -296,7 +296,7 @@
         came = along(jnp.concatenate([w_moved, t_given]), k, 0, side)
         w_line.append(came[:shard])
         t_line.append(came[shard:])
-    dest_owner, text_rows, hidden, _ = lax.optimization_barrier((dest_owner, text_rows, hidden, came))
+    dest_owner, text_rows, _ = lax.optimization_barrier((dest_owner, text_rows, came))
     w_line = w_line[::-1]
     w_line = cut(jnp.concatenate(w_line + w_line), ((2 * side - 1 - slab) & wrap) * shard, block)
     t_line = jnp.stack(t_line).reshape(side, side, chunk, half_kv)
@@ -401,7 +401,14 @@
     text_parts = both_sums[:, :width].reshape(half_rank, owners, shard).transpose(1, 0, 2)
     text_parts = lax.all_to_all(text_parts.astype(bf16), ("dp", "mp"), 0, 0, tiled=True)
     got = [turned(packed, "mp", k) for k in range(1, n_mp)]
-    enc_low_far, text_parts = lax.optimization_barrier((enc_low_far, text_parts))
+    text_here = jnp.sum(text_parts.astype(f32), axis=0)
+    here_high, here_low = split_two(text_here)
+    text_grad = dot(jnp.concatenate([here_high, here_low]), value_weight)
+    text_grad = text_grad[:half_rank] + text_grad[half_rank:] + both_sums[:, width:]
+    text_grad = text_grad + (
+        turned(text_grad, "mp", 1) + turned(text_grad, "mp", 2) + turned(text_grad, "mp", 3)
+    )
+    enc_low_far, text_grad = lax.optimization_barrier((enc_low_far, text_grad))
     mine, give = pl.pallas_call(
         functools.partial(image_kernel, block=block, step=mine_rows, **sizes),
         out_shape=(jax.ShapeDtypeStruct((half_rank, part_width + half_kv), f32),) * 2,
@@ -422,14 +429,6 @@
         a_part,
         *pieces,
         b_half,
-    )
-
-    text_here = jnp.sum(text_parts.astype(f32), axis=0)
-    here_high, here_low = split_two(text_here)
-    text_grad = dot(jnp.concatenate([here_high, here_low]), value_weight)
-    text_grad = text_grad[:half_rank] + text_grad[half_rank:] + both_sums[:, width:]
-    text_grad = text_grad + (
-        turned(text_grad, "mp", 1) + turned(text_grad, "mp", 2) + turned(text_grad, "mp", 3)
     )
 
     came = crossed(give)

time: 158 us -> 151 us (0.956)
  waiting for transfers between devices: 33.4 us -> 23.3 us
  local copies, waits for them, and re-layouts: 13.6 us -> 16.5 us
  Pallas kernels: 6.22 us -> 7.85 us
    ppermute x12, waiting for transfers between devices: 27.1 us -> 8.06 us  [turned(): lax.ppermute(array, axis, [(i, (i + step) % count) for i in range(count)])]
    ppermute x6, waiting for transfers between devices: 6.32 us -> 10.2 us  [along(): return lax.ppermute(array, 'dp', pairs)]
    all_to_all x1, waiting for transfers between devices: 0.01 us -> 3.38 us  [body(): lax.all_to_all(text_parts.astype(bf16), ('dp', 'mp'), 0, 0, tiled=True)]
    unnamed x45, local copies, waits for them, and re-layouts: 4.42 us -> 6.63 us
    all_to_all x1, starting transfers between devices: 7.33 us -> 5.49 us  [body(): lax.all_to_all(text_parts.astype(bf16), ('dp', 'mp'), 0, 0, tiled=True)]
    ppermute x5, waiting for transfers between devices: 0.01 us -> 1.63 us  [crossed(): return lax.ppermute(array, 'grp', [(0, 1), (1, 0)])]
  transfers between devices with their start and end apart: 26 -> 26, of which waited for: 9 -> 9; matrix products, arithmetic and copies ran while one was open for 21% -> 23% of each run, Pallas kernels for 2% -> 3%
where the time goes in v8:
time: 151 us; the launch traced here: 150 us
  starting transfers between devices  46.6 us (31%)
  blocking collectives  27.7 us (18%)
  waiting for transfers between devices  23.3 us (15%)
  local copies, waits for them, and re-layouts  16.5 us (11%)
  matrix products  16.1 us (11%)
  other arithmetic  10 us (7%)
  Pallas kernels  7.85 us (5%)
  between operations  2.05 us (1%)
    ppermute x12, starting transfers between devices, turned(): lax.ppermute(array, axis, [(i, (i + step) % count) for i in range(count)])  16.2 us
    all_to_all x1, blocking collectives, body(): mine = jnp.sum(lax.all_to_all(mine, 'dp', 0, 0, tiled=True), axis=0)  15.3 us
    dot_general x5, matrix products, dot(): return jnp.dot(a, b, preferred_element_type=f32)  14.7 us
    all_to_all x1, starting transfers between devices, to_everyone(): lax.all_to_all(jnp.broadcast_to(array[None], (count, *array.shape)), axes...  14.3 us
    all_to_all x1, blocking collectives, to_everyone(): lax.all_to_all(jnp.broadcast_to(array[None], (count, *array.shape)), axes...  12.4 us
    ppermute x6, waiting for transfers between devices, along(): return lax.ppermute(array, 'dp', pairs)  10.2 us
    ppermute x6, starting transfers between devices, along(): return lax.ppermute(array, 'dp', pairs)  9.19 us
    ppermute x12, waiting for transfers between devices, turned(): lax.ppermute(array, axis, [(i, (i + step) % count) for i in range(count)])  8.06 us
  transfers between devices with their start and end apart: 26, of which 9 were waited for; matrix products, arithmetic and copies ran while one was open for 23% of the time, Pallas kernels for 3%

profile of v8, /device:TPU:0, one launch (start us, length us, event | category | flops | bytes accessed | tf_op | source)
XLA Modules:
  0.0 150.1 jit_solution(6526920045017707748)
XLA Ops:
  2.5 3.1 %collective-permute-start.2 = (bf16[32,5120]{1,0:T(8,128)(2,1)}, bf16[32,5120]{1,0:T(8,128)(2,1)}, u32[]{:S(2)}, u32[]{:S(2)}) collective-permute-start(bf16[32,5120]{1,0:T(8,128)(2,1)} %constant_dynamic-slice_fusion.11), channel_id=1, source_target_pairs={{0,3},{1,0},{2,1},{3,2},{4,7},{5,4},{6,5},{7,6},{8,11},{9,8},{10,9... | collective-permute-start | bytes 983048 | tf_op jit(solution)/shard_map/ppermute | solution.py:40
  8.8 14.3 %all-to-all-start = ((bf16[64,32,128]{2,1,0:T(8,128)(2,1)}), bf16[64,32,128]{2,1,0:T(8,128)(2,1)}, u32[]{:S(2)}, u32[]{:S(2)}) async-start(bf16[64,32,128]{2,1,0:T(8,128)(2,1)} %broadcast_in_dim.41), calls=%async_computation | async-start | bytes 1048576 | tf_op jit(solution)/shard_map/all_to_all | solution.py:58
  24.8 3.0 %collective-permute-start.6 = (bf16[192,512]{1,0:T(8,128)(2,1)S(1)}, bf16[192,512]{1,0:T(8,128)(2,1)S(1)}, u32[]{:S(2)}, u32[]{:S(2)}) collective-permute-start(bf16[192,512]{1,0:T(8,128)(2,1)S(1)} %get-tuple-element.42), channel_id=1, source_target_pairs={{0,48},{4,52},{8,56},{12,60},{16,0},{20,4},{24,8},{28,12},{32,16},... | collective-permute-start | bytes 589832 | tf_op jit(solution)/shard_map/ppermute | solution.py:53
  29.5 6.5 %collective-permute-done.6 = bf16[192,512]{1,0:T(8,128)(2,1)S(1)} collective-permute-done((bf16[192,512]{1,0:T(8,128)(2,1)S(1)}, bf16[192,512]{1,0:T(8,128)(2,1)S(1)}, u32[]{:S(2)}, u32[]{:S(2)}) %collective-permute-start.6) | collective-permute-done | bytes 196640 | tf_op jit(solution)/shard_map/ppermute | solution.py:53
  36.2 1.7 %fusion = f32[80]{0:T(128)S(1)} fusion(bf16[160,8192]{1,0:T(8,128)(2,1)} %param.19, s32[]{:T(128)S(6)} %mul.124), kind=kLoop, calls=%fused_computation.3 | loop fusion | flops 1966000 | bytes 1311044 | tf_op jit(solution)/shard_map/reduce_sum | solution.py:315
  38.0 3.7 %collective-permute-done.8 = bf16[192,512]{1,0:T(8,128)(2,1)S(1)} collective-permute-done((bf16[192,512]{1,0:T(8,128)(2,1)S(1)}, bf16[192,512]{1,0:T(8,128)(2,1)S(1)}, u32[]{:S(2)}, u32[]{:S(2)}) %collective-permute-start.8) | collective-permute-done | bytes 196640 | tf_op jit(solution)/shard_map/ppermute | solution.py:53
  43.9 2.6 %collective-permute-start.10 = (bf16[576,512]{1,0:T(8,128)(2,1)}, bf16[576,512]{1,0:T(8,128)(2,1)S(1)}, u32[]{:S(2)}, u32[]{:S(2)}) collective-permute-start(bf16[576,512]{1,0:T(8,128)(2,1)} %get-tuple-element.26), channel_id=1, source_target_pairs={{0,8},{4,12},{8,0},{12,4},{16,24},{20,28},{24,16},{28,20},{32,40},... | collective-permute-start | bytes 1769480 | tf_op jit(solution)/shard_map/ppermute | solution.py:53
  51.1 1.8 %add_convert_fusion = (f32[256,1]{1,0:T(8,128)S(1)}, s32[256,1]{1,0:T(8,128)}) fusion(s32[256,1]{1,0:T(8,128)S(1)} %copy.87, s32[]{:T(128)S(6)} %axis_index.33, s32[]{:T(128)S(6)} %select_n.111, s32[256,1]{1,0:T(8,128)} %copy.77, s32[]{:T(128)} %and.209, s32[]{:T(128)S(6)} %axis_index.38), kind=kLoop, calls=%fused_computation.70 | loop fusion | flops 10240 | bytes 4112 | tf_op jit(solution)/shard_map/convert_element_type | solution.py:338
  55.3 4.9 %collective-permute-done.1 = bf16[32,5120]{1,0:T(8,128)(2,1)} collective-permute-done((bf16[32,5120]{1,0:T(8,128)(2,1)}, bf16[32,5120]{1,0:T(8,128)(2,1)}, u32[]{:S(2)}, u32[]{:S(2)}) %collective-permute-start.1) | collective-permute-done | bytes 327712 | tf_op jit(solution)/shard_map/ppermute | solution.py:40
  60.2 1.9 %convolution_convert_fusion = bf16[128,64]{1,0:T(8,128)(2,1)S(1)} fusion(bf16[5120,64]{0,1:T(8,128)(2,1)S(1)} %copy-done.16, bf16[32,5120]{1,0:T(8,128)(2,1)} %collective-permute-done.2, bf16[32,5120]{1,0:T(8,128)(2,1)} %collective-permute-done.1, bf16[32,5120]{1,0:T(8,128)(2,1)} %collective-permute-done, bf16[32,5120]{1,0:T(8,128)(2,1)} %constant_dynamic-slice_fusion.11), kind=kOutput, calls=%fused_computation.18 | convolution fusion | flops 89137152 | bytes 1982464 | tf_op jit(solution)/shard_map/dot_general | solution.py:17
  65.0 11.1 %fusion.4.near = bf16[128,2048]{1,0:T(8,128)(2,1)} fusion(f32[128,2048]{1,0:T(8,128)S(1)} %fusion.53, bf16[5120,2048]{1,0:T(8,128)(2,1)} %param.15, f32[2048]{0:T(1024)S(1)} %copy-done.13, bf16[32,5120]{1,0:T(8,128)(2,1)} %collective-permute-done.2, bf16[32,5120]{1,0:T(8,128)(2,1)} %collective-permute-done.1, bf16[32,5120]{1,0:T(8,128)(2,1)} %collective-permute-done, ...), kind=kOutput, calls=%fused_computation.8 | convolution fusion | flops 2690383872 | bytes 23863296 | tf_op jit(solution)/shard_map/dot_general | solution.py:17
  78.5 5.5 %all-to-all-start.1 = ((bf16[64,32,128]{2,1,0:T(8,128)(2,1)}), bf16[64,32,128]{2,1,0:T(8,128)(2,1)}, u32[]{:S(2)}, u32[]{:S(2)}) async-start(bf16[64,32,128]{2,1,0:T(8,128)(2,1)} %bitcast_bitcast_fusion), calls=%async_computation.1 | async-start | bytes 1048576 | tf_op jit(solution)/shard_map/all_to_all | solution.py:402
  86.4 3.2 %partial_products.1 = (f32[64,1152]{1,0:T(8,128)S(1)}, bf16[64,1152]{1,0:T(8,128)(2,1)}, bf16[64,1152]{1,0:T(8,128)(2,1)}, bf16[64,1152]{1,0:T(8,128)(2,1)}) custom-call(s32[1]{0:T(128)} %bitcast.place, bf16[128,2048]{1,0:T(8,128)(2,1)} %fusion.4.near, bf16[128,2048]{1,0:T(8,128)(2,1)} %collective-permute-done.3.far, f32[1,2048]{1,0:T(1,128)S(1)} %bitcast.72, ...), custom_call_target="tpu_custom_call" | custom-call | tf_op jit(solution)/shard_map/partial_products/pallas_call | solution.py:383
  90.3 2.4 %collective-permute-start.12 = (bf16[64,1152]{1,0:T(8,128)(2,1)}, bf16[64,1152]{1,0:T(8,128)(2,1)S(1)}, u32[]{:S(2)}, u32[]{:S(2)}) collective-permute-start(bf16[64,1152]{1,0:T(8,128)(2,1)} %get-tuple-element.14), channel_id=1, source_target_pairs={{0,3},{1,0},{2,1},{3,2},{4,7},{5,4},{6,5},{7,6},{8,11},{9,8},{10,9... | collective-permute-start | bytes 442376 | tf_op jit(solution)/shard_map/ppermute | solution.py:40
  94.4 3.4 %all-to-all-done.1 = bf16[64,32,128]{2,1,0:T(8,128)(2,1)} async-done(((bf16[64,32,128]{2,1,0:T(8,128)(2,1)}), bf16[64,32,128]{2,1,0:T(8,128)(2,1)}, u32[]{:S(2)}, u32[]{:S(2)}) %all-to-all-start.1) | async-done | bytes 524320 | tf_op jit(solution)/shard_map/all_to_all | solution.py:402
  101.7 1.5 collective-permute-start.20
  106.0 1.6 %row_work.1.packed = bf16[64,640]{1,0:T(8,128)(2,1)S(1)} custom-call(f32[64,1152]{1,0:T(8,128)S(1)} %copy-done.3, bf16[64,1152]{1,0:T(8,128)(2,1)S(1)} %collective-permute-done.12.got1, bf16[64,1152]{1,0:T(8,128)(2,1)} %collective-permute-done.13.got2, bf16[64,1152]{1,0:T(8,128)(2,1)} %collective-permute-done.14.got3, ...), custom_call_target="tpu_custom_call" | custom-call | tf_op jit(solution)/shard_map/row_work/pallas_call | solution.py:393
  107.6 1.8 %collective-permute-start.15 = (bf16[64,640]{1,0:T(8,128)(2,1)S(1)}, bf16[64,640]{1,0:T(8,128)(2,1)S(1)}, u32[]{:S(2)}, u32[]{:S(2)}) collective-permute-start(bf16[64,640]{1,0:T(8,128)(2,1)S(1)} %row_work.1.packed), channel_id=1, source_target_pairs={{0,1},{1,2},{2,3},{3,0},{4,5},{5,6},{6,7},{7,4},{8,9},{9,10},{10,1... | collective-permute-start | bytes 245768 | tf_op jit(solution)/shard_map/ppermute | solution.py:40
  109.4 2.3 %collective-permute-start.16 = (bf16[64,640]{1,0:T(8,128)(2,1)S(1)}, bf16[64,640]{1,0:T(8,128)(2,1)S(1)}, u32[]{:S(2)}, u32[]{:S(2)}) collective-permute-start(bf16[64,640]{1,0:T(8,128)(2,1)S(1)} %row_work.1.packed), channel_id=1, source_target_pairs={{0,2},{1,3},{2,0},{3,1},{4,6},{5,7},{6,4},{7,5},{8,10},{9,11},{10,... | collective-permute-start | bytes 245768 | tf_op jit(solution)/shard_map/ppermute | solution.py:40
  113.4 2.0 %collective-permute-done.16.got2 = bf16[64,640]{1,0:T(8,128)(2,1)S(1)} collective-permute-done((bf16[64,640]{1,0:T(8,128)(2,1)S(1)}, bf16[64,640]{1,0:T(8,128)(2,1)S(1)}, u32[]{:S(2)}, u32[]{:S(2)}) %collective-permute-start.16) | collective-permute-done | bytes 81952 | tf_op jit(solution)/shard_map/ppermute | solution.py:40
  116.1 3.0 %image_gradients.1 = (f32[32,2560]{1,0:T(8,128)S(1)}, f32[32,2560]{1,0:T(8,128)S(1)}) custom-call(s32[1]{0:T(128)} %bitcast.place, bf16[64,640]{1,0:T(8,128)(2,1)S(1)} %row_work.1.packed, bf16[64,640]{1,0:T(8,128)(2,1)S(1)} %collective-permute-done.15.got1, bf16[64,640]{1,0:T(8,128)(2,1)S(1)} %collective-permute-done.16.got2, ...), custom_call_target="tpu_custom_call" | custom-call | tf_op jit(solution)/shard_map/image_gradients/pallas_call | solution.py:412
  119.2 1.6 %collective-permute-done.23 = f32[32,2560]{1,0:T(8,128)S(1)} collective-permute-done((f32[32,2560]{1,0:T(8,128)S(1)}, f32[32,2560]{1,0:T(8,128)S(1)}, u32[]{:S(2)}, u32[]{:S(2)}) %collective-permute-start.23) | collective-permute-done | bytes 327712 | tf_op jit(solution)/shard_map/ppermute | solution.py:44
  121.0 15.3 %all_to_all.20 = f32[16,8,768]{2,1,0:T(8,128)S(1)} all-to-all(f32[16,8,768]{2,1,0:T(8,128)S(1)} %bitcast.75), channel_id=1, replica_groups=mesh['grp'=2,'dp'=16,'mp'=4] {'dp'}, dimensions={0} | all-to-all | bytes 786432 | tf_op jit(solution)/shard_map/all_to_all | solution.py:444
  136.3 12.4 %all_to_all.21 = f32[16,8,768]{2,1,0:T(8,128)S(1)} all-to-all(f32[16,8,768]{2,1,0:T(8,128)S(1)} %broadcast_in_dim.76), channel_id=1, replica_groups=mesh['grp'=2,'dp'=16,'mp'=4] {'dp'}, dimensions={0} | all-to-all | bytes 786432 | tf_op jit(solution)/shard_map/all_to_all | solution.py:58
  (149 shorter events, 37.7 us)
Async XLA Ops:
  2.5 52.7 %collective-permute-start.2 = (bf16[32,5120]{1,0:T(8,128)(2,1)}, bf16[32,5120]{1,0:T(8,128)(2,1)}, u32[]{:S(2)}, u32[]{:S(2)}) collective-permute-start(bf16[32,5120]{1,0:T(8,128)(2,1)} %constant_dynamic-slice_fusion.11), channel_id=1, source_target_pairs={{0,3},{1,0},{2,1},{3,2},{4,7},{5,4},{6,5},{7,6},{8,11},{9,8},{10,9... | collective-permute-start | bytes 983048 | tf_op jit(solution)/shard_map/ppermute | solution.py:40
  5.6 44.3 %collective-permute-start = (bf16[32,5120]{1,0:T(8,128)(2,1)}, bf16[32,5120]{1,0:T(8,128)(2,1)}, u32[]{:S(2)}, u32[]{:S(2)}) collective-permute-start(bf16[32,5120]{1,0:T(8,128)(2,1)} %constant_dynamic-slice_fusion.11), channel_id=1, source_target_pairs={{0,1},{1,2},{2,3},{3,0},{4,5},{5,6},{6,7},{7,4},{8,9},{9,10},{10,1... | collective-permute-start | bytes 983048 | tf_op jit(solution)/shard_map/ppermute | solution.py:40
  6.5 18.3 %collective-permute-start.5 = (bf16[128,512]{1,0:T(8,128)(2,1)S(1)}, bf16[128,512]{1,0:T(8,128)(2,1)S(1)}, u32[]{:S(2)}, u32[]{:S(2)}) collective-permute-start(bf16[128,512]{1,0:T(8,128)(2,1)S(1)} %constant_dynamic-slice_fusion.9), channel_id=1, source_target_pairs={{0,0},{1,16},{2,32},{3,48},{4,4},{5,20},{6,36},{7,52},{8,8},{9,24}... | collective-permute-start | bytes 393224 | tf_op jit(solution)/shard_map/ppermute | solution.py:286
  8.8 44.2 %all-to-all-start = ((bf16[64,32,128]{2,1,0:T(8,128)(2,1)}), bf16[64,32,128]{2,1,0:T(8,128)(2,1)}, u32[]{:S(2)}, u32[]{:S(2)}) async-start(bf16[64,32,128]{2,1,0:T(8,128)(2,1)} %broadcast_in_dim.41), calls=%async_computation | async-start | bytes 1048576 | tf_op jit(solution)/shard_map/all_to_all | solution.py:58
  24.8 11.1 %collective-permute-start.6 = (bf16[192,512]{1,0:T(8,128)(2,1)S(1)}, bf16[192,512]{1,0:T(8,128)(2,1)S(1)}, u32[]{:S(2)}, u32[]{:S(2)}) collective-permute-start(bf16[192,512]{1,0:T(8,128)(2,1)S(1)} %get-tuple-element.42), channel_id=1, source_target_pairs={{0,48},{4,52},{8,56},{12,60},{16,0},{20,4},{24,8},{28,12},{32,16},... | collective-permute-start | bytes 589832 | tf_op jit(solution)/shard_map/ppermute | solution.py:53
  27.8 10.1 %collective-permute-start.7 = (bf16[192,512]{1,0:T(8,128)(2,1)S(1)}, bf16[192,512]{1,0:T(8,128)(2,1)S(1)}, u32[]{:S(2)}, u32[]{:S(2)}) collective-permute-start(bf16[192,512]{1,0:T(8,128)(2,1)S(1)} %get-tuple-element.41), channel_id=1, source_target_pairs={{0,32},{4,36},{8,40},{12,44},{16,48},{20,52},{24,56},{28,60},{32,0... | collective-permute-start | bytes 589832 | tf_op jit(solution)/shard_map/ppermute | solution.py:53
  28.6 13.1 %collective-permute-start.8 = (bf16[192,512]{1,0:T(8,128)(2,1)S(1)}, bf16[192,512]{1,0:T(8,128)(2,1)S(1)}, u32[]{:S(2)}, u32[]{:S(2)}) collective-permute-start(bf16[192,512]{1,0:T(8,128)(2,1)S(1)} %get-tuple-element.40), channel_id=1, source_target_pairs={{0,16},{4,20},{8,24},{12,28},{16,32},{20,36},{24,40},{28,44},{32,4... | collective-permute-start | bytes 589832 | tf_op jit(solution)/shard_map/ppermute | solution.py:53
  43.3 42.1 %collective-permute-start.9 = (bf16[576,512]{1,0:T(8,128)(2,1)}, bf16[576,512]{1,0:T(8,128)(2,1)S(1)}, u32[]{:S(2)}, u32[]{:S(2)}) collective-permute-start(bf16[576,512]{1,0:T(8,128)(2,1)} %get-tuple-element.25), channel_id=1, source_target_pairs={{0,4},{4,8},{8,12},{12,0},{16,20},{20,24},{24,28},{28,16},{32,36},... | collective-permute-start | bytes 1769480 | tf_op jit(solution)/shard_map/ppermute | solution.py:53
  43.9 41.6 %collective-permute-start.10 = (bf16[576,512]{1,0:T(8,128)(2,1)}, bf16[576,512]{1,0:T(8,128)(2,1)S(1)}, u32[]{:S(2)}, u32[]{:S(2)}) collective-permute-start(bf16[576,512]{1,0:T(8,128)(2,1)} %get-tuple-element.26), channel_id=1, source_target_pairs={{0,8},{4,12},{8,0},{12,4},{16,24},{20,28},{24,16},{28,20},{32,40},... | collective-permute-start | bytes 1769480 | tf_op jit(solution)/shard_map/ppermute | solution.py:53
  46.5 39.0 %collective-permute-start.11 = (bf16[576,512]{1,0:T(8,128)(2,1)}, bf16[576,512]{1,0:T(8,128)(2,1)S(1)}, u32[]{:S(2)}, u32[]{:S(2)}) collective-permute-start(bf16[576,512]{1,0:T(8,128)(2,1)} %get-tuple-element.24), channel_id=1, source_target_pairs={{0,12},{4,0},{8,4},{12,8},{16,28},{20,16},{24,20},{28,24},{32,44},... | collective-permute-start | bytes 1769480 | tf_op jit(solution)/shard_map/ppermute | solution.py:53
  49.9 10.3 %collective-permute-start.1 = (bf16[32,5120]{1,0:T(8,128)(2,1)}, bf16[32,5120]{1,0:T(8,128)(2,1)}, u32[]{:S(2)}, u32[]{:S(2)}) collective-permute-start(bf16[32,5120]{1,0:T(8,128)(2,1)} %collective-permute-done), channel_id=1, source_target_pairs={{0,1},{1,2},{2,3},{3,0},{4,5},{5,6},{6,7},{7,4},{8,9},{9,10},{10,1... | collective-permute-start | bytes 983048 | tf_op jit(solution)/shard_map/ppermute | solution.py:40
  55.2 7.2 %collective-permute-start.4 = (bf16[32,8192]{1,0:T(8,128)(2,1)S(1)}, bf16[32,8192]{1,0:T(8,128)(2,1)S(1)}, u32[]{:S(2)}, u32[]{:S(2)}) collective-permute-start(bf16[32,8192]{1,0:T(8,128)(2,1)S(1)} %copy_bitcast_fusion), channel_id=1, source_target_pairs={{0,64},{64,0},{1,65},{65,1},{2,66},{66,2},{3,67},{67,3},{4,68},{68... | collective-permute-start | bytes 1572872 | tf_op jit(solution)/shard_map/ppermute | solution.py:44
  64.7 11.7 %collective-permute-start.19 = (f32[32,9216]{1,0:T(8,128)S(1)}, f32[32,9216]{1,0:T(8,128)S(1)}, u32[]{:S(2)}, u32[]{:S(2)}) collective-permute-start(f32[32,9216]{1,0:T(8,128)S(1)} %pad_maximum_fusion.1), channel_id=1, source_target_pairs={{0,64},{64,0},{1,65},{65,1},{2,66},{66,2},{3,67},{67,3},{4,68},{68... | collective-permute-start | bytes 3538952 | tf_op jit(solution)/shard_map/ppermute | solution.py:44
  76.2 9.3 %collective-permute-start.3 = (bf16[128,2048]{1,0:T(8,128)(2,1)}, bf16[128,2048]{1,0:T(8,128)(2,1)}, u32[]{:S(2)}, u32[]{:S(2)}) collective-permute-start(bf16[128,2048]{1,0:T(8,128)(2,1)} %fusion.4.near), channel_id=1, source_target_pairs={{0,64},{64,0},{1,65},{65,1},{2,66},{66,2},{3,67},{67,3},{4,68},{68... | collective-permute-start | bytes 1572872 | tf_op jit(solution)/shard_map/ppermute | solution.py:44
  78.5 19.3 %all-to-all-start.1 = ((bf16[64,32,128]{2,1,0:T(8,128)(2,1)}), bf16[64,32,128]{2,1,0:T(8,128)(2,1)}, u32[]{:S(2)}, u32[]{:S(2)}) async-start(bf16[64,32,128]{2,1,0:T(8,128)(2,1)} %bitcast_bitcast_fusion), calls=%async_computation.1 | async-start | bytes 1048576 | tf_op jit(solution)/shard_map/all_to_all | solution.py:402
  84.1 17.5 %collective-permute-start.18 = (bf16[128,64]{1,0:T(8,128)(2,1)S(1)}, bf16[128,64]{1,0:T(8,128)(2,1)}, u32[]{:S(2)}, u32[]{:S(2)}) collective-permute-start(bf16[128,64]{1,0:T(8,128)(2,1)S(1)} %maximum_select_fusion.1.low_near), channel_id=1, source_target_pairs={{0,64},{64,0},{1,65},{65,1},{2,66},{66,2},{3,67},{67,3},{4,68},{68... | collective-permute-start | bytes 49160 | tf_op jit(solution)/shard_map/ppermute | solution.py:44
  90.3 12.8 %collective-permute-start.12 = (bf16[64,1152]{1,0:T(8,128)(2,1)}, bf16[64,1152]{1,0:T(8,128)(2,1)S(1)}, u32[]{:S(2)}, u32[]{:S(2)}) collective-permute-start(bf16[64,1152]{1,0:T(8,128)(2,1)} %get-tuple-element.14), channel_id=1, source_target_pairs={{0,3},{1,0},{2,1},{3,2},{4,7},{5,4},{6,5},{7,6},{8,11},{9,8},{10,9... | collective-permute-start | bytes 442376 | tf_op jit(solution)/shard_map/ppermute | solution.py:40
  92.7 12.3 %collective-permute-start.13 = (bf16[64,1152]{1,0:T(8,128)(2,1)}, bf16[64,1152]{1,0:T(8,128)(2,1)}, u32[]{:S(2)}, u32[]{:S(2)}) collective-permute-start(bf16[64,1152]{1,0:T(8,128)(2,1)} %get-tuple-element.15), channel_id=1, source_target_pairs={{0,2},{1,3},{2,0},{3,1},{4,6},{5,7},{6,4},{7,5},{8,10},{9,11},{10,... | collective-permute-start | bytes 442376 | tf_op jit(solution)/shard_map/ppermute | solution.py:40
  93.6 11.5 %collective-permute-start.14 = (bf16[64,1152]{1,0:T(8,128)(2,1)}, bf16[64,1152]{1,0:T(8,128)(2,1)}, u32[]{:S(2)}, u32[]{:S(2)}) collective-permute-start(bf16[64,1152]{1,0:T(8,128)(2,1)} %get-tuple-element.16), channel_id=1, source_target_pairs={{0,1},{1,2},{2,3},{3,0},{4,5},{5,6},{6,7},{7,4},{8,9},{9,10},{10,1... | collective-permute-start | bytes 442376 | tf_op jit(solution)/shard_map/ppermute | solution.py:40
  101.0 10.7 %collective-permute-start.22 = (f32[32,1024]{1,0:T(8,128)S(1)}, f32[32,1024]{1,0:T(8,128)S(1)}, u32[]{:S(2)}, u32[]{:S(2)}) collective-permute-start(f32[32,1024]{1,0:T(8,128)S(1)} %slice_add_fusion.1), channel_id=1, source_target_pairs={{0,3},{1,0},{2,1},{3,2},{4,7},{5,4},{6,5},{7,6},{8,11},{9,8},{10,9... | collective-permute-start | bytes 393224 | tf_op jit(solution)/shard_map/ppermute | solution.py:40
  101.7 11.3 %collective-permute-start.20 = (f32[32,1024]{1,0:T(8,128)S(1)}, f32[32,1024]{1,0:T(8,128)S(1)}, u32[]{:S(2)}, u32[]{:S(2)}) collective-permute-start(f32[32,1024]{1,0:T(8,128)S(1)} %slice_add_fusion.1), channel_id=1, source_target_pairs={{0,1},{1,2},{2,3},{3,0},{4,5},{5,6},{6,7},{7,4},{8,9},{9,10},{10,1... | collective-permute-start | bytes 393224 | tf_op jit(solution)/shard_map/ppermute | solution.py:40
  103.1 9.9 %collective-permute-start.21 = (f32[32,1024]{1,0:T(8,128)S(1)}, f32[32,1024]{1,0:T(8,128)S(1)}, u32[]{:S(2)}, u32[]{:S(2)}) collective-permute-start(f32[32,1024]{1,0:T(8,128)S(1)} %slice_add_fusion.1), channel_id=1, source_target_pairs={{0,2},{1,3},{2,0},{3,1},{4,6},{5,7},{6,4},{7,5},{8,10},{9,11},{10,... | collective-permute-start | bytes 393224 | tf_op jit(solution)/shard_map/ppermute | solution.py:40
  107.6 5.7 %collective-permute-start.15 = (bf16[64,640]{1,0:T(8,128)(2,1)S(1)}, bf16[64,640]{1,0:T(8,128)(2,1)S(1)}, u32[]{:S(2)}, u32[]{:S(2)}) collective-permute-start(bf16[64,640]{1,0:T(8,128)(2,1)S(1)} %row_work.1.packed), channel_id=1, source_target_pairs={{0,1},{1,2},{2,3},{3,0},{4,5},{5,6},{6,7},{7,4},{8,9},{9,10},{10,1... | collective-permute-start | bytes 245768 | tf_op jit(solution)/shard_map/ppermute | solution.py:40
  109.4 5.9 %collective-permute-start.16 = (bf16[64,640]{1,0:T(8,128)(2,1)S(1)}, bf16[64,640]{1,0:T(8,128)(2,1)S(1)}, u32[]{:S(2)}, u32[]{:S(2)}) collective-permute-start(bf16[64,640]{1,0:T(8,128)(2,1)S(1)} %row_work.1.packed), channel_id=1, source_target_pairs={{0,2},{1,3},{2,0},{3,1},{4,6},{5,7},{6,4},{7,5},{8,10},{9,11},{10,... | collective-permute-start | bytes 245768 | tf_op jit(solution)/shard_map/ppermute | solution.py:40
  (21 other events, 168.9 us)

commit v9 on v8

--- a/solution.py
+++ b/solution.py
@@ -201,6 +201,7 @@
     mine,
     give,
     rows,
+    ranks,
     *,
     block,
     half_kv,
@@ -231,9 +232,9 @@
         dnormed = dot_nt(dvalues, piece[:block, :]) + dot(dlow, a_part[:, here])
         wide = jnp.concatenate([near[:, here], far[:, here]]).astype(f32)
         dimage = (inverse * (gain[:, here] * dnormed) - wide * factor).astype(bf16)
-        grad = dot_tn(enc_low, dimage)
-        mine[:, here] = grad[:half]
-        give[:, here] = grad[half:]
+        ranks[...] = dot_tn(enc_low, dimage)
+        mine[:, here] = ranks[pl.ds(pl.multiple_of(place[1] * half, half), half), :]
+        give[:, here] = ranks[pl.ds(pl.multiple_of((1 - place[1]) * half, half), half), :]
 
 
 def body(
@@ -372,10 +373,9 @@
     both_sums = jnp.concatenate([text_sum, rest_sum], axis=1)
     both_sums = both_sums[:half_rank] + crossed(both_sums[half_rank:])
     image_far = crossed(image)
-    enc_low = jnp.where(first, enc_low, jnp.roll(enc_low, half_rank, axis=1))
-    enc_low_far = jnp.roll(crossed(enc_low), half_rank, axis=1)
+    enc_low_far = crossed(enc_low)
     gain_part = cut(gain_wide, mp * part_width, part_width, 1)
-    where = col[None].astype(jnp.int32)
+    where = jnp.stack([col, grp]).astype(jnp.int32)
     sizes = dict(half_kv=half_kv, rank=rank)
     lanes = kv + 2 * rank
     tokens = 2 * mine_rows
@@ -414,7 +414,10 @@
         out_shape=(jax.ShapeDtypeStruct((half_rank, part_width + half_kv), f32),) * 2,
         in_specs=[SMEM] + [VMEM] * 15,
         out_specs=(VMEM, VMEM),
-        scratch_shapes=[pltpu.VMEM((ENC_DEV, half_kv + 2 * rank), bf16)],
+        scratch_shapes=[
+            pltpu.VMEM((ENC_DEV, half_kv + 2 * rank), bf16),
+            pltpu.VMEM((rank, block), f32),
+        ],
         compiler_params=PARAMS,
         name="image_gradients",
     )(

time: 151 us -> 149 us (0.987)
  other arithmetic: 10 us -> 5.25 us
  waiting for transfers between devices: 23.3 us -> 27.9 us
  local copies, waits for them, and re-layouts: 16.5 us -> 14.8 us
    ppermute x12, waiting for transfers between devices: 8.06 us -> 10.3 us  [turned(): lax.ppermute(array, axis, [(i, (i + step) % count) for i in range(count)])]
    ppermute x6, waiting for transfers between devices: 10.2 us -> 12.4 us  [along(): return lax.ppermute(array, 'dp', pairs)]
    convert_element_type x1, other arithmetic: 1.77 us -> 0.21 us  [body(): position = (slot * n_dp + dp).astype(f32)]
    unnamed x45 -> x41, local copies, waits for them, and re-layouts: 6.63 us -> 5.78 us
  transfers between devices with their start and end apart: 26 -> 26, of which waited for: 9 -> 8; matrix products, arithmetic and copies ran while one was open for 23% -> 20% of each run, Pallas kernels for 3% -> 3%
where the time goes in v9:
time: 149 us; the launch traced here: 148 us
  starting transfers between devices  47.1 us (32%)
  waiting for transfers between devices  27.9 us (19%)
  blocking collectives  27.3 us (18%)
  matrix products  16.1 us (11%)
  local copies, waits for them, and re-layouts  14.8 us (10%)
  Pallas kernels  7.89 us (5%)
  other arithmetic  5.25 us (4%)
  between operations  2.09 us (1%)
    ppermute x12, starting transfers between devices, turned(): lax.ppermute(array, axis, [(i, (i + step) % count) for i in range(count)])  16.4 us
    all_to_all x1, blocking collectives, body(): mine = jnp.sum(lax.all_to_all(mine, 'dp', 0, 0, tiled=True), axis=0)  14.9 us
    dot_general x5, matrix products, dot(): return jnp.dot(a, b, preferred_element_type=f32)  14.7 us
    all_to_all x1, starting transfers between devices, to_everyone(): lax.all_to_all(jnp.broadcast_to(array[None], (count, *array.shape)), axes...  14.3 us
    all_to_all x1, blocking collectives, to_everyone(): lax.all_to_all(jnp.broadcast_to(array[None], (count, *array.shape)), axes...  12.4 us
    ppermute x6, waiting for transfers between devices, along(): return lax.ppermute(array, 'dp', pairs)  12.4 us
    ppermute x12, waiting for transfers between devices, turned(): lax.ppermute(array, axis, [(i, (i + step) % count) for i in range(count)])  10.3 us
    ppermute x6, starting transfers between devices, along(): return lax.ppermute(array, 'dp', pairs)  9.31 us
  transfers between devices with their start and end apart: 26, of which 8 were waited for; matrix products, arithmetic and copies ran while one was open for 20% of the time, Pallas kernels for 3%

profile of v9, /device:TPU:0, one launch (start us, length us, event | category | flops | bytes accessed | tf_op | source)
XLA Modules:
  0.0 148.4 jit_solution(3460358914016514144)
XLA Ops:
  2.5 3.1 %collective-permute-start.2 = (bf16[32,5120]{1,0:T(8,128)(2,1)}, bf16[32,5120]{1,0:T(8,128)(2,1)}, u32[]{:S(2)}, u32[]{:S(2)}) collective-permute-start(bf16[32,5120]{1,0:T(8,128)(2,1)} %constant_dynamic-slice_fusion.11), channel_id=1, source_target_pairs={{0,3},{1,0},{2,1},{3,2},{4,7},{5,4},{6,5},{7,6},{8,11},{9,8},{10,9... | collective-permute-start | bytes 983048 | tf_op jit(solution)/shard_map/ppermute | solution.py:40
  8.8 14.3 %all-to-all-start = ((bf16[64,32,128]{2,1,0:T(8,128)(2,1)}), bf16[64,32,128]{2,1,0:T(8,128)(2,1)}, u32[]{:S(2)}, u32[]{:S(2)}) async-start(bf16[64,32,128]{2,1,0:T(8,128)(2,1)} %broadcast_in_dim.35), calls=%async_computation | async-start | bytes 1048576 | tf_op jit(solution)/shard_map/all_to_all | solution.py:58
  24.2 3.0 %collective-permute-start.6 = (bf16[192,512]{1,0:T(8,128)(2,1)S(1)}, bf16[192,512]{1,0:T(8,128)(2,1)S(1)}, u32[]{:S(2)}, u32[]{:S(2)}) collective-permute-start(bf16[192,512]{1,0:T(8,128)(2,1)S(1)} %get-tuple-element.42), channel_id=1, source_target_pairs={{0,48},{4,52},{8,56},{12,60},{16,0},{20,4},{24,8},{28,12},{32,16},... | collective-permute-start | bytes 589832 | tf_op jit(solution)/shard_map/ppermute | solution.py:53
  29.0 7.0 %collective-permute-done.6 = bf16[192,512]{1,0:T(8,128)(2,1)S(1)} collective-permute-done((bf16[192,512]{1,0:T(8,128)(2,1)S(1)}, bf16[192,512]{1,0:T(8,128)(2,1)S(1)}, u32[]{:S(2)}, u32[]{:S(2)}) %collective-permute-start.6) | collective-permute-done | bytes 196640 | tf_op jit(solution)/shard_map/ppermute | solution.py:53
  36.1 1.6 %collective-permute-done.7 = bf16[192,512]{1,0:T(8,128)(2,1)S(1)} collective-permute-done((bf16[192,512]{1,0:T(8,128)(2,1)S(1)}, bf16[192,512]{1,0:T(8,128)(2,1)S(1)}, u32[]{:S(2)}, u32[]{:S(2)}) %collective-permute-start.7) | collective-permute-done | bytes 196640 | tf_op jit(solution)/shard_map/ppermute | solution.py:53
  37.8 3.8 %collective-permute-done.8 = bf16[192,512]{1,0:T(8,128)(2,1)S(1)} collective-permute-done((bf16[192,512]{1,0:T(8,128)(2,1)S(1)}, bf16[192,512]{1,0:T(8,128)(2,1)S(1)}, u32[]{:S(2)}, u32[]{:S(2)}) %collective-permute-start.8) | collective-permute-done | bytes 196640 | tf_op jit(solution)/shard_map/ppermute | solution.py:53
  41.8 1.4 pad_maximum_fusion.5
  43.8 2.7 %collective-permute-start.10 = (bf16[576,512]{1,0:T(8,128)(2,1)}, bf16[576,512]{1,0:T(8,128)(2,1)S(1)}, u32[]{:S(2)}, u32[]{:S(2)}) collective-permute-start(bf16[576,512]{1,0:T(8,128)(2,1)} %get-tuple-element.26), channel_id=1, source_target_pairs={{0,8},{4,12},{8,0},{12,4},{16,24},{20,28},{24,16},{28,20},{32,40},... | collective-permute-start | bytes 1769480 | tf_op jit(solution)/shard_map/ppermute | solution.py:53
  51.6 7.0 %collective-permute-done.1 = bf16[32,5120]{1,0:T(8,128)(2,1)} collective-permute-done((bf16[32,5120]{1,0:T(8,128)(2,1)}, bf16[32,5120]{1,0:T(8,128)(2,1)}, u32[]{:S(2)}, u32[]{:S(2)}) %collective-permute-start.1) | collective-permute-done | bytes 327712 | tf_op jit(solution)/shard_map/ppermute | solution.py:40
  58.6 1.9 %convolution_convert_fusion.low_near = bf16[128,64]{1,0:T(8,128)(2,1)S(1)} fusion(bf16[5120,64]{0,1:T(8,128)(2,1)S(1)} %copy-done.15, bf16[32,5120]{1,0:T(8,128)(2,1)} %collective-permute-done.2, bf16[32,5120]{1,0:T(8,128)(2,1)} %collective-permute-done.1, bf16[32,5120]{1,0:T(8,128)(2,1)} %collective-permute-done, ...), kind=kOutput, calls=%fused_computation.18 | convolution fusion | flops 89137152 | bytes 1982464 | tf_op jit(solution)/shard_map/dot_general | solution.py:17
  63.5 11.1 %fusion.4.near = bf16[128,2048]{1,0:T(8,128)(2,1)} fusion(f32[128,2048]{1,0:T(8,128)S(1)} %fusion.51, bf16[5120,2048]{1,0:T(8,128)(2,1)} %param.15, f32[2048]{0:T(1024)S(1)} %convert_element_type.78, bf16[32,5120]{1,0:T(8,128)(2,1)} %collective-permute-done.2, bf16[32,5120]{1,0:T(8,128)(2,1)} %collective-permute-done.1, ...), kind=kOutput, calls=%fused_computation.8 | convolution fusion | flops 2690383872 | bytes 23863296 | tf_op jit(solution)/shard_map/dot_general | solution.py:17
  77.1 5.7 %all-to-all-start.1 = ((bf16[64,32,128]{2,1,0:T(8,128)(2,1)}), bf16[64,32,128]{2,1,0:T(8,128)(2,1)}, u32[]{:S(2)}, u32[]{:S(2)}) async-start(bf16[64,32,128]{2,1,0:T(8,128)(2,1)} %bitcast_bitcast_fusion), calls=%async_computation.1 | async-start | bytes 1048576 | tf_op jit(solution)/shard_map/all_to_all | solution.py:402
  84.6 3.2 %partial_products.1 = (f32[64,1152]{1,0:T(8,128)S(1)}, bf16[64,1152]{1,0:T(8,128)(2,1)}, bf16[64,1152]{1,0:T(8,128)(2,1)}, bf16[64,1152]{1,0:T(8,128)(2,1)}) custom-call(s32[2]{0:T(128)S(1)} %pad_add_fusion.place, bf16[128,2048]{1,0:T(8,128)(2,1)} %fusion.4.near, bf16[128,2048]{1,0:T(8,128)(2,1)} %collective-permute-done.3.far, f32[1,2048]{1,0:T(1,128)S(1)} %bitcast.73, ...), custom_call_target="tpu_custom_call" | custom-call | tf_op jit(solution)/shard_map/partial_products/pallas_call | solution.py:383
  88.5 2.6 %collective-permute-start.12 = (bf16[64,1152]{1,0:T(8,128)(2,1)}, bf16[64,1152]{1,0:T(8,128)(2,1)S(1)}, u32[]{:S(2)}, u32[]{:S(2)}) collective-permute-start(bf16[64,1152]{1,0:T(8,128)(2,1)} %get-tuple-element.14), channel_id=1, source_target_pairs={{0,3},{1,0},{2,1},{3,2},{4,7},{5,4},{6,5},{7,6},{8,11},{9,8},{10,9... | collective-permute-start | bytes 442376 | tf_op jit(solution)/shard_map/ppermute | solution.py:40
  92.8 3.6 %all-to-all-done.1 = bf16[64,32,128]{2,1,0:T(8,128)(2,1)} async-done(((bf16[64,32,128]{2,1,0:T(8,128)(2,1)}), bf16[64,32,128]{2,1,0:T(8,128)(2,1)}, u32[]{:S(2)}, u32[]{:S(2)}) %all-to-all-start.1) | async-done | bytes 524320 | tf_op jit(solution)/shard_map/all_to_all | solution.py:402
  100.3 1.4 collective-permute-start.20
  104.6 1.6 %row_work.1.packed = bf16[64,640]{1,0:T(8,128)(2,1)S(1)} custom-call(f32[64,1152]{1,0:T(8,128)S(1)} %copy-done.2, bf16[64,1152]{1,0:T(8,128)(2,1)S(1)} %collective-permute-done.12.got1, bf16[64,1152]{1,0:T(8,128)(2,1)} %collective-permute-done.13.got2, bf16[64,1152]{1,0:T(8,128)(2,1)} %collective-permute-done.14.got3, ...), custom_call_target="tpu_custom_call" | custom-call | tf_op jit(solution)/shard_map/row_work/pallas_call | solution.py:393
  106.2 1.8 %collective-permute-start.15 = (bf16[64,640]{1,0:T(8,128)(2,1)S(1)}, bf16[64,640]{1,0:T(8,128)(2,1)S(1)}, u32[]{:S(2)}, u32[]{:S(2)}) collective-permute-start(bf16[64,640]{1,0:T(8,128)(2,1)S(1)} %row_work.1.packed), channel_id=1, source_target_pairs={{0,1},{1,2},{2,3},{3,0},{4,5},{5,6},{6,7},{7,4},{8,9},{9,10},{10,1... | collective-permute-start | bytes 245768 | tf_op jit(solution)/shard_map/ppermute | solution.py:40
  108.0 2.2 %collective-permute-start.16 = (bf16[64,640]{1,0:T(8,128)(2,1)S(1)}, bf16[64,640]{1,0:T(8,128)(2,1)S(1)}, u32[]{:S(2)}, u32[]{:S(2)}) collective-permute-start(bf16[64,640]{1,0:T(8,128)(2,1)S(1)} %row_work.1.packed), channel_id=1, source_target_pairs={{0,2},{1,3},{2,0},{3,1},{4,6},{5,7},{6,4},{7,5},{8,10},{9,11},{10,... | collective-permute-start | bytes 245768 | tf_op jit(solution)/shard_map/ppermute | solution.py:40
  112.3 2.5 %collective-permute-done.16.got2 = bf16[64,640]{1,0:T(8,128)(2,1)S(1)} collective-permute-done((bf16[64,640]{1,0:T(8,128)(2,1)S(1)}, bf16[64,640]{1,0:T(8,128)(2,1)S(1)}, u32[]{:S(2)}, u32[]{:S(2)}) %collective-permute-start.16) | collective-permute-done | bytes 81952 | tf_op jit(solution)/shard_map/ppermute | solution.py:40
  114.8 3.0 %image_gradients.1 = (f32[32,2560]{1,0:T(8,128)S(1)}, f32[32,2560]{1,0:T(8,128)S(1)}) custom-call(s32[2]{0:T(128)S(1)} %pad_add_fusion.place, bf16[64,640]{1,0:T(8,128)(2,1)S(1)} %row_work.1.packed, bf16[64,640]{1,0:T(8,128)(2,1)S(1)} %collective-permute-done.15.got1, bf16[64,640]{1,0:T(8,128)(2,1)S(1)} %collective-permute-done.16.got2, ...), custom_call_target="tpu_custom_call" | custom-call | tf_op jit(solution)/shard_map/image_gradients/pallas_call | solution.py:412
  117.9 1.6 %collective-permute-done.23 = f32[32,2560]{1,0:T(8,128)S(1)} collective-permute-done((f32[32,2560]{1,0:T(8,128)S(1)}, f32[32,2560]{1,0:T(8,128)S(1)}, u32[]{:S(2)}, u32[]{:S(2)}) %collective-permute-start.23) | collective-permute-done | bytes 327712 | tf_op jit(solution)/shard_map/ppermute | solution.py:44
  119.7 14.9 %all_to_all.20 = f32[16,8,768]{2,1,0:T(8,128)S(1)} all-to-all(f32[16,8,768]{2,1,0:T(8,128)S(1)} %bitcast.76), channel_id=1, replica_groups=mesh['grp'=2,'dp'=16,'mp'=4] {'dp'}, dimensions={0} | all-to-all | bytes 786432 | tf_op jit(solution)/shard_map/all_to_all | solution.py:447
  134.6 12.4 %all_to_all.21 = f32[16,8,768]{2,1,0:T(8,128)S(1)} all-to-all(f32[16,8,768]{2,1,0:T(8,128)S(1)} %broadcast_in_dim.72), channel_id=1, replica_groups=mesh['grp'=2,'dp'=16,'mp'=4] {'dp'}, dimensions={0} | all-to-all | bytes 786432 | tf_op jit(solution)/shard_map/all_to_all | solution.py:58
  (142 shorter events, 33.0 us)
Async XLA Ops:
  2.5 49.0 %collective-permute-start.2 = (bf16[32,5120]{1,0:T(8,128)(2,1)}, bf16[32,5120]{1,0:T(8,128)(2,1)}, u32[]{:S(2)}, u32[]{:S(2)}) collective-permute-start(bf16[32,5120]{1,0:T(8,128)(2,1)} %constant_dynamic-slice_fusion.11), channel_id=1, source_target_pairs={{0,3},{1,0},{2,1},{3,2},{4,7},{5,4},{6,5},{7,6},{8,11},{9,8},{10,9... | collective-permute-start | bytes 983048 | tf_op jit(solution)/shard_map/ppermute | solution.py:40
  5.6 42.5 %collective-permute-start = (bf16[32,5120]{1,0:T(8,128)(2,1)}, bf16[32,5120]{1,0:T(8,128)(2,1)}, u32[]{:S(2)}, u32[]{:S(2)}) collective-permute-start(bf16[32,5120]{1,0:T(8,128)(2,1)} %constant_dynamic-slice_fusion.11), channel_id=1, source_target_pairs={{0,1},{1,2},{2,3},{3,0},{4,5},{5,6},{6,7},{7,4},{8,9},{9,10},{10,1... | collective-permute-start | bytes 983048 | tf_op jit(solution)/shard_map/ppermute | solution.py:40
  6.5 17.7 %collective-permute-start.5 = (bf16[128,512]{1,0:T(8,128)(2,1)S(1)}, bf16[128,512]{1,0:T(8,128)(2,1)S(1)}, u32[]{:S(2)}, u32[]{:S(2)}) collective-permute-start(bf16[128,512]{1,0:T(8,128)(2,1)S(1)} %constant_dynamic-slice_fusion.9), channel_id=1, source_target_pairs={{0,0},{1,16},{2,32},{3,48},{4,4},{5,20},{6,36},{7,52},{8,8},{9,24}... | collective-permute-start | bytes 393224 | tf_op jit(solution)/shard_map/ppermute | solution.py:287
  8.8 40.4 %all-to-all-start = ((bf16[64,32,128]{2,1,0:T(8,128)(2,1)}), bf16[64,32,128]{2,1,0:T(8,128)(2,1)}, u32[]{:S(2)}, u32[]{:S(2)}) async-start(bf16[64,32,128]{2,1,0:T(8,128)(2,1)} %broadcast_in_dim.35), calls=%async_computation | async-start | bytes 1048576 | tf_op jit(solution)/shard_map/all_to_all | solution.py:58
  24.2 11.7 %collective-permute-start.6 = (bf16[192,512]{1,0:T(8,128)(2,1)S(1)}, bf16[192,512]{1,0:T(8,128)(2,1)S(1)}, u32[]{:S(2)}, u32[]{:S(2)}) collective-permute-start(bf16[192,512]{1,0:T(8,128)(2,1)S(1)} %get-tuple-element.42), channel_id=1, source_target_pairs={{0,48},{4,52},{8,56},{12,60},{16,0},{20,4},{24,8},{28,12},{32,16},... | collective-permute-start | bytes 589832 | tf_op jit(solution)/shard_map/ppermute | solution.py:53
  27.3 10.5 %collective-permute-start.7 = (bf16[192,512]{1,0:T(8,128)(2,1)S(1)}, bf16[192,512]{1,0:T(8,128)(2,1)S(1)}, u32[]{:S(2)}, u32[]{:S(2)}) collective-permute-start(bf16[192,512]{1,0:T(8,128)(2,1)S(1)} %get-tuple-element.41), channel_id=1, source_target_pairs={{0,32},{4,36},{8,40},{12,44},{16,48},{20,52},{24,56},{28,60},{32,0... | collective-permute-start | bytes 589832 | tf_op jit(solution)/shard_map/ppermute | solution.py:53
  28.0 13.5 %collective-permute-start.8 = (bf16[192,512]{1,0:T(8,128)(2,1)S(1)}, bf16[192,512]{1,0:T(8,128)(2,1)S(1)}, u32[]{:S(2)}, u32[]{:S(2)}) collective-permute-start(bf16[192,512]{1,0:T(8,128)(2,1)S(1)} %get-tuple-element.40), channel_id=1, source_target_pairs={{0,16},{4,20},{8,24},{12,28},{16,32},{20,36},{24,40},{28,44},{32,4... | collective-permute-start | bytes 589832 | tf_op jit(solution)/shard_map/ppermute | solution.py:53
  43.2 41.3 %collective-permute-start.9 = (bf16[576,512]{1,0:T(8,128)(2,1)}, bf16[576,512]{1,0:T(8,128)(2,1)S(1)}, u32[]{:S(2)}, u32[]{:S(2)}) collective-permute-start(bf16[576,512]{1,0:T(8,128)(2,1)} %get-tuple-element.25), channel_id=1, source_target_pairs={{0,4},{4,8},{8,12},{12,0},{16,20},{20,24},{24,28},{28,16},{32,36},... | collective-permute-start | bytes 1769480 | tf_op jit(solution)/shard_map/ppermute | solution.py:53
  43.8 40.7 %collective-permute-start.10 = (bf16[576,512]{1,0:T(8,128)(2,1)}, bf16[576,512]{1,0:T(8,128)(2,1)S(1)}, u32[]{:S(2)}, u32[]{:S(2)}) collective-permute-start(bf16[576,512]{1,0:T(8,128)(2,1)} %get-tuple-element.26), channel_id=1, source_target_pairs={{0,8},{4,12},{8,0},{12,4},{16,24},{20,28},{24,16},{28,20},{32,40},... | collective-permute-start | bytes 1769480 | tf_op jit(solution)/shard_map/ppermute | solution.py:53
  46.5 38.1 %collective-permute-start.11 = (bf16[576,512]{1,0:T(8,128)(2,1)}, bf16[576,512]{1,0:T(8,128)(2,1)S(1)}, u32[]{:S(2)}, u32[]{:S(2)}) collective-permute-start(bf16[576,512]{1,0:T(8,128)(2,1)} %get-tuple-element.24), channel_id=1, source_target_pairs={{0,12},{4,0},{8,4},{12,8},{16,28},{20,16},{24,20},{28,24},{32,44},... | collective-permute-start | bytes 1769480 | tf_op jit(solution)/shard_map/ppermute | solution.py:53
  48.1 10.4 %collective-permute-start.1 = (bf16[32,5120]{1,0:T(8,128)(2,1)}, bf16[32,5120]{1,0:T(8,128)(2,1)}, u32[]{:S(2)}, u32[]{:S(2)}) collective-permute-start(bf16[32,5120]{1,0:T(8,128)(2,1)} %collective-permute-done), channel_id=1, source_target_pairs={{0,1},{1,2},{2,3},{3,0},{4,5},{5,6},{6,7},{7,4},{8,9},{9,10},{10,1... | collective-permute-start | bytes 983048 | tf_op jit(solution)/shard_map/ppermute | solution.py:40
  51.5 9.3 %collective-permute-start.4 = (bf16[32,8192]{1,0:T(8,128)(2,1)S(1)}, bf16[32,8192]{1,0:T(8,128)(2,1)S(1)}, u32[]{:S(2)}, u32[]{:S(2)}) collective-permute-start(bf16[32,8192]{1,0:T(8,128)(2,1)S(1)} %copy_bitcast_fusion), channel_id=1, source_target_pairs={{0,64},{64,0},{1,65},{65,1},{2,66},{66,2},{3,67},{67,3},{4,68},{68... | collective-permute-start | bytes 1572872 | tf_op jit(solution)/shard_map/ppermute | solution.py:44
  63.4 11.7 %collective-permute-start.19 = (f32[32,9216]{1,0:T(8,128)S(1)}, f32[32,9216]{1,0:T(8,128)S(1)}, u32[]{:S(2)}, u32[]{:S(2)}) collective-permute-start(f32[32,9216]{1,0:T(8,128)S(1)} %pad_maximum_fusion.1), channel_id=1, source_target_pairs={{0,64},{64,0},{1,65},{65,1},{2,66},{66,2},{3,67},{67,3},{4,68},{68... | collective-permute-start | bytes 3538952 | tf_op jit(solution)/shard_map/ppermute | solution.py:44
  74.6 9.9 %collective-permute-start.3 = (bf16[128,2048]{1,0:T(8,128)(2,1)}, bf16[128,2048]{1,0:T(8,128)(2,1)}, u32[]{:S(2)}, u32[]{:S(2)}) collective-permute-start(bf16[128,2048]{1,0:T(8,128)(2,1)} %fusion.4.near), channel_id=1, source_target_pairs={{0,64},{64,0},{1,65},{65,1},{2,66},{66,2},{3,67},{67,3},{4,68},{68... | collective-permute-start | bytes 1572872 | tf_op jit(solution)/shard_map/ppermute | solution.py:44
  77.1 19.3 %all-to-all-start.1 = ((bf16[64,32,128]{2,1,0:T(8,128)(2,1)}), bf16[64,32,128]{2,1,0:T(8,128)(2,1)}, u32[]{:S(2)}, u32[]{:S(2)}) async-start(bf16[64,32,128]{2,1,0:T(8,128)(2,1)} %bitcast_bitcast_fusion), calls=%async_computation.1 | async-start | bytes 1048576 | tf_op jit(solution)/shard_map/all_to_all | solution.py:402
  88.5 13.2 %collective-permute-start.12 = (bf16[64,1152]{1,0:T(8,128)(2,1)}, bf16[64,1152]{1,0:T(8,128)(2,1)S(1)}, u32[]{:S(2)}, u32[]{:S(2)}) collective-permute-start(bf16[64,1152]{1,0:T(8,128)(2,1)} %get-tuple-element.14), channel_id=1, source_target_pairs={{0,3},{1,0},{2,1},{3,2},{4,7},{5,4},{6,5},{7,6},{8,11},{9,8},{10,9... | collective-permute-start | bytes 442376 | tf_op jit(solution)/shard_map/ppermute | solution.py:40
  91.1 12.4 %collective-permute-start.13 = (bf16[64,1152]{1,0:T(8,128)(2,1)}, bf16[64,1152]{1,0:T(8,128)(2,1)}, u32[]{:S(2)}, u32[]{:S(2)}) collective-permute-start(bf16[64,1152]{1,0:T(8,128)(2,1)} %get-tuple-element.15), channel_id=1, source_target_pairs={{0,2},{1,3},{2,0},{3,1},{4,6},{5,7},{6,4},{7,5},{8,10},{9,11},{10,... | collective-permute-start | bytes 442376 | tf_op jit(solution)/shard_map/ppermute | solution.py:40
  92.0 11.6 %collective-permute-start.14 = (bf16[64,1152]{1,0:T(8,128)(2,1)}, bf16[64,1152]{1,0:T(8,128)(2,1)}, u32[]{:S(2)}, u32[]{:S(2)}) collective-permute-start(bf16[64,1152]{1,0:T(8,128)(2,1)} %get-tuple-element.16), channel_id=1, source_target_pairs={{0,1},{1,2},{2,3},{3,0},{4,5},{5,6},{6,7},{7,4},{8,9},{9,10},{10,1... | collective-permute-start | bytes 442376 | tf_op jit(solution)/shard_map/ppermute | solution.py:40
  99.6 8.4 %collective-permute-start.22 = (f32[32,1024]{1,0:T(8,128)S(1)}, f32[32,1024]{1,0:T(8,128)S(1)}, u32[]{:S(2)}, u32[]{:S(2)}) collective-permute-start(f32[32,1024]{1,0:T(8,128)S(1)} %slice_add_fusion.1), channel_id=1, source_target_pairs={{0,3},{1,0},{2,1},{3,2},{4,7},{5,4},{6,5},{7,6},{8,11},{9,8},{10,9... | collective-permute-start | bytes 393224 | tf_op jit(solution)/shard_map/ppermute | solution.py:40
  100.3 9.9 %collective-permute-start.20 = (f32[32,1024]{1,0:T(8,128)S(1)}, f32[32,1024]{1,0:T(8,128)S(1)}, u32[]{:S(2)}, u32[]{:S(2)}) collective-permute-start(f32[32,1024]{1,0:T(8,128)S(1)} %slice_add_fusion.1), channel_id=1, source_target_pairs={{0,1},{1,2},{2,3},{3,0},{4,5},{5,6},{6,7},{7,4},{8,9},{9,10},{10,1... | collective-permute-start | bytes 393224 | tf_op jit(solution)/shard_map/ppermute | solution.py:40
  101.7 9.8 %collective-permute-start.21 = (f32[32,1024]{1,0:T(8,128)S(1)}, f32[32,1024]{1,0:T(8,128)S(1)}, u32[]{:S(2)}, u32[]{:S(2)}) collective-permute-start(f32[32,1024]{1,0:T(8,128)S(1)} %slice_add_fusion.1), channel_id=1, source_target_pairs={{0,2},{1,3},{2,0},{3,1},{4,6},{5,7},{6,4},{7,5},{8,10},{9,11},{10,... | collective-permute-start | bytes 393224 | tf_op jit(solution)/shard_map/ppermute | solution.py:40
  103.6 7.9 %collective-permute-start.18 = (bf16[128,64]{1,0:T(8,128)(2,1)S(1)}, bf16[128,64]{1,0:T(8,128)(2,1)S(1)}, u32[]{:S(2)}, u32[]{:S(2)}) collective-permute-start(bf16[128,64]{1,0:T(8,128)(2,1)S(1)} %convolution_convert_fusion.low_near), channel_id=1, source_target_pairs={{0,64},{64,0},{1,65},{65,1},{2,66},{66,2},{3,67},{67,3},{4,68},{68... | collective-permute-start | bytes 49160 | tf_op jit(solution)/shard_map/ppermute | solution.py:44
  106.2 6.1 %collective-permute-start.15 = (bf16[64,640]{1,0:T(8,128)(2,1)S(1)}, bf16[64,640]{1,0:T(8,128)(2,1)S(1)}, u32[]{:S(2)}, u32[]{:S(2)}) collective-permute-start(bf16[64,640]{1,0:T(8,128)(2,1)S(1)} %row_work.1.packed), channel_id=1, source_target_pairs={{0,1},{1,2},{2,3},{3,0},{4,5},{5,6},{6,7},{7,4},{8,9},{9,10},{10,1... | collective-permute-start | bytes 245768 | tf_op jit(solution)/shard_map/ppermute | solution.py:40
  108.0 6.8 %collective-permute-start.16 = (bf16[64,640]{1,0:T(8,128)(2,1)S(1)}, bf16[64,640]{1,0:T(8,128)(2,1)S(1)}, u32[]{:S(2)}, u32[]{:S(2)}) collective-permute-start(bf16[64,640]{1,0:T(8,128)(2,1)S(1)} %row_work.1.packed), channel_id=1, source_target_pairs={{0,2},{1,3},{2,0},{3,1},{4,6},{5,7},{6,4},{7,5},{8,10},{9,11},{10,... | collective-permute-start | bytes 245768 | tf_op jit(solution)/shard_map/ppermute | solution.py:40
  (19 other events, 202.7 us)

commit v10 on v9

--- a/solution.py
+++ b/solution.py
@@ -237,6 +237,17 @@
         give[:, here] = ranks[pl.ds(pl.multiple_of((1 - place[1]) * half, half), half), :]
 
 
+def place_kernel(whole, enc, llm, *, side):
+    rows = whole.shape[1]
+    enc_step, llm_step = enc.shape[1] // side, llm.shape[1] // side
+    for i in range(side):
+        for j in range(side):
+            here = slice(i * rows, (i + 1) * rows)
+            part = whole[i * side + j]
+            enc[here, j * enc_step : (j + 1) * enc_step] = part[:, :enc_step]
+            llm[here, j * llm_step : (j + 1) * llm_step] = part[:, enc_step:]
+
+
 def body(
     hidden,
     enc_weight,
@@ -316,8 +327,9 @@
     text_inverse = lax.rsqrt(jnp.mean(text_wide * text_wide, axis=1, keepdims=True) + epsilon)
 
     a_half = cut(llm_frozen.T, grp * half_rank, half_rank)
-    a_mine = to_everyone(a_half, ("dp", "mp")).transpose(1, 0, 2).reshape(half_rank, width)
-    a_all = jnp.concatenate([a_mine, crossed(a_mine)])
+    a_mine = to_everyone(a_half, ("dp", "mp"))
+    a_both = [a.transpose(1, 0, 2).reshape(half_rank, width) for a in (a_mine, crossed(a_mine))]
+    a_all = jnp.concatenate(a_both)
     a_part = cut(a_all, mp * part_width, part_width, 1)
     b_all = jnp.where(first, llm_adapter, jnp.roll(llm_adapter, half_rank, axis=0))
     b_half = cut(b_all, grp * half_kv, half_kv, 1)
@@ -445,9 +457,18 @@
     ).reshape(side, 8, side, -1)
     mine = jnp.concatenate([enc, llm], axis=3).transpose(0, 2, 1, 3).reshape(n_dp, 8, -1)
     mine = jnp.sum(lax.all_to_all(mine, "dp", 0, 0, tiled=True), axis=0)
-    whole = to_everyone(mine, "dp").reshape(side, side, 8, -1).transpose(0, 2, 1, 3)
-    at = part_width // side
-    return whole[..., :at].reshape(half_rank, -1), whole[..., at:].reshape(half_rank, -1)
+    whole = to_everyone(mine, "dp")
+    return pl.pallas_call(
+        functools.partial(place_kernel, side=side),
+        out_shape=(
+            jax.ShapeDtypeStruct((half_rank, part_width), f32),
+            jax.ShapeDtypeStruct((half_rank, kv), f32),
+        ),
+        in_specs=[VMEM],
+        out_specs=(VMEM, VMEM),
+        compiler_params=PARAMS,
+        name="placed",
+    )(whole)
 
 
 def solution(mesh):

time: 149 us -> 149 us (level)
  local copies, waits for them, and re-layouts: 14.8 us -> 12.2 us
    unnamed x41 -> x39, local copies, waits for them, and re-layouts: 5.78 us -> 5.65 us
  transfers between devices with their start and end apart: 26 -> 26, of which waited for: 8 -> 8; matrix products, arithmetic and copies ran while one was open for 20% -> 19% of each run, Pallas kernels for 3% -> 3%
where the time goes in v10:
time: 149 us; the launch traced here: 148 us
  starting transfers between devices  47.1 us (32%)
  waiting for transfers between devices  29 us (19%)
  blocking collectives  27.3 us (18%)
  matrix products  16.4 us (11%)
  local copies, waits for them, and re-layouts  12.2 us (8%)
  Pallas kernels  8.65 us (6%)
  other arithmetic  5.26 us (4%)
  between operations  2.08 us (1%)
    ppermute x12, starting transfers between devices, turned(): lax.ppermute(array, axis, [(i, (i + step) % count) for i in range(count)])  16.4 us
    all_to_all x1, blocking collectives, body(): mine = jnp.sum(lax.all_to_all(mine, 'dp', 0, 0, tiled=True), axis=0)  14.9 us
    dot_general x5, matrix products, dot(): return jnp.dot(a, b, preferred_element_type=f32)  14.9 us
    all_to_all x1, starting transfers between devices, to_everyone(): lax.all_to_all(jnp.broadcast_to(array[None], (count, *array.shape)), axes...  14.3 us
    all_to_all x1, blocking collectives, to_everyone(): lax.all_to_all(jnp.broadcast_to(array[None], (count, *array.shape)), axes...  12.4 us
    ppermute x6, waiting for transfers between devices, along(): return lax.ppermute(array, 'dp', pairs)  12.4 us
    ppermute x12, waiting for transfers between devices, turned(): lax.ppermute(array, axis, [(i, (i + step) % count) for i in range(count)])  11.5 us
    ppermute x6, starting transfers between devices, along(): return lax.ppermute(array, 'dp', pairs)  9.31 us
  transfers between devices with their start and end apart: 26, of which 8 were waited for; matrix products, arithmetic and copies ran while one was open for 19% of the time, Pallas kernels for 3%

profile of v10, /device:TPU:0, one launch (start us, length us, event | category | flops | bytes accessed | tf_op | source)
XLA Modules:
  0.0 147.9 jit_solution(11556656863206085884)
XLA Ops:
  2.5 3.1 %collective-permute-start.2 = (bf16[32,5120]{1,0:T(8,128)(2,1)}, bf16[32,5120]{1,0:T(8,128)(2,1)}, u32[]{:S(2)}, u32[]{:S(2)}) collective-permute-start(bf16[32,5120]{1,0:T(8,128)(2,1)} %constant_dynamic-slice_fusion.11), channel_id=1, source_target_pairs={{0,3},{1,0},{2,1},{3,2},{4,7},{5,4},{6,5},{7,6},{8,11},{9,8},{10,9... | collective-permute-start | bytes 983048 | tf_op jit(solution)/shard_map/ppermute | solution.py:40
  8.7 14.3 %all-to-all-start = ((bf16[64,32,128]{2,1,0:T(8,128)(2,1)}), bf16[64,32,128]{2,1,0:T(8,128)(2,1)}, u32[]{:S(2)}, u32[]{:S(2)}) async-start(bf16[64,32,128]{2,1,0:T(8,128)(2,1)} %broadcast_in_dim.35), calls=%async_computation | async-start | bytes 1048576 | tf_op jit(solution)/shard_map/all_to_all | solution.py:58
  24.2 3.0 %collective-permute-start.6 = (bf16[192,512]{1,0:T(8,128)(2,1)S(1)}, bf16[192,512]{1,0:T(8,128)(2,1)S(1)}, u32[]{:S(2)}, u32[]{:S(2)}) collective-permute-start(bf16[192,512]{1,0:T(8,128)(2,1)S(1)} %get-tuple-element.42), channel_id=1, source_target_pairs={{0,48},{4,52},{8,56},{12,60},{16,0},{20,4},{24,8},{28,12},{32,16},... | collective-permute-start | bytes 589832 | tf_op jit(solution)/shard_map/ppermute | solution.py:53
  28.9 7.0 %collective-permute-done.6 = bf16[192,512]{1,0:T(8,128)(2,1)S(1)} collective-permute-done((bf16[192,512]{1,0:T(8,128)(2,1)S(1)}, bf16[192,512]{1,0:T(8,128)(2,1)S(1)}, u32[]{:S(2)}, u32[]{:S(2)}) %collective-permute-start.6) | collective-permute-done | bytes 196640 | tf_op jit(solution)/shard_map/ppermute | solution.py:53
  36.1 1.6 %collective-permute-done.7 = bf16[192,512]{1,0:T(8,128)(2,1)S(1)} collective-permute-done((bf16[192,512]{1,0:T(8,128)(2,1)S(1)}, bf16[192,512]{1,0:T(8,128)(2,1)S(1)}, u32[]{:S(2)}, u32[]{:S(2)}) %collective-permute-start.7) | collective-permute-done | bytes 196640 | tf_op jit(solution)/shard_map/ppermute | solution.py:53
  37.7 3.8 %collective-permute-done.8 = bf16[192,512]{1,0:T(8,128)(2,1)S(1)} collective-permute-done((bf16[192,512]{1,0:T(8,128)(2,1)S(1)}, bf16[192,512]{1,0:T(8,128)(2,1)S(1)}, u32[]{:S(2)}, u32[]{:S(2)}) %collective-permute-start.8) | collective-permute-done | bytes 196640 | tf_op jit(solution)/shard_map/ppermute | solution.py:53
  41.8 1.4 pad_maximum_fusion.5
  43.8 2.7 %collective-permute-start.10 = (bf16[576,512]{1,0:T(8,128)(2,1)}, bf16[576,512]{1,0:T(8,128)(2,1)S(1)}, u32[]{:S(2)}, u32[]{:S(2)}) collective-permute-start(bf16[576,512]{1,0:T(8,128)(2,1)} %get-tuple-element.26), channel_id=1, source_target_pairs={{0,8},{4,12},{8,0},{12,4},{16,24},{20,28},{24,16},{28,20},{32,40},... | collective-permute-start | bytes 1769480 | tf_op jit(solution)/shard_map/ppermute | solution.py:53
  50.4 8.2 %collective-permute-done.1 = bf16[32,5120]{1,0:T(8,128)(2,1)} collective-permute-done((bf16[32,5120]{1,0:T(8,128)(2,1)}, bf16[32,5120]{1,0:T(8,128)(2,1)}, u32[]{:S(2)}, u32[]{:S(2)}) %collective-permute-start.1) | collective-permute-done | bytes 327712 | tf_op jit(solution)/shard_map/ppermute | solution.py:40
  58.6 2.1 %convolution_convert_fusion.low_near = bf16[128,64]{1,0:T(8,128)(2,1)S(1)} fusion(bf16[5120,64]{0,1:T(8,128)(2,1)} %param.17, bf16[32,5120]{1,0:T(8,128)(2,1)} %collective-permute-done.2, bf16[32,5120]{1,0:T(8,128)(2,1)} %collective-permute-done.1, bf16[32,5120]{1,0:T(8,128)(2,1)} %collective-permute-done, bf16[32,5120]{1,0:T(8,128)(2,1)} %constant_dynamic-slice_fusion.11), kind=kOutput, calls=%fused_computation.18 | convolution fusion | flops 89137152 | bytes 1982464 | tf_op jit(solution)/shard_map/dot_general | solution.py:17
  63.7 11.1 %fusion.4.near = bf16[128,2048]{1,0:T(8,128)(2,1)} fusion(f32[128,2048]{1,0:T(8,128)S(1)} %fusion.51, bf16[5120,2048]{1,0:T(8,128)(2,1)} %param.15, f32[2048]{0:T(1024)S(1)} %convert_element_type.78, bf16[32,5120]{1,0:T(8,128)(2,1)} %collective-permute-done.2, bf16[32,5120]{1,0:T(8,128)(2,1)} %collective-permute-done.1, ...), kind=kOutput, calls=%fused_computation.8 | convolution fusion | flops 2690383872 | bytes 23863296 | tf_op jit(solution)/shard_map/dot_general | solution.py:17
  77.3 5.7 %all-to-all-start.1 = ((bf16[64,32,128]{2,1,0:T(8,128)(2,1)}), bf16[64,32,128]{2,1,0:T(8,128)(2,1)}, u32[]{:S(2)}, u32[]{:S(2)}) async-start(bf16[64,32,128]{2,1,0:T(8,128)(2,1)} %bitcast_bitcast_fusion), calls=%async_computation.1 | async-start | bytes 1048576 | tf_op jit(solution)/shard_map/all_to_all | solution.py:414
  84.7 3.2 %partial_products.1 = (f32[64,1152]{1,0:T(8,128)S(1)}, bf16[64,1152]{1,0:T(8,128)(2,1)}, bf16[64,1152]{1,0:T(8,128)(2,1)}, bf16[64,1152]{1,0:T(8,128)(2,1)}) custom-call(s32[2]{0:T(128)S(1)} %pad_add_fusion.place, bf16[128,2048]{1,0:T(8,128)(2,1)} %fusion.4.near, bf16[128,2048]{1,0:T(8,128)(2,1)} %collective-permute-done.3.far, f32[1,2048]{1,0:T(1,128)S(1)} %bitcast.70, ...), custom_call_target="tpu_custom_call" | custom-call | tf_op jit(solution)/shard_map/partial_products/pallas_call | solution.py:395
  88.7 2.6 %collective-permute-start.12 = (bf16[64,1152]{1,0:T(8,128)(2,1)}, bf16[64,1152]{1,0:T(8,128)(2,1)S(1)}, u32[]{:S(2)}, u32[]{:S(2)}) collective-permute-start(bf16[64,1152]{1,0:T(8,128)(2,1)} %get-tuple-element.14), channel_id=1, source_target_pairs={{0,3},{1,0},{2,1},{3,2},{4,7},{5,4},{6,5},{7,6},{8,11},{9,8},{10,9... | collective-permute-start | bytes 442376 | tf_op jit(solution)/shard_map/ppermute | solution.py:40
  93.0 3.6 %all-to-all-done.1 = bf16[64,32,128]{2,1,0:T(8,128)(2,1)} async-done(((bf16[64,32,128]{2,1,0:T(8,128)(2,1)}), bf16[64,32,128]{2,1,0:T(8,128)(2,1)}, u32[]{:S(2)}, u32[]{:S(2)}) %all-to-all-start.1) | async-done | bytes 524320 | tf_op jit(solution)/shard_map/all_to_all | solution.py:414
  100.5 1.4 collective-permute-start.20
  104.7 1.6 %row_work.1.packed = bf16[64,640]{1,0:T(8,128)(2,1)S(1)} custom-call(f32[64,1152]{1,0:T(8,128)S(1)} %copy-done.2, bf16[64,1152]{1,0:T(8,128)(2,1)S(1)} %collective-permute-done.12.got1, bf16[64,1152]{1,0:T(8,128)(2,1)} %collective-permute-done.13.got2, bf16[64,1152]{1,0:T(8,128)(2,1)} %collective-permute-done.14.got3, ...), custom_call_target="tpu_custom_call" | custom-call | tf_op jit(solution)/shard_map/row_work/pallas_call | solution.py:405
  106.4 1.8 %collective-permute-start.15 = (bf16[64,640]{1,0:T(8,128)(2,1)S(1)}, bf16[64,640]{1,0:T(8,128)(2,1)S(1)}, u32[]{:S(2)}, u32[]{:S(2)}) collective-permute-start(bf16[64,640]{1,0:T(8,128)(2,1)S(1)} %row_work.1.packed), channel_id=1, source_target_pairs={{0,1},{1,2},{2,3},{3,0},{4,5},{5,6},{6,7},{7,4},{8,9},{9,10},{10,1... | collective-permute-start | bytes 245768 | tf_op jit(solution)/shard_map/ppermute | solution.py:40
  108.2 2.2 %collective-permute-start.16 = (bf16[64,640]{1,0:T(8,128)(2,1)S(1)}, bf16[64,640]{1,0:T(8,128)(2,1)S(1)}, u32[]{:S(2)}, u32[]{:S(2)}) collective-permute-start(bf16[64,640]{1,0:T(8,128)(2,1)S(1)} %row_work.1.packed), channel_id=1, source_target_pairs={{0,2},{1,3},{2,0},{3,1},{4,6},{5,7},{6,4},{7,5},{8,10},{9,11},{10,... | collective-permute-start | bytes 245768 | tf_op jit(solution)/shard_map/ppermute | solution.py:40
  112.5 2.5 %collective-permute-done.16.got2 = bf16[64,640]{1,0:T(8,128)(2,1)S(1)} collective-permute-done((bf16[64,640]{1,0:T(8,128)(2,1)S(1)}, bf16[64,640]{1,0:T(8,128)(2,1)S(1)}, u32[]{:S(2)}, u32[]{:S(2)}) %collective-permute-start.16) | collective-permute-done | bytes 81952 | tf_op jit(solution)/shard_map/ppermute | solution.py:40
  115.0 3.0 %image_gradients.1 = (f32[32,2560]{1,0:T(8,128)S(1)}, f32[32,2560]{1,0:T(8,128)S(1)}) custom-call(s32[2]{0:T(128)S(1)} %pad_add_fusion.place, bf16[64,640]{1,0:T(8,128)(2,1)S(1)} %row_work.1.packed, bf16[64,640]{1,0:T(8,128)(2,1)S(1)} %collective-permute-done.15.got1, bf16[64,640]{1,0:T(8,128)(2,1)S(1)} %collective-permute-done.16.got2, ...), custom_call_target="tpu_custom_call" | custom-call | tf_op jit(solution)/shard_map/image_gradients/pallas_call | solution.py:424
  118.1 1.6 %collective-permute-done.23 = f32[32,2560]{1,0:T(8,128)S(1)} collective-permute-done((f32[32,2560]{1,0:T(8,128)S(1)}, f32[32,2560]{1,0:T(8,128)S(1)}, u32[]{:S(2)}, u32[]{:S(2)}) %collective-permute-start.23) | collective-permute-done | bytes 327712 | tf_op jit(solution)/shard_map/ppermute | solution.py:44
  119.8 14.9 %all_to_all.20 = f32[16,8,768]{2,1,0:T(8,128)S(1)} all-to-all(f32[16,8,768]{2,1,0:T(8,128)S(1)} %bitcast.73), channel_id=1, replica_groups=mesh['grp'=2,'dp'=16,'mp'=4] {'dp'}, dimensions={0} | all-to-all | bytes 786432 | tf_op jit(solution)/shard_map/all_to_all | solution.py:459
  134.8 12.4 %all_to_all.21.whole = f32[16,8,768]{2,1,0:T(8,128)S(1)} all-to-all(f32[16,8,768]{2,1,0:T(8,128)S(1)} %broadcast_in_dim.72), channel_id=1, replica_groups=mesh['grp'=2,'dp'=16,'mp'=4] {'dp'}, dimensions={0} | all-to-all | bytes 786432 | tf_op jit(solution)/shard_map/all_to_all | solution.py:58
  (138 shorter events, 31.2 us)
Async XLA Ops:
  2.5 47.8 %collective-permute-start.2 = (bf16[32,5120]{1,0:T(8,128)(2,1)}, bf16[32,5120]{1,0:T(8,128)(2,1)}, u32[]{:S(2)}, u32[]{:S(2)}) collective-permute-start(bf16[32,5120]{1,0:T(8,128)(2,1)} %constant_dynamic-slice_fusion.11), channel_id=1, source_target_pairs={{0,3},{1,0},{2,1},{3,2},{4,7},{5,4},{6,5},{7,6},{8,11},{9,8},{10,9... | collective-permute-start | bytes 983048 | tf_op jit(solution)/shard_map/ppermute | solution.py:40
  5.6 42.6 %collective-permute-start = (bf16[32,5120]{1,0:T(8,128)(2,1)}, bf16[32,5120]{1,0:T(8,128)(2,1)}, u32[]{:S(2)}, u32[]{:S(2)}) collective-permute-start(bf16[32,5120]{1,0:T(8,128)(2,1)} %constant_dynamic-slice_fusion.11), channel_id=1, source_target_pairs={{0,1},{1,2},{2,3},{3,0},{4,5},{5,6},{6,7},{7,4},{8,9},{9,10},{10,1... | collective-permute-start | bytes 983048 | tf_op jit(solution)/shard_map/ppermute | solution.py:40
  6.5 17.7 %collective-permute-start.5 = (bf16[128,512]{1,0:T(8,128)(2,1)S(1)}, bf16[128,512]{1,0:T(8,128)(2,1)S(1)}, u32[]{:S(2)}, u32[]{:S(2)}) collective-permute-start(bf16[128,512]{1,0:T(8,128)(2,1)S(1)} %constant_dynamic-slice_fusion.9), channel_id=1, source_target_pairs={{0,0},{1,16},{2,32},{3,48},{4,4},{5,20},{6,36},{7,52},{8,8},{9,24}... | collective-permute-start | bytes 393224 | tf_op jit(solution)/shard_map/ppermute | solution.py:298
  8.7 40.4 %all-to-all-start = ((bf16[64,32,128]{2,1,0:T(8,128)(2,1)}), bf16[64,32,128]{2,1,0:T(8,128)(2,1)}, u32[]{:S(2)}, u32[]{:S(2)}) async-start(bf16[64,32,128]{2,1,0:T(8,128)(2,1)} %broadcast_in_dim.35), calls=%async_computation | async-start | bytes 1048576 | tf_op jit(solution)/shard_map/all_to_all | solution.py:58
  24.2 11.7 %collective-permute-start.6 = (bf16[192,512]{1,0:T(8,128)(2,1)S(1)}, bf16[192,512]{1,0:T(8,128)(2,1)S(1)}, u32[]{:S(2)}, u32[]{:S(2)}) collective-permute-start(bf16[192,512]{1,0:T(8,128)(2,1)S(1)} %get-tuple-element.42), channel_id=1, source_target_pairs={{0,48},{4,52},{8,56},{12,60},{16,0},{20,4},{24,8},{28,12},{32,16},... | collective-permute-start | bytes 589832 | tf_op jit(solution)/shard_map/ppermute | solution.py:53
  27.3 10.5 %collective-permute-start.7 = (bf16[192,512]{1,0:T(8,128)(2,1)S(1)}, bf16[192,512]{1,0:T(8,128)(2,1)S(1)}, u32[]{:S(2)}, u32[]{:S(2)}) collective-permute-start(bf16[192,512]{1,0:T(8,128)(2,1)S(1)} %get-tuple-element.41), channel_id=1, source_target_pairs={{0,32},{4,36},{8,40},{12,44},{16,48},{20,52},{24,56},{28,60},{32,0... | collective-permute-start | bytes 589832 | tf_op jit(solution)/shard_map/ppermute | solution.py:53
  28.0 13.5 %collective-permute-start.8 = (bf16[192,512]{1,0:T(8,128)(2,1)S(1)}, bf16[192,512]{1,0:T(8,128)(2,1)S(1)}, u32[]{:S(2)}, u32[]{:S(2)}) collective-permute-start(bf16[192,512]{1,0:T(8,128)(2,1)S(1)} %get-tuple-element.40), channel_id=1, source_target_pairs={{0,16},{4,20},{8,24},{12,28},{16,32},{20,36},{24,40},{28,44},{32,4... | collective-permute-start | bytes 589832 | tf_op jit(solution)/shard_map/ppermute | solution.py:53
  43.2 41.5 %collective-permute-start.9 = (bf16[576,512]{1,0:T(8,128)(2,1)}, bf16[576,512]{1,0:T(8,128)(2,1)S(1)}, u32[]{:S(2)}, u32[]{:S(2)}) collective-permute-start(bf16[576,512]{1,0:T(8,128)(2,1)} %get-tuple-element.25), channel_id=1, source_target_pairs={{0,4},{4,8},{8,12},{12,0},{16,20},{20,24},{24,28},{28,16},{32,36},... | collective-permute-start | bytes 1769480 | tf_op jit(solution)/shard_map/ppermute | solution.py:53
  43.8 40.9 %collective-permute-start.10 = (bf16[576,512]{1,0:T(8,128)(2,1)}, bf16[576,512]{1,0:T(8,128)(2,1)S(1)}, u32[]{:S(2)}, u32[]{:S(2)}) collective-permute-start(bf16[576,512]{1,0:T(8,128)(2,1)} %get-tuple-element.26), channel_id=1, source_target_pairs={{0,8},{4,12},{8,0},{12,4},{16,24},{20,28},{24,16},{28,20},{32,40},... | collective-permute-start | bytes 1769480 | tf_op jit(solution)/shard_map/ppermute | solution.py:53
  46.5 38.2 %collective-permute-start.11 = (bf16[576,512]{1,0:T(8,128)(2,1)}, bf16[576,512]{1,0:T(8,128)(2,1)S(1)}, u32[]{:S(2)}, u32[]{:S(2)}) collective-permute-start(bf16[576,512]{1,0:T(8,128)(2,1)} %get-tuple-element.24), channel_id=1, source_target_pairs={{0,12},{4,0},{8,4},{12,8},{16,28},{20,16},{24,20},{28,24},{32,44},... | collective-permute-start | bytes 1769480 | tf_op jit(solution)/shard_map/ppermute | solution.py:53
  48.1 10.4 %collective-permute-start.1 = (bf16[32,5120]{1,0:T(8,128)(2,1)}, bf16[32,5120]{1,0:T(8,128)(2,1)}, u32[]{:S(2)}, u32[]{:S(2)}) collective-permute-start(bf16[32,5120]{1,0:T(8,128)(2,1)} %collective-permute-done), channel_id=1, source_target_pairs={{0,1},{1,2},{2,3},{3,0},{4,5},{5,6},{6,7},{7,4},{8,9},{9,10},{10,1... | collective-permute-start | bytes 983048 | tf_op jit(solution)/shard_map/ppermute | solution.py:40
  50.3 10.7 %collective-permute-start.4 = (bf16[64,32,128]{2,1,0:T(8,128)(2,1)}, bf16[64,32,128]{2,1,0:T(8,128)(2,1)S(1)}, u32[]{:S(2)}, u32[]{:S(2)}) collective-permute-start(bf16[64,32,128]{2,1,0:T(8,128)(2,1)} %all-to-all-done), channel_id=1, source_target_pairs={{0,64},{64,0},{1,65},{65,1},{2,66},{66,2},{3,67},{67,3},{4,68},{68... | collective-permute-start | bytes 1572872 | tf_op jit(solution)/shard_map/ppermute | solution.py:44
  63.6 11.7 %collective-permute-start.19 = (f32[32,9216]{1,0:T(8,128)S(1)}, f32[32,9216]{1,0:T(8,128)S(1)}, u32[]{:S(2)}, u32[]{:S(2)}) collective-permute-start(f32[32,9216]{1,0:T(8,128)S(1)} %pad_maximum_fusion.1), channel_id=1, source_target_pairs={{0,64},{64,0},{1,65},{65,1},{2,66},{66,2},{3,67},{67,3},{4,68},{68... | collective-permute-start | bytes 3538952 | tf_op jit(solution)/shard_map/ppermute | solution.py:44
  74.8 10.0 %collective-permute-start.3 = (bf16[128,2048]{1,0:T(8,128)(2,1)}, bf16[128,2048]{1,0:T(8,128)(2,1)}, u32[]{:S(2)}, u32[]{:S(2)}) collective-permute-start(bf16[128,2048]{1,0:T(8,128)(2,1)} %fusion.4.near), channel_id=1, source_target_pairs={{0,64},{64,0},{1,65},{65,1},{2,66},{66,2},{3,67},{67,3},{4,68},{68... | collective-permute-start | bytes 1572872 | tf_op jit(solution)/shard_map/ppermute | solution.py:44
  77.3 19.3 %all-to-all-start.1 = ((bf16[64,32,128]{2,1,0:T(8,128)(2,1)}), bf16[64,32,128]{2,1,0:T(8,128)(2,1)}, u32[]{:S(2)}, u32[]{:S(2)}) async-start(bf16[64,32,128]{2,1,0:T(8,128)(2,1)} %bitcast_bitcast_fusion), calls=%async_computation.1 | async-start | bytes 1048576 | tf_op jit(solution)/shard_map/all_to_all | solution.py:414
  88.7 13.2 %collective-permute-start.12 = (bf16[64,1152]{1,0:T(8,128)(2,1)}, bf16[64,1152]{1,0:T(8,128)(2,1)S(1)}, u32[]{:S(2)}, u32[]{:S(2)}) collective-permute-start(bf16[64,1152]{1,0:T(8,128)(2,1)} %get-tuple-element.14), channel_id=1, source_target_pairs={{0,3},{1,0},{2,1},{3,2},{4,7},{5,4},{6,5},{7,6},{8,11},{9,8},{10,9... | collective-permute-start | bytes 442376 | tf_op jit(solution)/shard_map/ppermute | solution.py:40
  91.3 12.5 %collective-permute-start.13 = (bf16[64,1152]{1,0:T(8,128)(2,1)}, bf16[64,1152]{1,0:T(8,128)(2,1)}, u32[]{:S(2)}, u32[]{:S(2)}) collective-permute-start(bf16[64,1152]{1,0:T(8,128)(2,1)} %get-tuple-element.15), channel_id=1, source_target_pairs={{0,2},{1,3},{2,0},{3,1},{4,6},{5,7},{6,4},{7,5},{8,10},{9,11},{10,... | collective-permute-start | bytes 442376 | tf_op jit(solution)/shard_map/ppermute | solution.py:40
  92.1 11.6 %collective-permute-start.14 = (bf16[64,1152]{1,0:T(8,128)(2,1)}, bf16[64,1152]{1,0:T(8,128)(2,1)}, u32[]{:S(2)}, u32[]{:S(2)}) collective-permute-start(bf16[64,1152]{1,0:T(8,128)(2,1)} %get-tuple-element.16), channel_id=1, source_target_pairs={{0,1},{1,2},{2,3},{3,0},{4,5},{5,6},{6,7},{7,4},{8,9},{9,10},{10,1... | collective-permute-start | bytes 442376 | tf_op jit(solution)/shard_map/ppermute | solution.py:40
  99.8 8.4 %collective-permute-start.22 = (f32[32,1024]{1,0:T(8,128)S(1)}, f32[32,1024]{1,0:T(8,128)S(1)}, u32[]{:S(2)}, u32[]{:S(2)}) collective-permute-start(f32[32,1024]{1,0:T(8,128)S(1)} %slice_add_fusion.1), channel_id=1, source_target_pairs={{0,3},{1,0},{2,1},{3,2},{4,7},{5,4},{6,5},{7,6},{8,11},{9,8},{10,9... | collective-permute-start | bytes 393224 | tf_op jit(solution)/shard_map/ppermute | solution.py:40
  100.5 9.9 %collective-permute-start.20 = (f32[32,1024]{1,0:T(8,128)S(1)}, f32[32,1024]{1,0:T(8,128)S(1)}, u32[]{:S(2)}, u32[]{:S(2)}) collective-permute-start(f32[32,1024]{1,0:T(8,128)S(1)} %slice_add_fusion.1), channel_id=1, source_target_pairs={{0,1},{1,2},{2,3},{3,0},{4,5},{5,6},{6,7},{7,4},{8,9},{9,10},{10,1... | collective-permute-start | bytes 393224 | tf_op jit(solution)/shard_map/ppermute | solution.py:40
  101.9 9.8 %collective-permute-start.21 = (f32[32,1024]{1,0:T(8,128)S(1)}, f32[32,1024]{1,0:T(8,128)S(1)}, u32[]{:S(2)}, u32[]{:S(2)}) collective-permute-start(f32[32,1024]{1,0:T(8,128)S(1)} %slice_add_fusion.1), channel_id=1, source_target_pairs={{0,2},{1,3},{2,0},{3,1},{4,6},{5,7},{6,4},{7,5},{8,10},{9,11},{10,... | collective-permute-start | bytes 393224 | tf_op jit(solution)/shard_map/ppermute | solution.py:40
  103.8 7.9 %collective-permute-start.18 = (bf16[128,64]{1,0:T(8,128)(2,1)S(1)}, bf16[128,64]{1,0:T(8,128)(2,1)S(1)}, u32[]{:S(2)}, u32[]{:S(2)}) collective-permute-start(bf16[128,64]{1,0:T(8,128)(2,1)S(1)} %convolution_convert_fusion.low_near), channel_id=1, source_target_pairs={{0,64},{64,0},{1,65},{65,1},{2,66},{66,2},{3,67},{67,3},{4,68},{68... | collective-permute-start | bytes 49160 | tf_op jit(solution)/shard_map/ppermute | solution.py:44
  106.4 6.1 %collective-permute-start.15 = (bf16[64,640]{1,0:T(8,128)(2,1)S(1)}, bf16[64,640]{1,0:T(8,128)(2,1)S(1)}, u32[]{:S(2)}, u32[]{:S(2)}) collective-permute-start(bf16[64,640]{1,0:T(8,128)(2,1)S(1)} %row_work.1.packed), channel_id=1, source_target_pairs={{0,1},{1,2},{2,3},{3,0},{4,5},{5,6},{6,7},{7,4},{8,9},{9,10},{10,1... | collective-permute-start | bytes 245768 | tf_op jit(solution)/shard_map/ppermute | solution.py:40
  108.2 6.8 %collective-permute-start.16 = (bf16[64,640]{1,0:T(8,128)(2,1)S(1)}, bf16[64,640]{1,0:T(8,128)(2,1)S(1)}, u32[]{:S(2)}, u32[]{:S(2)}) collective-permute-start(bf16[64,640]{1,0:T(8,128)(2,1)S(1)} %row_work.1.packed), channel_id=1, source_target_pairs={{0,2},{1,3},{2,0},{3,1},{4,6},{5,7},{6,4},{7,5},{8,10},{9,11},{10,... | collective-permute-start | bytes 245768 | tf_op jit(solution)/shard_map/ppermute | solution.py:40
  (18 other events, 195.0 us)

commit v11 on v10

--- a/solution.py
+++ b/solution.py
@@ -149,7 +149,7 @@
                 own[h * step : (h + 1) * step, half_kv : half_kv + 2 * rank] = extra
 
 
-def row_kernel(own, got1, got2, got3, b_half, bias, packed, *, half_kv, rank, width):
+def row_kernel(own, got1, got2, got3, b_half, bias, text, packed, *, half_kv, rank, width):
     total = own[...]
     for got in (got1, got2, got3):
         total = total + got[...].astype(f32)
@@ -178,7 +178,11 @@
             extra = jnp.where(lane == 3 * i + j, part, extra)
             number = number - part
     packed[:, :half_kv] = dvalues
-    packed[:, half_kv:] = jnp.concatenate([low.astype(f32), extra], axis=1).astype(bf16)
+    at = half_kv + 2 * rank
+    packed[:, half_kv:at] = jnp.concatenate([low.astype(f32), extra], axis=1).astype(bf16)
+    half = text.shape[0]
+    packed[:half, at:] = text[:, :half_kv].astype(bf16)
+    packed[half:, at:] = text[:, half_kv:].astype(bf16)
 
 
 def image_kernel(
@@ -200,6 +204,7 @@
     b_half,
     mine,
     give,
+    text,
     rows,
     ranks,
     *,
@@ -214,7 +219,12 @@
     for k, source in enumerate((packed, got1, got2, got3)):
         for h in range(2):
             start = h * count + k * step
-            rows[pl.ds(start, step), :] = source[h * step : (h + 1) * step, :]
+            rows[pl.ds(start, step), :] = source[h * step : (h + 1) * step, :half_kv + 2 * rank]
+    total = packed[:, half_kv + 2 * rank :].astype(f32)
+    for source in (got1, got2, got3):
+        total = total + source[:, half_kv + 2 * rank :].astype(f32)
+    text[:, :half_kv] = total[:step]
+    text[:, half_kv:] = total[step:]
     dvalues = rows[:, :half_kv]
     extra = rows[:, half_kv:]
     low = extra[:, :rank]
@@ -402,30 +412,27 @@
         name="partial_products",
     )(where, image, image_far, gain_part, a_part, *pieces, line[:, None], position[:, None])
     got = [turned(to[k - 1], "mp", -k) for k in range(1, n_mp)]
-    packed = pl.pallas_call(
-        functools.partial(row_kernel, width=float(width), **sizes),
-        out_shape=jax.ShapeDtypeStruct((tokens, half_kv + 2 * rank), bf16),
-        in_specs=[VMEM] * 6,
-        out_specs=VMEM,
-        compiler_params=PARAMS,
-        name="row_work",
-    )(own, *got, b_half, bias_half)
     text_parts = both_sums[:, :width].reshape(half_rank, owners, shard).transpose(1, 0, 2)
     text_parts = lax.all_to_all(text_parts.astype(bf16), ("dp", "mp"), 0, 0, tiled=True)
-    got = [turned(packed, "mp", k) for k in range(1, n_mp)]
     text_here = jnp.sum(text_parts.astype(f32), axis=0)
     here_high, here_low = split_two(text_here)
     text_grad = dot(jnp.concatenate([here_high, here_low]), value_weight)
     text_grad = text_grad[:half_rank] + text_grad[half_rank:] + both_sums[:, width:]
-    text_grad = text_grad + (
-        turned(text_grad, "mp", 1) + turned(text_grad, "mp", 2) + turned(text_grad, "mp", 3)
-    )
-    enc_low_far, text_grad = lax.optimization_barrier((enc_low_far, text_grad))
-    mine, give = pl.pallas_call(
+    packed = pl.pallas_call(
+        functools.partial(row_kernel, width=float(width), **sizes),
+        out_shape=jax.ShapeDtypeStruct((tokens, kv + 2 * rank), bf16),
+        in_specs=[VMEM] * 7,
+        out_specs=VMEM,
+        compiler_params=PARAMS,
+        name="row_work",
+    )(own, *got, b_half, bias_half, text_grad)
+    got = [turned(packed, "mp", k) for k in range(1, n_mp)]
+    mine, give, text_grad = pl.pallas_call(
         functools.partial(image_kernel, block=block, step=mine_rows, **sizes),
-        out_shape=(jax.ShapeDtypeStruct((half_rank, part_width + half_kv), f32),) * 2,
+        out_shape=(jax.ShapeDtypeStruct((half_rank, part_width + half_kv), f32),) * 2
+        + (jax.ShapeDtypeStruct((half_rank, kv), f32),),
         in_specs=[SMEM] + [VMEM] * 15,
-        out_specs=(VMEM, VMEM),
+        out_specs=(VMEM, VMEM, VMEM),
         scratch_shapes=[
             pltpu.VMEM((ENC_DEV, half_kv + 2 * rank), bf16),
             pltpu.VMEM((rank, block), f32),

time: 149 us -> 149 us (level)
  starting transfers between devices: 47.1 us -> 40.8 us
  waiting for transfers between devices: 29 us -> 34.4 us
  blocking collectives: 27.3 us -> 29.7 us
    ppermute x12 -> x9, starting transfers between devices: 16.4 us -> 11.8 us  [turned(): lax.ppermute(array, axis, [(i, (i + step) % count) for i in range(count)])]
    ppermute x12 -> x9, waiting for transfers between devices: 11.5 us -> 15.7 us  [turned(): lax.ppermute(array, axis, [(i, (i + step) % count) for i in range(count)])]
    all_to_all x1, blocking collectives: 14.9 us -> 17.3 us  [body(): mine = jnp.sum(lax.all_to_all(mine, 'dp', 0, 0, tiled=True), axis=0)]
    unnamed x39 -> x37, local copies, waits for them, and re-layouts: 5.65 us -> 5.33 us
  transfers between devices with their start and end apart: 26 -> 23, of which waited for: 8 -> 11; matrix products, arithmetic and copies ran while one was open for 19% -> 19% of each run, Pallas kernels for 3% -> 2%
where the time goes in v11:
time: 149 us; the launch traced here: 148 us
  starting transfers between devices  40.8 us (27%)
  waiting for transfers between devices  34.4 us (23%)
  blocking collectives  29.7 us (20%)
  matrix products  16.4 us (11%)
  local copies, waits for them, and re-layouts  11.1 us (7%)
  Pallas kernels  8.68 us (6%)
  other arithmetic  5.21 us (3%)
  between operations  2.04 us (1%)
    all_to_all x1, blocking collectives, body(): mine = jnp.sum(lax.all_to_all(mine, 'dp', 0, 0, tiled=True), axis=0)  17.3 us
    ppermute x9, waiting for transfers between devices, turned(): lax.ppermute(array, axis, [(i, (i + step) % count) for i in range(count)])  15.7 us
    dot_general x5, matrix products, dot(): return jnp.dot(a, b, preferred_element_type=f32)  14.9 us
    all_to_all x1, starting transfers between devices, to_everyone(): lax.all_to_all(jnp.broadcast_to(array[None], (count, *array.shape)), axes...  13.3 us
    all_to_all x1, blocking collectives, to_everyone(): lax.all_to_all(jnp.broadcast_to(array[None], (count, *array.shape)), axes...  12.4 us
    ppermute x6, waiting for transfers between devices, along(): return lax.ppermute(array, 'dp', pairs)  12.3 us
    ppermute x9, starting transfers between devices, turned(): lax.ppermute(array, axis, [(i, (i + step) % count) for i in range(count)])  11.8 us
    ppermute x6, starting transfers between devices, along(): return lax.ppermute(array, 'dp', pairs)  8.64 us
  transfers between devices with their start and end apart: 23, of which 11 were waited for; matrix products, arithmetic and copies ran while one was open for 19% of the time, Pallas kernels for 2%

profile of v11, /device:TPU:0, one launch (start us, length us, event | category | flops | bytes accessed | tf_op | source)
XLA Modules:
  0.0 148.3 jit_solution(11991857084889958052)
XLA Ops:
  2.5 1.7 %collective-permute-start = (bf16[32,5120]{1,0:T(8,128)(2,1)}, bf16[32,5120]{1,0:T(8,128)(2,1)}, u32[]{:S(2)}, u32[]{:S(2)}) collective-permute-start(bf16[32,5120]{1,0:T(8,128)(2,1)} %constant_dynamic-slice_fusion.11), channel_id=1, source_target_pairs={{0,1},{1,2},{2,3},{3,0},{4,5},{5,6},{6,7},{7,4},{8,9},{9,10},{10,1... | collective-permute-start | bytes 983048 | tf_op jit(solution)/shard_map/ppermute | solution.py:40
  4.1 1.6 %collective-permute-start.2 = (bf16[32,5120]{1,0:T(8,128)(2,1)}, bf16[32,5120]{1,0:T(8,128)(2,1)}, u32[]{:S(2)}, u32[]{:S(2)}) collective-permute-start(bf16[32,5120]{1,0:T(8,128)(2,1)} %constant_dynamic-slice_fusion.11), channel_id=1, source_target_pairs={{0,3},{1,0},{2,1},{3,2},{4,7},{5,4},{6,5},{7,6},{8,11},{9,8},{10,9... | collective-permute-start | bytes 983048 | tf_op jit(solution)/shard_map/ppermute | solution.py:40
  8.9 13.3 %all-to-all-start = ((bf16[64,32,128]{2,1,0:T(8,128)(2,1)}), bf16[64,32,128]{2,1,0:T(8,128)(2,1)}, u32[]{:S(2)}, u32[]{:S(2)}) async-start(bf16[64,32,128]{2,1,0:T(8,128)(2,1)} %broadcast_in_dim.35), calls=%async_computation | async-start | bytes 1048576 | tf_op jit(solution)/shard_map/all_to_all | solution.py:58
  23.4 3.0 %collective-permute-start.6 = (bf16[192,512]{1,0:T(8,128)(2,1)S(1)}, bf16[192,512]{1,0:T(8,128)(2,1)S(1)}, u32[]{:S(2)}, u32[]{:S(2)}) collective-permute-start(bf16[192,512]{1,0:T(8,128)(2,1)S(1)} %get-tuple-element.42), channel_id=1, source_target_pairs={{0,48},{4,52},{8,56},{12,60},{16,0},{20,4},{24,8},{28,12},{32,16},... | collective-permute-start | bytes 589832 | tf_op jit(solution)/shard_map/ppermute | solution.py:53
  28.1 6.9 %collective-permute-done.6 = bf16[192,512]{1,0:T(8,128)(2,1)S(1)} collective-permute-done((bf16[192,512]{1,0:T(8,128)(2,1)S(1)}, bf16[192,512]{1,0:T(8,128)(2,1)S(1)}, u32[]{:S(2)}, u32[]{:S(2)}) %collective-permute-start.6) | collective-permute-done | bytes 196640 | tf_op jit(solution)/shard_map/ppermute | solution.py:53
  35.3 1.6 %collective-permute-done.7 = bf16[192,512]{1,0:T(8,128)(2,1)S(1)} collective-permute-done((bf16[192,512]{1,0:T(8,128)(2,1)S(1)}, bf16[192,512]{1,0:T(8,128)(2,1)S(1)}, u32[]{:S(2)}, u32[]{:S(2)}) %collective-permute-start.7) | collective-permute-done | bytes 196640 | tf_op jit(solution)/shard_map/ppermute | solution.py:53
  36.9 3.8 %collective-permute-done.8 = bf16[192,512]{1,0:T(8,128)(2,1)S(1)} collective-permute-done((bf16[192,512]{1,0:T(8,128)(2,1)S(1)}, bf16[192,512]{1,0:T(8,128)(2,1)S(1)}, u32[]{:S(2)}, u32[]{:S(2)}) %collective-permute-start.8) | collective-permute-done | bytes 196640 | tf_op jit(solution)/shard_map/ppermute | solution.py:53
  42.3 2.0 %collective-permute-start.10 = (bf16[576,512]{1,0:T(8,128)(2,1)}, bf16[576,512]{1,0:T(8,128)(2,1)S(1)}, u32[]{:S(2)}, u32[]{:S(2)}) collective-permute-start(bf16[576,512]{1,0:T(8,128)(2,1)} %get-tuple-element.24), channel_id=1, source_target_pairs={{0,8},{4,12},{8,0},{12,4},{16,24},{20,28},{24,16},{28,20},{32,40},... | collective-permute-start | bytes 1769480 | tf_op jit(solution)/shard_map/ppermute | solution.py:53
  48.9 8.2 %collective-permute-done.1 = bf16[32,5120]{1,0:T(8,128)(2,1)} collective-permute-done((bf16[32,5120]{1,0:T(8,128)(2,1)}, bf16[32,5120]{1,0:T(8,128)(2,1)}, u32[]{:S(2)}, u32[]{:S(2)}) %collective-permute-start.1) | collective-permute-done | bytes 327712 | tf_op jit(solution)/shard_map/ppermute | solution.py:40
  57.1 2.1 %convolution_convert_fusion.low_near = bf16[128,64]{1,0:T(8,128)(2,1)S(1)} fusion(bf16[5120,64]{0,1:T(8,128)(2,1)} %param.17, bf16[32,5120]{1,0:T(8,128)(2,1)} %collective-permute-done.2, bf16[32,5120]{1,0:T(8,128)(2,1)} %collective-permute-done.1, bf16[32,5120]{1,0:T(8,128)(2,1)} %collective-permute-done, bf16[32,5120]{1,0:T(8,128)(2,1)} %constant_dynamic-slice_fusion.11), kind=kOutput, calls=%fused_computation.18 | convolution fusion | flops 89137152 | bytes 1982464 | tf_op jit(solution)/shard_map/dot_general | solution.py:17
  61.9 11.1 %fusion.4.near = bf16[128,2048]{1,0:T(8,128)(2,1)} fusion(f32[128,2048]{1,0:T(8,128)S(1)} %fusion.51, bf16[5120,2048]{1,0:T(8,128)(2,1)} %param.15, f32[2048]{0:T(1024)S(1)} %convert_element_type.78, bf16[32,5120]{1,0:T(8,128)(2,1)} %collective-permute-done.2, bf16[32,5120]{1,0:T(8,128)(2,1)} %collective-permute-done.1, ...), kind=kOutput, calls=%fused_computation.8 | convolution fusion | flops 2690383872 | bytes 23863296 | tf_op jit(solution)/shard_map/dot_general | solution.py:17
  75.5 5.7 %all-to-all-start.1 = ((bf16[64,32,128]{2,1,0:T(8,128)(2,1)}), bf16[64,32,128]{2,1,0:T(8,128)(2,1)}, u32[]{:S(2)}, u32[]{:S(2)}) async-start(bf16[64,32,128]{2,1,0:T(8,128)(2,1)} %bitcast_bitcast_fusion), calls=%async_computation.1 | async-start | bytes 1048576 | tf_op jit(solution)/shard_map/all_to_all | solution.py:416
  82.9 3.2 %partial_products.1 = (f32[64,1152]{1,0:T(8,128)S(1)}, bf16[64,1152]{1,0:T(8,128)(2,1)}, bf16[64,1152]{1,0:T(8,128)(2,1)}, bf16[64,1152]{1,0:T(8,128)(2,1)}) custom-call(s32[2]{0:T(128)S(1)} %pad_add_fusion.place, bf16[128,2048]{1,0:T(8,128)(2,1)} %fusion.4.near, bf16[128,2048]{1,0:T(8,128)(2,1)} %collective-permute-done.3.far, f32[1,2048]{1,0:T(1,128)S(1)} %bitcast.70, ...), custom_call_target="tpu_custom_call" | custom-call | tf_op jit(solution)/shard_map/partial_products/pallas_call | solution.py:405
  86.9 2.7 %collective-permute-start.12 = (bf16[64,1152]{1,0:T(8,128)(2,1)}, bf16[64,1152]{1,0:T(8,128)(2,1)S(1)}, u32[]{:S(2)}, u32[]{:S(2)}) collective-permute-start(bf16[64,1152]{1,0:T(8,128)(2,1)} %get-tuple-element.13), channel_id=1, source_target_pairs={{0,3},{1,0},{2,1},{3,2},{4,7},{5,4},{6,5},{7,6},{8,11},{9,8},{10,9... | collective-permute-start | bytes 442376 | tf_op jit(solution)/shard_map/ppermute | solution.py:40
  91.2 3.5 %all-to-all-done.1 = bf16[64,32,128]{2,1,0:T(8,128)(2,1)} async-done(((bf16[64,32,128]{2,1,0:T(8,128)(2,1)}), bf16[64,32,128]{2,1,0:T(8,128)(2,1)}, u32[]{:S(2)}, u32[]{:S(2)}) %all-to-all-start.1) | async-done | bytes 524320 | tf_op jit(solution)/shard_map/all_to_all | solution.py:416
  98.1 1.6 %collective-permute-done.14.got3 = bf16[64,1152]{1,0:T(8,128)(2,1)} collective-permute-done((bf16[64,1152]{1,0:T(8,128)(2,1)}, bf16[64,1152]{1,0:T(8,128)(2,1)}, u32[]{:S(2)}, u32[]{:S(2)}) %collective-permute-start.14) | collective-permute-done | bytes 147488 | tf_op jit(solution)/shard_map/ppermute | solution.py:40
  100.6 1.6 %row_work.1.packed = bf16[64,1152]{1,0:T(8,128)(2,1)S(1)} custom-call(f32[64,1152]{1,0:T(8,128)S(1)} %copy-done.2, bf16[64,1152]{1,0:T(8,128)(2,1)S(1)} %collective-permute-done.12.got1, bf16[64,1152]{1,0:T(8,128)(2,1)} %collective-permute-done.13.got2, bf16[64,1152]{1,0:T(8,128)(2,1)} %collective-permute-done.14.got3, ...), custom_call_target="tpu_custom_call" | custom-call | tf_op jit(solution)/shard_map/row_work/pallas_call | solution.py:421
  102.3 2.0 %collective-permute-start.17 = (bf16[64,1152]{1,0:T(8,128)(2,1)S(1)}, bf16[64,1152]{1,0:T(8,128)(2,1)S(1)}, u32[]{:S(2)}, u32[]{:S(2)}) collective-permute-start(bf16[64,1152]{1,0:T(8,128)(2,1)S(1)} %row_work.1.packed), channel_id=1, source_target_pairs={{0,2},{1,3},{2,0},{3,1},{4,6},{5,7},{6,4},{7,5},{8,10},{9,11},{10,... | collective-permute-start | bytes 442376 | tf_op jit(solution)/shard_map/ppermute | solution.py:40
  104.3 1.4 collective-permute-start.18
  107.0 5.2 %collective-permute-done.16.got1 = bf16[64,1152]{1,0:T(8,128)(2,1)S(1)} collective-permute-done((bf16[64,1152]{1,0:T(8,128)(2,1)S(1)}, bf16[64,1152]{1,0:T(8,128)(2,1)S(1)}, u32[]{:S(2)}, u32[]{:S(2)}) %collective-permute-start.16) | collective-permute-done | bytes 147488 | tf_op jit(solution)/shard_map/ppermute | solution.py:40
  112.9 3.1 %image_gradients.1 = (f32[32,2560]{1,0:T(8,128)S(1)}, f32[32,2560]{1,0:T(8,128)S(1)}, f32[32,1024]{1,0:T(8,128)S(1)}) custom-call(s32[2]{0:T(128)S(1)} %pad_add_fusion.place, bf16[64,1152]{1,0:T(8,128)(2,1)S(1)} %row_work.1.packed, bf16[64,1152]{1,0:T(8,128)(2,1)S(1)} %collective-permute-done.16.got1, bf16[64,1152]{1,0:T(8,128)(2,1)S(1)} %collective-permute-done.17.got2, ...), custom_call_target="tpu_custom_call" | custom-call | tf_op jit(solution)/shard_map/image_gradients/pallas_call | solution.py:430
  116.0 1.6 %collective-permute-done.20 = f32[32,2560]{1,0:T(8,128)S(1)} collective-permute-done((f32[32,2560]{1,0:T(8,128)S(1)}, f32[32,2560]{1,0:T(8,128)S(1)}, u32[]{:S(2)}, u32[]{:S(2)}) %collective-permute-start.20) | collective-permute-done | bytes 327712 | tf_op jit(solution)/shard_map/ppermute | solution.py:44
  117.8 17.3 %all_to_all.20 = f32[16,8,768]{2,1,0:T(8,128)S(1)} all-to-all(f32[16,8,768]{2,1,0:T(8,128)S(1)} %bitcast.73), channel_id=1, replica_groups=mesh['grp'=2,'dp'=16,'mp'=4] {'dp'}, dimensions={0} | all-to-all | bytes 786432 | tf_op jit(solution)/shard_map/all_to_all | solution.py:466
  135.1 12.4 %all_to_all.21.whole = f32[16,8,768]{2,1,0:T(8,128)S(1)} all-to-all(f32[16,8,768]{2,1,0:T(8,128)S(1)} %broadcast_in_dim.72), channel_id=1, replica_groups=mesh['grp'=2,'dp'=16,'mp'=4] {'dp'}, dimensions={0} | all-to-all | bytes 786432 | tf_op jit(solution)/shard_map/all_to_all | solution.py:58
  (129 shorter events, 29.7 us)
Async XLA Ops:
  0.7 21.7 %copy-start.12 = (bf16[1024]{0:T(1024)(128)(2,1)S(1)}, bf16[1024]{0:T(1024)(128)(2,1)}, u32[]{:S(2)}) copy-start(bf16[1024]{0:T(1024)(128)(2,1)} %param.22) | copy-start | bytes 6148
  2.5 44.2 %collective-permute-start = (bf16[32,5120]{1,0:T(8,128)(2,1)}, bf16[32,5120]{1,0:T(8,128)(2,1)}, u32[]{:S(2)}, u32[]{:S(2)}) collective-permute-start(bf16[32,5120]{1,0:T(8,128)(2,1)} %constant_dynamic-slice_fusion.11), channel_id=1, source_target_pairs={{0,1},{1,2},{2,3},{3,0},{4,5},{5,6},{6,7},{7,4},{8,9},{9,10},{10,1... | collective-permute-start | bytes 983048 | tf_op jit(solution)/shard_map/ppermute | solution.py:40
  4.1 44.7 %collective-permute-start.2 = (bf16[32,5120]{1,0:T(8,128)(2,1)}, bf16[32,5120]{1,0:T(8,128)(2,1)}, u32[]{:S(2)}, u32[]{:S(2)}) collective-permute-start(bf16[32,5120]{1,0:T(8,128)(2,1)} %constant_dynamic-slice_fusion.11), channel_id=1, source_target_pairs={{0,3},{1,0},{2,1},{3,2},{4,7},{5,4},{6,5},{7,6},{8,11},{9,8},{10,9... | collective-permute-start | bytes 983048 | tf_op jit(solution)/shard_map/ppermute | solution.py:40
  6.6 16.7 %collective-permute-start.5 = (bf16[128,512]{1,0:T(8,128)(2,1)S(1)}, bf16[128,512]{1,0:T(8,128)(2,1)S(1)}, u32[]{:S(2)}, u32[]{:S(2)}) collective-permute-start(bf16[128,512]{1,0:T(8,128)(2,1)S(1)} %constant_dynamic-slice_fusion.9), channel_id=1, source_target_pairs={{0,0},{1,16},{2,32},{3,48},{4,4},{5,20},{6,36},{7,52},{8,8},{9,24}... | collective-permute-start | bytes 393224 | tf_op jit(solution)/shard_map/ppermute | solution.py:308
  8.9 38.8 %all-to-all-start = ((bf16[64,32,128]{2,1,0:T(8,128)(2,1)}), bf16[64,32,128]{2,1,0:T(8,128)(2,1)}, u32[]{:S(2)}, u32[]{:S(2)}) async-start(bf16[64,32,128]{2,1,0:T(8,128)(2,1)} %broadcast_in_dim.35), calls=%async_computation | async-start | bytes 1048576 | tf_op jit(solution)/shard_map/all_to_all | solution.py:58
  23.4 11.6 %collective-permute-start.6 = (bf16[192,512]{1,0:T(8,128)(2,1)S(1)}, bf16[192,512]{1,0:T(8,128)(2,1)S(1)}, u32[]{:S(2)}, u32[]{:S(2)}) collective-permute-start(bf16[192,512]{1,0:T(8,128)(2,1)S(1)} %get-tuple-element.42), channel_id=1, source_target_pairs={{0,48},{4,52},{8,56},{12,60},{16,0},{20,4},{24,8},{28,12},{32,16},... | collective-permute-start | bytes 589832 | tf_op jit(solution)/shard_map/ppermute | solution.py:53
  26.5 10.4 %collective-permute-start.7 = (bf16[192,512]{1,0:T(8,128)(2,1)S(1)}, bf16[192,512]{1,0:T(8,128)(2,1)S(1)}, u32[]{:S(2)}, u32[]{:S(2)}) collective-permute-start(bf16[192,512]{1,0:T(8,128)(2,1)S(1)} %get-tuple-element.41), channel_id=1, source_target_pairs={{0,32},{4,36},{8,40},{12,44},{16,48},{20,52},{24,56},{28,60},{32,0... | collective-permute-start | bytes 589832 | tf_op jit(solution)/shard_map/ppermute | solution.py:53
  27.2 13.5 %collective-permute-start.8 = (bf16[192,512]{1,0:T(8,128)(2,1)S(1)}, bf16[192,512]{1,0:T(8,128)(2,1)S(1)}, u32[]{:S(2)}, u32[]{:S(2)}) collective-permute-start(bf16[192,512]{1,0:T(8,128)(2,1)S(1)} %get-tuple-element.40), channel_id=1, source_target_pairs={{0,16},{4,20},{8,24},{12,28},{16,32},{20,36},{24,40},{28,44},{32,4... | collective-permute-start | bytes 589832 | tf_op jit(solution)/shard_map/ppermute | solution.py:53
  42.3 40.6 %collective-permute-start.10 = (bf16[576,512]{1,0:T(8,128)(2,1)}, bf16[576,512]{1,0:T(8,128)(2,1)S(1)}, u32[]{:S(2)}, u32[]{:S(2)}) collective-permute-start(bf16[576,512]{1,0:T(8,128)(2,1)} %get-tuple-element.24), channel_id=1, source_target_pairs={{0,8},{4,12},{8,0},{12,4},{16,24},{20,28},{24,16},{28,20},{32,40},... | collective-permute-start | bytes 1769480 | tf_op jit(solution)/shard_map/ppermute | solution.py:53
  44.3 38.6 %collective-permute-start.11 = (bf16[576,512]{1,0:T(8,128)(2,1)}, bf16[576,512]{1,0:T(8,128)(2,1)S(1)}, u32[]{:S(2)}, u32[]{:S(2)}) collective-permute-start(bf16[576,512]{1,0:T(8,128)(2,1)} %get-tuple-element.22), channel_id=1, source_target_pairs={{0,12},{4,0},{8,4},{12,8},{16,28},{20,16},{24,20},{28,24},{32,44},... | collective-permute-start | bytes 1769480 | tf_op jit(solution)/shard_map/ppermute | solution.py:53
  45.6 37.3 %collective-permute-start.9 = (bf16[576,512]{1,0:T(8,128)(2,1)}, bf16[576,512]{1,0:T(8,128)(2,1)S(1)}, u32[]{:S(2)}, u32[]{:S(2)}) collective-permute-start(bf16[576,512]{1,0:T(8,128)(2,1)} %get-tuple-element.23), channel_id=1, source_target_pairs={{0,4},{4,8},{8,12},{12,0},{16,20},{20,24},{24,28},{28,16},{32,36},... | collective-permute-start | bytes 1769480 | tf_op jit(solution)/shard_map/ppermute | solution.py:53
  46.6 10.4 %collective-permute-start.1 = (bf16[32,5120]{1,0:T(8,128)(2,1)}, bf16[32,5120]{1,0:T(8,128)(2,1)}, u32[]{:S(2)}, u32[]{:S(2)}) collective-permute-start(bf16[32,5120]{1,0:T(8,128)(2,1)} %collective-permute-done), channel_id=1, source_target_pairs={{0,1},{1,2},{2,3},{3,0},{4,5},{5,6},{6,7},{7,4},{8,9},{9,10},{10,1... | collective-permute-start | bytes 983048 | tf_op jit(solution)/shard_map/ppermute | solution.py:40
  48.8 10.7 %collective-permute-start.4 = (bf16[64,32,128]{2,1,0:T(8,128)(2,1)}, bf16[64,32,128]{2,1,0:T(8,128)(2,1)S(1)}, u32[]{:S(2)}, u32[]{:S(2)}) collective-permute-start(bf16[64,32,128]{2,1,0:T(8,128)(2,1)} %all-to-all-done), channel_id=1, source_target_pairs={{0,64},{64,0},{1,65},{65,1},{2,66},{66,2},{3,67},{67,3},{4,68},{68... | collective-permute-start | bytes 1572872 | tf_op jit(solution)/shard_map/ppermute | solution.py:44
  61.8 11.7 %collective-permute-start.15 = (f32[32,9216]{1,0:T(8,128)S(1)}, f32[32,9216]{1,0:T(8,128)S(1)}, u32[]{:S(2)}, u32[]{:S(2)}) collective-permute-start(f32[32,9216]{1,0:T(8,128)S(1)} %pad_maximum_fusion.1), channel_id=1, source_target_pairs={{0,64},{64,0},{1,65},{65,1},{2,66},{66,2},{3,67},{67,3},{4,68},{68... | collective-permute-start | bytes 3538952 | tf_op jit(solution)/shard_map/ppermute | solution.py:44
  73.0 9.9 %collective-permute-start.3 = (bf16[128,2048]{1,0:T(8,128)(2,1)}, bf16[128,2048]{1,0:T(8,128)(2,1)}, u32[]{:S(2)}, u32[]{:S(2)}) collective-permute-start(bf16[128,2048]{1,0:T(8,128)(2,1)} %fusion.4.near), channel_id=1, source_target_pairs={{0,64},{64,0},{1,65},{65,1},{2,66},{66,2},{3,67},{67,3},{4,68},{68... | collective-permute-start | bytes 1572872 | tf_op jit(solution)/shard_map/ppermute | solution.py:44
  75.5 19.2 %all-to-all-start.1 = ((bf16[64,32,128]{2,1,0:T(8,128)(2,1)}), bf16[64,32,128]{2,1,0:T(8,128)(2,1)}, u32[]{:S(2)}, u32[]{:S(2)}) async-start(bf16[64,32,128]{2,1,0:T(8,128)(2,1)} %bitcast_bitcast_fusion), calls=%async_computation.1 | async-start | bytes 1048576 | tf_op jit(solution)/shard_map/all_to_all | solution.py:416
  86.9 11.1 %collective-permute-start.12 = (bf16[64,1152]{1,0:T(8,128)(2,1)}, bf16[64,1152]{1,0:T(8,128)(2,1)S(1)}, u32[]{:S(2)}, u32[]{:S(2)}) collective-permute-start(bf16[64,1152]{1,0:T(8,128)(2,1)} %get-tuple-element.13), channel_id=1, source_target_pairs={{0,3},{1,0},{2,1},{3,2},{4,7},{5,4},{6,5},{7,6},{8,11},{9,8},{10,9... | collective-permute-start | bytes 442376 | tf_op jit(solution)/shard_map/ppermute | solution.py:40
  89.5 8.5 %collective-permute-start.13 = (bf16[64,1152]{1,0:T(8,128)(2,1)}, bf16[64,1152]{1,0:T(8,128)(2,1)}, u32[]{:S(2)}, u32[]{:S(2)}) collective-permute-start(bf16[64,1152]{1,0:T(8,128)(2,1)} %get-tuple-element.14), channel_id=1, source_target_pairs={{0,2},{1,3},{2,0},{3,1},{4,6},{5,7},{6,4},{7,5},{8,10},{9,11},{10,... | collective-permute-start | bytes 442376 | tf_op jit(solution)/shard_map/ppermute | solution.py:40
  90.4 9.3 %collective-permute-start.14 = (bf16[64,1152]{1,0:T(8,128)(2,1)}, bf16[64,1152]{1,0:T(8,128)(2,1)}, u32[]{:S(2)}, u32[]{:S(2)}) collective-permute-start(bf16[64,1152]{1,0:T(8,128)(2,1)} %get-tuple-element.15), channel_id=1, source_target_pairs={{0,1},{1,2},{2,3},{3,0},{4,5},{5,6},{6,7},{7,4},{8,9},{9,10},{10,1... | collective-permute-start | bytes 442376 | tf_op jit(solution)/shard_map/ppermute | solution.py:40
  102.3 10.0 %collective-permute-start.16 = (bf16[64,1152]{1,0:T(8,128)(2,1)S(1)}, bf16[64,1152]{1,0:T(8,128)(2,1)S(1)}, u32[]{:S(2)}, u32[]{:S(2)}) collective-permute-start(bf16[64,1152]{1,0:T(8,128)(2,1)S(1)} %row_work.1.packed), channel_id=1, source_target_pairs={{0,1},{1,2},{2,3},{3,0},{4,5},{5,6},{6,7},{7,4},{8,9},{9,10},{10,1... | collective-permute-start | bytes 442376 | tf_op jit(solution)/shard_map/ppermute | solution.py:40
  102.3 9.9 %collective-permute-start.17 = (bf16[64,1152]{1,0:T(8,128)(2,1)S(1)}, bf16[64,1152]{1,0:T(8,128)(2,1)S(1)}, u32[]{:S(2)}, u32[]{:S(2)}) collective-permute-start(bf16[64,1152]{1,0:T(8,128)(2,1)S(1)} %row_work.1.packed), channel_id=1, source_target_pairs={{0,2},{1,3},{2,0},{3,1},{4,6},{5,7},{6,4},{7,5},{8,10},{9,11},{10,... | collective-permute-start | bytes 442376 | tf_op jit(solution)/shard_map/ppermute | solution.py:40
  104.3 8.5 %collective-permute-start.18 = (bf16[64,1152]{1,0:T(8,128)(2,1)S(1)}, bf16[64,1152]{1,0:T(8,128)(2,1)S(1)}, u32[]{:S(2)}, u32[]{:S(2)}) collective-permute-start(bf16[64,1152]{1,0:T(8,128)(2,1)S(1)} %row_work.1.packed), channel_id=1, source_target_pairs={{0,3},{1,0},{2,1},{3,2},{4,7},{5,4},{6,5},{7,6},{8,11},{9,8},{10,9... | collective-permute-start | bytes 442376 | tf_op jit(solution)/shard_map/ppermute | solution.py:40
  105.8 1.2 collective-permute-start.19
  115.9 1.7 %collective-permute-start.20 = (f32[32,2560]{1,0:T(8,128)S(1)}, f32[32,2560]{1,0:T(8,128)S(1)}, u32[]{:S(2)}, u32[]{:S(2)}) collective-permute-start(f32[32,2560]{1,0:T(8,128)S(1)} %get-tuple-element.18), channel_id=1, source_target_pairs={{0,64},{64,0},{1,65},{65,1},{2,66},{66,2},{3,67},{67,3},{4,68},{68... | collective-permute-start | bytes 983048 | tf_op jit(solution)/shard_map/ppermute | solution.py:44
  (14 other events, 136.5 us)

commit v12 on v10

--- a/solution.py
+++ b/solution.py
@@ -306,9 +306,10 @@
     for k in range(1, side):
         t_given = cut(t_half, (slab + k) & wrap, 1)[0]
         came = along(jnp.concatenate([w_moved, t_given]), k, 0, side)
+        if k == 1:
+            dest_owner, text_rows, _ = lax.optimization_barrier((dest_owner, text_rows, came))
         w_line.append(came[:shard])
         t_line.append(came[shard:])
-    dest_owner, text_rows, _ = lax.optimization_barrier((dest_owner, text_rows, came))
     w_line = w_line[::-1]
     w_line = cut(jnp.concatenate(w_line + w_line), ((2 * side - 1 - slab) & wrap) * shard, block)
     t_line = jnp.stack(t_line).reshape(side, side, chunk, half_kv)

time: 149 us -> 149 us (level)
  transfers between devices with their start and end apart: 26 -> 26, of which waited for: 8 -> 7; matrix products, arithmetic and copies ran while one was open for 19% -> 19% of each run, Pallas kernels for 3% -> 3%
where the time goes in v12:
time: 149 us; the launch traced here: 148 us
  starting transfers between devices  48.1 us (32%)
  waiting for transfers between devices  27.8 us (19%)
  blocking collectives  27.3 us (18%)
  matrix products  16.4 us (11%)
  local copies, waits for them, and re-layouts  12.2 us (8%)
  Pallas kernels  8.69 us (6%)
  other arithmetic  5.23 us (4%)
  between operations  2.08 us (1%)
    ppermute x12, starting transfers between devices, turned(): lax.ppermute(array, axis, [(i, (i + step) % count) for i in range(count)])  16.4 us
    all_to_all x1, blocking collectives, body(): mine = jnp.sum(lax.all_to_all(mine, 'dp', 0, 0, tiled=True), axis=0)  14.9 us
    dot_general x5, matrix products, dot(): return jnp.dot(a, b, preferred_element_type=f32)  14.9 us
    all_to_all x1, starting transfers between devices, to_everyone(): lax.all_to_all(jnp.broadcast_to(array[None], (count, *array.shape)), axes...  14.3 us
    all_to_all x1, blocking collectives, to_everyone(): lax.all_to_all(jnp.broadcast_to(array[None], (count, *array.shape)), axes...  12.4 us
    ppermute x12, waiting for transfers between devices, turned(): lax.ppermute(array, axis, [(i, (i + step) % count) for i in range(count)])  11.3 us
    ppermute x6, waiting for transfers between devices, along(): return lax.ppermute(array, 'dp', pairs)  11.3 us
    ppermute x6, starting transfers between devices, along(): return lax.ppermute(array, 'dp', pairs)  10.4 us
  transfers between devices with their start and end apart: 26, of which 7 were waited for; matrix products, arithmetic and copies ran while one was open for 19% of the time, Pallas kernels for 3%

profile of v12, /device:TPU:0, one launch (start us, length us, event | category | flops | bytes accessed | tf_op | source)
XLA Modules:
  0.0 147.8 jit_solution(7328326399960365241)
XLA Ops:
  2.5 3.1 %collective-permute-start.2 = (bf16[32,5120]{1,0:T(8,128)(2,1)}, bf16[32,5120]{1,0:T(8,128)(2,1)}, u32[]{:S(2)}, u32[]{:S(2)}) collective-permute-start(bf16[32,5120]{1,0:T(8,128)(2,1)} %constant_dynamic-slice_fusion.11), channel_id=1, source_target_pairs={{0,3},{1,0},{2,1},{3,2},{4,7},{5,4},{6,5},{7,6},{8,11},{9,8},{10,9... | collective-permute-start | bytes 983048 | tf_op jit(solution)/shard_map/ppermute | solution.py:40
  8.7 14.3 %all-to-all-start = ((bf16[64,32,128]{2,1,0:T(8,128)(2,1)}), bf16[64,32,128]{2,1,0:T(8,128)(2,1)}, u32[]{:S(2)}, u32[]{:S(2)}) async-start(bf16[64,32,128]{2,1,0:T(8,128)(2,1)} %broadcast_in_dim.35), calls=%async_computation | async-start | bytes 1048576 | tf_op jit(solution)/shard_map/all_to_all | solution.py:58
  24.2 1.6 %collective-permute-start.8 = (bf16[192,512]{1,0:T(8,128)(2,1)S(1)}, bf16[192,512]{1,0:T(8,128)(2,1)S(1)}, u32[]{:S(2)}, u32[]{:S(2)}) collective-permute-start(bf16[192,512]{1,0:T(8,128)(2,1)S(1)} %get-tuple-element.41), channel_id=1, source_target_pairs={{0,16},{4,20},{8,24},{12,28},{16,32},{20,36},{24,40},{28,44},{32,4... | collective-permute-start | bytes 589832 | tf_op jit(solution)/shard_map/ppermute | solution.py:53
  25.8 1.7 %collective-permute-start.6 = (bf16[192,512]{1,0:T(8,128)(2,1)S(1)}, bf16[192,512]{1,0:T(8,128)(2,1)S(1)}, u32[]{:S(2)}, u32[]{:S(2)}) collective-permute-start(bf16[192,512]{1,0:T(8,128)(2,1)S(1)} %get-tuple-element.42), channel_id=1, source_target_pairs={{0,48},{4,52},{8,56},{12,60},{16,0},{20,4},{24,8},{28,12},{32,16},... | collective-permute-start | bytes 589832 | tf_op jit(solution)/shard_map/ppermute | solution.py:53
  27.6 1.9 %collective-permute-start.7 = (bf16[192,512]{1,0:T(8,128)(2,1)S(1)}, bf16[192,512]{1,0:T(8,128)(2,1)S(1)}, u32[]{:S(2)}, u32[]{:S(2)}) collective-permute-start(bf16[192,512]{1,0:T(8,128)(2,1)S(1)} %get-tuple-element.40), channel_id=1, source_target_pairs={{0,32},{4,36},{8,40},{12,44},{16,48},{20,52},{24,56},{28,60},{32,0... | collective-permute-start | bytes 589832 | tf_op jit(solution)/shard_map/ppermute | solution.py:53
  29.5 7.1 %collective-permute-done.8 = bf16[192,512]{1,0:T(8,128)(2,1)S(1)} collective-permute-done((bf16[192,512]{1,0:T(8,128)(2,1)S(1)}, bf16[192,512]{1,0:T(8,128)(2,1)S(1)}, u32[]{:S(2)}, u32[]{:S(2)}) %collective-permute-start.8) | collective-permute-done | bytes 196640 | tf_op jit(solution)/shard_map/ppermute | solution.py:53
  36.8 4.2 %collective-permute-done.7 = bf16[192,512]{1,0:T(8,128)(2,1)S(1)} collective-permute-done((bf16[192,512]{1,0:T(8,128)(2,1)S(1)}, bf16[192,512]{1,0:T(8,128)(2,1)S(1)}, u32[]{:S(2)}, u32[]{:S(2)}) %collective-permute-start.7) | collective-permute-done | bytes 196640 | tf_op jit(solution)/shard_map/ppermute | solution.py:53
  43.7 2.8 %collective-permute-start.10 = (bf16[576,512]{1,0:T(8,128)(2,1)}, bf16[576,512]{1,0:T(8,128)(2,1)S(1)}, u32[]{:S(2)}, u32[]{:S(2)}) collective-permute-start(bf16[576,512]{1,0:T(8,128)(2,1)} %get-tuple-element.26), channel_id=1, source_target_pairs={{0,8},{4,12},{8,0},{12,4},{16,24},{20,28},{24,16},{28,20},{32,40},... | collective-permute-start | bytes 1769480 | tf_op jit(solution)/shard_map/ppermute | solution.py:53
  50.4 8.0 %collective-permute-done.1 = bf16[32,5120]{1,0:T(8,128)(2,1)} collective-permute-done((bf16[32,5120]{1,0:T(8,128)(2,1)}, bf16[32,5120]{1,0:T(8,128)(2,1)}, u32[]{:S(2)}, u32[]{:S(2)}) %collective-permute-start.1) | collective-permute-done | bytes 327712 | tf_op jit(solution)/shard_map/ppermute | solution.py:40
  58.4 2.1 %convolution_convert_fusion.low_near = bf16[128,64]{1,0:T(8,128)(2,1)S(1)} fusion(bf16[5120,64]{0,1:T(8,128)(2,1)} %param.17, bf16[32,5120]{1,0:T(8,128)(2,1)} %collective-permute-done.2, bf16[32,5120]{1,0:T(8,128)(2,1)} %collective-permute-done.1, bf16[32,5120]{1,0:T(8,128)(2,1)} %collective-permute-done, bf16[32,5120]{1,0:T(8,128)(2,1)} %constant_dynamic-slice_fusion.11), kind=kOutput, calls=%fused_computation.18 | convolution fusion | flops 89137152 | bytes 1982464 | tf_op jit(solution)/shard_map/dot_general | solution.py:17
  63.5 11.1 %fusion.4.near = bf16[128,2048]{1,0:T(8,128)(2,1)} fusion(f32[128,2048]{1,0:T(8,128)S(1)} %fusion.51, bf16[5120,2048]{1,0:T(8,128)(2,1)} %param.15, f32[2048]{0:T(1024)S(1)} %convert_element_type.78, bf16[32,5120]{1,0:T(8,128)(2,1)} %collective-permute-done.2, bf16[32,5120]{1,0:T(8,128)(2,1)} %collective-permute-done.1, ...), kind=kOutput, calls=%fused_computation.8 | convolution fusion | flops 2690383872 | bytes 23863296 | tf_op jit(solution)/shard_map/dot_general | solution.py:17
  77.2 5.7 %all-to-all-start.1 = ((bf16[64,32,128]{2,1,0:T(8,128)(2,1)}), bf16[64,32,128]{2,1,0:T(8,128)(2,1)}, u32[]{:S(2)}, u32[]{:S(2)}) async-start(bf16[64,32,128]{2,1,0:T(8,128)(2,1)} %bitcast_bitcast_fusion), calls=%async_computation.1 | async-start | bytes 1048576 | tf_op jit(solution)/shard_map/all_to_all | solution.py:415
  84.6 3.3 %partial_products.1 = (f32[64,1152]{1,0:T(8,128)S(1)}, bf16[64,1152]{1,0:T(8,128)(2,1)}, bf16[64,1152]{1,0:T(8,128)(2,1)}, bf16[64,1152]{1,0:T(8,128)(2,1)}) custom-call(s32[2]{0:T(128)S(1)} %pad_add_fusion.place, bf16[128,2048]{1,0:T(8,128)(2,1)} %fusion.4.near, bf16[128,2048]{1,0:T(8,128)(2,1)} %collective-permute-done.3.far, f32[1,2048]{1,0:T(1,128)S(1)} %bitcast.70, ...), custom_call_target="tpu_custom_call" | custom-call | tf_op jit(solution)/shard_map/partial_products/pallas_call | solution.py:396
  88.6 2.6 %collective-permute-start.12 = (bf16[64,1152]{1,0:T(8,128)(2,1)}, bf16[64,1152]{1,0:T(8,128)(2,1)S(1)}, u32[]{:S(2)}, u32[]{:S(2)}) collective-permute-start(bf16[64,1152]{1,0:T(8,128)(2,1)} %get-tuple-element.14), channel_id=1, source_target_pairs={{0,3},{1,0},{2,1},{3,2},{4,7},{5,4},{6,5},{7,6},{8,11},{9,8},{10,9... | collective-permute-start | bytes 442376 | tf_op jit(solution)/shard_map/ppermute | solution.py:40
  92.9 3.5 %all-to-all-done.1 = bf16[64,32,128]{2,1,0:T(8,128)(2,1)} async-done(((bf16[64,32,128]{2,1,0:T(8,128)(2,1)}), bf16[64,32,128]{2,1,0:T(8,128)(2,1)}, u32[]{:S(2)}, u32[]{:S(2)}) %all-to-all-start.1) | async-done | bytes 524320 | tf_op jit(solution)/shard_map/all_to_all | solution.py:415
  100.4 1.4 collective-permute-start.20
  104.6 1.6 %row_work.1.packed = bf16[64,640]{1,0:T(8,128)(2,1)S(1)} custom-call(f32[64,1152]{1,0:T(8,128)S(1)} %copy-done.2, bf16[64,1152]{1,0:T(8,128)(2,1)S(1)} %collective-permute-done.12.got1, bf16[64,1152]{1,0:T(8,128)(2,1)} %collective-permute-done.13.got2, bf16[64,1152]{1,0:T(8,128)(2,1)} %collective-permute-done.14.got3, ...), custom_call_target="tpu_custom_call" | custom-call | tf_op jit(solution)/shard_map/row_work/pallas_call | solution.py:406
  106.2 1.8 %collective-permute-start.15 = (bf16[64,640]{1,0:T(8,128)(2,1)S(1)}, bf16[64,640]{1,0:T(8,128)(2,1)S(1)}, u32[]{:S(2)}, u32[]{:S(2)}) collective-permute-start(bf16[64,640]{1,0:T(8,128)(2,1)S(1)} %row_work.1.packed), channel_id=1, source_target_pairs={{0,1},{1,2},{2,3},{3,0},{4,5},{5,6},{6,7},{7,4},{8,9},{9,10},{10,1... | collective-permute-start | bytes 245768 | tf_op jit(solution)/shard_map/ppermute | solution.py:40
  108.1 2.2 %collective-permute-start.16 = (bf16[64,640]{1,0:T(8,128)(2,1)S(1)}, bf16[64,640]{1,0:T(8,128)(2,1)S(1)}, u32[]{:S(2)}, u32[]{:S(2)}) collective-permute-start(bf16[64,640]{1,0:T(8,128)(2,1)S(1)} %row_work.1.packed), channel_id=1, source_target_pairs={{0,2},{1,3},{2,0},{3,1},{4,6},{5,7},{6,4},{7,5},{8,10},{9,11},{10,... | collective-permute-start | bytes 245768 | tf_op jit(solution)/shard_map/ppermute | solution.py:40
  112.4 2.5 %collective-permute-done.16.got2 = bf16[64,640]{1,0:T(8,128)(2,1)S(1)} collective-permute-done((bf16[64,640]{1,0:T(8,128)(2,1)S(1)}, bf16[64,640]{1,0:T(8,128)(2,1)S(1)}, u32[]{:S(2)}, u32[]{:S(2)}) %collective-permute-start.16) | collective-permute-done | bytes 81952 | tf_op jit(solution)/shard_map/ppermute | solution.py:40
  114.8 3.0 %image_gradients.1 = (f32[32,2560]{1,0:T(8,128)S(1)}, f32[32,2560]{1,0:T(8,128)S(1)}) custom-call(s32[2]{0:T(128)S(1)} %pad_add_fusion.place, bf16[64,640]{1,0:T(8,128)(2,1)S(1)} %row_work.1.packed, bf16[64,640]{1,0:T(8,128)(2,1)S(1)} %collective-permute-done.15.got1, bf16[64,640]{1,0:T(8,128)(2,1)S(1)} %collective-permute-done.16.got2, ...), custom_call_target="tpu_custom_call" | custom-call | tf_op jit(solution)/shard_map/image_gradients/pallas_call | solution.py:425
  118.0 1.6 %collective-permute-done.23 = f32[32,2560]{1,0:T(8,128)S(1)} collective-permute-done((f32[32,2560]{1,0:T(8,128)S(1)}, f32[32,2560]{1,0:T(8,128)S(1)}, u32[]{:S(2)}, u32[]{:S(2)}) %collective-permute-start.23) | collective-permute-done | bytes 327712 | tf_op jit(solution)/shard_map/ppermute | solution.py:44
  119.7 14.9 %all_to_all.20 = f32[16,8,768]{2,1,0:T(8,128)S(1)} all-to-all(f32[16,8,768]{2,1,0:T(8,128)S(1)} %bitcast.73), channel_id=1, replica_groups=mesh['grp'=2,'dp'=16,'mp'=4] {'dp'}, dimensions={0} | all-to-all | bytes 786432 | tf_op jit(solution)/shard_map/all_to_all | solution.py:460
  134.7 12.4 %all_to_all.21.whole = f32[16,8,768]{2,1,0:T(8,128)S(1)} all-to-all(f32[16,8,768]{2,1,0:T(8,128)S(1)} %broadcast_in_dim.72), channel_id=1, replica_groups=mesh['grp'=2,'dp'=16,'mp'=4] {'dp'}, dimensions={0} | all-to-all | bytes 786432 | tf_op jit(solution)/shard_map/all_to_all | solution.py:58
  (138 shorter events, 31.3 us)
Async XLA Ops:
  2.5 47.8 %collective-permute-start.2 = (bf16[32,5120]{1,0:T(8,128)(2,1)}, bf16[32,5120]{1,0:T(8,128)(2,1)}, u32[]{:S(2)}, u32[]{:S(2)}) collective-permute-start(bf16[32,5120]{1,0:T(8,128)(2,1)} %constant_dynamic-slice_fusion.11), channel_id=1, source_target_pairs={{0,3},{1,0},{2,1},{3,2},{4,7},{5,4},{6,5},{7,6},{8,11},{9,8},{10,9... | collective-permute-start | bytes 983048 | tf_op jit(solution)/shard_map/ppermute | solution.py:40
  5.6 42.5 %collective-permute-start = (bf16[32,5120]{1,0:T(8,128)(2,1)}, bf16[32,5120]{1,0:T(8,128)(2,1)}, u32[]{:S(2)}, u32[]{:S(2)}) collective-permute-start(bf16[32,5120]{1,0:T(8,128)(2,1)} %constant_dynamic-slice_fusion.11), channel_id=1, source_target_pairs={{0,1},{1,2},{2,3},{3,0},{4,5},{5,6},{6,7},{7,4},{8,9},{9,10},{10,1... | collective-permute-start | bytes 983048 | tf_op jit(solution)/shard_map/ppermute | solution.py:40
  6.5 17.7 %collective-permute-start.5 = (bf16[128,512]{1,0:T(8,128)(2,1)S(1)}, bf16[128,512]{1,0:T(8,128)(2,1)S(1)}, u32[]{:S(2)}, u32[]{:S(2)}) collective-permute-start(bf16[128,512]{1,0:T(8,128)(2,1)S(1)} %constant_dynamic-slice_fusion.9), channel_id=1, source_target_pairs={{0,0},{1,16},{2,32},{3,48},{4,4},{5,20},{6,36},{7,52},{8,8},{9,24}... | collective-permute-start | bytes 393224 | tf_op jit(solution)/shard_map/ppermute | solution.py:298
  8.7 40.4 %all-to-all-start = ((bf16[64,32,128]{2,1,0:T(8,128)(2,1)}), bf16[64,32,128]{2,1,0:T(8,128)(2,1)}, u32[]{:S(2)}, u32[]{:S(2)}) async-start(bf16[64,32,128]{2,1,0:T(8,128)(2,1)} %broadcast_in_dim.35), calls=%async_computation | async-start | bytes 1048576 | tf_op jit(solution)/shard_map/all_to_all | solution.py:58
  24.2 12.4 %collective-permute-start.8 = (bf16[192,512]{1,0:T(8,128)(2,1)S(1)}, bf16[192,512]{1,0:T(8,128)(2,1)S(1)}, u32[]{:S(2)}, u32[]{:S(2)}) collective-permute-start(bf16[192,512]{1,0:T(8,128)(2,1)S(1)} %get-tuple-element.41), channel_id=1, source_target_pairs={{0,16},{4,20},{8,24},{12,28},{16,32},{20,36},{24,40},{28,44},{32,4... | collective-permute-start | bytes 589832 | tf_op jit(solution)/shard_map/ppermute | solution.py:53
  25.8 11.0 %collective-permute-start.6 = (bf16[192,512]{1,0:T(8,128)(2,1)S(1)}, bf16[192,512]{1,0:T(8,128)(2,1)S(1)}, u32[]{:S(2)}, u32[]{:S(2)}) collective-permute-start(bf16[192,512]{1,0:T(8,128)(2,1)S(1)} %get-tuple-element.42), channel_id=1, source_target_pairs={{0,48},{4,52},{8,56},{12,60},{16,0},{20,4},{24,8},{28,12},{32,16},... | collective-permute-start | bytes 589832 | tf_op jit(solution)/shard_map/ppermute | solution.py:53
  27.6 13.4 %collective-permute-start.7 = (bf16[192,512]{1,0:T(8,128)(2,1)S(1)}, bf16[192,512]{1,0:T(8,128)(2,1)S(1)}, u32[]{:S(2)}, u32[]{:S(2)}) collective-permute-start(bf16[192,512]{1,0:T(8,128)(2,1)S(1)} %get-tuple-element.40), channel_id=1, source_target_pairs={{0,32},{4,36},{8,40},{12,44},{16,48},{20,52},{24,56},{28,60},{32,0... | collective-permute-start | bytes 589832 | tf_op jit(solution)/shard_map/ppermute | solution.py:53
  42.6 41.9 %collective-permute-start.9 = (bf16[576,512]{1,0:T(8,128)(2,1)}, bf16[576,512]{1,0:T(8,128)(2,1)S(1)}, u32[]{:S(2)}, u32[]{:S(2)}) collective-permute-start(bf16[576,512]{1,0:T(8,128)(2,1)} %get-tuple-element.25), channel_id=1, source_target_pairs={{0,4},{4,8},{8,12},{12,0},{16,20},{20,24},{24,28},{28,16},{32,36},... | collective-permute-start | bytes 1769480 | tf_op jit(solution)/shard_map/ppermute | solution.py:53
  43.7 40.9 %collective-permute-start.10 = (bf16[576,512]{1,0:T(8,128)(2,1)}, bf16[576,512]{1,0:T(8,128)(2,1)S(1)}, u32[]{:S(2)}, u32[]{:S(2)}) collective-permute-start(bf16[576,512]{1,0:T(8,128)(2,1)} %get-tuple-element.26), channel_id=1, source_target_pairs={{0,8},{4,12},{8,0},{12,4},{16,24},{20,28},{24,16},{28,20},{32,40},... | collective-permute-start | bytes 1769480 | tf_op jit(solution)/shard_map/ppermute | solution.py:53
  46.5 38.1 %collective-permute-start.11 = (bf16[576,512]{1,0:T(8,128)(2,1)}, bf16[576,512]{1,0:T(8,128)(2,1)S(1)}, u32[]{:S(2)}, u32[]{:S(2)}) collective-permute-start(bf16[576,512]{1,0:T(8,128)(2,1)} %get-tuple-element.24), channel_id=1, source_target_pairs={{0,12},{4,0},{8,4},{12,8},{16,28},{20,16},{24,20},{28,24},{32,44},... | collective-permute-start | bytes 1769480 | tf_op jit(solution)/shard_map/ppermute | solution.py:53
  48.1 10.3 %collective-permute-start.1 = (bf16[32,5120]{1,0:T(8,128)(2,1)}, bf16[32,5120]{1,0:T(8,128)(2,1)}, u32[]{:S(2)}, u32[]{:S(2)}) collective-permute-start(bf16[32,5120]{1,0:T(8,128)(2,1)} %collective-permute-done), channel_id=1, source_target_pairs={{0,1},{1,2},{2,3},{3,0},{4,5},{5,6},{6,7},{7,4},{8,9},{9,10},{10,1... | collective-permute-start | bytes 983048 | tf_op jit(solution)/shard_map/ppermute | solution.py:40
  50.3 10.6 %collective-permute-start.4 = (bf16[64,32,128]{2,1,0:T(8,128)(2,1)}, bf16[64,32,128]{2,1,0:T(8,128)(2,1)S(1)}, u32[]{:S(2)}, u32[]{:S(2)}) collective-permute-start(bf16[64,32,128]{2,1,0:T(8,128)(2,1)} %all-to-all-done), channel_id=1, source_target_pairs={{0,64},{64,0},{1,65},{65,1},{2,66},{66,2},{3,67},{67,3},{4,68},{68... | collective-permute-start | bytes 1572872 | tf_op jit(solution)/shard_map/ppermute | solution.py:44
  63.4 11.7 %collective-permute-start.19 = (f32[32,9216]{1,0:T(8,128)S(1)}, f32[32,9216]{1,0:T(8,128)S(1)}, u32[]{:S(2)}, u32[]{:S(2)}) collective-permute-start(f32[32,9216]{1,0:T(8,128)S(1)} %pad_maximum_fusion.1), channel_id=1, source_target_pairs={{0,64},{64,0},{1,65},{65,1},{2,66},{66,2},{3,67},{67,3},{4,68},{68... | collective-permute-start | bytes 3538952 | tf_op jit(solution)/shard_map/ppermute | solution.py:44
  74.6 10.0 %collective-permute-start.3 = (bf16[128,2048]{1,0:T(8,128)(2,1)}, bf16[128,2048]{1,0:T(8,128)(2,1)}, u32[]{:S(2)}, u32[]{:S(2)}) collective-permute-start(bf16[128,2048]{1,0:T(8,128)(2,1)} %fusion.4.near), channel_id=1, source_target_pairs={{0,64},{64,0},{1,65},{65,1},{2,66},{66,2},{3,67},{67,3},{4,68},{68... | collective-permute-start | bytes 1572872 | tf_op jit(solution)/shard_map/ppermute | solution.py:44
  77.2 19.3 %all-to-all-start.1 = ((bf16[64,32,128]{2,1,0:T(8,128)(2,1)}), bf16[64,32,128]{2,1,0:T(8,128)(2,1)}, u32[]{:S(2)}, u32[]{:S(2)}) async-start(bf16[64,32,128]{2,1,0:T(8,128)(2,1)} %bitcast_bitcast_fusion), calls=%async_computation.1 | async-start | bytes 1048576 | tf_op jit(solution)/shard_map/all_to_all | solution.py:415
  88.6 13.2 %collective-permute-start.12 = (bf16[64,1152]{1,0:T(8,128)(2,1)}, bf16[64,1152]{1,0:T(8,128)(2,1)S(1)}, u32[]{:S(2)}, u32[]{:S(2)}) collective-permute-start(bf16[64,1152]{1,0:T(8,128)(2,1)} %get-tuple-element.14), channel_id=1, source_target_pairs={{0,3},{1,0},{2,1},{3,2},{4,7},{5,4},{6,5},{7,6},{8,11},{9,8},{10,9... | collective-permute-start | bytes 442376 | tf_op jit(solution)/shard_map/ppermute | solution.py:40
  91.2 12.4 %collective-permute-start.13 = (bf16[64,1152]{1,0:T(8,128)(2,1)}, bf16[64,1152]{1,0:T(8,128)(2,1)}, u32[]{:S(2)}, u32[]{:S(2)}) collective-permute-start(bf16[64,1152]{1,0:T(8,128)(2,1)} %get-tuple-element.15), channel_id=1, source_target_pairs={{0,2},{1,3},{2,0},{3,1},{4,6},{5,7},{6,4},{7,5},{8,10},{9,11},{10,... | collective-permute-start | bytes 442376 | tf_op jit(solution)/shard_map/ppermute | solution.py:40
  92.0 11.6 %collective-permute-start.14 = (bf16[64,1152]{1,0:T(8,128)(2,1)}, bf16[64,1152]{1,0:T(8,128)(2,1)}, u32[]{:S(2)}, u32[]{:S(2)}) collective-permute-start(bf16[64,1152]{1,0:T(8,128)(2,1)} %get-tuple-element.16), channel_id=1, source_target_pairs={{0,1},{1,2},{2,3},{3,0},{4,5},{5,6},{6,7},{7,4},{8,9},{9,10},{10,1... | collective-permute-start | bytes 442376 | tf_op jit(solution)/shard_map/ppermute | solution.py:40
  99.7 8.4 %collective-permute-start.22 = (f32[32,1024]{1,0:T(8,128)S(1)}, f32[32,1024]{1,0:T(8,128)S(1)}, u32[]{:S(2)}, u32[]{:S(2)}) collective-permute-start(f32[32,1024]{1,0:T(8,128)S(1)} %slice_add_fusion.1), channel_id=1, source_target_pairs={{0,3},{1,0},{2,1},{3,2},{4,7},{5,4},{6,5},{7,6},{8,11},{9,8},{10,9... | collective-permute-start | bytes 393224 | tf_op jit(solution)/shard_map/ppermute | solution.py:40
  100.4 9.9 %collective-permute-start.20 = (f32[32,1024]{1,0:T(8,128)S(1)}, f32[32,1024]{1,0:T(8,128)S(1)}, u32[]{:S(2)}, u32[]{:S(2)}) collective-permute-start(f32[32,1024]{1,0:T(8,128)S(1)} %slice_add_fusion.1), channel_id=1, source_target_pairs={{0,1},{1,2},{2,3},{3,0},{4,5},{5,6},{6,7},{7,4},{8,9},{9,10},{10,1... | collective-permute-start | bytes 393224 | tf_op jit(solution)/shard_map/ppermute | solution.py:40
  101.7 9.8 %collective-permute-start.21 = (f32[32,1024]{1,0:T(8,128)S(1)}, f32[32,1024]{1,0:T(8,128)S(1)}, u32[]{:S(2)}, u32[]{:S(2)}) collective-permute-start(f32[32,1024]{1,0:T(8,128)S(1)} %slice_add_fusion.1), channel_id=1, source_target_pairs={{0,2},{1,3},{2,0},{3,1},{4,6},{5,7},{6,4},{7,5},{8,10},{9,11},{10,... | collective-permute-start | bytes 393224 | tf_op jit(solution)/shard_map/ppermute | solution.py:40
  103.6 7.9 %collective-permute-start.18 = (bf16[128,64]{1,0:T(8,128)(2,1)S(1)}, bf16[128,64]{1,0:T(8,128)(2,1)S(1)}, u32[]{:S(2)}, u32[]{:S(2)}) collective-permute-start(bf16[128,64]{1,0:T(8,128)(2,1)S(1)} %convolution_convert_fusion.low_near), channel_id=1, source_target_pairs={{0,64},{64,0},{1,65},{65,1},{2,66},{66,2},{3,67},{67,3},{4,68},{68... | collective-permute-start | bytes 49160 | tf_op jit(solution)/shard_map/ppermute | solution.py:44
  106.2 6.1 %collective-permute-start.15 = (bf16[64,640]{1,0:T(8,128)(2,1)S(1)}, bf16[64,640]{1,0:T(8,128)(2,1)S(1)}, u32[]{:S(2)}, u32[]{:S(2)}) collective-permute-start(bf16[64,640]{1,0:T(8,128)(2,1)S(1)} %row_work.1.packed), channel_id=1, source_target_pairs={{0,1},{1,2},{2,3},{3,0},{4,5},{5,6},{6,7},{7,4},{8,9},{9,10},{10,1... | collective-permute-start | bytes 245768 | tf_op jit(solution)/shard_map/ppermute | solution.py:40
  108.1 6.8 %collective-permute-start.16 = (bf16[64,640]{1,0:T(8,128)(2,1)S(1)}, bf16[64,640]{1,0:T(8,128)(2,1)S(1)}, u32[]{:S(2)}, u32[]{:S(2)}) collective-permute-start(bf16[64,640]{1,0:T(8,128)(2,1)S(1)} %row_work.1.packed), channel_id=1, source_target_pairs={{0,2},{1,3},{2,0},{3,1},{4,6},{5,7},{6,4},{7,5},{8,10},{9,11},{10,... | collective-permute-start | bytes 245768 | tf_op jit(solution)/shard_map/ppermute | solution.py:40
  (18 other events, 196.8 us)
